TPU v7x, 32 devices: a whole 2x2x4 slice. The times are simulated.
32 devices in a mesh: groups: 2 (over x), ctx: 8 (over z, y), chan: 2 (over core).
Axes of the slice: x: 2, y: 2, z: 4, core: 2. Of those that a mesh axis runs over, the one named last changes fastest.
Arguments:
- tokens: int32 [4, 512], P('groups', 'ctx'), parts along dimension 0, may hold values from 0 to 511
- embed_table: bfloat16 [512, 4096], replicated, may hold values from -8 to 8
- norm_gain: float32 [4096], replicated, may hold values from 0.1 to 1.9
- input_proj: bfloat16 [4096, 3, 2048], P('ctx', None, 'chan'), may hold values from -0.09375 to 0.09375
- short_filter: float32 [3, 128, 3], P(None, 'chan'), may hold values from -3.5 to 3.5
- pole_rate: float32 [128, 16], P('chan'), may hold values from 0.0005859375 to 0.2
- residue: float32 [128, 16], P('chan'), may hold values from -1.5 to 1.5
- skip_gain: float32 [2048], P('chan'), may hold values from -3 to 3
- output_proj: bfloat16 [2048, 4096], P('chan', 'ctx'), may hold values from -0.125 to 0.125
Outputs:
- block_out: bfloat16 [4, 512, 4096], P('groups', 'ctx', 'chan'), parts along dimension 0
There are 2 independent parts, one for each index of `groups`. A program takes and returns all parts, laid end to end along the dimension named above; an argument that names none is the same for every part. Nothing has to cross between parts.
All inputs are finite; a program needn't handle non-finite values.
Results may differ from a plain program's by a relative error of at most 0.0078.
Values may be sent and summed in bfloat16 or wider, within the bound.
No kernel may reach another device: no remote copies, remote signals or barrier semaphores. Data moves between devices by JAX's collectives and lax.ppermute only.
A program may use at most 128 MiB of HBM per device.

v0:
```python
import jax
import jax.numpy as jnp
from jax import lax
from jax.sharding import PartitionSpec as P

epsilon = 1e-06
highest = lax.Precision.HIGHEST


def passed_along(shard, axis, by):
    count = lax.axis_size(axis)
    pairs = [(i, i + by) for i in range(count) if 0 <= i + by < count]
    return lax.ppermute(shard, axis, pairs)


def entering(shard, axis, combine, identity):
    count, mine = (lax.axis_size(axis), lax.axis_index(axis))
    everything = jax.tree.map(lambda part: lax.all_gather(part, axis), shard)
    start = jax.tree.map(
        lambda part, zero: jnp.broadcast_to(jnp.asarray(zero, part.dtype), part.shape),
        shard,
        identity,
    )

    def hop(k, before):
        reached = k < mine
        new = combine(before, jax.tree.map(lambda part: part[k], everything))
        return jax.tree.map(lambda a, b: jnp.where(reached, a, b), new, before)

    return lax.fori_loop(0, count, hop, start)


def local_block(operands):
    rising, falling, inputs = operands
    length = rising.shape[2]
    toeplitz = jnp.einsum("gnt,gns->gts", rising, falling, precision=highest)
    causal = jnp.arange(length)[:, None] >= jnp.arange(length)[None, :]
    toeplitz = jnp.where(causal[None], toeplitz, 0.0)
    return jnp.einsum("gms,gts->gmt", inputs, toeplitz, precision=highest)


def lookup_rows(token_block, embed_table):
    vocab_count = embed_table.shape[0]
    onehot = (token_block[:, None] == jnp.arange(vocab_count, dtype=jnp.int32)[None, :]).astype(
        jnp.bfloat16
    )
    return jnp.dot(onehot, embed_table, preferred_element_type=jnp.float32)


def body(
    tokens,
    embed_table,
    norm_gain,
    input_proj,
    short_filter,
    pole_rate,
    residue,
    skip_gain,
    output_proj,
):
    genome_count, row_count = tokens.shape
    part_rows, branch_count, channels = input_proj.shape
    groups = pole_rate.shape[0]
    group_size = channels // groups
    tap_count = short_filter.shape[2]
    flat_count = genome_count * row_count
    flat_tokens = tokens.reshape(flat_count)
    widened = lookup_rows(flat_tokens, embed_table)
    inv_rms = lax.rsqrt(jnp.mean(widened * widened, axis=-1, keepdims=True) + epsilon)
    normed = (widened * inv_rms * norm_gain).astype(jnp.bfloat16)
    proj_cols = branch_count * channels
    flat_weight = input_proj.reshape(part_rows, proj_cols)
    spread = lax.all_to_all(normed, "ctx", split_axis=1, concat_axis=0, tiled=True)
    summed = lax.psum_scatter(
        jnp.dot(spread, flat_weight, preferred_element_type=jnp.float32),
        "ctx",
        scatter_dimension=0,
        tiled=True,
    )
    projected = summed.astype(jnp.bfloat16).reshape(genome_count, row_count, branch_count, channels)
    rim = passed_along(projected[:, row_count - (tap_count - 1) :], "ctx", 1)
    extended = jnp.concatenate([rim, projected], axis=1).astype(jnp.float32)
    taps_full = jnp.broadcast_to(
        short_filter[:, :, None, :], (branch_count, groups, group_size, tap_count)
    ).reshape(branch_count, channels, tap_count)
    filtered = jnp.zeros((genome_count, row_count, branch_count, channels), jnp.float32)
    for lag in range(tap_count):
        first_row = tap_count - 1 - lag
        filtered = filtered + taps_full[:, :, lag] * extended[:, first_row : first_row + row_count]
    query_part = filtered[:, :, 0]
    product = filtered[:, :, 1] * filtered[:, :, 2]
    mixes = genome_count * group_size
    grouped = (
        product.reshape(genome_count, row_count, groups, group_size)
        .transpose(2, 0, 3, 1)
        .reshape(groups, mixes, row_count)
    )
    positions = jnp.arange(row_count, dtype=jnp.float32)
    middle = float(row_count // 2)
    powers = jnp.exp(-pole_rate[:, :, None] * positions)
    next_powers = jnp.exp(-pole_rate[:, :, None] * (positions + 1.0))
    pole_amp = residue * jnp.sqrt(-jnp.expm1(-2.0 * pole_rate))
    rising = pole_amp[:, :, None] * jnp.exp(-pole_rate[:, :, None] * (positions - middle))
    falling = jnp.exp(-pole_rate[:, :, None] * (middle - positions))
    block_size = 8
    blocks = groups // block_size
    poles = pole_rate.shape[1]
    local_part = lax.map(
        local_block,
        (
            rising.reshape(blocks, block_size, poles, row_count),
            falling.reshape(blocks, block_size, poles, row_count),
            grouped.reshape(blocks, block_size, mixes, row_count),
        ),
    )
    local_part = local_part.reshape(groups, mixes, row_count)
    end_state = jnp.einsum("gms,gns->gmn", grouped, powers[:, :, ::-1], precision=highest)
    block_decay = jnp.exp(-pole_rate * row_count)

    def combine(earlier, later):
        return (earlier[0] * later[0], later[0][:, None, :] * earlier[1] + later[1])

    identity = (jnp.ones_like(block_decay), jnp.zeros_like(end_state))
    incoming = entering((block_decay, end_state), "ctx", combine, identity)[1]
    weighted = incoming * pole_amp[:, None, :]
    correction = jnp.einsum("gmn,gnt->gmt", weighted, next_powers, precision=highest)
    long_conv = (
        (local_part + correction)
        .reshape(groups, genome_count, group_size, row_count)
        .transpose(1, 3, 0, 2)
        .reshape(genome_count, row_count, channels)
    )
    gated = (
        (query_part * (long_conv + skip_gain * product))
        .astype(jnp.bfloat16)
        .reshape(flat_count, channels)
    )
    partial_value = jnp.dot(
        gated,
        lax.all_gather(output_proj, "ctx", axis=1, tiled=True),
        preferred_element_type=jnp.float32,
    )
    own_share = lax.psum_scatter(partial_value, "chan", scatter_dimension=1, tiled=True)
    half_width = own_share.shape[1]
    residual_part = lax.dynamic_slice_in_dim(
        widened, lax.axis_index("chan") * half_width, half_width, 1
    )
    block_out = (residual_part + own_share).astype(jnp.bfloat16)
    return block_out.reshape(genome_count, row_count, half_width)


def solution(mesh):
    return jax.shard_map(
        body,
        mesh=mesh,
        in_specs=(
            P("groups", "ctx"),
            P(),
            P(),
            P("ctx", None, "chan"),
            P(None, "chan", None),
            P("chan", None),
            P("chan", None),
            P("chan"),
            P("chan", "ctx"),
        ),
        out_specs=P("groups", "ctx", "chan"),
        check_vma=False,
    )
```

profile of v0, /device:TPU:0, one launch (start us, length us, event | category | flops | bytes accessed | tf_op | source)
XLA Modules:
  0.0 502.3 jit_solution(10771387078758091748)
XLA Ops:
  7.3 3.0 multiply_reduce_fusion
  11.7 7.3 %all-to-all-start = ((bf16[128,8,512]{2,0,1:T(8,128)(2,1)}), bf16[128,8,512]{2,0,1:T(8,128)(2,1)S(1)}, u32[]{:S(2)}, u32[]{:S(2)}) async-start(bf16[128,8,512]{2,0,1:T(8,128)(2,1)} %bitcast.64), calls=%async_computation | async-start | bytes 2097152 | tf_op jit(solution)/shard_map/all_to_all | solution.py:73
  19.0 4.7 copy.61
  23.7 21.0 %all-to-all-done = bf16[128,8,512]{2,0,1:T(8,128)(2,1)S(1)} async-done(((bf16[128,8,512]{2,0,1:T(8,128)(2,1)}), bf16[128,8,512]{2,0,1:T(8,128)(2,1)S(1)}, u32[]{:S(2)}, u32[]{:S(2)}) %all-to-all-start) | async-done | bytes 1048608 | tf_op jit(solution)/shard_map/all_to_all | solution.py:73
  44.8 8.3 %fusion.22 = f32[1024,3072]{1,0:T(8,128)} fusion(bf16[1024,512]{1,0:T(8,128)(2,1)S(1)} %bitcast.92, bf16[512,3072]{0,1:T(8,128)(2,1)} %bitcast.88), kind=kOutput, calls=%fused_computation.54 | convolution fusion | flops 3221225472 | bytes 16777216 | tf_op jit(solution)/shard_map/dot_general | solution.py:75
  55.8 203.9 %reduce-scatter.3.cloned.1.call-done = f32[128,3072]{1,0:T(8,128)} async-done(((f32[1024,3072]{1,0:T(8,128)}), f32[128,3072]{1,0:T(8,128)}) %reduce-scatter.3.cloned.1.call-update) | async-done | bytes 1572880 | tf_op jit(solution)/shard_map/reduce_scatter | solution.py:74
  259.6 2.4 convert_element_type.18
  262.0 2.7 reshape.90
  264.8 3.4 collective-permute-start
  268.2 2.0 rev.3
  271.6 1.8 slice_multiply_fusion.3
  273.3 1.3 copy.62
  274.6 1.4 copy.63
  276.0 3.6 fusion.23
  280.6 31.0 %all-gather.2 = f32[8,64,16]{1,2,0:T(8,128)S(1)} all-gather(f32[1,64,16]{1,2,0:T(8,128)S(1)} %copy.66), channel_id=2, replica_groups=mesh['groups'=2,'ctx'=8,'chan'=2] {'ctx'}, dimensions={0}, use_global_device_ids=true | all-gather | bytes 36864 | tf_op jit(solution)/shard_map/all_gather | solution.py:18
  311.6 2.1 multiply_exponential_fusion.1
  313.7 2.0 copy.77
  315.7 2.0 copy.71
  317.7 1.9 copy.76
  319.7 2.0 copy.72
  321.7 21.5 %while.24 = (s32[]{:T(128)}, f32[8,8,32,64]{3,2,1,0:T(8,128)}, f32[8,8,32,64]{3,2,1,0:T(8,128)S(1)}, f32[8,8,16,64]{3,2,1,0:T(8,128)}, f32[8,8,16,64]{3,2,1,0:T(8,128)}, /*index=5*/s32[]{:T(128)}) while((s32[]{:T(128)}, f32[8,8,32,64]{3,2,1,0:T(8,128)}, f32[8,8,32,64]{3,2,1,0:T(8,128)S(1)}, f32[8,8,16,64]{3,2,1,0:T(8,128)}, ...), condition=%wide.region_3.4_spmd, body=%wide.region_2.3_spmd.sunk | while | flops 18911232 | bytes 796741 | solution.py:108
  321.7 1.5 convolution_select_fusion.2
  323.2 1.2 fusion.42
  324.4 1.5 convolution_select_fusion.2
  325.9 1.2 fusion.42
  327.1 1.5 convolution_select_fusion.2
  328.6 1.2 fusion.42
  329.8 1.5 convolution_select_fusion.2
  331.3 1.2 fusion.42
  332.5 1.5 convolution_select_fusion.2
  333.9 1.2 fusion.42
  335.1 1.5 convolution_select_fusion.2
  336.6 1.2 fusion.42
  337.8 1.5 convolution_select_fusion.2
  339.3 1.2 fusion.42
  340.5 1.5 convolution_select_fusion.2
  342.0 1.2 fusion.42
  343.2 10.0 %all-gather.8.cloned.1.call-done = f32[512,32,16]{1,2,0:T(8,128)} async-done(((f32[64,32,16]{1,2,0:T(8,128)}), f32[512,32,16]{1,2,0:T(8,128)}) %all-gather.8.cloned.1.call-update) | async-done | bytes 1048592 | tf_op jit(solution)/shard_map/all_gather | solution.py:18
  353.1 4.5 copy.68
  357.6 9.6 %while.25 = (s32[]{:T(128)}, f32[64,32,16]{0,2,1:T(8,128)S(1)}, s32[]{:T(128)}, f32[8,64,16]{1,2,0:T(8,128)S(1)}, f32[8,64,32,16]{1,3,2,0:T(8,128)}, /*index=5*/s32[]{:T(128)}, s32[]{:T(128)}) while((s32[]{:T(128)}, f32[64,32,16]{0,2,1:T(8,128)S(1)}, s32[]{:T(128)}, f32[8,64,16]{1,2,0:T(8,128)S(1)}, f32[8,64,32,16]{1,3,2,0:T(8,128)}, ...), condition=%wide.region_5.6_spmd.clone, body=%wide.region_4.5_spmd.clone.sunk | while | flops 131076 | bytes 405609 | solution.py:30
  360.0 1.2 fusion.43
  361.2 1.2 fusion.43
  367.5 3.2 convolution_add_fusion
  371.3 1.4 reshape.94
  372.7 106.2 %all-gather.6.cloned.1.call-done = bf16[1024,4096]{1,0:T(8,128)(2,1)} async-done(((bf16[1024,512]{1,0:T(8,128)(2,1)}), bf16[1024,4096]{1,0:T(8,128)(2,1)}) %all-gather.6.cloned.1.call-update) | async-done | bytes 8388624 | tf_op jit(solution)/shard_map/all_gather | solution.py:140
  479.0 6.7 %fusion.14 = f32[128,4096]{1,0:T(8,128)} fusion(bf16[1024,4096]{1,0:T(8,128)(2,1)} %all-gather.6.cloned.1.call-done, f32[128,1024]{0,1:T(8,128)} %copy.72, f32[128,1024]{0,1:T(8,128)} %reshape.94, f32[128,1024]{0,1:T(8,128)} %copy.71, f32[1024]{0:T(1024)S(1)} %copy-done.1), kind=kOutput, calls=%fused_computation.34 | convolution fusion | flops 1074266112 | bytes 12062720 | tf_op jit(solution)/shard_map/dot_general | solution.py:138
  485.6 7.9 %reduce-scatter.5.cloned.1.call-done = f32[128,2048]{1,0:T(8,128)} async-done(((f32[128,4096]{1,0:T(8,128)}), f32[128,2048]{1,0:T(8,128)}) %reduce-scatter.5.cloned.1.call-update) | async-done | bytes 1048592 | tf_op jit(solution)/shard_map/reduce_scatter | solution.py:143
  493.6 2.1 add_convert_fusion
  (68 shorter events, 15.1 us)
Async XLA Ops:
  7.3 3.1 copy-start.3
  11.7 33.0 %all-to-all-start = ((bf16[128,8,512]{2,0,1:T(8,128)(2,1)}), bf16[128,8,512]{2,0,1:T(8,128)(2,1)S(1)}, u32[]{:S(2)}, u32[]{:S(2)}) async-start(bf16[128,8,512]{2,0,1:T(8,128)(2,1)} %bitcast.64), calls=%async_computation | async-start | bytes 2097152 | tf_op jit(solution)/shard_map/all_to_all | solution.py:73
  19.0 240.6 %reduce-scatter.3.cloned.1.call-start = ((), (), s32[]{:S(2)}) async-start(), calls=%async_computation.3 | async-start | bytes 14155776 | tf_op jit(solution)/shard_map/reduce_scatter | solution.py:74
  53.0 0.7 copy-start.5
  53.0 1.0 copy-start.2
  53.1 300.1 %all-gather.8.cloned.1.call-start = ((), (), s32[]{:S(2)}) async-start(), calls=%async_computation.6 | async-start | bytes 4718592 | tf_op jit(solution)/shard_map/all_gather | solution.py:18
  264.8 5.5 %collective-permute-start = (bf16[2,2,3,1024]{3,2,1,0:T(4,128)(2,1)S(1)}, bf16[2,2,3,1024]{3,2,1,0:T(4,128)(2,1)S(1)}, u32[]{:S(2)}, u32[]{:S(2)}) collective-permute-start(bf16[2,2,3,1024]{3,2,1,0:T(4,128)(2,1)S(1)} %slice.41), channel_id=1, source_target_pairs={{0,2},{2,4},{4,6},{6,8},{8,10},{10,12},{12,14},{1,3},{3,5},{5,7},{... | collective-permute-start | bytes 73736 | tf_op jit(solution)/shard_map/ppermute | solution.py:13
  273.3 1.3 copy-start
  275.9 4.5 copy-start.4
  279.6 199.3 %all-gather.6.cloned.1.call-start = ((), (), s32[]{:S(2)}) async-start(), calls=%async_computation.4 | async-start | bytes 9437184 | tf_op jit(solution)/shard_map/all_gather | solution.py:140
  280.4 213.2 %reduce-scatter.5.cloned.1.call-start = ((), (), s32[]{:S(2)}) async-start(), calls=%async_computation.5 | async-start | bytes 3145728 | tf_op jit(solution)/shard_map/reduce_scatter | solution.py:143
  370.8 108.2 %copy-start.1 = (f32[1024]{0:T(1024)S(1)}, f32[1024]{0:T(1024)}, u32[]{:S(2)}) copy-start(f32[1024]{0:T(1024)} %param.20) | copy-start | bytes 12292
Sparse Core Ops, SparseCore 0:
  53.2 206.4 reduce-scatter.2
  279.8 73.3 all-gather.7
  355.2 123.7 all-gather.5
  485.8 7.7 reduce-scatter.4
where the time goes:
time: 504 us; the launch traced here: 502 us
  waiting for transfers between devices  350 us (69%)
  matrix products  46.2 us (9%)
  blocking collectives  31 us (6%)
  local copies, waits for them, and re-layouts  29.9 us (6%)
  other arithmetic  21 us (4%)
  between operations  13.3 us (3%)
  starting transfers between devices  10.8 us (2%)
    reduce_scatter x1, waiting for transfers between devices, body(): lax.psum_scatter(jnp.dot(spread, flat_weight, preferred_element_type=jnp....  204 us
    all_gather x1, waiting for transfers between devices, body(): lax.all_gather(output_proj, 'ctx', axis=1, tiled=True)  106 us
    all_gather x1, blocking collectives, entering(): everything = jax.tree.map(lambda part: lax.all_gather(part, axis), shard)  31 us
    all_to_all x1, waiting for transfers between devices, body(): lax.all_to_all(normed, 'ctx', split_axis=1, concat_axis=0, tiled=True)  21 us
    unnamed x20, local copies, waits for them, and re-layouts  13.9 us
    dot_general x8, matrix products, local_block(): toeplitz = jnp.einsum('gnt,gns->gts', rising, falling, precision=highest)  11.9 us
  transfers between devices with their start and end apart: 6, of which 5 were waited for; matrix products, arithmetic and copies ran while one was open for 12% of the time, Pallas kernels for 0%

commit v1 on v0

--- a/solution.py
+++ b/solution.py
@@ -1,10 +1,19 @@
+import functools
+
 import jax
 import jax.numpy as jnp
 from jax import lax
+from jax.experimental import pallas as pl
+from jax.experimental.pallas import tpu as pltpu
 from jax.sharding import PartitionSpec as P
 
 epsilon = 1e-06
 highest = lax.Precision.HIGHEST
+f32 = jnp.float32
+bf16 = jnp.bfloat16
+CHUNK = 128
+LANES = 128
+VMEM_LIMIT = 48 * 1024 * 1024
 
 
 def passed_along(shard, axis, by):
@@ -47,7 +56,7 @@
     return jnp.dot(onehot, embed_table, preferred_element_type=jnp.float32)
 
 
-def body(
+def general_body(
     tokens,
     embed_table,
     norm_gain,
@@ -149,9 +158,364 @@
     return block_out.reshape(genome_count, row_count, half_width)
 
 
+def swapped(value, axis, mask):
+    count = lax.axis_size(axis)
+    return lax.ppermute(value, axis, [(i, i ^ mask) for i in range(count)])
+
+
+def swapped_both(value, ctx_mask):
+    count, cores = lax.axis_size("ctx"), lax.axis_size("chan")
+    pairs = [
+        (i * cores + c, (i ^ ctx_mask) * cores + (c ^ 1)) for i in range(count) for c in range(cores)
+    ]
+    return lax.ppermute(value, ("ctx", "chan"), pairs)
+
+
+def split(value):
+    high = value.astype(bf16)
+    return high, (value - high.astype(f32)).astype(bf16)
+
+
+def dot3(a_high, a_low, b):
+    b_high, b_low = split(b)
+    total = jnp.dot(a_high, b_high, preferred_element_type=f32)
+    total += jnp.dot(a_low, b_high, preferred_element_type=f32)
+    return total + jnp.dot(a_high, b_low, preferred_element_type=f32)
+
+
+def lane_half(shape):
+    return lax.broadcasted_iota(jnp.int32, shape, len(shape) - 1) < LANES // 2
+
+
+def half_turn(value):
+    return pltpu.roll(value, LANES // 2, value.ndim - 1)
+
+
+def filter_kernel(rate_ref, rate_col_ref, amp_ref, high_ref, low_ref, ends_high_ref, ends_low_ref, fade_ref):
+    square = (CHUNK, LANES)
+    rate, amp = rate_ref[...], amp_ref[...]
+    row = lax.broadcasted_iota(jnp.int32, square, 0)
+    col = lax.broadcasted_iota(jnp.int32, square, 1)
+    place = row.astype(f32)
+    middle = float(CHUNK // 2)
+    rising = amp * jnp.exp(-rate * (place - middle))
+    falling = jnp.exp(-rate * (middle - place))
+    poles = 16
+    count = LANES // poles
+    for g in range(count):
+        own = jnp.where(col // poles == g, falling, 0.0)
+        block = lax.dot_general(
+            rising, own, (((1,), (1,)), ((), ())), precision=highest, preferred_element_type=f32
+        )
+        block = jnp.where(row >= col, block, 0.0)
+        high, low = split(block)
+        high_ref[:, g * CHUNK : (g + 1) * CHUNK] = high
+        low_ref[:, g * CHUNK : (g + 1) * CHUNK] = low
+    high, low = split(amp * jnp.exp(-rate * (place + 1.0)))
+    high_ref[:, count * CHUNK :] = high
+    low_ref[:, count * CHUNK :] = low
+    rate_col = rate_col_ref[...]
+    high, low = split(jnp.exp(-rate_col * (float(CHUNK - 1) - col.astype(f32))))
+    ends_high_ref[...] = high
+    ends_low_ref[...] = low
+    fade_ref[...] = jnp.exp(-rate_col * float(CHUNK)) + jnp.zeros(square, f32)
+
+
+def partial_kernel(place_ref, normed_ref, *refs):
+    weight_refs, (keep_ref, send_ref) = refs[:-2], refs[-2:]
+    quad, half = place_ref[0], place_ref[1]
+    depth = weight_refs[0].shape[1]
+    rows = normed_ref.shape[0]
+    for j in range(weight_refs[0].shape[0]):
+        total = jnp.zeros((rows, LANES), f32)
+        for m, weight_ref in enumerate(weight_refs):
+            first = pl.multiple_of((quad ^ m) * depth, depth)
+            total += jnp.dot(
+                normed_ref[:, pl.ds(first, depth)], weight_ref[j], preferred_element_type=f32
+            )
+        total = jnp.where(half == 0, total, half_turn(total))
+        top, bottom = total[: rows // 2], total[rows // 2 :]
+        left = lane_half(top.shape)
+        keep_ref[j] = jnp.where(left, top, half_turn(bottom))
+        send_ref[j] = jnp.where(left, half_turn(top), bottom).astype(bf16)
+
+
+def conv_kernel(
+    place_ref, token_ref, own_ref, other_ref, taps_ref, skip_ref, high_ref, low_ref, ends_high_ref, ends_low_ref, fade_ref, out_ref, *, genomes
+):
+    group = place_ref[2]
+    branches, half_vocab, _ = own_ref.shape
+    positions = token_ref.shape[0]
+    length = positions // genomes
+    vocab = lax.broadcasted_iota(jnp.int32, (positions, 2 * half_vocab), 1)
+    picked = (token_ref[...] == vocab).astype(f32).astype(bf16)
+    row = lax.broadcasted_iota(jnp.int32, (positions, LANES), 0) % length
+    filtered = []
+    for j in range(branches):
+        mine, theirs = own_ref[j].astype(f32), other_ref[j].astype(f32)
+        first = jnp.where(group == 0, mine, theirs)
+        second = jnp.where(group == 0, theirs, mine)
+        left = lane_half(first.shape)
+        top = jnp.where(left, first, half_turn(second))
+        bottom = jnp.where(left, half_turn(first), second)
+        table = jnp.concatenate([top, bottom], axis=0).astype(bf16)
+        now = jnp.dot(picked, table, preferred_element_type=f32)
+        total = taps_ref[3 * j : 3 * j + 1] * now
+        for lag in (1, 2):
+            late = jnp.where(row >= lag, pltpu.roll(now, lag, 0), 0.0)
+            total += taps_ref[3 * j + lag : 3 * j + lag + 1] * late
+        filtered.append(total)
+    query = filtered[0]
+    product = filtered[1] * filtered[2]
+    size = 16
+    count = LANES // size
+    width = genomes * LANES
+    lane = lax.broadcasted_iota(jnp.int32, (CHUNK, width), 1) % LANES
+    pole_row = lax.broadcasted_iota(jnp.int32, (LANES, width), 0)
+    same = pole_row // size == (lax.broadcasted_iota(jnp.int32, (LANES, width), 1) % LANES) // size
+    fade = jnp.concatenate([fade_ref[...]] * genomes, axis=1)
+    state = jnp.zeros((LANES, width), f32)
+    chunks = length // CHUNK
+    for c in range(chunks):
+        spans = [slice(b * length + c * CHUNK, b * length + (c + 1) * CHUNK) for b in range(genomes)]
+        block = jnp.concatenate([product[span] for span in spans], axis=1)
+        stacked = jnp.concatenate(
+            [jnp.where(lane // size == g, block, 0.0) for g in range(count)] + [state], axis=0
+        )
+        conv = dot3(high_ref[...], low_ref[...], stacked)
+        for b, span in enumerate(spans):
+            value = conv[:, b * LANES : (b + 1) * LANES] + skip_ref[...] * product[span]
+            out_ref[span, :] = (query[span] * value).astype(bf16)
+        if c < chunks - 1:
+            ends = dot3(ends_high_ref[...], ends_low_ref[...], block)
+            state = fade * state + jnp.where(same, ends, 0.0)
+
+
+def output_kernel(place_ref, token_ref, rows_ref, far_rows_ref, *refs):
+    piece_refs, (near_own, near_far, core_own, core_far, out_ref) = refs[:4], refs[4:]
+    quad, half, core = place_ref[0], place_ref[1], place_ref[3]
+    count = token_ref.shape[0]
+    vocab = lax.broadcasted_iota(jnp.int32, (count, rows_ref.shape[0]), 1)
+    picked = (token_ref[...] == vocab).astype(f32).astype(bf16)
+    block = 2 * LANES
+    joined = []
+    for piece_ref in piece_refs:
+        pair = []
+        for other_core in (0, 1):
+            near = piece_ref[other_core].astype(f32)
+            far = piece_ref[2 + other_core].astype(f32)
+            first = jnp.where(half == 0, near, far)
+            second = jnp.where(half == 0, far, near)
+            left = lane_half(first.shape)
+            pair.append(
+                jnp.concatenate(
+                    [
+                        jnp.where(left, first, half_turn(second)),
+                        jnp.where(left, half_turn(first), second),
+                    ],
+                    axis=1,
+                ).astype(bf16)
+            )
+        joined.append(pair)
+    for far, (table_ref, weights) in enumerate(
+        ((rows_ref, (near_own, core_own)), (far_rows_ref, (near_far, core_far)))
+    ):
+        total = jnp.dot(picked, table_ref[...], preferred_element_type=f32)
+        mixed = jnp.zeros(total.shape, f32)
+        for m in range(4):
+            first = pl.multiple_of((quad ^ m) * block, block)
+            for other_core in (0, 1):
+                mixed += jnp.dot(
+                    joined[m][other_core],
+                    weights[other_core][pl.ds(first, block), :],
+                    preferred_element_type=f32,
+                )
+        out_ref[half ^ far ^ core] = (total + mixed).astype(bf16)
+
+
+def place_kernel(place_ref, *refs):
+    piece_refs, out_ref = refs[:4], refs[4]
+    quad, core = place_ref[0], place_ref[3]
+    width = piece_refs[0].shape[2]
+    for m, piece_ref in enumerate(piece_refs):
+        first = pl.multiple_of((quad ^ m) * width, width)
+        for g in (0, 1):
+            out_ref[core ^ g, :, pl.ds(first, width)] = piece_ref[g]
+
+
+def called(kernel, out_shape, scalars, *operands, flops=0, moved=0):
+    smem = pl.BlockSpec(memory_space=pltpu.SMEM)
+    vmem = pl.BlockSpec(memory_space=pltpu.VMEM)
+    many = isinstance(out_shape, (list, tuple))
+    return pl.pallas_call(
+        kernel,
+        out_shape=out_shape,
+        in_specs=[smem] * len(scalars) + [vmem] * len(operands),
+        out_specs=[vmem] * len(out_shape) if many else vmem,
+        compiler_params=pltpu.CompilerParams(vmem_limit_bytes=VMEM_LIMIT),
+        cost_estimate=pl.CostEstimate(flops=flops, bytes_accessed=moved, transcendentals=0),
+    )(*scalars, *operands)
+
+
+def shaped(*shape, dtype=f32):
+    return jax.ShapeDtypeStruct(shape, dtype)
+
+
+def quad_body(
+    tokens,
+    embed_table,
+    norm_gain,
+    input_proj,
+    short_filter,
+    pole_rate,
+    residue,
+    skip_gain,
+    output_proj,
+):
+    genomes, rows = tokens.shape
+    depth, branches, channels = input_proj.shape
+    vocab, features = embed_table.shape
+    tap_count = short_filter.shape[2]
+    poles = pole_rate.shape[1]
+    members = lax.axis_size("ctx") // 2
+    ctx, core, group = (lax.axis_index(name) for name in ("ctx", "chan", "groups"))
+    quad, half = ctx % members, ctx // members
+    place = jnp.stack([quad, half, group, core]).astype(jnp.int32)
+    block = channels // members
+
+    weights = input_proj.transpose(1, 0, 2)
+
+    def columns(member):
+        return lax.dynamic_slice_in_dim(weights, member * block + group * LANES, LANES, 2)
+
+    gathered = [columns(quad)] + [swapped(columns(quad ^ m), "ctx", m) for m in range(1, members)]
+
+    near = jnp.concatenate([tokens, swapped(tokens, "ctx", members)], axis=0)
+    all_tokens = [near] + [swapped(near, "ctx", m) for m in range(1, members)]
+    stacked = jnp.stack(all_tokens).reshape(members, 2, genomes, rows)
+    order = jnp.arange(members) ^ quad
+    stacked = stacked[order][:, jnp.arange(2) ^ half]
+    group_tokens = stacked.transpose(2, 1, 0, 3).reshape(genomes, 2 * members * rows)
+    length = group_tokens.shape[1]
+
+    widened = embed_table.astype(f32)
+    inv_rms = lax.rsqrt(jnp.mean(widened * widened, axis=-1, keepdims=True) + epsilon)
+    part = features // 2
+    own_half = lax.dynamic_slice_in_dim(embed_table, half * part, part, 1).astype(f32)
+    own_gain = lax.dynamic_slice_in_dim(norm_gain, half * part, part, 0)
+    normed = (own_half * inv_rms * own_gain).astype(bf16)
+
+    def own_rows(array, axis):
+        per = array.shape[axis] // (members * 4)
+        first = quad * 4 * per + half * per
+        return jnp.concatenate(
+            [lax.dynamic_slice_in_dim(array, first + i * 2 * per, per, axis) for i in (0, 1)], axis
+        )
+
+    own_rate, own_residue = own_rows(pole_rate, 0), own_rows(residue, 0)
+    own_amp = own_residue * jnp.sqrt(-jnp.expm1(-2.0 * own_rate))
+    own_skip = own_rows(skip_gain, 0).reshape(1, LANES)
+    own_taps = jnp.repeat(own_rows(short_filter, 1).transpose(0, 2, 1), LANES // own_rate.shape[0], axis=2)
+    own_taps = own_taps.reshape(branches * tap_count, LANES)
+    filters = called(
+        filter_kernel,
+        [
+            shaped(CHUNK, 9 * CHUNK, dtype=bf16),
+            shaped(CHUNK, 9 * CHUNK, dtype=bf16),
+            shaped(LANES, CHUNK, dtype=bf16),
+            shaped(LANES, CHUNK, dtype=bf16),
+            shaped(LANES, LANES),
+        ],
+        (),
+        own_rate.reshape(1, LANES),
+        own_rate.reshape(LANES, 1),
+        own_amp.reshape(1, LANES),
+    )
+
+    keep, send = called(
+        partial_kernel,
+        [shaped(branches, vocab // 2, LANES), shaped(branches, vocab // 2, LANES, dtype=bf16)],
+        (place,),
+        normed,
+        *gathered,
+        flops=2 * vocab * part * branches * LANES,
+        moved=4 << 20,
+    )
+    summed = (keep + swapped(send, "ctx", members).astype(f32)).astype(bf16)
+    other = swapped(summed, "groups", 1)
+
+    gated = called(
+        functools.partial(conv_kernel, genomes=genomes),
+        shaped(genomes * length, LANES, dtype=bf16),
+        (place,),
+        group_tokens.reshape(genomes * length, 1),
+        summed,
+        other,
+        own_taps,
+        own_skip,
+        *filters,
+    ).reshape(genomes, 2, length // 2, LANES)
+
+    def span(genome, part_index):
+        return lax.dynamic_slice(
+            gated, (genome, part_index, 0, 0), (1, 1, length // 2, LANES)
+        ).reshape(length // 2, LANES)
+
+    piece = jnp.stack(
+        [
+            span(core, half),
+            swapped(span(core ^ 1, half), "chan", 1),
+            swapped(span(core, half ^ 1), "ctx", members),
+            swapped_both(span(core ^ 1, half ^ 1), members),
+        ]
+    )
+    pieces = [piece] + [swapped(piece, "ctx", m) for m in range(1, members)]
+
+    half_rows = output_proj.shape[0] // 2
+    fetched = swapped(
+        lax.dynamic_slice_in_dim(output_proj, group * half_rows, half_rows, 0), "ctx", members
+    )
+    shared = swapped(fetched, "groups", 1)
+    far_proj = jnp.where(
+        group == 0,
+        jnp.concatenate([fetched, shared], axis=0),
+        jnp.concatenate([shared, fetched], axis=0),
+    )
+    core_own = swapped(output_proj, "chan", 1)
+    core_far = swapped(far_proj, "chan", 1)
+
+    width = output_proj.shape[1]
+    own_tokens = lax.dynamic_slice(
+        group_tokens, (core, half * (length // 2)), (1, length // 2)
+    ).reshape(length // 2, 1)
+    results = called(
+        output_kernel,
+        shaped(2, length // 2, width, dtype=bf16),
+        (place,),
+        own_tokens,
+        lax.dynamic_slice_in_dim(embed_table, ctx * width, width, 1),
+        lax.dynamic_slice_in_dim(embed_table, (ctx ^ members) * width, width, 1),
+        *pieces,
+        output_proj,
+        far_proj,
+        core_own,
+        core_far,
+    )
+    both = jnp.stack([results[0], swapped(results[1], "chan", 1)])
+
+    def rows_of(member):
+        return lax.dynamic_slice_in_dim(both, member * rows, rows, 1)
+
+    arrived = [rows_of(quad)] + [swapped(rows_of(quad ^ m), "ctx", m) for m in range(1, members)]
+    return called(
+        place_kernel, shaped(genomes, rows, members * width, dtype=bf16), (place,), *arrived
+    )
+
+
 def solution(mesh):
+    sizes = tuple(mesh.shape[name] for name in ("groups", "ctx", "chan"))
     return jax.shard_map(
-        body,
+        quad_body if sizes == (2, 8, 2) else general_body,
         mesh=mesh,
         in_specs=(
             P("groups", "ctx"),

time: 504 us -> 106 us (0.21)
  waiting for transfers between devices: 350 us -> 47.4 us
  matrix products: 46.2 us -> 0 us
  blocking collectives: 31 us -> 0 us
  local copies, waits for them, and re-layouts: 29.9 us -> 10.7 us
  starting transfers between devices: 10.8 us -> 28.4 us
  other arithmetic: 21 us -> 6.12 us
  between operations: 13.3 us -> 0.34 us
  Pallas kernels: 0 us -> 12.6 us
    reduce_scatter x2 -> x0, waiting for transfers between devices: 212 us -> none  [the longest x1 204 us: body(): lax.psum_scatter(jnp.dot(spread, flat_weight, preferred_element_type=jnp....]
    all_gather x2 -> x0, waiting for transfers between devices: 116 us -> none  [the longest x1 106 us: body(): lax.all_gather(output_proj, 'ctx', axis=1, tiled=True)]
    ppermute x1 -> x23, waiting for transfers between devices: 0.01 us -> 47.4 us  [the longest x22 46.9 us: swapped(): return lax.ppermute(value, axis, [(i, i ^ mask) for i in range(count)])]
    dot_general x21 -> x0, matrix products: 46.2 us -> none  [the longest x8 11.9 us: local_block(): toeplitz = jnp.einsum('gnt,gns->gts', rising, falling, precision=highest)]
    all_gather x1 -> x0, blocking collectives: 31 us -> none  [entering(): everything = jax.tree.map(lambda part: lax.all_gather(part, axis), shard)]
    ppermute x1 -> x23, starting transfers between devices: 3.38 us -> 28.4 us  [the longest x22 26.7 us: swapped(): return lax.ppermute(value, axis, [(i, i ^ mask) for i in range(count)])]
    all_to_all x1 -> x0, waiting for transfers between devices: 21 us -> none  [body(): lax.all_to_all(normed, 'ctx', split_axis=1, concat_axis=0, tiled=True)]
    unnamed x20 -> x12, local copies, waits for them, and re-layouts: 13.9 us -> 0.02 us
  transfers between devices with their start and end apart: 6 -> 23, of which waited for: 5 -> 13; matrix products, arithmetic and copies ran while one was open for 12% -> 13% of each run, Pallas kernels for 0% -> 7%
where the time goes in v1:
time: 106 us
  waiting for transfers between devices  47.4 us (45%)
  starting transfers between devices  28.4 us (27%)
  Pallas kernels  12.6 us (12%)
  local copies, waits for them, and re-layouts  10.7 us (10%)
  other arithmetic  6.12 us (6%)
    ppermute x22, waiting for transfers between devices, swapped(): return lax.ppermute(value, axis, [(i, i ^ mask) for i in range(count)])  46.9 us
    ppermute x22, starting transfers between devices, swapped(): return lax.ppermute(value, axis, [(i, i ^ mask) for i in range(count)])  26.7 us
    pallas_call x5, Pallas kernels, called(): pl.pallas_call(kernel, out_shape=out_shape, in_specs=[smem] * len(scalars...  12.6 us
    reduce_sum x1, other arithmetic, quad_body(): jnp.mean(widened * widened, axis=-1, keepdims=True) + epsilon  3.38 us
    dynamic_slice x1, local copies, waits for them, and re-layouts, columns(): lax.dynamic_slice_in_dim(weights, member * block + group * LANES, LANES, 2)  2.49 us
  transfers between devices with their start and end apart: 23, of which 13 were waited for; matrix products, arithmetic and copies ran while one was open for 13% of the time, Pallas kernels for 7%

profile of v1, /device:TPU:0, one launch (start us, length us, event | category | flops | bytes accessed | tf_op | source)
XLA Modules:
  0.0 105.7 jit_solution(7792253054529762546)
XLA Ops:
  0.0 2.5 %dynamic-slice_bitcast_fusion = (bf16[3,512,128]{2,1,0:T(8,128)(2,1)}, bf16[3,512,128]{2,1,0:T(8,128)(2,1)}, bf16[3,512,128]{2,1,0:T(8,128)(2,1)S(1)}, bf16[3,512,128]{2,1,0:T(8,128)(2,1)}) fusion(bf16[512,3,1024]{2,0,1:T(8,128)(2,1)} %param.12, s32[]{:T(128)S(6)} %select_n.124, s32[]{:T(128)S(6)} %select_n.122, s32[]{:T(128)S(6)} %select_n.121, ...), kind=kLoop, calls=%fused_computation.14 | loop fusion | bytes 3145744 | tf_op jit(solution)/shard_map/dynamic_slice | solution.py:389
  2.5 3.0 %collective-permute-start.4 = (bf16[3,512,128]{2,1,0:T(8,128)(2,1)}, bf16[3,512,128]{2,1,0:T(8,128)(2,1)S(1)}, u32[]{:S(2)}, u32[]{:S(2)}) collective-permute-start(bf16[3,512,128]{2,1,0:T(8,128)(2,1)} %get-tuple-element.22), channel_id=1, source_target_pairs={{0,2},{2,0},{4,6},{6,4},{8,10},{10,8},{12,14},{14,12},{1,3},{3,1},... | collective-permute-start | bytes 1179656 | tf_op jit(solution)/shard_map/ppermute | solution.py:163
  5.5 1.6 %collective-permute-start.5 = (bf16[3,512,128]{2,1,0:T(8,128)(2,1)}, bf16[3,512,128]{2,1,0:T(8,128)(2,1)S(1)}, u32[]{:S(2)}, u32[]{:S(2)}) collective-permute-start(bf16[3,512,128]{2,1,0:T(8,128)(2,1)} %get-tuple-element.24), channel_id=1, source_target_pairs={{0,4},{2,6},{4,0},{6,2},{8,12},{10,14},{12,8},{14,10},{1,5},{3,7},... | collective-permute-start | bytes 1179656 | tf_op jit(solution)/shard_map/ppermute | solution.py:163
  7.1 1.1 %constant_dynamic-slice_fusion = bf16[512,512]{1,0:T(8,128)(2,1)S(1)} fusion(bf16[1024,512]{1,0:T(8,128)(2,1)} %refs_4_.1, s32[]{:T(128)S(6)} %select_n.133), kind=kLoop, calls=%fused_computation.31 | loop fusion | bytes 1048580 | tf_op jit(solution)/shard_map/dynamic_slice | solution.py:476
  8.1 3.0 %collective-permute-start.15 = (bf16[512,512]{1,0:T(8,128)(2,1)S(1)}, bf16[512,512]{1,0:T(8,128)(2,1)S(1)}, u32[]{:S(2)}, u32[]{:S(2)}) collective-permute-start(bf16[512,512]{1,0:T(8,128)(2,1)S(1)} %constant_dynamic-slice_fusion), channel_id=1, source_target_pairs={{0,8},{2,10},{4,12},{6,14},{8,0},{10,2},{12,4},{14,6},{1,9},{3,11}... | collective-permute-start | bytes 1572872 | tf_op jit(solution)/shard_map/ppermute | solution.py:163
  11.8 0.6 pad_clamp_fusion.1
  12.4 0.6 pad_clamp_fusion
  13.2 0.9 fusion.6
  14.2 3.4 %multiply_reduce_fusion = f32[512]{0:T(512)S(1)} fusion(bf16[512,4096]{1,0:T(8,128)(2,1)} %param.10), kind=kLoop, calls=%fused_computation.2 | loop fusion | flops 6290944 | bytes 4196352 | tf_op jit(solution)/shard_map/reduce_sum | solution.py:402
  17.6 17.5 %collective-permute-done.15 = bf16[512,512]{1,0:T(8,128)(2,1)S(1)} collective-permute-done((bf16[512,512]{1,0:T(8,128)(2,1)S(1)}, bf16[512,512]{1,0:T(8,128)(2,1)S(1)}, u32[]{:S(2)}, u32[]{:S(2)}) %collective-permute-start.15) | collective-permute-done | bytes 524320 | tf_op jit(solution)/shard_map/ppermute | solution.py:163
  35.0 1.5 %collective-permute-start.16 = (bf16[512,512]{1,0:T(8,128)(2,1)S(1)}, bf16[512,512]{1,0:T(8,128)(2,1)S(1)}, u32[]{:S(2)}, u32[]{:S(2)}) collective-permute-start(bf16[512,512]{1,0:T(8,128)(2,1)S(1)} %collective-permute-done.15), channel_id=1, source_target_pairs={{0,16},{16,0},{1,17},{17,1},{2,18},{18,2},{3,19},{19,3},{4,20},{20... | collective-permute-start | bytes 1572872 | tf_op jit(solution)/shard_map/ppermute | solution.py:163
  36.5 0.5 multiply_convert_fusion.normed_ref
  37.1 3.4 %collective-permute-start = (s32[2,64]{1,0:T(2,128)S(1)}, s32[2,64]{1,0:T(2,128)S(1)}, u32[]{:S(2)}, u32[]{:S(2)}) collective-permute-start(s32[2,64]{1,0:T(2,128)S(1)} %copy-done.5), channel_id=1, source_target_pairs={{0,8},{2,10},{4,12},{6,14},{8,0},{10,2},{12,4},{14,6},{1,9},{3,11}... | collective-permute-start | bytes 1544 | tf_op jit(solution)/shard_map/ppermute | solution.py:163
  40.6 2.5 %shard_map.91 = (f32[3,256,128]{2,1,0:T(8,128)S(1)}, bf16[3,256,128]{2,1,0:T(8,128)(2,1)S(1)}) custom-call(s32[4]{0:T(128)S(1)} %pad_add_fusion.2.place_ref, bf16[512,2048]{1,0:T(8,128)(2,1)S(1)} %multiply_convert_fusion.normed_ref, bf16[3,512,128]{2,1,0:T(8,128)(2,1)S(1)} %get-tuple-element.23.refs_0_, ...), custom_call_target="tpu_custom_call" | custom-call | flops 805306368 | bytes 4194304 | tf_op jit(solution)/shard_map/pallas_call | solution.py:350
  43.2 4.3 %collective-permute-done.16 = bf16[512,512]{1,0:T(8,128)(2,1)S(1)} collective-permute-done((bf16[512,512]{1,0:T(8,128)(2,1)S(1)}, bf16[512,512]{1,0:T(8,128)(2,1)S(1)}, u32[]{:S(2)}, u32[]{:S(2)}) %collective-permute-start.16) | collective-permute-done | bytes 524320 | tf_op jit(solution)/shard_map/ppermute | solution.py:163
  47.5 0.5 maximum_select_fusion.refs_5_
  48.1 0.6 collective-permute-start.1
  48.7 3.4 %collective-permute-start.2 = (s32[4,64]{1,0:T(4,128)S(1)}, s32[4,64]{1,0:T(4,128)S(1)}, u32[]{:S(2)}, u32[]{:S(2)}) collective-permute-start(s32[4,64]{1,0:T(4,128)S(1)} %pad_add_fusion.1), channel_id=1, source_target_pairs={{0,4},{2,6},{4,0},{6,2},{8,12},{10,14},{12,8},{14,10},{1,5},{3,7},... | collective-permute-start | bytes 3080 | tf_op jit(solution)/shard_map/ppermute | solution.py:163
  52.1 0.9 collective-permute-done.7
  53.2 1.6 %collective-permute-start.8 = (bf16[3,256,128]{2,1,0:T(8,128)(2,1)S(1)}, bf16[3,256,128]{2,1,0:T(8,128)(2,1)}, u32[]{:S(2)}, u32[]{:S(2)}) collective-permute-start(bf16[3,256,128]{2,1,0:T(8,128)(2,1)S(1)} %add_convert_fusion.own_ref), channel_id=1, source_target_pairs={{0,16},{16,0},{1,17},{17,1},{2,18},{18,2},{3,19},{19,3},{4,20},{20... | collective-permute-start | bytes 589832 | tf_op jit(solution)/shard_map/ppermute | solution.py:163
  55.0 1.2 %shard_map.92 = (bf16[128,1152]{1,0:T(8,128)(2,1)S(1)}, bf16[128,1152]{1,0:T(8,128)(2,1)S(1)}, bf16[128,128]{1,0:T(8,128)(2,1)S(1)}, bf16[128,128]{1,0:T(8,128)(2,1)S(1)}, f32[128,128]{1,0:T(8,128)S(1)}) custom-call(f32[1,128]{1,0:T(1,128)S(1)} %reshape.110.rate_ref, f32[128,1]{1,0:T(8,128)S(1)} %reshape.132.rate_col_ref, f32[1,128]{1,0:T(1,128)S(1)} %sqrt_multiply_fusion.amp_ref), custom_call_target="tpu_custom_call" | custom-call | tf_op jit(solution)/shard_map/pallas_call | solution.py:350
  56.3 1.2 %collective-permute-done.3 = s32[4,64]{1,0:T(4,128)S(1)} collective-permute-done((s32[4,64]{1,0:T(4,128)S(1)}, s32[4,64]{1,0:T(4,128)S(1)}, u32[]{:S(2)}, u32[]{:S(2)}) %collective-permute-start.3) | collective-permute-done | bytes 1056 | tf_op jit(solution)/shard_map/ppermute | solution.py:163
  57.5 0.7 gather_fusion
  58.2 0.7 gather_fusion.1
  58.9 0.6 copy.22
  59.5 1.2 %reshape_reshape.8.token_ref = s32[1024,1]{1,0:T(8,128)S(1)} reshape(s32[2,2,4,64]{3,2,1,0:T(4,128)} %copy.22) | data formatting | bytes 8192 | tf_op jit(solution)/shard_map/reshape;reshape | solution.py:451
  60.7 4.1 %shard_map.93 = bf16[1024,128]{1,0:T(8,128)(2,1)S(1)} custom-call(s32[4]{0:T(128)S(1)} %pad_add_fusion.2.place_ref, s32[1024,1]{1,0:T(8,128)S(1)} %reshape_reshape.8.token_ref, bf16[3,256,128]{2,1,0:T(8,128)(2,1)S(1)} %add_convert_fusion.own_ref, bf16[3,256,128]{2,1,0:T(8,128)(2,1)} %collective-permute-done.8.other_ref, ...), custom_call_target="tpu_custom_call" | custom-call | tf_op jit(solution)/shard_map/pallas_call | solution.py:350
  64.9 1.1 %collective-permute-start.10 = (bf16[256,128]{1,0:T(8,128)(2,1)S(1)}, bf16[256,128]{1,0:T(8,128)(2,1)S(1)}, u32[]{:S(2)}, u32[]{:S(2)}) collective-permute-start(bf16[256,128]{1,0:T(8,128)(2,1)S(1)} %get-tuple-element.33), channel_id=1, source_target_pairs={{0,8},{2,10},{4,12},{6,14},{8,0},{10,2},{12,4},{14,6},{1,9},{3,11}... | collective-permute-start | bytes 196616 | tf_op jit(solution)/shard_map/ppermute | solution.py:163
  66.0 1.7 %collective-permute-start.11 = (bf16[256,128]{1,0:T(8,128)(2,1)S(1)}, bf16[256,128]{1,0:T(8,128)(2,1)S(1)}, u32[]{:S(2)}, u32[]{:S(2)}) collective-permute-start(bf16[256,128]{1,0:T(8,128)(2,1)S(1)} %get-tuple-element.32), channel_id=1, source_target_pairs={{0,9},{1,8},{2,11},{3,10},{4,13},{5,12},{6,15},{7,14},{8,1},{9,0},... | collective-permute-start | bytes 196616 | tf_op jit(solution)/shard_map/ppermute | solution.py:171
  67.7 5.9 %collective-permute-done.10 = bf16[256,128]{1,0:T(8,128)(2,1)S(1)} collective-permute-done((bf16[256,128]{1,0:T(8,128)(2,1)S(1)}, bf16[256,128]{1,0:T(8,128)(2,1)S(1)}, u32[]{:S(2)}, u32[]{:S(2)}) %collective-permute-start.10) | collective-permute-done | bytes 65568 | tf_op jit(solution)/shard_map/ppermute | solution.py:163
  73.6 0.5 collective-permute-done.11
  74.1 0.8 collective-permute-start.12
  74.9 2.8 %collective-permute-start.14 = (bf16[4,256,128]{2,1,0:T(8,128)(2,1)S(1)}, bf16[4,256,128]{2,1,0:T(8,128)(2,1)}, u32[]{:S(2)}, u32[]{:S(2)}) collective-permute-start(bf16[4,256,128]{2,1,0:T(8,128)(2,1)S(1)} %pad_maximum_fusion.refs_0_), channel_id=1, source_target_pairs={{0,6},{2,4},{4,2},{6,0},{8,14},{10,12},{12,10},{14,8},{1,7},{3,5},... | collective-permute-start | bytes 786440 | tf_op jit(solution)/shard_map/ppermute | solution.py:163
  77.7 1.3 %constant_dynamic-slice_fusion.7 = (bf16[512,512]{1,0:T(8,128)(2,1)S(1)}, bf16[512,512]{1,0:T(8,128)(2,1)S(1)}) fusion(bf16[512,4096]{1,0:T(8,128)(2,1)} %param.10, s32[]{:T(128)S(6)} %select_n.119, s32[]{:T(128)S(6)} %select_n.118), kind=kLoop, calls=%fused_computation.38 | loop fusion | bytes 2097160 | tf_op jit(solution)/shard_map/dynamic_slice | solution.py:497
  79.0 0.8 reshape.107
  79.8 0.1 copy.29.token_ref
  80.0 2.8 %collective-permute-done.12.refs_1_ = bf16[4,256,128]{2,1,0:T(8,128)(2,1)} collective-permute-done((bf16[4,256,128]{2,1,0:T(8,128)(2,1)S(1)}, bf16[4,256,128]{2,1,0:T(8,128)(2,1)}, u32[]{:S(2)}, u32[]{:S(2)}) %collective-permute-start.12) | collective-permute-done | bytes 262176 | tf_op jit(solution)/shard_map/ppermute | solution.py:163
  82.8 1.4 %collective-permute-done.13.refs_2_ = bf16[4,256,128]{2,1,0:T(8,128)(2,1)} collective-permute-done((bf16[4,256,128]{2,1,0:T(8,128)(2,1)S(1)}, bf16[4,256,128]{2,1,0:T(8,128)(2,1)}, u32[]{:S(2)}, u32[]{:S(2)}) %collective-permute-start.13) | collective-permute-done | bytes 262176 | tf_op jit(solution)/shard_map/ppermute | solution.py:163
  84.2 5.4 %collective-permute-done.14.refs_3_ = bf16[4,256,128]{2,1,0:T(8,128)(2,1)} collective-permute-done((bf16[4,256,128]{2,1,0:T(8,128)(2,1)S(1)}, bf16[4,256,128]{2,1,0:T(8,128)(2,1)}, u32[]{:S(2)}, u32[]{:S(2)}) %collective-permute-start.14) | collective-permute-done | bytes 262176 | tf_op jit(solution)/shard_map/ppermute | solution.py:163
  89.6 3.4 %shard_map.94 = bf16[2,256,512]{2,1,0:T(8,128)(2,1)S(1)} custom-call(s32[4]{0:T(128)S(1)} %pad_add_fusion.2.place_ref, s32[256,1]{1,0:T(8,128)S(1)} %copy.29.token_ref, bf16[512,512]{1,0:T(8,128)(2,1)S(1)} %get-tuple-element.20.rows_ref, bf16[512,512]{1,0:T(8,128)(2,1)S(1)} %get-tuple-element.19.far_rows_ref, ...), custom_call_target="tpu_custom_call" | custom-call | tf_op jit(solution)/shard_map/pallas_call | solution.py:350
  93.1 1.5 %collective-permute-done.19 = bf16[256,512]{1,0:T(8,128)(2,1)S(1)} collective-permute-done((bf16[256,512]{1,0:T(8,128)(2,1)S(1)}, bf16[256,512]{1,0:T(8,128)(2,1)S(1)}, u32[]{:S(2)}, u32[]{:S(2)}) %collective-permute-start.19) | collective-permute-done | bytes 262176 | tf_op jit(solution)/shard_map/ppermute | solution.py:163
  94.7 0.7 collective-permute-start.20
  95.4 0.3 collective-permute-start.21
  95.7 2.6 %collective-permute-start.22 = (bf16[2,64,512]{2,1,0:T(8,128)(2,1)S(1)}, bf16[2,64,512]{2,1,0:T(8,128)(2,1)S(1)}, u32[]{:S(2)}, u32[]{:S(2)}) collective-permute-start(bf16[2,64,512]{2,1,0:T(8,128)(2,1)S(1)} %get-tuple-element.25), channel_id=1, source_target_pairs={{0,6},{2,4},{4,2},{6,0},{8,14},{10,12},{12,10},{14,8},{1,7},{3,5},... | collective-permute-start | bytes 393224 | tf_op jit(solution)/shard_map/ppermute | solution.py:163
  98.2 2.0 %collective-permute-done.20.refs_1_ = bf16[2,64,512]{2,1,0:T(8,128)(2,1)S(1)} collective-permute-done((bf16[2,64,512]{2,1,0:T(8,128)(2,1)S(1)}, bf16[2,64,512]{2,1,0:T(8,128)(2,1)S(1)}, u32[]{:S(2)}, u32[]{:S(2)}) %collective-permute-start.20) | collective-permute-done | bytes 131104 | tf_op jit(solution)/shard_map/ppermute | solution.py:163
  100.3 1.5 %collective-permute-done.21.refs_2_ = bf16[2,64,512]{2,1,0:T(8,128)(2,1)S(1)} collective-permute-done((bf16[2,64,512]{2,1,0:T(8,128)(2,1)S(1)}, bf16[2,64,512]{2,1,0:T(8,128)(2,1)S(1)}, u32[]{:S(2)}, u32[]{:S(2)}) %collective-permute-start.21) | collective-permute-done | bytes 131104 | tf_op jit(solution)/shard_map/ppermute | solution.py:163
  101.8 2.5 %collective-permute-done.22.refs_3_ = bf16[2,64,512]{2,1,0:T(8,128)(2,1)S(1)} collective-permute-done((bf16[2,64,512]{2,1,0:T(8,128)(2,1)S(1)}, bf16[2,64,512]{2,1,0:T(8,128)(2,1)S(1)}, u32[]{:S(2)}, u32[]{:S(2)}) %collective-permute-start.22) | collective-permute-done | bytes 131104 | tf_op jit(solution)/shard_map/ppermute | solution.py:163
  104.3 1.4 %shard_map.95 = bf16[2,64,2048]{2,1,0:T(8,128)(2,1)} custom-call(s32[4]{0:T(128)S(1)} %pad_add_fusion.2.place_ref, bf16[2,64,512]{2,1,0:T(8,128)(2,1)S(1)} %get-tuple-element.26.refs_0_, bf16[2,64,512]{2,1,0:T(8,128)(2,1)S(1)} %collective-permute-done.20.refs_1_, bf16[2,64,512]{2,1,0:T(8,128)(2,1)S(1)} %collective-permute-done.21.refs_2_, ...), custom_call_target="tpu_custom_call" | custom-call | tf_op jit(solution)/shard_map/pallas_call | solution.py:350
  (59 shorter events, 1.8 us)
Async XLA Ops:
  0.0 11.2 %copy-start.3 = (f32[64,16]{0,1:T(8,128)S(1)}, f32[64,16]{0,1:T(8,128)}, u32[]{:S(2)}) copy-start(f32[64,16]{0,1:T(8,128)} %param.14) | copy-start | bytes 12292
  0.0 11.2 %copy-start.2 = (f32[64,16]{0,1:T(8,128)S(1)}, f32[64,16]{0,1:T(8,128)}, u32[]{:S(2)}) copy-start(f32[64,16]{0,1:T(8,128)} %param.15) | copy-start | bytes 12292
  0.0 13.0 %copy-start.4 = (f32[3,64,3]{1,2,0:T(4,128)S(1)}, f32[3,64,3]{1,2,0:T(4,128)}, u32[]{:S(2)}) copy-start(f32[3,64,3]{1,2,0:T(4,128)} %param.13) | copy-start | bytes 6916
  2.5 34.6 %collective-permute-start.4 = (bf16[3,512,128]{2,1,0:T(8,128)(2,1)}, bf16[3,512,128]{2,1,0:T(8,128)(2,1)S(1)}, u32[]{:S(2)}, u32[]{:S(2)}) collective-permute-start(bf16[3,512,128]{2,1,0:T(8,128)(2,1)} %get-tuple-element.22), channel_id=1, source_target_pairs={{0,2},{2,0},{4,6},{6,4},{8,10},{10,8},{12,14},{14,12},{1,3},{3,1},... | collective-permute-start | bytes 1179656 | tf_op jit(solution)/shard_map/ppermute | solution.py:163
  5.5 35.1 %collective-permute-start.5 = (bf16[3,512,128]{2,1,0:T(8,128)(2,1)}, bf16[3,512,128]{2,1,0:T(8,128)(2,1)S(1)}, u32[]{:S(2)}, u32[]{:S(2)}) collective-permute-start(bf16[3,512,128]{2,1,0:T(8,128)(2,1)} %get-tuple-element.24), channel_id=1, source_target_pairs={{0,4},{2,6},{4,0},{6,2},{8,12},{10,14},{12,8},{14,10},{1,5},{3,7},... | collective-permute-start | bytes 1179656 | tf_op jit(solution)/shard_map/ppermute | solution.py:163
  7.1 33.5 %collective-permute-start.6 = (bf16[3,512,128]{2,1,0:T(8,128)(2,1)}, bf16[3,512,128]{2,1,0:T(8,128)(2,1)S(1)}, u32[]{:S(2)}, u32[]{:S(2)}) collective-permute-start(bf16[3,512,128]{2,1,0:T(8,128)(2,1)} %get-tuple-element.21), channel_id=1, source_target_pairs={{0,6},{2,4},{4,2},{6,0},{8,14},{10,12},{12,10},{14,8},{1,7},{3,5},... | collective-permute-start | bytes 1179656 | tf_op jit(solution)/shard_map/ppermute | solution.py:163
  7.1 72.9 %collective-permute-start.17 = (bf16[1024,512]{1,0:T(8,128)(2,1)}, bf16[1024,512]{1,0:T(8,128)(2,1)}, u32[]{:S(2)}, u32[]{:S(2)}) collective-permute-start(bf16[1024,512]{1,0:T(8,128)(2,1)} %refs_4_.1), channel_id=1, source_target_pairs={{0,1},{1,0},{2,3},{3,2},{4,5},{5,4},{6,7},{7,6},{8,9},{9,8},{10,11... | collective-permute-start | bytes 3145736 | tf_op jit(solution)/shard_map/ppermute | solution.py:163
  8.1 26.9 %collective-permute-start.15 = (bf16[512,512]{1,0:T(8,128)(2,1)S(1)}, bf16[512,512]{1,0:T(8,128)(2,1)S(1)}, u32[]{:S(2)}, u32[]{:S(2)}) collective-permute-start(bf16[512,512]{1,0:T(8,128)(2,1)S(1)} %constant_dynamic-slice_fusion), channel_id=1, source_target_pairs={{0,8},{2,10},{4,12},{6,14},{8,0},{10,2},{12,4},{14,6},{1,9},{3,11}... | collective-permute-start | bytes 1572872 | tf_op jit(solution)/shard_map/ppermute | solution.py:163
  13.1 23.5 %dynamic-slice-start = ((f32[4096]{0:T(1024)}, s32[]{:T(128)}), f32[2048]{0:T(1024)S(1)}, s32[]{:S(2)}) async-start(f32[4096]{0:T(1024)} %param.11, s32[]{:T(128)} %select_n.120), calls=%async_computation | async-start | bytes 16896 | tf_op jit(solution)/shard_map/dynamic_slice | solution.py:405
  13.2 23.4 %copy-start.1 = (bf16[512,4096]{1,0:T(8,128)(2,1)S(1)}, bf16[512,4096]{1,0:T(8,128)(2,1)}, u32[]{:S(2)}) copy-start(bf16[512,4096]{1,0:T(8,128)(2,1)} %param.10) | copy-start | bytes 12582916
  14.2 22.9 %copy-start.5 = (s32[2,64]{1,0:T(2,128)S(1)}, s32[2,64]{1,0:T(2,128)}, u32[]{:S(2)}) copy-start(s32[2,64]{1,0:T(2,128)} %param.9) | copy-start | bytes 1540
  35.0 12.5 %collective-permute-start.16 = (bf16[512,512]{1,0:T(8,128)(2,1)S(1)}, bf16[512,512]{1,0:T(8,128)(2,1)S(1)}, u32[]{:S(2)}, u32[]{:S(2)}) collective-permute-start(bf16[512,512]{1,0:T(8,128)(2,1)S(1)} %collective-permute-done.15), channel_id=1, source_target_pairs={{0,16},{16,0},{1,17},{17,1},{2,18},{18,2},{3,19},{19,3},{4,20},{20... | collective-permute-start | bytes 1572872 | tf_op jit(solution)/shard_map/ppermute | solution.py:163
  37.1 10.9 %collective-permute-start = (s32[2,64]{1,0:T(2,128)S(1)}, s32[2,64]{1,0:T(2,128)S(1)}, u32[]{:S(2)}, u32[]{:S(2)}) collective-permute-start(s32[2,64]{1,0:T(2,128)S(1)} %copy-done.5), channel_id=1, source_target_pairs={{0,8},{2,10},{4,12},{6,14},{8,0},{10,2},{12,4},{14,6},{1,9},{3,11}... | collective-permute-start | bytes 1544 | tf_op jit(solution)/shard_map/ppermute | solution.py:163
  43.1 46.5 %copy-start = (bf16[1024,512]{1,0:T(8,128)(2,1)S(1)}, bf16[1024,512]{1,0:T(8,128)(2,1)}, u32[]{:S(2)}) copy-start(bf16[1024,512]{1,0:T(8,128)(2,1)} %refs_4_.1) | copy-start | bytes 3145732
  43.1 9.9 %collective-permute-start.7 = (bf16[3,256,128]{2,1,0:T(8,128)(2,1)S(1)}, bf16[3,256,128]{2,1,0:T(8,128)(2,1)S(1)}, u32[]{:S(2)}, u32[]{:S(2)}) collective-permute-start(bf16[3,256,128]{2,1,0:T(8,128)(2,1)S(1)} %get-tuple-element.13), channel_id=1, source_target_pairs={{0,8},{2,10},{4,12},{6,14},{8,0},{10,2},{12,4},{14,6},{1,9},{3,11}... | collective-permute-start | bytes 589832 | tf_op jit(solution)/shard_map/ppermute | solution.py:163
  48.0 41.6 %collective-permute-start.18 = (bf16[1024,512]{1,0:T(8,128)(2,1)S(1)}, bf16[1024,512]{1,0:T(8,128)(2,1)}, u32[]{:S(2)}, u32[]{:S(2)}) collective-permute-start(bf16[1024,512]{1,0:T(8,128)(2,1)S(1)} %maximum_select_fusion.refs_5_), channel_id=1, source_target_pairs={{0,1},{1,0},{2,3},{3,2},{4,5},{5,4},{6,7},{7,6},{8,9},{9,8},{10,11... | collective-permute-start | bytes 3145736 | tf_op jit(solution)/shard_map/ppermute | solution.py:163
  48.1 5.1 %collective-permute-start.1 = (s32[4,64]{1,0:T(4,128)S(1)}, s32[4,64]{1,0:T(4,128)S(1)}, u32[]{:S(2)}, u32[]{:S(2)}) collective-permute-start(s32[4,64]{1,0:T(4,128)S(1)} %pad_add_fusion.1), channel_id=1, source_target_pairs={{0,2},{2,0},{4,6},{6,4},{8,10},{10,8},{12,14},{14,12},{1,3},{3,1},... | collective-permute-start | bytes 3080 | tf_op jit(solution)/shard_map/ppermute | solution.py:163
  48.7 7.6 %collective-permute-start.2 = (s32[4,64]{1,0:T(4,128)S(1)}, s32[4,64]{1,0:T(4,128)S(1)}, u32[]{:S(2)}, u32[]{:S(2)}) collective-permute-start(s32[4,64]{1,0:T(4,128)S(1)} %pad_add_fusion.1), channel_id=1, source_target_pairs={{0,4},{2,6},{4,0},{6,2},{8,12},{10,14},{12,8},{14,10},{1,5},{3,7},... | collective-permute-start | bytes 3080 | tf_op jit(solution)/shard_map/ppermute | solution.py:163
  53.0 4.5 %collective-permute-start.3 = (s32[4,64]{1,0:T(4,128)S(1)}, s32[4,64]{1,0:T(4,128)S(1)}, u32[]{:S(2)}, u32[]{:S(2)}) collective-permute-start(s32[4,64]{1,0:T(4,128)S(1)} %pad_add_fusion.1), channel_id=1, source_target_pairs={{0,6},{2,4},{4,2},{6,0},{8,14},{10,12},{12,10},{14,8},{1,7},{3,5},... | collective-permute-start | bytes 3080 | tf_op jit(solution)/shard_map/ppermute | solution.py:163
  53.2 7.5 %collective-permute-start.8 = (bf16[3,256,128]{2,1,0:T(8,128)(2,1)S(1)}, bf16[3,256,128]{2,1,0:T(8,128)(2,1)}, u32[]{:S(2)}, u32[]{:S(2)}) collective-permute-start(bf16[3,256,128]{2,1,0:T(8,128)(2,1)S(1)} %add_convert_fusion.own_ref), channel_id=1, source_target_pairs={{0,16},{16,0},{1,17},{17,1},{2,18},{18,2},{3,19},{19,3},{4,20},{20... | collective-permute-start | bytes 589832 | tf_op jit(solution)/shard_map/ppermute | solution.py:163
  64.9 2.8 %collective-permute-start.9 = (bf16[256,128]{1,0:T(8,128)(2,1)S(1)}, bf16[256,128]{1,0:T(8,128)(2,1)S(1)}, u32[]{:S(2)}, u32[]{:S(2)}) collective-permute-start(bf16[256,128]{1,0:T(8,128)(2,1)S(1)} %get-tuple-element.34), channel_id=1, source_target_pairs={{0,1},{1,0},{2,3},{3,2},{4,5},{5,4},{6,7},{7,6},{8,9},{9,8},{10,11... | collective-permute-start | bytes 196616 | tf_op jit(solution)/shard_map/ppermute | solution.py:163
  64.9 8.7 %collective-permute-start.10 = (bf16[256,128]{1,0:T(8,128)(2,1)S(1)}, bf16[256,128]{1,0:T(8,128)(2,1)S(1)}, u32[]{:S(2)}, u32[]{:S(2)}) collective-permute-start(bf16[256,128]{1,0:T(8,128)(2,1)S(1)} %get-tuple-element.33), channel_id=1, source_target_pairs={{0,8},{2,10},{4,12},{6,14},{8,0},{10,2},{12,4},{14,6},{1,9},{3,11}... | collective-permute-start | bytes 196616 | tf_op jit(solution)/shard_map/ppermute | solution.py:163
  66.0 8.1 %collective-permute-start.11 = (bf16[256,128]{1,0:T(8,128)(2,1)S(1)}, bf16[256,128]{1,0:T(8,128)(2,1)S(1)}, u32[]{:S(2)}, u32[]{:S(2)}) collective-permute-start(bf16[256,128]{1,0:T(8,128)(2,1)S(1)} %get-tuple-element.32), channel_id=1, source_target_pairs={{0,9},{1,8},{2,11},{3,10},{4,13},{5,12},{6,15},{7,14},{8,1},{9,0},... | collective-permute-start | bytes 196616 | tf_op jit(solution)/shard_map/ppermute | solution.py:171
  74.1 8.7 %collective-permute-start.12 = (bf16[4,256,128]{2,1,0:T(8,128)(2,1)S(1)}, bf16[4,256,128]{2,1,0:T(8,128)(2,1)}, u32[]{:S(2)}, u32[]{:S(2)}) collective-permute-start(bf16[4,256,128]{2,1,0:T(8,128)(2,1)S(1)} %pad_maximum_fusion.refs_0_), channel_id=1, source_target_pairs={{0,2},{2,0},{4,6},{6,4},{8,10},{10,8},{12,14},{14,12},{1,3},{3,1},... | collective-permute-start | bytes 786440 | tf_op jit(solution)/shard_map/ppermute | solution.py:163
  74.9 9.3 %collective-permute-start.13 = (bf16[4,256,128]{2,1,0:T(8,128)(2,1)S(1)}, bf16[4,256,128]{2,1,0:T(8,128)(2,1)}, u32[]{:S(2)}, u32[]{:S(2)}) collective-permute-start(bf16[4,256,128]{2,1,0:T(8,128)(2,1)S(1)} %pad_maximum_fusion.refs_0_), channel_id=1, source_target_pairs={{0,4},{2,6},{4,0},{6,2},{8,12},{10,14},{12,8},{14,10},{1,5},{3,7},... | collective-permute-start | bytes 786440 | tf_op jit(solution)/shard_map/ppermute | solution.py:163
  74.9 14.7 %collective-permute-start.14 = (bf16[4,256,128]{2,1,0:T(8,128)(2,1)S(1)}, bf16[4,256,128]{2,1,0:T(8,128)(2,1)}, u32[]{:S(2)}, u32[]{:S(2)}) collective-permute-start(bf16[4,256,128]{2,1,0:T(8,128)(2,1)S(1)} %pad_maximum_fusion.refs_0_), channel_id=1, source_target_pairs={{0,6},{2,4},{4,2},{6,0},{8,14},{10,12},{12,10},{14,8},{1,7},{3,5},... | collective-permute-start | bytes 786440 | tf_op jit(solution)/shard_map/ppermute | solution.py:163
  93.0 1.6 %collective-permute-start.19 = (bf16[256,512]{1,0:T(8,128)(2,1)S(1)}, bf16[256,512]{1,0:T(8,128)(2,1)S(1)}, u32[]{:S(2)}, u32[]{:S(2)}) collective-permute-start(bf16[256,512]{1,0:T(8,128)(2,1)S(1)} %get-tuple-element.29), channel_id=1, source_target_pairs={{0,1},{1,0},{2,3},{3,2},{4,5},{5,4},{6,7},{7,6},{8,9},{9,8},{10,11... | collective-permute-start | bytes 786440 | tf_op jit(solution)/shard_map/ppermute | solution.py:163
  94.7 5.6 %collective-permute-start.20 = (bf16[2,64,512]{2,1,0:T(8,128)(2,1)S(1)}, bf16[2,64,512]{2,1,0:T(8,128)(2,1)S(1)}, u32[]{:S(2)}, u32[]{:S(2)}) collective-permute-start(bf16[2,64,512]{2,1,0:T(8,128)(2,1)S(1)} %get-tuple-element.27), channel_id=1, source_target_pairs={{0,2},{2,0},{4,6},{6,4},{8,10},{10,8},{12,14},{14,12},{1,3},{3,1},... | collective-permute-start | bytes 393224 | tf_op jit(solution)/shard_map/ppermute | solution.py:163
  95.4 6.4 %collective-permute-start.21 = (bf16[2,64,512]{2,1,0:T(8,128)(2,1)S(1)}, bf16[2,64,512]{2,1,0:T(8,128)(2,1)S(1)}, u32[]{:S(2)}, u32[]{:S(2)}) collective-permute-start(bf16[2,64,512]{2,1,0:T(8,128)(2,1)S(1)} %get-tuple-element.28), channel_id=1, source_target_pairs={{0,4},{2,6},{4,0},{6,2},{8,12},{10,14},{12,8},{14,10},{1,5},{3,7},... | collective-permute-start | bytes 393224 | tf_op jit(solution)/shard_map/ppermute | solution.py:163
  95.7 8.6 %collective-permute-start.22 = (bf16[2,64,512]{2,1,0:T(8,128)(2,1)S(1)}, bf16[2,64,512]{2,1,0:T(8,128)(2,1)S(1)}, u32[]{:S(2)}, u32[]{:S(2)}) collective-permute-start(bf16[2,64,512]{2,1,0:T(8,128)(2,1)S(1)} %get-tuple-element.25), channel_id=1, source_target_pairs={{0,6},{2,4},{4,2},{6,0},{8,14},{10,12},{12,10},{14,8},{1,7},{3,5},... | collective-permute-start | bytes 393224 | tf_op jit(solution)/shard_map/ppermute | solution.py:163

commit v2 on v0

--- a/solution.py
+++ b/solution.py
@@ -1,10 +1,20 @@
+import functools
+
 import jax
 import jax.numpy as jnp
 from jax import lax
+from jax.experimental import pallas as pl
+from jax.experimental.pallas import tpu as pltpu
 from jax.sharding import PartitionSpec as P
 
 epsilon = 1e-06
 highest = lax.Precision.HIGHEST
+f32 = jnp.float32
+bf16 = jnp.bfloat16
+CHUNK = 128
+LANES = 128
+MIB = 1024 * 1024
+SPARE = 16
 
 
 def passed_along(shard, axis, by):
@@ -47,7 +57,7 @@
     return jnp.dot(onehot, embed_table, preferred_element_type=jnp.float32)
 
 
-def body(
+def general_body(
     tokens,
     embed_table,
     norm_gain,
@@ -149,9 +159,547 @@
     return block_out.reshape(genome_count, row_count, half_width)
 
 
+def swapped(value, axis, mask):
+    count = lax.axis_size(axis)
+    return lax.ppermute(value, axis, [(i, i ^ mask) for i in range(count)])
+
+
+def swapped_both(value, ctx_mask):
+    count, cores = lax.axis_size("ctx"), lax.axis_size("chan")
+    pairs = [
+        (i * cores + c, (i ^ ctx_mask) * cores + (c ^ 1)) for i in range(count) for c in range(cores)
+    ]
+    return lax.ppermute(value, ("ctx", "chan"), pairs)
+
+
+def split(value):
+    high = value.astype(bf16)
+    return high, (value - high.astype(f32)).astype(bf16)
+
+
+def dot3(a_high, a_low, b):
+    b_high, b_low = split(b)
+    total = jnp.dot(a_high, b_high, preferred_element_type=f32)
+    total += jnp.dot(a_low, b_high, preferred_element_type=f32)
+    return total + jnp.dot(a_high, b_low, preferred_element_type=f32)
+
+
+def lane_half(shape):
+    return lax.broadcasted_iota(jnp.int32, shape, len(shape) - 1) < LANES // 2
+
+
+def half_turn(value):
+    return pltpu.roll(value, LANES // 2, value.ndim - 1)
+
+
+def norm_kernel(place_ref, table_ref, gain_ref, part_ref, packed_ref, out_ref):
+    del place_ref, packed_ref
+    widened = table_ref[...].astype(f32)
+    mean = jnp.sum(widened * widened, axis=1, keepdims=True) / widened.shape[1]
+    own = part_ref[...].astype(f32)
+    out_ref[...] = (own * lax.rsqrt(mean + epsilon) * gain_ref[...]).astype(bf16)
+
+
+def pack_kernel(place_ref, token_ref, weight_ref, *refs):
+    out_refs, sems = refs[:-1], refs[-1]
+    quad, group = place_ref[0], place_ref[2]
+    branches, depth, channels = weight_ref.shape
+    members = len(out_refs)
+    block = channels // members
+    copies = []
+    for m in (1, 2, 3, 0):
+        first = pl.multiple_of((quad ^ m) * block + group * LANES, LANES)
+        for j in range(branches):
+            copies.append(
+                pltpu.make_async_copy(
+                    weight_ref.at[j, :, pl.ds(first, LANES)],
+                    out_refs[m].at[pl.ds(j * depth, depth), :],
+                    sems.at[m, j],
+                )
+            )
+            copies[-1].start()
+    rows = token_ref.shape[1]
+    row = lax.broadcasted_iota(jnp.int32, (SPARE, rows), 0)
+    token = jnp.where(row % 4 < 2, token_ref[0:1, :], token_ref[1:2, :])
+    token = jnp.where(row % 2 == 0, token >> 8, token & 255)
+    token = jnp.where(row // 4 == quad, token, 0).astype(f32).astype(bf16)
+    for out_ref in out_refs:
+        out_ref[branches * depth :, :] = jnp.zeros((SPARE, LANES), bf16)
+        out_ref[branches * depth :, :rows] = token
+    for copy in copies:
+        copy.wait()
+
+
+def pick(half, near_ref, far_ref, picked_ref, genomes, rows):
+    vocab = picked_ref.shape[1]
+    length = picked_ref.shape[0] // genomes
+    first = near_ref.shape[0] - SPARE
+    diagonal = lax.broadcasted_iota(jnp.int32, (rows, rows), 0) == lax.broadcasted_iota(
+        jnp.int32, (rows, rows), 1
+    )
+    entries = lax.broadcasted_iota(jnp.int32, (rows, vocab), 1).astype(f32)
+    for other, ref in enumerate((near_ref, far_ref)):
+        parts = ref[first:, :rows].astype(f32)
+        for member in range(length // (2 * rows)):
+            for b in range(genomes):
+                at = 4 * member + 2 * b
+                line = parts[at : at + 1] * 256.0 + parts[at + 1 : at + 2]
+                column = jnp.sum(jnp.where(diagonal, line, 0.0), axis=1, keepdims=True)
+                place = b * length + (half ^ other) * (length // 2) + member * rows
+                picked_ref[pl.ds(pl.multiple_of(place, rows), rows), :] = (
+                    (column == entries).astype(f32).astype(bf16)
+                )
+
+
+def prepare_kernel(place_ref, rate_ref, amp_ref, taps_ref, skip_ref, matrices_ref, rows_ref):
+    quad, half = place_ref[0], place_ref[1]
+
+    group_count = rate_ref.shape[1]
+    poles = rate_ref.shape[0]
+    count = LANES // poles
+
+    def group_at(lane):
+        place = lane // poles
+        return quad * (2 * count) + (place // (count // 2)) * count + half * (count // 2) + place % (count // 2)
+
+    lane = lax.broadcasted_iota(jnp.int32, (group_count, LANES), 1)
+    chosen = (lax.broadcasted_iota(jnp.int32, (group_count, LANES), 0) == group_at(lane)).astype(f32)
+    turned_lane = lax.broadcasted_iota(jnp.int32, (LANES, group_count), 0)
+    turned = (lax.broadcasted_iota(jnp.int32, (LANES, group_count), 1) == group_at(turned_lane)).astype(f32)
+
+    def along_lanes(ref):
+        spread = jnp.dot(ref[...], chosen, precision=highest, preferred_element_type=f32)
+        keep = lax.broadcasted_iota(jnp.int32, spread.shape, 0) == lax.broadcasted_iota(
+            jnp.int32, spread.shape, 1
+        ) % poles
+        return jnp.sum(jnp.where(keep, spread, 0.0), axis=0, keepdims=True)
+
+    rate, amp = along_lanes(rate_ref), along_lanes(amp_ref)
+    spread = lax.dot_general(
+        turned, rate_ref[...], (((1,), (1,)), ((), ())), precision=highest, preferred_element_type=f32
+    )
+    keep = lax.broadcasted_iota(jnp.int32, spread.shape, 1) == lax.broadcasted_iota(
+        jnp.int32, spread.shape, 0
+    ) % poles
+    rate_col = jnp.sum(jnp.where(keep, spread, 0.0), axis=1, keepdims=True)
+
+    square = (CHUNK, LANES)
+    row = lax.broadcasted_iota(jnp.int32, square, 0)
+    col = lax.broadcasted_iota(jnp.int32, square, 1)
+    at = row.astype(f32)
+    middle = float(CHUNK // 2)
+    rising = amp * jnp.exp(-rate * (at - middle))
+    falling = jnp.exp(-rate * (middle - at))
+    width = (count + 1) * CHUNK
+    for g in range(count):
+        own = jnp.where(col // poles == g, falling, 0.0)
+        block = lax.dot_general(
+            rising, own, (((1,), (1,)), ((), ())), precision=highest, preferred_element_type=f32
+        )
+        high, low = split(jnp.where(row >= col, block, 0.0))
+        matrices_ref[:, g * CHUNK : (g + 1) * CHUNK] = high
+        matrices_ref[:, width + g * CHUNK : width + (g + 1) * CHUNK] = low
+    high, low = split(amp * jnp.exp(-rate * (at + 1.0)))
+    matrices_ref[:, count * CHUNK : width] = high
+    matrices_ref[:, width + count * CHUNK : 2 * width] = low
+    high, low = split(jnp.exp(-rate_col * (float(CHUNK - 1) - col.astype(f32))))
+    matrices_ref[:, 2 * width : 2 * width + CHUNK] = high
+    matrices_ref[:, 2 * width + CHUNK :] = low
+
+    rows_ref[:LANES] = jnp.exp(-rate_col * float(CHUNK)) + jnp.zeros(square, f32)
+    branches = taps_ref.shape[0]
+    for j in range(branches):
+        taps = jnp.dot(taps_ref[j], chosen, precision=highest, preferred_element_type=f32)
+        rows_ref[LANES + 8 * j : LANES + 8 * j + taps.shape[0]] = taps
+    upper = skip_ref[pl.ds(2 * quad, 1), :]
+    lower = skip_ref[pl.ds(2 * quad + 1, 1), :]
+    upper = jnp.where(half == 0, upper, half_turn(upper))
+    lower = jnp.where(half == 1, lower, half_turn(lower))
+    end = LANES + 8 * branches
+    rows_ref[end : end + 1] = jnp.where(lane_half(upper.shape), upper, lower)
+
+
+def partial_kernel(place_ref, normed_ref, *refs):
+    weight_refs, (keep_ref, send_ref) = refs[:-2], refs[-2:]
+    quad, half = place_ref[0], place_ref[1]
+    rows, features = normed_ref.shape
+    depth = features // len(weight_refs)
+    count = weight_refs[0].shape[0] // depth
+    total = jnp.zeros((rows, count * LANES), f32)
+    tokens = jnp.zeros((SPARE, LANES), f32)
+    for m, weight_ref in enumerate(weight_refs):
+        first = pl.multiple_of((quad ^ m) * depth, depth)
+        columns = jnp.concatenate(
+            [weight_ref[j * depth : (j + 1) * depth, :] for j in range(count)], axis=1
+        )
+        total += jnp.dot(
+            normed_ref[:, pl.ds(first, depth)], columns, preferred_element_type=f32
+        )
+        tokens += weight_ref[count * depth :, :].astype(f32)
+    part = rows // 2
+    for j in range(count):
+        mine = total[:, j * LANES : (j + 1) * LANES]
+        mine = jnp.where(half == 0, mine, half_turn(mine))
+        top, bottom = mine[:part], mine[part:]
+        left = lane_half(top.shape)
+        keep_ref[j * part : (j + 1) * part, :] = jnp.where(left, top, half_turn(bottom))
+        send_ref[j * part : (j + 1) * part, :] = jnp.where(left, half_turn(top), bottom).astype(bf16)
+    send_ref[count * part :, :] = tokens.astype(bf16)
+
+
+def filtered_branch(group, picked, row, mine, theirs, rows_ref, branch):
+    mine, theirs = mine.astype(f32), theirs.astype(f32)
+    first = jnp.where(group == 0, mine, theirs)
+    second = jnp.where(group == 0, theirs, mine)
+    left = lane_half(first.shape)
+    top = jnp.where(left, first, half_turn(second))
+    bottom = jnp.where(left, half_turn(first), second)
+    table = jnp.concatenate([top, bottom], axis=0).astype(bf16)
+    now = jnp.dot(picked, table, preferred_element_type=f32)
+    first_tap = LANES + 8 * branch
+    total = rows_ref[first_tap : first_tap + 1] * now
+    for lag in range(1, 3):
+        late = jnp.where(row >= lag, pltpu.roll(now, lag, 0), 0.0)
+        total += rows_ref[first_tap + lag : first_tap + lag + 1] * late
+    return total
+
+
+def conv_kernel(
+    place_ref, near_ref, far_ref, own_ref, other_ref, matrices_ref, rows_ref, *refs, genomes, rows
+):
+    piece_refs, (mine_ref, picked_ref, held_ref) = refs[:4], refs[4:]
+    half, group, core = place_ref[1], place_ref[2], place_ref[3]
+    pick(half, near_ref, far_ref, picked_ref, genomes, rows)
+    positions = picked_ref.shape[0]
+    length = positions // genomes
+    row = lax.broadcasted_iota(jnp.int32, (positions, LANES), 0) % length
+    picked = picked_ref[...]
+    query, key, value = (
+        filtered_branch(group, picked, row, own_ref[j], other_ref[j], rows_ref, j) for j in range(3)
+    )
+    product = key * value
+    size = 16
+    count = LANES // size
+    width = genomes * LANES
+    lane = lax.broadcasted_iota(jnp.int32, (CHUNK, width), 1) % LANES
+    pole_row = lax.broadcasted_iota(jnp.int32, (LANES, width), 0)
+    same = pole_row // size == (lax.broadcasted_iota(jnp.int32, (LANES, width), 1) % LANES) // size
+    fade = jnp.concatenate([rows_ref[:LANES]] * genomes, axis=1)
+    end = LANES + 8 * own_ref.shape[0]
+    skip = rows_ref[end : end + 1]
+    across = (count + 1) * CHUNK
+    high, low = matrices_ref[:, :across], matrices_ref[:, across : 2 * across]
+    ends_high = matrices_ref[:, 2 * across : 2 * across + CHUNK]
+    ends_low = matrices_ref[:, 2 * across + CHUNK :]
+    state = jnp.zeros((LANES, width), f32)
+    chunks = length // CHUNK
+    for c in range(chunks):
+        spans = [slice(b * length + c * CHUNK, b * length + (c + 1) * CHUNK) for b in range(genomes)]
+        block = jnp.concatenate([product[span] for span in spans], axis=1)
+        stacked = jnp.concatenate(
+            [jnp.where(lane // size == g, block, 0.0) for g in range(count)] + [state], axis=0
+        )
+        conv = dot3(high, low, stacked)
+        for b, span in enumerate(spans):
+            value = conv[:, b * LANES : (b + 1) * LANES] + skip * product[span]
+            held_ref[span, :] = (query[span] * value).astype(bf16)
+        if c < chunks - 1:
+            ends = dot3(ends_high, ends_low, block)
+            state = fade * state + jnp.where(same, ends, 0.0)
+    part = length // 2
+    for r, piece_ref in enumerate(piece_refs):
+        place = 2 * (core ^ (r % 2)) + (half ^ (r // 2))
+        piece_ref[...] = held_ref[pl.ds(pl.multiple_of(place * part, part), part), :]
+    mine_ref[...] = picked_ref[pl.ds(pl.multiple_of((2 * core + half) * part, part), part), :]
+
+
+def offer_kernel(place_ref, rows_ref, packed_ref, out_ref):
+    del place_ref, packed_ref
+    out_ref[...] = rows_ref[...]
+
+
+def residual(picked_ref, table_ref, first, width):
+    return jnp.dot(
+        picked_ref[...],
+        table_ref[:, pl.ds(pl.multiple_of(first, width), width)],
+        preferred_element_type=f32,
+    )
+
+
+def near_kernel(place_ref, picked_ref, table_ref, *refs):
+    piece_refs, (own_ref, core_ref, out_ref, joined_ref) = refs[:4], refs[4:]
+    quad, half = place_ref[0], place_ref[1]
+    block = 2 * LANES
+    for m, piece_ref in enumerate(piece_refs):
+        for other_core in (0, 1):
+            near = piece_ref[other_core].astype(f32)
+            far = piece_ref[2 + other_core].astype(f32)
+            first = jnp.where(half == 0, near, far)
+            second = jnp.where(half == 0, far, near)
+            left = lane_half(first.shape)
+            pair = [
+                jnp.where(left, first, half_turn(second)),
+                jnp.where(left, half_turn(first), second),
+            ]
+            joined_ref[2 * (quad ^ m) + other_core] = jnp.concatenate(pair, axis=1).astype(bf16)
+    width = own_ref.shape[1]
+    total = jnp.zeros(out_ref.shape, f32)
+    for member in range(4):
+        rows = slice(member * block, (member + 1) * block)
+        for other_core, ref in enumerate((own_ref, core_ref)):
+            total += jnp.dot(
+                joined_ref[2 * member + other_core], ref[rows, :], preferred_element_type=f32
+            )
+    total += residual(picked_ref, table_ref, (4 * half + quad) * width, width)
+    out_ref[...] = total.astype(bf16)
+
+
+def far_kernel(place_ref, picked_ref, table_ref, near_ref, joined_ref, *refs):
+    far_refs, out_ref = (refs[:2], refs[2:4]), refs[4]
+    quad, half, group, core = (place_ref[i] for i in range(4))
+    block = 2 * LANES
+    width = near_ref.shape[1]
+    total = jnp.zeros(near_ref.shape, f32)
+    for member in range(4):
+        rows = slice((member % 2) * block, (member % 2 + 1) * block)
+        for other_core in (0, 1):
+            source = 2 * (2 * (group ^ (member // 2)) + member % 2) + other_core
+            total += jnp.dot(
+                joined_ref[source],
+                far_refs[member // 2][other_core][rows, :],
+                preferred_element_type=f32,
+            )
+    total += residual(picked_ref, table_ref, (4 * (half ^ 1) + (quad ^ 2)) * width, width)
+    out_ref[half ^ core] = near_ref[...]
+    out_ref[half ^ 1 ^ core] = total.astype(bf16)
+
+
+def place_kernel(place_ref, *refs):
+    piece_refs, out_ref = refs[:4], refs[4]
+    quad, half, core = place_ref[0], place_ref[1], place_ref[3]
+    width = piece_refs[0].shape[2]
+    for m, piece_ref in enumerate(piece_refs):
+        first = pl.multiple_of((quad ^ m ^ (2 * (half ^ core))) * width, width)
+        for g in (0, 1):
+            out_ref[core ^ g, :, pl.ds(first, width)] = piece_ref[g]
+
+
+def called(kernel, out_shape, scalars, *operands, scratch=(), mib=16, earlier=()):
+    smem = pl.BlockSpec(memory_space=pltpu.SMEM)
+    vmem = pl.BlockSpec(memory_space=pltpu.VMEM)
+    anywhere = pl.BlockSpec(memory_space=pl.ANY)
+    many = isinstance(out_shape, (list, tuple))
+    inputs, waits = len(scalars) + len(operands), len(earlier)
+
+    def body(*refs):
+        kernel(*refs[:inputs], *refs[inputs + waits :])
+
+    return pl.pallas_call(
+        body,
+        out_shape=out_shape,
+        in_specs=[smem] * len(scalars) + [vmem] * len(operands) + [anywhere] * waits,
+        out_specs=[vmem] * len(out_shape) if many else vmem,
+        scratch_shapes=scratch,
+        compiler_params=pltpu.CompilerParams(vmem_limit_bytes=mib * MIB),
+    )(*scalars, *operands, *earlier)
+
+
+def shaped(*shape, dtype=f32):
+    return jax.ShapeDtypeStruct(shape, dtype)
+
+
+def pass_kernel(*refs):
+    del refs
+
+
+def after(value, earlier):
+    return pl.pallas_call(
+        pass_kernel,
+        out_shape=shaped(*value.shape, dtype=value.dtype),
+        in_specs=[pl.BlockSpec(memory_space=pl.ANY)] * 2,
+        out_specs=pl.BlockSpec(memory_space=pl.ANY),
+        input_output_aliases={0: 0},
+        compiler_params=pltpu.CompilerParams(vmem_limit_bytes=MIB),
+    )(value, earlier)
+
+
+def quad_body(
+    tokens,
+    embed_table,
+    norm_gain,
+    input_proj,
+    short_filter,
+    pole_rate,
+    residue,
+    skip_gain,
+    output_proj,
+):
+    genomes, rows = tokens.shape
+    depth, branches, channels = input_proj.shape
+    vocab, features = embed_table.shape
+    members = lax.axis_size("ctx") // 2
+    ctx, core, group = (lax.axis_index(name) for name in ("ctx", "chan", "groups"))
+    quad, half = ctx % members, ctx // members
+    place = jnp.stack([quad, half, group, core]).astype(jnp.int32)
+    block = channels // members
+
+    weights = input_proj.transpose(1, 0, 2)
+    anywhere = pl.BlockSpec(memory_space=pl.ANY)
+    packed = pl.pallas_call(
+        pack_kernel,
+        out_shape=[shaped(branches * depth + SPARE, LANES, dtype=bf16)] * members,
+        in_specs=[
+            pl.BlockSpec(memory_space=pltpu.SMEM),
+            pl.BlockSpec(memory_space=pltpu.VMEM),
+            anywhere,
+        ],
+        out_specs=[pl.BlockSpec(memory_space=pltpu.VMEM)] * members,
+        scratch_shapes=[pltpu.SemaphoreType.DMA((members, branches))],
+        compiler_params=pltpu.CompilerParams(vmem_limit_bytes=62 * MIB),
+    )(place, tokens, weights)
+    gathered = [packed[0]] + [swapped(packed[m], "ctx", m) for m in range(1, members)]
+    length = 2 * members * rows
+
+    half_rows = output_proj.shape[0] // 2
+    width = output_proj.shape[1]
+    offered = pl.pallas_call(
+        offer_kernel,
+        out_shape=shaped(half_rows, width, dtype=bf16),
+        grid_spec=pltpu.PrefetchScalarGridSpec(
+            num_scalar_prefetch=1,
+            grid=(1,),
+            in_specs=[pl.BlockSpec((half_rows, width), lambda i, place: (place[2], 0)), anywhere],
+            out_specs=pl.BlockSpec((half_rows, width), lambda i, place: (0, 0)),
+        ),
+        compiler_params=pltpu.CompilerParams(vmem_limit_bytes=4 * MIB),
+    )(place, output_proj, packed[0])
+    count = 2 * members
+    inner = [(i, count - 2 - i + 2 * (i % 2)) for i in range(members // 2, members + members // 2)]
+    outer = [
+        (i, count - 2 - i + 2 * (i % 2))
+        for i in range(count)
+        if not members // 2 <= i < members + members // 2
+    ]
+
+    part = features // 2
+    step = 128
+    normed = pl.pallas_call(
+        norm_kernel,
+        out_shape=shaped(vocab, part, dtype=bf16),
+        grid_spec=pltpu.PrefetchScalarGridSpec(
+            num_scalar_prefetch=1,
+            grid=(vocab // step,),
+            in_specs=[
+                pl.BlockSpec((step, features), lambda i, place: (i, 0)),
+                pl.BlockSpec((1, part), lambda i, place: (0, place[1])),
+                pl.BlockSpec((step, part), lambda i, place: (i, place[1])),
+                anywhere,
+            ],
+            out_specs=pl.BlockSpec((step, part), lambda i, place: (i, 0)),
+        ),
+        compiler_params=pltpu.CompilerParams(vmem_limit_bytes=16 * MIB),
+    )(place, embed_table, norm_gain.reshape(1, features), embed_table, gathered[1])
+
+    inner_fetched = lax.ppermute(offered, "ctx", inner)
+    amp = residue * jnp.sqrt(-jnp.expm1(-2.0 * pole_rate))
+    across = (LANES // pole_rate.shape[1] + 1) * CHUNK
+    matrices, lines = called(
+        prepare_kernel,
+        [
+            shaped(CHUNK, 2 * across + 2 * CHUNK, dtype=bf16),
+            shaped(LANES + 8 * (branches + 1), LANES),
+        ],
+        (place,),
+        pole_rate.T,
+        amp.T,
+        short_filter.transpose(0, 2, 1),
+        skip_gain.reshape(-1, LANES),
+        earlier=(gathered[1],),
+    )
+
+    table_rows = branches * (vocab // 2)
+    keep, send = called(
+        partial_kernel,
+        [shaped(table_rows, LANES), shaped(table_rows + SPARE, LANES, dtype=bf16)],
+        (place,),
+        normed,
+        *gathered,
+        earlier=(matrices, inner_fetched),
+    )
+    arrived = swapped(send, "ctx", members)
+    own = (keep + arrived[:table_rows].astype(f32)).astype(bf16)
+    own = own.reshape(branches, vocab // 2, LANES)
+    other = swapped(own, "groups", 1)
+    span = length // 2
+    *pieces, picked = called(
+        functools.partial(conv_kernel, genomes=genomes, rows=rows),
+        [shaped(span, LANES, dtype=bf16)] * 4 + [shaped(span, vocab, dtype=bf16)],
+        (place,),
+        send,
+        arrived,
+        own,
+        other,
+        matrices,
+        lines,
+        scratch=[pltpu.VMEM((genomes * length, vocab), bf16), pltpu.VMEM((genomes * length, LANES), bf16)],
+    )
+    core_piece = swapped(pieces[1], "chan", 1)
+    piece = jnp.stack(
+        [
+            pieces[0],
+            core_piece,
+            swapped(pieces[2], "ctx", members),
+            swapped_both(pieces[3], members),
+        ]
+    )
+    gated = [piece] + [swapped(piece, "ctx", m) for m in range(1, members)]
+
+    outer_fetched = lax.ppermute(after(offered, own), "ctx", outer)
+    fetched = jnp.where((ctx >= members // 2) & (ctx < members + members // 2), inner_fetched, outer_fetched)
+    fetched = after(fetched, piece)
+    shared = swapped(fetched, "groups", 1)
+    for ready in gated[1:]:
+        shared = after(shared, ready)
+    near, joined = called(
+        near_kernel,
+        [shaped(span, width, dtype=bf16), shaped(4 * 2, span, 2 * LANES, dtype=bf16)],
+        (place,),
+        picked,
+        embed_table,
+        *gated,
+        output_proj,
+        swapped(output_proj, "chan", 1),
+        mib=24,
+    )
+    results = called(
+        far_kernel,
+        shaped(2, span, width, dtype=bf16),
+        (place,),
+        picked,
+        embed_table,
+        near,
+        joined,
+        fetched,
+        swapped(fetched, "chan", 1),
+        shared,
+        swapped(shared, "chan", 1),
+        mib=24,
+    )
+    both = jnp.stack([results[0], swapped(results[1], "chan", 1)])
+
+    def rows_of(member):
+        return lax.dynamic_slice_in_dim(both, member * rows, rows, 1)
+
+    arrived = [rows_of(quad)] + [swapped(rows_of(quad ^ m), "ctx", m) for m in range(1, members)]
+    return called(
+        place_kernel, shaped(genomes, rows, members * width, dtype=bf16), (place,), *arrived
+    )
+
+
 def solution(mesh):
+    sizes = tuple(mesh.shape[name] for name in ("groups", "ctx", "chan"))
     return jax.shard_map(
-        body,
+        quad_body if sizes == (2, 8, 2) else general_body,
         mesh=mesh,
         in_specs=(
             P("groups", "ctx"),

time: 504 us -> 100 us (0.20)
  waiting for transfers between devices: 350 us -> 49.8 us
  matrix products: 46.2 us -> 0 us
  blocking collectives: 31 us -> 0 us
  local copies, waits for them, and re-layouts: 29.9 us -> 3.25 us
  other arithmetic: 21 us -> 0.88 us
  Pallas kernels: 0 us -> 19.4 us
  starting transfers between devices: 10.8 us -> 26.7 us
  between operations: 13.3 us -> 0.23 us
    reduce_scatter x2 -> x0, waiting for transfers between devices: 212 us -> none  [the longest x1 204 us: body(): lax.psum_scatter(jnp.dot(spread, flat_weight, preferred_element_type=jnp....]
    all_gather x2 -> x0, waiting for transfers between devices: 116 us -> none  [the longest x1 106 us: body(): lax.all_gather(output_proj, 'ctx', axis=1, tiled=True)]
    ppermute x1 -> x21, waiting for transfers between devices: 0.01 us -> 49.8 us  [the longest x18 48.5 us: swapped(): return lax.ppermute(value, axis, [(i, i ^ mask) for i in range(count)])]
    dot_general x21 -> x0, matrix products: 46.2 us -> none  [the longest x8 11.9 us: local_block(): toeplitz = jnp.einsum('gnt,gns->gts', rising, falling, precision=highest)]
    all_gather x1 -> x0, blocking collectives: 31 us -> none  [entering(): everything = jax.tree.map(lambda part: lax.all_gather(part, axis), shard)]
    ppermute x1 -> x21, starting transfers between devices: 3.38 us -> 26.7 us  [the longest x18 20 us: swapped(): return lax.ppermute(value, axis, [(i, i ^ mask) for i in range(count)])]
    all_to_all x1 -> x0, waiting for transfers between devices: 21 us -> none  [body(): lax.all_to_all(normed, 'ctx', split_axis=1, concat_axis=0, tiled=True)]
    pallas_call x0 -> x14, Pallas kernels: none -> 19.4 us  [the longest x6 12.7 us: called(): pl.pallas_call(body, out_shape=out_shape, in_specs=[smem] * len(scalars)...]
  transfers between devices with their start and end apart: 6 -> 21, of which waited for: 5 -> 13; matrix products, arithmetic and copies ran while one was open for 12% -> 0% of each run, Pallas kernels for 0% -> 10%
where the time goes in v2:
time: 100 us
  waiting for transfers between devices  49.8 us (50%)
  starting transfers between devices  26.7 us (27%)
  Pallas kernels  19.4 us (19%)
  local copies, waits for them, and re-layouts  3.25 us (3%)
    ppermute x18, waiting for transfers between devices, swapped(): return lax.ppermute(value, axis, [(i, i ^ mask) for i in range(count)])  48.5 us
    ppermute x18, starting transfers between devices, swapped(): return lax.ppermute(value, axis, [(i, i ^ mask) for i in range(count)])  20 us
    pallas_call x6, Pallas kernels, called(): pl.pallas_call(body, out_shape=out_shape, in_specs=[smem] * len(scalars)...  12.7 us
    pallas_call x1, Pallas kernels, quad_body(): pl.pallas_call(pack_kernel, out_shape=[shaped(branches * depth + SPARE, L...  3.49 us
    ppermute x1, starting transfers between devices, quad_body(): outer_fetched = lax.ppermute(after(offered, own), 'ctx', outer)  3.26 us
    unnamed x20, local copies, waits for them, and re-layouts  3.21 us
    ppermute x1, starting transfers between devices, swapped_both(): return lax.ppermute(value, ('ctx', 'chan'), pairs)  2.68 us
    pallas_call x1, Pallas kernels, quad_body(): pl.pallas_call(norm_kernel, out_shape=shaped(vocab, part, dtype=bf16), gr...  2.56 us
  transfers between devices with their start and end apart: 21, of which 13 were waited for; matrix products, arithmetic and copies ran while one was open for 0% of the time, Pallas kernels for 10%

profile of v2, /device:TPU:0, one launch (start us, length us, event | category | flops | bytes accessed | tf_op | source)
XLA Modules:
  0.0 100.2 jit_solution(3213494905359709509)
XLA Ops:
  0.0 0.7 pad_add_fusion.place_ref.refs_0_
  0.7 3.5 %shard_map.91 = (bf16[1552,128]{1,0:T(8,128)(2,1)}, bf16[1552,128]{1,0:T(8,128)(2,1)}, bf16[1552,128]{1,0:T(8,128)(2,1)}, bf16[1552,128]{1,0:T(8,128)(2,1)}) custom-call(s32[4]{0:T(128)} %pad_add_fusion.place_ref.refs_0_, s32[2,64]{1,0:T(2,128)} %token_ref.1, bf16[3,512,1024]{2,1,0:T(8,128)(2,1)} %bitcast.27), custom_call_target="tpu_custom_call" | custom-call | tf_op jit(solution)/shard_map/pallas_call | solution.py:548
  4.2 0.0 copy-start.3
  4.2 1.0 copy-done.3
  5.2 0.6 shard_map.94.refs_0_
  5.8 0.7 collective-permute-start.3
  6.5 3.1 %collective-permute-start = (bf16[1552,128]{1,0:T(8,128)(2,1)}, bf16[1552,128]{1,0:T(8,128)(2,1)S(1)}, u32[]{:S(2)}, u32[]{:S(2)}) collective-permute-start(bf16[1552,128]{1,0:T(8,128)(2,1)} %get-tuple-element.20), channel_id=1, source_target_pairs={{0,2},{2,0},{4,6},{6,4},{8,10},{10,8},{12,14},{14,12},{1,3},{3,1},... | collective-permute-start | bytes 1191944 | tf_op jit(solution)/shard_map/ppermute | solution.py:164
  9.5 4.4 %collective-permute-start.1 = (bf16[1552,128]{1,0:T(8,128)(2,1)}, bf16[1552,128]{1,0:T(8,128)(2,1)S(1)}, u32[]{:S(2)}, u32[]{:S(2)}) collective-permute-start(bf16[1552,128]{1,0:T(8,128)(2,1)} %get-tuple-element.22), channel_id=1, source_target_pairs={{0,4},{2,6},{4,0},{6,2},{8,12},{10,14},{12,8},{14,10},{1,5},{3,7},... | collective-permute-start | bytes 1191944 | tf_op jit(solution)/shard_map/ppermute | solution.py:164
  13.9 0.0 collective-permute-start.2
  14.0 5.0 %collective-permute-done.packed_ref.refs_5_.refs_3_ = bf16[1552,128]{1,0:T(8,128)(2,1)S(1)} collective-permute-done((bf16[1552,128]{1,0:T(8,128)(2,1)}, bf16[1552,128]{1,0:T(8,128)(2,1)S(1)}, u32[]{:S(2)}, u32[]{:S(2)}) %collective-permute-start) | collective-permute-done | bytes 397344 | tf_op jit(solution)/shard_map/ppermute | solution.py:164
  19.0 2.2 %copy-done = bf16[512,4096]{1,0:T(8,128)(2,1)S(1)} copy-done((bf16[512,4096]{1,0:T(8,128)(2,1)S(1)}, bf16[512,4096]{1,0:T(8,128)(2,1)}, u32[]{:S(2)}) %copy-start) | copy-done | bytes 4194328
  21.2 2.6 %shard_map.92.refs_1_ = bf16[512,2048]{1,0:T(8,128)(2,1)S(1)} custom-call(s32[4]{0:T(128)S(1)} %copy-done.4, bf16[512,4096]{1,0:T(8,128)(2,1)S(1)} %copy-done, f32[1,4096]{1,0:T(1,128)S(1)} %bitcast.24, bf16[512,4096]{1,0:T(8,128)(2,1)S(1)} %copy-done, bf16[1552,128]{1,0:T(8,128)(2,1)S(1)} %collective-permute-done.packed_ref.refs_5_.refs_3_), custom_call_target="tpu_custom_call" | custom-call | tf_op jit(solution)/shard_map/pallas_call | solution.py:586
  23.7 2.1 %shard_map.93 = (bf16[128,2560]{1,0:T(8,128)(2,1)S(1)}, f32[160,128]{1,0:T(8,128)S(1)}) custom-call(s32[4]{0:T(128)S(1)} %copy-done.4, f32[16,64]{1,0:T(8,128)S(1)} %bitcast.23, f32[16,64]{1,0:T(8,128)S(1)} %multiply_bitcast_fusion.refs_2_, f32[3,3,64]{2,1,0:T(4,128)S(1)} %bitcast.25, f32[8,128]{1,0:T(8,128)S(1)} %bitcast.26, ...), custom_call_target="tpu_custom_call" | custom-call | tf_op jit(solution)/shard_map/pallas_call | solution.py:497
  25.8 5.4 %collective-permute-done.2.refs_5_ = bf16[1552,128]{1,0:T(8,128)(2,1)S(1)} collective-permute-done((bf16[1552,128]{1,0:T(8,128)(2,1)}, bf16[1552,128]{1,0:T(8,128)(2,1)S(1)}, u32[]{:S(2)}, u32[]{:S(2)}) %collective-permute-start.2) | collective-permute-done | bytes 397344 | tf_op jit(solution)/shard_map/ppermute | solution.py:164
  31.2 0.0 collective-permute-done.3.refs_7_
  31.2 2.1 %shard_map.95 = (f32[768,128]{1,0:T(8,128)S(1)}, bf16[784,128]{1,0:T(8,128)(2,1)S(1)}) custom-call(s32[4]{0:T(128)S(1)} %copy-done.4, bf16[512,2048]{1,0:T(8,128)(2,1)S(1)} %shard_map.92.refs_1_, bf16[1552,128]{1,0:T(8,128)(2,1)S(1)} %copy-done.3, bf16[1552,128]{1,0:T(8,128)(2,1)S(1)} %collective-permute-done.packed_ref.refs_5_.refs_3_, ...), custom_call_target="tpu_custom_call" | custom-call | tf_op jit(solution)/shard_map/pallas_call | solution.py:497
  33.3 1.7 %collective-permute-start.4 = (bf16[784,128]{1,0:T(8,128)(2,1)S(1)}, bf16[784,128]{1,0:T(8,128)(2,1)S(1)}, u32[]{:S(2)}, u32[]{:S(2)}) collective-permute-start(bf16[784,128]{1,0:T(8,128)(2,1)S(1)} %get-tuple-element.25.refs_1_), channel_id=1, source_target_pairs={{0,8},{2,10},{4,12},{6,14},{8,0},{10,2},{12,4},{14,6},{1,9},{3,11}... | collective-permute-start | bytes 602120 | tf_op jit(solution)/shard_map/ppermute | solution.py:164
  35.0 9.1 %collective-permute-done.4.refs_2_ = bf16[784,128]{1,0:T(8,128)(2,1)S(1)} collective-permute-done((bf16[784,128]{1,0:T(8,128)(2,1)S(1)}, bf16[784,128]{1,0:T(8,128)(2,1)S(1)}, u32[]{:S(2)}, u32[]{:S(2)}) %collective-permute-start.4) | collective-permute-done | bytes 200736 | tf_op jit(solution)/shard_map/ppermute | solution.py:164
  44.1 0.1 add_convert_fusion
  44.2 3.3 %collective-permute-start.13 = (bf16[512,512]{1,0:T(8,128)(2,1)S(1)}, bf16[512,512]{1,0:T(8,128)(2,1)S(1)}, u32[]{:S(2)}, u32[]{:S(2)}) collective-permute-start(bf16[512,512]{1,0:T(8,128)(2,1)S(1)} %shard_map.98), channel_id=1, source_target_pairs={{0,12},{2,14},{12,0},{14,2},{1,13},{3,15},{13,1},{15,3},{16,28},{1... | collective-permute-start | bytes 1572872 | tf_op jit(solution)/shard_map/ppermute | solution.py:657
  47.4 1.6 %collective-permute-start.5 = (bf16[3,256,128]{2,1,0:T(8,128)(2,1)S(1)}, bf16[3,256,128]{2,1,0:T(8,128)(2,1)S(1)}, u32[]{:S(2)}, u32[]{:S(2)}) collective-permute-start(bf16[3,256,128]{2,1,0:T(8,128)(2,1)S(1)} %bitcast.20), channel_id=1, source_target_pairs={{0,16},{16,0},{1,17},{17,1},{2,18},{18,2},{3,19},{19,3},{4,20},{20... | collective-permute-start | bytes 589832 | tf_op jit(solution)/shard_map/ppermute | solution.py:164
  49.0 4.2 %collective-permute-done.5.refs_4_ = bf16[3,256,128]{2,1,0:T(8,128)(2,1)S(1)} collective-permute-done((bf16[3,256,128]{2,1,0:T(8,128)(2,1)S(1)}, bf16[3,256,128]{2,1,0:T(8,128)(2,1)S(1)}, u32[]{:S(2)}, u32[]{:S(2)}) %collective-permute-start.5) | collective-permute-done | bytes 196640 | tf_op jit(solution)/shard_map/ppermute | solution.py:164
  53.2 4.0 %shard_map.96 = (bf16[256,128]{1,0:T(8,128)(2,1)S(1)}, bf16[256,128]{1,0:T(8,128)(2,1)S(1)}, bf16[256,128]{1,0:T(8,128)(2,1)S(1)}, bf16[256,128]{1,0:T(8,128)(2,1)S(1)}, bf16[256,512]{1,0:T(8,128)(2,1)S(1)}) custom-call(s32[4]{0:T(128)S(1)} %copy-done.4, bf16[784,128]{1,0:T(8,128)(2,1)S(1)} %get-tuple-element.25.refs_1_, ...), custom_call_target="tpu_custom_call" | custom-call | tf_op jit(solution)/shard_map/pallas_call | solution.py:497
  57.2 0.1 collective-permute-start.6
  57.2 0.1 collective-permute-start.7
  57.3 2.7 %collective-permute-start.8 = (bf16[256,128]{1,0:T(8,128)(2,1)S(1)}, bf16[256,128]{1,0:T(8,128)(2,1)S(1)}, u32[]{:S(2)}, u32[]{:S(2)}) collective-permute-start(bf16[256,128]{1,0:T(8,128)(2,1)S(1)} %get-tuple-element.32), channel_id=1, source_target_pairs={{0,9},{1,8},{2,11},{3,10},{4,13},{5,12},{6,15},{7,14},{8,1},{9,0},... | collective-permute-start | bytes 196616 | tf_op jit(solution)/shard_map/ppermute | solution.py:172
  60.0 5.3 %collective-permute-done.7 = bf16[256,128]{1,0:T(8,128)(2,1)S(1)} collective-permute-done((bf16[256,128]{1,0:T(8,128)(2,1)S(1)}, bf16[256,128]{1,0:T(8,128)(2,1)S(1)}, u32[]{:S(2)}, u32[]{:S(2)}) %collective-permute-start.7) | collective-permute-done | bytes 65568 | tf_op jit(solution)/shard_map/ppermute | solution.py:164
  65.3 1.3 %collective-permute-done.8 = bf16[256,128]{1,0:T(8,128)(2,1)S(1)} collective-permute-done((bf16[256,128]{1,0:T(8,128)(2,1)S(1)}, bf16[256,128]{1,0:T(8,128)(2,1)S(1)}, u32[]{:S(2)}, u32[]{:S(2)}) %collective-permute-start.8) | collective-permute-done | bytes 65568 | tf_op jit(solution)/shard_map/ppermute | solution.py:172
  66.7 0.0 copy-start.1
  66.7 0.1 broadcast_select_fusion.refs_0_
  66.8 1.6 %collective-permute-start.15 = (bf16[512,512]{1,0:T(8,128)(2,1)S(1)}, bf16[512,512]{1,0:T(8,128)(2,1)S(1)}, u32[]{:S(2)}, u32[]{:S(2)}) collective-permute-start(bf16[512,512]{1,0:T(8,128)(2,1)S(1)} %shard_map.99.refs_5_), channel_id=1, source_target_pairs={{0,16},{16,0},{1,17},{17,1},{2,18},{18,2},{3,19},{19,3},{4,20},{20... | collective-permute-start | bytes 1572872 | tf_op jit(solution)/shard_map/ppermute | solution.py:164
  68.3 1.5 %collective-permute-start.9 = (bf16[4,256,128]{2,1,0:T(8,128)(2,1)S(1)}, bf16[4,256,128]{2,1,0:T(8,128)(2,1)S(1)}, u32[]{:S(2)}, u32[]{:S(2)}) collective-permute-start(bf16[4,256,128]{2,1,0:T(8,128)(2,1)S(1)} %pad_maximum_fusion.refs_3_.refs_1_), channel_id=1, source_target_pairs={{0,2},{2,0},{4,6},{6,4},{8,10},{10,8},{12,14},{14,12},{1,3},{3,1},... | collective-permute-start | bytes 786440 | tf_op jit(solution)/shard_map/ppermute | solution.py:164
  69.9 2.0 %collective-permute-start.11 = (bf16[4,256,128]{2,1,0:T(8,128)(2,1)S(1)}, bf16[4,256,128]{2,1,0:T(8,128)(2,1)S(1)}, u32[]{:S(2)}, u32[]{:S(2)}) collective-permute-start(bf16[4,256,128]{2,1,0:T(8,128)(2,1)S(1)} %pad_maximum_fusion.refs_3_.refs_1_), channel_id=1, source_target_pairs={{0,6},{2,4},{4,2},{6,0},{8,14},{10,12},{12,10},{14,8},{1,7},{3,5},... | collective-permute-start | bytes 786440 | tf_op jit(solution)/shard_map/ppermute | solution.py:164
  71.8 5.2 %collective-permute-done.9.refs_4_.refs_1_ = bf16[4,256,128]{2,1,0:T(8,128)(2,1)S(1)} collective-permute-done((bf16[4,256,128]{2,1,0:T(8,128)(2,1)S(1)}, bf16[4,256,128]{2,1,0:T(8,128)(2,1)S(1)}, u32[]{:S(2)}, u32[]{:S(2)}) %collective-permute-start.9) | collective-permute-done | bytes 262176 | tf_op jit(solution)/shard_map/ppermute | solution.py:164
  77.1 3.7 %collective-permute-done.15.refs_0_ = bf16[512,512]{1,0:T(8,128)(2,1)S(1)} collective-permute-done((bf16[512,512]{1,0:T(8,128)(2,1)S(1)}, bf16[512,512]{1,0:T(8,128)(2,1)S(1)}, u32[]{:S(2)}, u32[]{:S(2)}) %collective-permute-start.15) | collective-permute-done | bytes 524320 | tf_op jit(solution)/shard_map/ppermute | solution.py:164
  80.8 3.1 %collective-permute-done.11.refs_6_.refs_1_ = bf16[4,256,128]{2,1,0:T(8,128)(2,1)S(1)} collective-permute-done((bf16[4,256,128]{2,1,0:T(8,128)(2,1)S(1)}, bf16[4,256,128]{2,1,0:T(8,128)(2,1)S(1)}, u32[]{:S(2)}, u32[]{:S(2)}) %collective-permute-start.11) | collective-permute-done | bytes 262176 | tf_op jit(solution)/shard_map/ppermute | solution.py:164
  83.9 1.9 %shard_map.97 = (bf16[256,512]{1,0:T(8,128)(2,1)S(1)}, bf16[8,256,256]{2,1,0:T(8,128)(2,1)S(1)}) custom-call(s32[4]{0:T(128)S(1)} %copy-done.4, bf16[256,512]{1,0:T(8,128)(2,1)S(1)} %get-tuple-element.28.refs_1_, bf16[512,4096]{1,0:T(8,128)(2,1)S(1)} %copy-done.1, bf16[4,256,128]{2,1,0:T(8,128)(2,1)S(1)} %pad_maximum_fusion.refs_3_.refs_1_, ...), custom_call_target="tpu_custom_call" | custom-call | tf_op jit(solution)/shard_map/pallas_call | solution.py:497
  85.8 0.0 collective-permute-done.16.refs_8_
  85.8 1.4 %shard_map.103 = bf16[2,256,512]{2,1,0:T(8,128)(2,1)S(1)} custom-call(s32[4]{0:T(128)S(1)} %copy-done.4, bf16[256,512]{1,0:T(8,128)(2,1)S(1)} %get-tuple-element.28.refs_1_, bf16[512,4096]{1,0:T(8,128)(2,1)S(1)} %copy-done.1, bf16[256,512]{1,0:T(8,128)(2,1)S(1)} %get-tuple-element.33.refs_3_, bf16[8,256,256]{2,1,0:T(8,128)(2,1)S(1)} %get-tuple-element.34.refs_4_, ...), custom_call_target="tpu_custom_call" | custom-call | tf_op jit(solution)/shard_map/pallas_call | solution.py:497
  87.2 0.6 collective-permute-start.17
  87.8 1.2 %collective-permute-done.17 = bf16[256,512]{1,0:T(8,128)(2,1)S(1)} collective-permute-done((bf16[256,512]{1,0:T(8,128)(2,1)S(1)}, bf16[256,512]{1,0:T(8,128)(2,1)S(1)}, u32[]{:S(2)}, u32[]{:S(2)}) %collective-permute-start.17) | collective-permute-done | bytes 262176 | tf_op jit(solution)/shard_map/ppermute | solution.py:164
  89.0 1.6 %collective-permute-start.18 = (bf16[2,64,512]{2,1,0:T(8,128)(2,1)S(1)}, bf16[2,64,512]{2,1,0:T(8,128)(2,1)S(1)}, u32[]{:S(2)}, u32[]{:S(2)}) collective-permute-start(bf16[2,64,512]{2,1,0:T(8,128)(2,1)S(1)} %get-tuple-element.37), channel_id=1, source_target_pairs={{0,2},{2,0},{4,6},{6,4},{8,10},{10,8},{12,14},{14,12},{1,3},{3,1},... | collective-permute-start | bytes 393224 | tf_op jit(solution)/shard_map/ppermute | solution.py:164
  90.6 0.3 collective-permute-start.19
  90.8 1.7 %collective-permute-start.20 = (bf16[2,64,512]{2,1,0:T(8,128)(2,1)S(1)}, bf16[2,64,512]{2,1,0:T(8,128)(2,1)S(1)}, u32[]{:S(2)}, u32[]{:S(2)}) collective-permute-start(bf16[2,64,512]{2,1,0:T(8,128)(2,1)S(1)} %get-tuple-element.35), channel_id=1, source_target_pairs={{0,6},{2,4},{4,2},{6,0},{8,14},{10,12},{12,10},{14,8},{1,7},{3,5},... | collective-permute-start | bytes 393224 | tf_op jit(solution)/shard_map/ppermute | solution.py:164
  92.5 2.3 %collective-permute-done.18.refs_2_ = bf16[2,64,512]{2,1,0:T(8,128)(2,1)S(1)} collective-permute-done((bf16[2,64,512]{2,1,0:T(8,128)(2,1)S(1)}, bf16[2,64,512]{2,1,0:T(8,128)(2,1)S(1)}, u32[]{:S(2)}, u32[]{:S(2)}) %collective-permute-start.18) | collective-permute-done | bytes 131104 | tf_op jit(solution)/shard_map/ppermute | solution.py:164
  94.8 2.1 %collective-permute-done.19.refs_3_ = bf16[2,64,512]{2,1,0:T(8,128)(2,1)S(1)} collective-permute-done((bf16[2,64,512]{2,1,0:T(8,128)(2,1)S(1)}, bf16[2,64,512]{2,1,0:T(8,128)(2,1)S(1)}, u32[]{:S(2)}, u32[]{:S(2)}) %collective-permute-start.19) | collective-permute-done | bytes 131104 | tf_op jit(solution)/shard_map/ppermute | solution.py:164
  96.9 1.9 %collective-permute-done.20.refs_4_ = bf16[2,64,512]{2,1,0:T(8,128)(2,1)S(1)} collective-permute-done((bf16[2,64,512]{2,1,0:T(8,128)(2,1)S(1)}, bf16[2,64,512]{2,1,0:T(8,128)(2,1)S(1)}, u32[]{:S(2)}, u32[]{:S(2)}) %collective-permute-start.20) | collective-permute-done | bytes 131104 | tf_op jit(solution)/shard_map/ppermute | solution.py:164
  98.8 1.4 %shard_map.104 = bf16[2,64,2048]{2,1,0:T(8,128)(2,1)} custom-call(s32[4]{0:T(128)S(1)} %copy-done.4, bf16[2,64,512]{2,1,0:T(8,128)(2,1)S(1)} %get-tuple-element.36.refs_1_, bf16[2,64,512]{2,1,0:T(8,128)(2,1)S(1)} %collective-permute-done.18.refs_2_, bf16[2,64,512]{2,1,0:T(8,128)(2,1)S(1)} %collective-permute-done.19.refs_3_, ...), custom_call_target="tpu_custom_call" | custom-call | tf_op jit(solution)/shard_map/pallas_call | solution.py:497
  (35 shorter events, 0.2 us)
Async XLA Ops:
  0.0 4.2 %copy-start.2 = (bf16[1024,512]{1,0:T(8,128)(2,1)S(1)}, bf16[1024,512]{1,0:T(8,128)(2,1)}, u32[]{:S(2)}) copy-start(bf16[1024,512]{1,0:T(8,128)(2,1)} %refs_7_.1) | copy-start | bytes 3145732
  0.0 13.9 %copy-start.5 = (f32[64,16]{0,1:T(8,128)S(1)}, f32[64,16]{0,1:T(8,128)}, u32[]{:S(2)}) copy-start(f32[64,16]{0,1:T(8,128)} %param.14) | copy-start | bytes 12292
  0.0 13.9 %copy-start.9 = (f32[64,16]{0,1:T(8,128)S(1)}, f32[64,16]{0,1:T(8,128)}, u32[]{:S(2)}) copy-start(f32[64,16]{0,1:T(8,128)} %param.15) | copy-start | bytes 12292
  0.0 19.0 %copy-start.6 = (f32[4096]{0:T(1024)S(1)}, f32[4096]{0:T(1024)}, u32[]{:S(2)}) copy-start(f32[4096]{0:T(1024)} %param.11) | copy-start | bytes 49156
  0.7 3.5 %copy-start.4 = (s32[4]{0:T(128)S(1)}, s32[4]{0:T(128)}, u32[]{:S(2)}) copy-start(s32[4]{0:T(128)} %pad_add_fusion.place_ref.refs_0_) | copy-start | bytes 52
  4.2 1.0 copy-start.3
  5.8 25.4 %collective-permute-start.3 = (bf16[512,512]{1,0:T(8,128)(2,1)S(1)}, bf16[512,512]{1,0:T(8,128)(2,1)S(1)}, u32[]{:S(2)}, u32[]{:S(2)}) collective-permute-start(bf16[512,512]{1,0:T(8,128)(2,1)S(1)} %shard_map.94.refs_0_), channel_id=1, source_target_pairs={{4,8},{6,10},{8,4},{10,6},{5,9},{7,11},{9,5},{11,7},{20,24},{22,26... | collective-permute-start | bytes 1572872 | tf_op jit(solution)/shard_map/ppermute | solution.py:603
  6.5 12.5 %collective-permute-start = (bf16[1552,128]{1,0:T(8,128)(2,1)}, bf16[1552,128]{1,0:T(8,128)(2,1)S(1)}, u32[]{:S(2)}, u32[]{:S(2)}) collective-permute-start(bf16[1552,128]{1,0:T(8,128)(2,1)} %get-tuple-element.20), channel_id=1, source_target_pairs={{0,2},{2,0},{4,6},{6,4},{8,10},{10,8},{12,14},{14,12},{1,3},{3,1},... | collective-permute-start | bytes 1191944 | tf_op jit(solution)/shard_map/ppermute | solution.py:164
  9.5 16.3 %collective-permute-start.1 = (bf16[1552,128]{1,0:T(8,128)(2,1)}, bf16[1552,128]{1,0:T(8,128)(2,1)S(1)}, u32[]{:S(2)}, u32[]{:S(2)}) collective-permute-start(bf16[1552,128]{1,0:T(8,128)(2,1)} %get-tuple-element.22), channel_id=1, source_target_pairs={{0,4},{2,6},{4,0},{6,2},{8,12},{10,14},{12,8},{14,10},{1,5},{3,7},... | collective-permute-start | bytes 1191944 | tf_op jit(solution)/shard_map/ppermute | solution.py:164
  13.9 17.3 %collective-permute-start.2 = (bf16[1552,128]{1,0:T(8,128)(2,1)}, bf16[1552,128]{1,0:T(8,128)(2,1)S(1)}, u32[]{:S(2)}, u32[]{:S(2)}) collective-permute-start(bf16[1552,128]{1,0:T(8,128)(2,1)} %get-tuple-element.23), channel_id=1, source_target_pairs={{0,6},{2,4},{4,2},{6,0},{8,14},{10,12},{12,10},{14,8},{1,7},{3,5},... | collective-permute-start | bytes 1191944 | tf_op jit(solution)/shard_map/ppermute | solution.py:164
  19.0 2.2 %copy-start = (bf16[512,4096]{1,0:T(8,128)(2,1)S(1)}, bf16[512,4096]{1,0:T(8,128)(2,1)}, u32[]{:S(2)}) copy-start(bf16[512,4096]{1,0:T(8,128)(2,1)} %refs_2_.3) | copy-start | bytes 12582916
  21.2 2.6 %copy-start.7 = (f32[3,64,3]{1,2,0:T(4,128)S(1)}, f32[3,64,3]{1,2,0:T(4,128)}, u32[]{:S(2)}) copy-start(f32[3,64,3]{1,2,0:T(4,128)} %param.13) | copy-start | bytes 6916
  21.2 2.6 %copy-start.8 = (f32[1024]{0:T(1024)S(1)}, f32[1024]{0:T(1024)}, u32[]{:S(2)}) copy-start(f32[1024]{0:T(1024)} %param.16) | copy-start | bytes 12292
  33.3 10.8 %collective-permute-start.4 = (bf16[784,128]{1,0:T(8,128)(2,1)S(1)}, bf16[784,128]{1,0:T(8,128)(2,1)S(1)}, u32[]{:S(2)}, u32[]{:S(2)}) collective-permute-start(bf16[784,128]{1,0:T(8,128)(2,1)S(1)} %get-tuple-element.25.refs_1_), channel_id=1, source_target_pairs={{0,8},{2,10},{4,12},{6,14},{8,0},{10,2},{12,4},{14,6},{1,9},{3,11}... | collective-permute-start | bytes 602120 | tf_op jit(solution)/shard_map/ppermute | solution.py:164
  44.2 22.5 %collective-permute-start.13 = (bf16[512,512]{1,0:T(8,128)(2,1)S(1)}, bf16[512,512]{1,0:T(8,128)(2,1)S(1)}, u32[]{:S(2)}, u32[]{:S(2)}) collective-permute-start(bf16[512,512]{1,0:T(8,128)(2,1)S(1)} %shard_map.98), channel_id=1, source_target_pairs={{0,12},{2,14},{12,0},{14,2},{1,13},{3,15},{13,1},{15,3},{16,28},{1... | collective-permute-start | bytes 1572872 | tf_op jit(solution)/shard_map/ppermute | solution.py:657
  47.4 5.7 %collective-permute-start.5 = (bf16[3,256,128]{2,1,0:T(8,128)(2,1)S(1)}, bf16[3,256,128]{2,1,0:T(8,128)(2,1)S(1)}, u32[]{:S(2)}, u32[]{:S(2)}) collective-permute-start(bf16[3,256,128]{2,1,0:T(8,128)(2,1)S(1)} %bitcast.20), channel_id=1, source_target_pairs={{0,16},{16,0},{1,17},{17,1},{2,18},{18,2},{3,19},{19,3},{4,20},{20... | collective-permute-start | bytes 589832 | tf_op jit(solution)/shard_map/ppermute | solution.py:164
  57.2 2.8 %collective-permute-start.6 = (bf16[256,128]{1,0:T(8,128)(2,1)S(1)}, bf16[256,128]{1,0:T(8,128)(2,1)S(1)}, u32[]{:S(2)}, u32[]{:S(2)}) collective-permute-start(bf16[256,128]{1,0:T(8,128)(2,1)S(1)} %get-tuple-element.30), channel_id=1, source_target_pairs={{0,1},{1,0},{2,3},{3,2},{4,5},{5,4},{6,7},{7,6},{8,9},{9,8},{10,11... | collective-permute-start | bytes 196616 | tf_op jit(solution)/shard_map/ppermute | solution.py:164
  57.2 8.1 %collective-permute-start.7 = (bf16[256,128]{1,0:T(8,128)(2,1)S(1)}, bf16[256,128]{1,0:T(8,128)(2,1)S(1)}, u32[]{:S(2)}, u32[]{:S(2)}) collective-permute-start(bf16[256,128]{1,0:T(8,128)(2,1)S(1)} %get-tuple-element.31), channel_id=1, source_target_pairs={{0,8},{2,10},{4,12},{6,14},{8,0},{10,2},{12,4},{14,6},{1,9},{3,11}... | collective-permute-start | bytes 196616 | tf_op jit(solution)/shard_map/ppermute | solution.py:164
  57.3 9.3 %collective-permute-start.8 = (bf16[256,128]{1,0:T(8,128)(2,1)S(1)}, bf16[256,128]{1,0:T(8,128)(2,1)S(1)}, u32[]{:S(2)}, u32[]{:S(2)}) collective-permute-start(bf16[256,128]{1,0:T(8,128)(2,1)S(1)} %get-tuple-element.32), channel_id=1, source_target_pairs={{0,9},{1,8},{2,11},{3,10},{4,13},{5,12},{6,15},{7,14},{8,1},{9,0},... | collective-permute-start | bytes 196616 | tf_op jit(solution)/shard_map/ppermute | solution.py:172
  66.7 17.2 %copy-start.1 = (bf16[512,4096]{1,0:T(8,128)(2,1)S(1)}, bf16[512,4096]{1,0:T(8,128)(2,1)}, u32[]{:S(2)}) copy-start(bf16[512,4096]{1,0:T(8,128)(2,1)} %refs_2_.3) | copy-start | bytes 12582916
  66.8 14.0 %collective-permute-start.15 = (bf16[512,512]{1,0:T(8,128)(2,1)S(1)}, bf16[512,512]{1,0:T(8,128)(2,1)S(1)}, u32[]{:S(2)}, u32[]{:S(2)}) collective-permute-start(bf16[512,512]{1,0:T(8,128)(2,1)S(1)} %shard_map.99.refs_5_), channel_id=1, source_target_pairs={{0,16},{16,0},{1,17},{17,1},{2,18},{18,2},{3,19},{19,3},{4,20},{20... | collective-permute-start | bytes 1572872 | tf_op jit(solution)/shard_map/ppermute | solution.py:164
  68.3 15.5 %collective-permute-start.12 = (bf16[1024,512]{1,0:T(8,128)(2,1)S(1)}, bf16[1024,512]{1,0:T(8,128)(2,1)S(1)}, u32[]{:S(2)}, u32[]{:S(2)}) collective-permute-start(bf16[1024,512]{1,0:T(8,128)(2,1)S(1)} %copy-done.2), channel_id=1, source_target_pairs={{0,1},{1,0},{2,3},{3,2},{4,5},{5,4},{6,7},{7,6},{8,9},{9,8},{10,11... | collective-permute-start | bytes 3145736 | tf_op jit(solution)/shard_map/ppermute | solution.py:164
  68.3 8.7 %collective-permute-start.9 = (bf16[4,256,128]{2,1,0:T(8,128)(2,1)S(1)}, bf16[4,256,128]{2,1,0:T(8,128)(2,1)S(1)}, u32[]{:S(2)}, u32[]{:S(2)}) collective-permute-start(bf16[4,256,128]{2,1,0:T(8,128)(2,1)S(1)} %pad_maximum_fusion.refs_3_.refs_1_), channel_id=1, source_target_pairs={{0,2},{2,0},{4,6},{6,4},{8,10},{10,8},{12,14},{14,12},{1,3},{3,1},... | collective-permute-start | bytes 786440 | tf_op jit(solution)/shard_map/ppermute | solution.py:164
  69.9 10.9 %collective-permute-start.10 = (bf16[4,256,128]{2,1,0:T(8,128)(2,1)S(1)}, bf16[4,256,128]{2,1,0:T(8,128)(2,1)S(1)}, u32[]{:S(2)}, u32[]{:S(2)}) collective-permute-start(bf16[4,256,128]{2,1,0:T(8,128)(2,1)S(1)} %pad_maximum_fusion.refs_3_.refs_1_), channel_id=1, source_target_pairs={{0,4},{2,6},{4,0},{6,2},{8,12},{10,14},{12,8},{14,10},{1,5},{3,7},... | collective-permute-start | bytes 786440 | tf_op jit(solution)/shard_map/ppermute | solution.py:164
  69.9 14.0 %collective-permute-start.11 = (bf16[4,256,128]{2,1,0:T(8,128)(2,1)S(1)}, bf16[4,256,128]{2,1,0:T(8,128)(2,1)S(1)}, u32[]{:S(2)}, u32[]{:S(2)}) collective-permute-start(bf16[4,256,128]{2,1,0:T(8,128)(2,1)S(1)} %pad_maximum_fusion.refs_3_.refs_1_), channel_id=1, source_target_pairs={{0,6},{2,4},{4,2},{6,0},{8,14},{10,12},{12,10},{14,8},{1,7},{3,5},... | collective-permute-start | bytes 786440 | tf_op jit(solution)/shard_map/ppermute | solution.py:164
  77.1 8.7 %collective-permute-start.14 = (bf16[512,512]{1,0:T(8,128)(2,1)S(1)}, bf16[512,512]{1,0:T(8,128)(2,1)S(1)}, u32[]{:S(2)}, u32[]{:S(2)}) collective-permute-start(bf16[512,512]{1,0:T(8,128)(2,1)S(1)} %shard_map.99.refs_5_), channel_id=1, source_target_pairs={{0,1},{1,0},{2,3},{3,2},{4,5},{5,4},{6,7},{7,6},{8,9},{9,8},{10,11... | collective-permute-start | bytes 1572872 | tf_op jit(solution)/shard_map/ppermute | solution.py:164
  83.9 1.9 %collective-permute-start.16 = (bf16[512,512]{1,0:T(8,128)(2,1)S(1)}, bf16[512,512]{1,0:T(8,128)(2,1)S(1)}, u32[]{:S(2)}, u32[]{:S(2)}) collective-permute-start(bf16[512,512]{1,0:T(8,128)(2,1)S(1)} %shard_map.102.refs_7_), channel_id=1, source_target_pairs={{0,1},{1,0},{2,3},{3,2},{4,5},{5,4},{6,7},{7,6},{8,9},{9,8},{10,11... | collective-permute-start | bytes 1572872 | tf_op jit(solution)/shard_map/ppermute | solution.py:164
  87.2 1.7 %collective-permute-start.17 = (bf16[256,512]{1,0:T(8,128)(2,1)S(1)}, bf16[256,512]{1,0:T(8,128)(2,1)S(1)}, u32[]{:S(2)}, u32[]{:S(2)}) collective-permute-start(bf16[256,512]{1,0:T(8,128)(2,1)S(1)} %get-tuple-element.39), channel_id=1, source_target_pairs={{0,1},{1,0},{2,3},{3,2},{4,5},{5,4},{6,7},{7,6},{8,9},{9,8},{10,11... | collective-permute-start | bytes 786440 | tf_op jit(solution)/shard_map/ppermute | solution.py:164
  89.0 5.8 %collective-permute-start.18 = (bf16[2,64,512]{2,1,0:T(8,128)(2,1)S(1)}, bf16[2,64,512]{2,1,0:T(8,128)(2,1)S(1)}, u32[]{:S(2)}, u32[]{:S(2)}) collective-permute-start(bf16[2,64,512]{2,1,0:T(8,128)(2,1)S(1)} %get-tuple-element.37), channel_id=1, source_target_pairs={{0,2},{2,0},{4,6},{6,4},{8,10},{10,8},{12,14},{14,12},{1,3},{3,1},... | collective-permute-start | bytes 393224 | tf_op jit(solution)/shard_map/ppermute | solution.py:164
  90.6 6.4 %collective-permute-start.19 = (bf16[2,64,512]{2,1,0:T(8,128)(2,1)S(1)}, bf16[2,64,512]{2,1,0:T(8,128)(2,1)S(1)}, u32[]{:S(2)}, u32[]{:S(2)}) collective-permute-start(bf16[2,64,512]{2,1,0:T(8,128)(2,1)S(1)} %get-tuple-element.38), channel_id=1, source_target_pairs={{0,4},{2,6},{4,0},{6,2},{8,12},{10,14},{12,8},{14,10},{1,5},{3,7},... | collective-permute-start | bytes 393224 | tf_op jit(solution)/shard_map/ppermute | solution.py:164
  90.8 8.0 %collective-permute-start.20 = (bf16[2,64,512]{2,1,0:T(8,128)(2,1)S(1)}, bf16[2,64,512]{2,1,0:T(8,128)(2,1)S(1)}, u32[]{:S(2)}, u32[]{:S(2)}) collective-permute-start(bf16[2,64,512]{2,1,0:T(8,128)(2,1)S(1)} %get-tuple-element.35), channel_id=1, source_target_pairs={{0,6},{2,4},{4,2},{6,0},{8,14},{10,12},{12,10},{14,8},{1,7},{3,5},... | collective-permute-start | bytes 393224 | tf_op jit(solution)/shard_map/ppermute | solution.py:164

commit v3 on v2

--- a/solution.py
+++ b/solution.py
@@ -200,11 +200,11 @@
     out_ref[...] = (own * lax.rsqrt(mean + epsilon) * gain_ref[...]).astype(bf16)
 
 
-def pack_kernel(place_ref, token_ref, weight_ref, *refs):
+def pack_kernel(token_ref, weight_ref, *refs):
     out_refs, sems = refs[:-1], refs[-1]
-    quad, group = place_ref[0], place_ref[2]
     branches, depth, channels = weight_ref.shape
     members = len(out_refs)
+    quad, group = lax.axis_index("ctx") % members, lax.axis_index("groups")
     block = channels // members
     copies = []
     for m in (1, 2, 3, 0):
@@ -413,9 +413,11 @@
     mine_ref[...] = picked_ref[pl.ds(pl.multiple_of((2 * core + half) * part, part), part), :]
 
 
-def offer_kernel(place_ref, rows_ref, packed_ref, out_ref):
+def offer_kernel(place_ref, rows_ref, packed_ref, first_ref, second_ref):
     del place_ref, packed_ref
-    out_ref[...] = rows_ref[...]
+    count = first_ref.shape[0]
+    first_ref[...] = rows_ref[:count]
+    second_ref[...] = rows_ref[count:]
 
 
 def residual(picked_ref, table_ref, first, width):
@@ -548,15 +550,11 @@
     packed = pl.pallas_call(
         pack_kernel,
         out_shape=[shaped(branches * depth + SPARE, LANES, dtype=bf16)] * members,
-        in_specs=[
-            pl.BlockSpec(memory_space=pltpu.SMEM),
-            pl.BlockSpec(memory_space=pltpu.VMEM),
-            anywhere,
-        ],
+        in_specs=[pl.BlockSpec(memory_space=pltpu.VMEM), anywhere],
         out_specs=[pl.BlockSpec(memory_space=pltpu.VMEM)] * members,
         scratch_shapes=[pltpu.SemaphoreType.DMA((members, branches))],
-        compiler_params=pltpu.CompilerParams(vmem_limit_bytes=62 * MIB),
-    )(place, tokens, weights)
+        compiler_params=pltpu.CompilerParams(vmem_limit_bytes=61 * MIB),
+    )(tokens, weights)
     gathered = [packed[0]] + [swapped(packed[m], "ctx", m) for m in range(1, members)]
     length = 2 * members * rows
 
@@ -564,15 +562,15 @@
     width = output_proj.shape[1]
     offered = pl.pallas_call(
         offer_kernel,
-        out_shape=shaped(half_rows, width, dtype=bf16),
+        out_shape=[shaped(half_rows // 2, width, dtype=bf16)] * 2,
         grid_spec=pltpu.PrefetchScalarGridSpec(
             num_scalar_prefetch=1,
             grid=(1,),
             in_specs=[pl.BlockSpec((half_rows, width), lambda i, place: (place[2], 0)), anywhere],
-            out_specs=pl.BlockSpec((half_rows, width), lambda i, place: (0, 0)),
+            out_specs=[pl.BlockSpec((half_rows // 2, width), lambda i, place: (0, 0))] * 2,
         ),
         compiler_params=pltpu.CompilerParams(vmem_limit_bytes=4 * MIB),
-    )(place, output_proj, packed[0])
+    )(place, output_proj, packed[1])
     count = 2 * members
     inner = [(i, count - 2 - i + 2 * (i % 2)) for i in range(members // 2, members + members // 2)]
     outer = [
@@ -600,7 +598,7 @@
         compiler_params=pltpu.CompilerParams(vmem_limit_bytes=16 * MIB),
     )(place, embed_table, norm_gain.reshape(1, features), embed_table, gathered[1])
 
-    inner_fetched = lax.ppermute(offered, "ctx", inner)
+    inner_fetched = [lax.ppermute(rows_part, "ctx", inner) for rows_part in offered]
     amp = residue * jnp.sqrt(-jnp.expm1(-2.0 * pole_rate))
     across = (LANES // pole_rate.shape[1] + 1) * CHUNK
     matrices, lines = called(
@@ -624,7 +622,7 @@
         (place,),
         normed,
         *gathered,
-        earlier=(matrices, inner_fetched),
+        earlier=(matrices, *inner_fetched),
     )
     arrived = swapped(send, "ctx", members)
     own = (keep + arrived[:table_rows].astype(f32)).astype(bf16)
@@ -654,8 +652,12 @@
     )
     gated = [piece] + [swapped(piece, "ctx", m) for m in range(1, members)]
 
-    outer_fetched = lax.ppermute(after(offered, own), "ctx", outer)
-    fetched = jnp.where((ctx >= members // 2) & (ctx < members + members // 2), inner_fetched, outer_fetched)
+    outer_fetched = [lax.ppermute(after(rows_part, own), "ctx", outer) for rows_part in offered]
+    fetched = jnp.where(
+        (ctx >= members // 2) & (ctx < members + members // 2),
+        jnp.concatenate(inner_fetched),
+        jnp.concatenate(outer_fetched),
+    )
     fetched = after(fetched, piece)
     shared = swapped(fetched, "groups", 1)
     for ready in gated[1:]:

time: 100 us -> 96 us (0.960)
  waiting for transfers between devices: 49.8 us -> 43.7 us
  starting transfers between devices: 26.7 us -> 28.8 us
    ppermute x18, waiting for transfers between devices: 48.5 us -> 42.3 us  [swapped(): return lax.ppermute(value, axis, [(i, i ^ mask) for i in range(count)])]
    ppermute x2 -> x4, starting transfers between devices: 3.95 us -> 8.98 us  [the longest x2 7.63 us: quad_body(): lax.ppermute(after(rows_part, own), 'ctx', outer)]
    ppermute x18, starting transfers between devices: 20 us -> 17.2 us  [swapped(): return lax.ppermute(value, axis, [(i, i ^ mask) for i in range(count)])]
  transfers between devices with their start and end apart: 21 -> 23, of which waited for: 13 -> 12; matrix products, arithmetic and copies ran while one was open for 0% -> 0% of each run, Pallas kernels for 10% -> 12%
where the time goes in v3:
time: 96 us; the launch traced here: 95.7 us
  waiting for transfers between devices  43.7 us (46%)
  starting transfers between devices  28.8 us (30%)
  Pallas kernels  19.4 us (20%)
  local copies, waits for them, and re-layouts  3.26 us (3%)
    ppermute x18, waiting for transfers between devices, swapped(): return lax.ppermute(value, axis, [(i, i ^ mask) for i in range(count)])  42.3 us
    ppermute x18, starting transfers between devices, swapped(): return lax.ppermute(value, axis, [(i, i ^ mask) for i in range(count)])  17.2 us
    pallas_call x6, Pallas kernels, called(): pl.pallas_call(body, out_shape=out_shape, in_specs=[smem] * len(scalars)...  12.7 us
    ppermute x2, starting transfers between devices, quad_body(): lax.ppermute(after(rows_part, own), 'ctx', outer)  7.63 us
    pallas_call x1, Pallas kernels, quad_body(): pl.pallas_call(pack_kernel, out_shape=[shaped(branches * depth + SPARE, L...  3.5 us
    unnamed x20, local copies, waits for them, and re-layouts  3.22 us
    ppermute x1, starting transfers between devices, swapped_both(): return lax.ppermute(value, ('ctx', 'chan'), pairs)  2.68 us
    pallas_call x1, Pallas kernels, quad_body(): pl.pallas_call(norm_kernel, out_shape=shaped(vocab, part, dtype=bf16), gr...  2.56 us
  transfers between devices with their start and end apart: 23, of which 12 were waited for; matrix products, arithmetic and copies ran while one was open for 0% of the time, Pallas kernels for 12%

profile of v3, /device:TPU:0, one launch (start us, length us, event | category | flops | bytes accessed | tf_op | source)
XLA Modules:
  0.0 95.7 jit_solution(5520188060259565295)
XLA Ops:
  0.0 3.5 %shard_map.91 = (bf16[1552,128]{1,0:T(8,128)(2,1)}, bf16[1552,128]{1,0:T(8,128)(2,1)}, bf16[1552,128]{1,0:T(8,128)(2,1)}, bf16[1552,128]{1,0:T(8,128)(2,1)}) custom-call(s32[2,64]{1,0:T(2,128)} %token_ref.1, bf16[3,512,1024]{2,1,0:T(8,128)(2,1)} %bitcast.28), custom_call_target="tpu_custom_call" | custom-call | tf_op jit(solution)/shard_map/pallas_call | solution.py:550
  3.5 3.0 %collective-permute-start = (bf16[1552,128]{1,0:T(8,128)(2,1)}, bf16[1552,128]{1,0:T(8,128)(2,1)S(1)}, u32[]{:S(2)}, u32[]{:S(2)}) collective-permute-start(bf16[1552,128]{1,0:T(8,128)(2,1)} %get-tuple-element.22.packed_ref), channel_id=1, source_target_pairs={{0,2},{2,0},{4,6},{6,4},{8,10},{10,8},{12,14},{14,12},{1,3},{3,1},... | collective-permute-start | bytes 1191944 | tf_op jit(solution)/shard_map/ppermute | solution.py:164
  6.6 1.6 %collective-permute-start.1 = (bf16[1552,128]{1,0:T(8,128)(2,1)}, bf16[1552,128]{1,0:T(8,128)(2,1)S(1)}, u32[]{:S(2)}, u32[]{:S(2)}) collective-permute-start(bf16[1552,128]{1,0:T(8,128)(2,1)} %get-tuple-element.24), channel_id=1, source_target_pairs={{0,4},{2,6},{4,0},{6,2},{8,12},{10,14},{12,8},{14,10},{1,5},{3,7},... | collective-permute-start | bytes 1191944 | tf_op jit(solution)/shard_map/ppermute | solution.py:164
  8.1 0.1 pad_add_fusion.place_ref.refs_0_
  8.2 1.0 %copy-done.4 = bf16[1552,128]{1,0:T(8,128)(2,1)S(1)} copy-done((bf16[1552,128]{1,0:T(8,128)(2,1)S(1)}, bf16[1552,128]{1,0:T(8,128)(2,1)}, u32[]{:S(2)}) %copy-start.4) | copy-done | bytes 397336
  9.2 0.6 shard_map.94
  9.8 0.7 collective-permute-start.3
  10.5 0.7 collective-permute-start.4
  11.2 4.8 %collective-permute-done.packed_ref.refs_5_.refs_3_ = bf16[1552,128]{1,0:T(8,128)(2,1)S(1)} collective-permute-done((bf16[1552,128]{1,0:T(8,128)(2,1)}, bf16[1552,128]{1,0:T(8,128)(2,1)S(1)}, u32[]{:S(2)}, u32[]{:S(2)}) %collective-permute-start) | collective-permute-done | bytes 397344 | tf_op jit(solution)/shard_map/ppermute | solution.py:164
  16.0 2.2 %copy-done = bf16[512,4096]{1,0:T(8,128)(2,1)S(1)} copy-done((bf16[512,4096]{1,0:T(8,128)(2,1)S(1)}, bf16[512,4096]{1,0:T(8,128)(2,1)}, u32[]{:S(2)}) %copy-start) | copy-done | bytes 4194328
  18.2 2.6 %shard_map.92.refs_1_ = bf16[512,2048]{1,0:T(8,128)(2,1)S(1)} custom-call(s32[4]{0:T(128)S(1)} %pad_add_fusion.place_ref.refs_0_, bf16[512,4096]{1,0:T(8,128)(2,1)S(1)} %copy-done, f32[1,4096]{1,0:T(1,128)S(1)} %bitcast.25, bf16[512,4096]{1,0:T(8,128)(2,1)S(1)} %copy-done, bf16[1552,128]{1,0:T(8,128)(2,1)S(1)} %collective-permute-done.packed_ref.refs_5_.refs_3_), custom_call_target="tpu_custom_call" | custom-call | tf_op jit(solution)/shard_map/pallas_call | solution.py:584
  20.8 2.1 %shard_map.93 = (bf16[128,2560]{1,0:T(8,128)(2,1)S(1)}, f32[160,128]{1,0:T(8,128)S(1)}) custom-call(s32[4]{0:T(128)S(1)} %pad_add_fusion.place_ref.refs_0_, f32[16,64]{1,0:T(8,128)S(1)} %bitcast.24, f32[16,64]{1,0:T(8,128)S(1)} %multiply_bitcast_fusion.refs_2_, f32[3,3,64]{2,1,0:T(4,128)S(1)} %bitcast.26, f32[8,128]{1,0:T(8,128)S(1)} %bitcast.27, ...), custom_call_target="tpu_custom_call" | custom-call | tf_op jit(solution)/shard_map/pallas_call | solution.py:499
  22.8 0.0 collective-permute-done.1.refs_4_
  22.9 2.9 %collective-permute-done.2.refs_5_ = bf16[1552,128]{1,0:T(8,128)(2,1)S(1)} collective-permute-done((bf16[1552,128]{1,0:T(8,128)(2,1)}, bf16[1552,128]{1,0:T(8,128)(2,1)S(1)}, u32[]{:S(2)}, u32[]{:S(2)}) %collective-permute-start.2) | collective-permute-done | bytes 397344 | tf_op jit(solution)/shard_map/ppermute | solution.py:164
  25.7 2.1 %shard_map.95 = (f32[768,128]{1,0:T(8,128)S(1)}, bf16[784,128]{1,0:T(8,128)(2,1)S(1)}) custom-call(s32[4]{0:T(128)S(1)} %pad_add_fusion.place_ref.refs_0_, bf16[512,2048]{1,0:T(8,128)(2,1)S(1)} %shard_map.92.refs_1_, bf16[1552,128]{1,0:T(8,128)(2,1)S(1)} %copy-done.3, bf16[1552,128]{1,0:T(8,128)(2,1)S(1)} %collective-permute-done.packed_ref.refs_5_.refs_3_, ...), custom_call_target="tpu_custom_call" | custom-call | tf_op jit(solution)/shard_map/pallas_call | solution.py:499
  27.8 2.8 %collective-permute-start.5 = (bf16[784,128]{1,0:T(8,128)(2,1)S(1)}, bf16[784,128]{1,0:T(8,128)(2,1)S(1)}, u32[]{:S(2)}, u32[]{:S(2)}) collective-permute-start(bf16[784,128]{1,0:T(8,128)(2,1)S(1)} %get-tuple-element.29.refs_1_), channel_id=1, source_target_pairs={{0,8},{2,10},{4,12},{6,14},{8,0},{10,2},{12,4},{14,6},{1,9},{3,11}... | collective-permute-start | bytes 602120 | tf_op jit(solution)/shard_map/ppermute | solution.py:164
  30.6 8.3 %collective-permute-done.5.refs_2_ = bf16[784,128]{1,0:T(8,128)(2,1)S(1)} collective-permute-done((bf16[784,128]{1,0:T(8,128)(2,1)S(1)}, bf16[784,128]{1,0:T(8,128)(2,1)S(1)}, u32[]{:S(2)}, u32[]{:S(2)}) %collective-permute-start.5) | collective-permute-done | bytes 200736 | tf_op jit(solution)/shard_map/ppermute | solution.py:164
  39.0 1.4 %collective-permute-start.6 = (bf16[3,256,128]{2,1,0:T(8,128)(2,1)S(1)}, bf16[3,256,128]{2,1,0:T(8,128)(2,1)S(1)}, u32[]{:S(2)}, u32[]{:S(2)}) collective-permute-start(bf16[3,256,128]{2,1,0:T(8,128)(2,1)S(1)} %bitcast.19), channel_id=1, source_target_pairs={{0,16},{16,0},{1,17},{17,1},{2,18},{18,2},{3,19},{19,3},{4,20},{20... | collective-permute-start | bytes 589832 | tf_op jit(solution)/shard_map/ppermute | solution.py:164
  40.4 5.4 %collective-permute-start.14 = (bf16[256,512]{1,0:T(8,128)(2,1)S(1)}, bf16[256,512]{1,0:T(8,128)(2,1)S(1)}, u32[]{:S(2)}, u32[]{:S(2)}) collective-permute-start(bf16[256,512]{1,0:T(8,128)(2,1)S(1)} %shard_map.98), channel_id=1, source_target_pairs={{0,12},{2,14},{12,0},{14,2},{1,13},{3,15},{13,1},{15,3},{16,28},{1... | collective-permute-start | bytes 786440 | tf_op jit(solution)/shard_map/ppermute | solution.py:655
  45.8 2.2 %collective-permute-start.15 = (bf16[256,512]{1,0:T(8,128)(2,1)S(1)}, bf16[256,512]{1,0:T(8,128)(2,1)S(1)}, u32[]{:S(2)}, u32[]{:S(2)}) collective-permute-start(bf16[256,512]{1,0:T(8,128)(2,1)S(1)} %shard_map.99), channel_id=1, source_target_pairs={{0,12},{2,14},{12,0},{14,2},{1,13},{3,15},{13,1},{15,3},{16,28},{1... | collective-permute-start | bytes 786440 | tf_op jit(solution)/shard_map/ppermute | solution.py:655
  48.0 4.0 %shard_map.96 = (bf16[256,128]{1,0:T(8,128)(2,1)S(1)}, bf16[256,128]{1,0:T(8,128)(2,1)S(1)}, bf16[256,128]{1,0:T(8,128)(2,1)S(1)}, bf16[256,128]{1,0:T(8,128)(2,1)S(1)}, bf16[256,512]{1,0:T(8,128)(2,1)S(1)}) custom-call(s32[4]{0:T(128)S(1)} %pad_add_fusion.place_ref.refs_0_, bf16[784,128]{1,0:T(8,128)(2,1)S(1)} %get-tuple-element.29.refs_1_, ...), custom_call_target="tpu_custom_call" | custom-call | tf_op jit(solution)/shard_map/pallas_call | solution.py:499
  52.0 0.1 collective-permute-start.7
  52.1 0.1 collective-permute-start.8
  52.2 2.7 %collective-permute-start.9 = (bf16[256,128]{1,0:T(8,128)(2,1)S(1)}, bf16[256,128]{1,0:T(8,128)(2,1)S(1)}, u32[]{:S(2)}, u32[]{:S(2)}) collective-permute-start(bf16[256,128]{1,0:T(8,128)(2,1)S(1)} %get-tuple-element.36), channel_id=1, source_target_pairs={{0,9},{1,8},{2,11},{3,10},{4,13},{5,12},{6,15},{7,14},{8,1},{9,0},... | collective-permute-start | bytes 196616 | tf_op jit(solution)/shard_map/ppermute | solution.py:172
  54.9 0.0 collective-permute-done.7
  54.9 6.9 %collective-permute-done.8 = bf16[256,128]{1,0:T(8,128)(2,1)S(1)} collective-permute-done((bf16[256,128]{1,0:T(8,128)(2,1)S(1)}, bf16[256,128]{1,0:T(8,128)(2,1)S(1)}, u32[]{:S(2)}, u32[]{:S(2)}) %collective-permute-start.8) | collective-permute-done | bytes 65568 | tf_op jit(solution)/shard_map/ppermute | solution.py:164
  61.8 1.3 %collective-permute-done.9 = bf16[256,128]{1,0:T(8,128)(2,1)S(1)} collective-permute-done((bf16[256,128]{1,0:T(8,128)(2,1)S(1)}, bf16[256,128]{1,0:T(8,128)(2,1)S(1)}, u32[]{:S(2)}, u32[]{:S(2)}) %collective-permute-start.9) | collective-permute-done | bytes 65568 | tf_op jit(solution)/shard_map/ppermute | solution.py:172
  63.1 0.0 copy-start.1
  63.1 0.1 maximum_select_fusion.refs_0_
  63.3 0.6 collective-permute-start.17
  63.9 1.5 %collective-permute-start.10 = (bf16[4,256,128]{2,1,0:T(8,128)(2,1)S(1)}, bf16[4,256,128]{2,1,0:T(8,128)(2,1)S(1)}, u32[]{:S(2)}, u32[]{:S(2)}) collective-permute-start(bf16[4,256,128]{2,1,0:T(8,128)(2,1)S(1)} %pad_maximum_fusion.refs_3_.refs_1_), channel_id=1, source_target_pairs={{0,2},{2,0},{4,6},{6,4},{8,10},{10,8},{12,14},{14,12},{1,3},{3,1},... | collective-permute-start | bytes 786440 | tf_op jit(solution)/shard_map/ppermute | solution.py:164
  65.4 0.8 collective-permute-start.11
  66.2 1.2 %collective-permute-start.12 = (bf16[4,256,128]{2,1,0:T(8,128)(2,1)S(1)}, bf16[4,256,128]{2,1,0:T(8,128)(2,1)S(1)}, u32[]{:S(2)}, u32[]{:S(2)}) collective-permute-start(bf16[4,256,128]{2,1,0:T(8,128)(2,1)S(1)} %pad_maximum_fusion.refs_3_.refs_1_), channel_id=1, source_target_pairs={{0,6},{2,4},{4,2},{6,0},{8,14},{10,12},{12,10},{14,8},{1,7},{3,5},... | collective-permute-start | bytes 786440 | tf_op jit(solution)/shard_map/ppermute | solution.py:164
  67.4 5.2 %collective-permute-done.10.refs_4_.refs_1_ = bf16[4,256,128]{2,1,0:T(8,128)(2,1)S(1)} collective-permute-done((bf16[4,256,128]{2,1,0:T(8,128)(2,1)S(1)}, bf16[4,256,128]{2,1,0:T(8,128)(2,1)S(1)}, u32[]{:S(2)}, u32[]{:S(2)}) %collective-permute-start.10) | collective-permute-done | bytes 262176 | tf_op jit(solution)/shard_map/ppermute | solution.py:164
  72.6 4.7 %collective-permute-done.17.refs_0_ = bf16[512,512]{1,0:T(8,128)(2,1)S(1)} collective-permute-done((bf16[512,512]{1,0:T(8,128)(2,1)S(1)}, bf16[512,512]{1,0:T(8,128)(2,1)S(1)}, u32[]{:S(2)}, u32[]{:S(2)}) %collective-permute-start.17) | collective-permute-done | bytes 524320 | tf_op jit(solution)/shard_map/ppermute | solution.py:164
  77.3 2.1 %collective-permute-done.12.refs_6_.refs_1_ = bf16[4,256,128]{2,1,0:T(8,128)(2,1)S(1)} collective-permute-done((bf16[4,256,128]{2,1,0:T(8,128)(2,1)S(1)}, bf16[4,256,128]{2,1,0:T(8,128)(2,1)S(1)}, u32[]{:S(2)}, u32[]{:S(2)}) %collective-permute-start.12) | collective-permute-done | bytes 262176 | tf_op jit(solution)/shard_map/ppermute | solution.py:164
  79.4 1.9 %shard_map.97 = (bf16[256,512]{1,0:T(8,128)(2,1)S(1)}, bf16[8,256,256]{2,1,0:T(8,128)(2,1)S(1)}) custom-call(s32[4]{0:T(128)S(1)} %pad_add_fusion.place_ref.refs_0_, bf16[256,512]{1,0:T(8,128)(2,1)S(1)} %get-tuple-element.32.refs_1_, bf16[512,4096]{1,0:T(8,128)(2,1)S(1)} %copy-done.1, bf16[4,256,128]{2,1,0:T(8,128)(2,1)S(1)} %pad_maximum_fusion.refs_3_.refs_1_, ...), custom_call_target="tpu_custom_call" | custom-call | tf_op jit(solution)/shard_map/pallas_call | solution.py:499
  81.3 0.0 collective-permute-done.18.refs_8_
  81.3 1.4 %shard_map.104 = bf16[2,256,512]{2,1,0:T(8,128)(2,1)S(1)} custom-call(s32[4]{0:T(128)S(1)} %pad_add_fusion.place_ref.refs_0_, bf16[256,512]{1,0:T(8,128)(2,1)S(1)} %get-tuple-element.32.refs_1_, bf16[512,4096]{1,0:T(8,128)(2,1)S(1)} %copy-done.1, bf16[256,512]{1,0:T(8,128)(2,1)S(1)} %get-tuple-element.37.refs_3_, ...), custom_call_target="tpu_custom_call" | custom-call | tf_op jit(solution)/shard_map/pallas_call | solution.py:499
  82.8 0.6 collective-permute-start.19
  83.3 1.2 %collective-permute-done.19 = bf16[256,512]{1,0:T(8,128)(2,1)S(1)} collective-permute-done((bf16[256,512]{1,0:T(8,128)(2,1)S(1)}, bf16[256,512]{1,0:T(8,128)(2,1)S(1)}, u32[]{:S(2)}, u32[]{:S(2)}) %collective-permute-start.19) | collective-permute-done | bytes 262176 | tf_op jit(solution)/shard_map/ppermute | solution.py:164
  84.5 1.6 %collective-permute-start.20 = (bf16[2,64,512]{2,1,0:T(8,128)(2,1)S(1)}, bf16[2,64,512]{2,1,0:T(8,128)(2,1)S(1)}, u32[]{:S(2)}, u32[]{:S(2)}) collective-permute-start(bf16[2,64,512]{2,1,0:T(8,128)(2,1)S(1)} %get-tuple-element.41), channel_id=1, source_target_pairs={{0,2},{2,0},{4,6},{6,4},{8,10},{10,8},{12,14},{14,12},{1,3},{3,1},... | collective-permute-start | bytes 393224 | tf_op jit(solution)/shard_map/ppermute | solution.py:164
  86.1 0.8 collective-permute-start.21
  86.9 1.2 %collective-permute-start.22 = (bf16[2,64,512]{2,1,0:T(8,128)(2,1)S(1)}, bf16[2,64,512]{2,1,0:T(8,128)(2,1)S(1)}, u32[]{:S(2)}, u32[]{:S(2)}) collective-permute-start(bf16[2,64,512]{2,1,0:T(8,128)(2,1)S(1)} %get-tuple-element.39), channel_id=1, source_target_pairs={{0,6},{2,4},{4,2},{6,0},{8,14},{10,12},{12,10},{14,8},{1,7},{3,5},... | collective-permute-start | bytes 393224 | tf_op jit(solution)/shard_map/ppermute | solution.py:164
  88.1 2.3 %collective-permute-done.20.refs_2_ = bf16[2,64,512]{2,1,0:T(8,128)(2,1)S(1)} collective-permute-done((bf16[2,64,512]{2,1,0:T(8,128)(2,1)S(1)}, bf16[2,64,512]{2,1,0:T(8,128)(2,1)S(1)}, u32[]{:S(2)}, u32[]{:S(2)}) %collective-permute-start.20) | collective-permute-done | bytes 131104 | tf_op jit(solution)/shard_map/ppermute | solution.py:164
  90.4 2.1 %collective-permute-done.21.refs_3_ = bf16[2,64,512]{2,1,0:T(8,128)(2,1)S(1)} collective-permute-done((bf16[2,64,512]{2,1,0:T(8,128)(2,1)S(1)}, bf16[2,64,512]{2,1,0:T(8,128)(2,1)S(1)}, u32[]{:S(2)}, u32[]{:S(2)}) %collective-permute-start.21) | collective-permute-done | bytes 131104 | tf_op jit(solution)/shard_map/ppermute | solution.py:164
  92.5 1.9 %collective-permute-done.22.refs_4_ = bf16[2,64,512]{2,1,0:T(8,128)(2,1)S(1)} collective-permute-done((bf16[2,64,512]{2,1,0:T(8,128)(2,1)S(1)}, bf16[2,64,512]{2,1,0:T(8,128)(2,1)S(1)}, u32[]{:S(2)}, u32[]{:S(2)}) %collective-permute-start.22) | collective-permute-done | bytes 131104 | tf_op jit(solution)/shard_map/ppermute | solution.py:164
  94.4 1.4 %shard_map.105 = bf16[2,64,2048]{2,1,0:T(8,128)(2,1)} custom-call(s32[4]{0:T(128)S(1)} %pad_add_fusion.place_ref.refs_0_, bf16[2,64,512]{2,1,0:T(8,128)(2,1)S(1)} %get-tuple-element.40.refs_1_, bf16[2,64,512]{2,1,0:T(8,128)(2,1)S(1)} %collective-permute-done.20.refs_2_, bf16[2,64,512]{2,1,0:T(8,128)(2,1)S(1)} %collective-permute-done.21.refs_3_, ...), custom_call_target="tpu_custom_call" | custom-call | tf_op jit(solution)/shard_map/pallas_call | solution.py:499
  (40 shorter events, 0.2 us)
Async XLA Ops:
  0.0 8.2 %copy-start.2 = (bf16[1024,512]{1,0:T(8,128)(2,1)S(1)}, bf16[1024,512]{1,0:T(8,128)(2,1)}, u32[]{:S(2)}) copy-start(bf16[1024,512]{1,0:T(8,128)(2,1)} %refs_7_.1) | copy-start | bytes 3145732
  0.0 11.2 %copy-start.5 = (f32[64,16]{0,1:T(8,128)S(1)}, f32[64,16]{0,1:T(8,128)}, u32[]{:S(2)}) copy-start(f32[64,16]{0,1:T(8,128)} %param.14) | copy-start | bytes 12292
  0.0 11.2 %copy-start.9 = (f32[64,16]{0,1:T(8,128)S(1)}, f32[64,16]{0,1:T(8,128)}, u32[]{:S(2)}) copy-start(f32[64,16]{0,1:T(8,128)} %param.15) | copy-start | bytes 12292
  0.0 16.0 %copy-start.6 = (f32[4096]{0:T(1024)S(1)}, f32[4096]{0:T(1024)}, u32[]{:S(2)}) copy-start(f32[4096]{0:T(1024)} %param.11) | copy-start | bytes 49156
  3.5 12.5 %collective-permute-start = (bf16[1552,128]{1,0:T(8,128)(2,1)}, bf16[1552,128]{1,0:T(8,128)(2,1)S(1)}, u32[]{:S(2)}, u32[]{:S(2)}) collective-permute-start(bf16[1552,128]{1,0:T(8,128)(2,1)} %get-tuple-element.22.packed_ref), channel_id=1, source_target_pairs={{0,2},{2,0},{4,6},{6,4},{8,10},{10,8},{12,14},{14,12},{1,3},{3,1},... | collective-permute-start | bytes 1191944 | tf_op jit(solution)/shard_map/ppermute | solution.py:164
  6.6 16.3 %collective-permute-start.1 = (bf16[1552,128]{1,0:T(8,128)(2,1)}, bf16[1552,128]{1,0:T(8,128)(2,1)S(1)}, u32[]{:S(2)}, u32[]{:S(2)}) collective-permute-start(bf16[1552,128]{1,0:T(8,128)(2,1)} %get-tuple-element.24), channel_id=1, source_target_pairs={{0,4},{2,6},{4,0},{6,2},{8,12},{10,14},{12,8},{14,10},{1,5},{3,7},... | collective-permute-start | bytes 1191944 | tf_op jit(solution)/shard_map/ppermute | solution.py:164
  8.1 17.6 %collective-permute-start.2 = (bf16[1552,128]{1,0:T(8,128)(2,1)}, bf16[1552,128]{1,0:T(8,128)(2,1)S(1)}, u32[]{:S(2)}, u32[]{:S(2)}) collective-permute-start(bf16[1552,128]{1,0:T(8,128)(2,1)} %get-tuple-element.25), channel_id=1, source_target_pairs={{0,6},{2,4},{4,2},{6,0},{8,14},{10,12},{12,10},{14,8},{1,7},{3,5},... | collective-permute-start | bytes 1191944 | tf_op jit(solution)/shard_map/ppermute | solution.py:164
  8.2 1.0 %copy-start.4 = (bf16[1552,128]{1,0:T(8,128)(2,1)S(1)}, bf16[1552,128]{1,0:T(8,128)(2,1)}, u32[]{:S(2)}) copy-start(bf16[1552,128]{1,0:T(8,128)(2,1)} %get-tuple-element.22.packed_ref) | copy-start | bytes 1191940
  9.8 13.0 %collective-permute-start.3 = (bf16[256,512]{1,0:T(8,128)(2,1)S(1)}, bf16[256,512]{1,0:T(8,128)(2,1)S(1)}, u32[]{:S(2)}, u32[]{:S(2)}) collective-permute-start(bf16[256,512]{1,0:T(8,128)(2,1)S(1)} %get-tuple-element.27.refs_0_), channel_id=1, source_target_pairs={{4,8},{6,10},{8,4},{10,6},{5,9},{7,11},{9,5},{11,7},{20,24},{22,26... | collective-permute-start | bytes 786440 | tf_op jit(solution)/shard_map/ppermute | solution.py:601
  10.5 12.3 %collective-permute-start.4 = (bf16[256,512]{1,0:T(8,128)(2,1)S(1)}, bf16[256,512]{1,0:T(8,128)(2,1)S(1)}, u32[]{:S(2)}, u32[]{:S(2)}) collective-permute-start(bf16[256,512]{1,0:T(8,128)(2,1)S(1)} %get-tuple-element.28.refs_0_), channel_id=1, source_target_pairs={{4,8},{6,10},{8,4},{10,6},{5,9},{7,11},{9,5},{11,7},{20,24},{22,26... | collective-permute-start | bytes 786440 | tf_op jit(solution)/shard_map/ppermute | solution.py:601
  16.0 2.2 %copy-start = (bf16[512,4096]{1,0:T(8,128)(2,1)S(1)}, bf16[512,4096]{1,0:T(8,128)(2,1)}, u32[]{:S(2)}) copy-start(bf16[512,4096]{1,0:T(8,128)(2,1)} %refs_2_.3) | copy-start | bytes 12582916
  18.2 2.6 %copy-start.7 = (f32[3,64,3]{1,2,0:T(4,128)S(1)}, f32[3,64,3]{1,2,0:T(4,128)}, u32[]{:S(2)}) copy-start(f32[3,64,3]{1,2,0:T(4,128)} %param.13) | copy-start | bytes 6916
  18.2 2.6 %copy-start.8 = (f32[1024]{0:T(1024)S(1)}, f32[1024]{0:T(1024)}, u32[]{:S(2)}) copy-start(f32[1024]{0:T(1024)} %param.16) | copy-start | bytes 12292
  18.2 7.6 %copy-start.3 = (bf16[1552,128]{1,0:T(8,128)(2,1)S(1)}, bf16[1552,128]{1,0:T(8,128)(2,1)}, u32[]{:S(2)}) copy-start(bf16[1552,128]{1,0:T(8,128)(2,1)} %get-tuple-element.23.refs_2_) | copy-start | bytes 1191940
  27.8 11.1 %collective-permute-start.5 = (bf16[784,128]{1,0:T(8,128)(2,1)S(1)}, bf16[784,128]{1,0:T(8,128)(2,1)S(1)}, u32[]{:S(2)}, u32[]{:S(2)}) collective-permute-start(bf16[784,128]{1,0:T(8,128)(2,1)S(1)} %get-tuple-element.29.refs_1_), channel_id=1, source_target_pairs={{0,8},{2,10},{4,12},{6,14},{8,0},{10,2},{12,4},{14,6},{1,9},{3,11}... | collective-permute-start | bytes 602120 | tf_op jit(solution)/shard_map/ppermute | solution.py:164
  39.0 9.0 %collective-permute-start.6 = (bf16[3,256,128]{2,1,0:T(8,128)(2,1)S(1)}, bf16[3,256,128]{2,1,0:T(8,128)(2,1)S(1)}, u32[]{:S(2)}, u32[]{:S(2)}) collective-permute-start(bf16[3,256,128]{2,1,0:T(8,128)(2,1)S(1)} %bitcast.19), channel_id=1, source_target_pairs={{0,16},{16,0},{1,17},{17,1},{2,18},{18,2},{3,19},{19,3},{4,20},{20... | collective-permute-start | bytes 589832 | tf_op jit(solution)/shard_map/ppermute | solution.py:164
  40.4 22.7 %collective-permute-start.14 = (bf16[256,512]{1,0:T(8,128)(2,1)S(1)}, bf16[256,512]{1,0:T(8,128)(2,1)S(1)}, u32[]{:S(2)}, u32[]{:S(2)}) collective-permute-start(bf16[256,512]{1,0:T(8,128)(2,1)S(1)} %shard_map.98), channel_id=1, source_target_pairs={{0,12},{2,14},{12,0},{14,2},{1,13},{3,15},{13,1},{15,3},{16,28},{1... | collective-permute-start | bytes 786440 | tf_op jit(solution)/shard_map/ppermute | solution.py:655
  45.8 17.4 %collective-permute-start.15 = (bf16[256,512]{1,0:T(8,128)(2,1)S(1)}, bf16[256,512]{1,0:T(8,128)(2,1)S(1)}, u32[]{:S(2)}, u32[]{:S(2)}) collective-permute-start(bf16[256,512]{1,0:T(8,128)(2,1)S(1)} %shard_map.99), channel_id=1, source_target_pairs={{0,12},{2,14},{12,0},{14,2},{1,13},{3,15},{13,1},{15,3},{16,28},{1... | collective-permute-start | bytes 786440 | tf_op jit(solution)/shard_map/ppermute | solution.py:655
  52.0 2.8 %collective-permute-start.7 = (bf16[256,128]{1,0:T(8,128)(2,1)S(1)}, bf16[256,128]{1,0:T(8,128)(2,1)S(1)}, u32[]{:S(2)}, u32[]{:S(2)}) collective-permute-start(bf16[256,128]{1,0:T(8,128)(2,1)S(1)} %get-tuple-element.34), channel_id=1, source_target_pairs={{0,1},{1,0},{2,3},{3,2},{4,5},{5,4},{6,7},{7,6},{8,9},{9,8},{10,11... | collective-permute-start | bytes 196616 | tf_op jit(solution)/shard_map/ppermute | solution.py:164
  52.1 9.7 %collective-permute-start.8 = (bf16[256,128]{1,0:T(8,128)(2,1)S(1)}, bf16[256,128]{1,0:T(8,128)(2,1)S(1)}, u32[]{:S(2)}, u32[]{:S(2)}) collective-permute-start(bf16[256,128]{1,0:T(8,128)(2,1)S(1)} %get-tuple-element.35), channel_id=1, source_target_pairs={{0,8},{2,10},{4,12},{6,14},{8,0},{10,2},{12,4},{14,6},{1,9},{3,11}... | collective-permute-start | bytes 196616 | tf_op jit(solution)/shard_map/ppermute | solution.py:164
  52.2 10.9 %collective-permute-start.9 = (bf16[256,128]{1,0:T(8,128)(2,1)S(1)}, bf16[256,128]{1,0:T(8,128)(2,1)S(1)}, u32[]{:S(2)}, u32[]{:S(2)}) collective-permute-start(bf16[256,128]{1,0:T(8,128)(2,1)S(1)} %get-tuple-element.36), channel_id=1, source_target_pairs={{0,9},{1,8},{2,11},{3,10},{4,13},{5,12},{6,15},{7,14},{8,1},{9,0},... | collective-permute-start | bytes 196616 | tf_op jit(solution)/shard_map/ppermute | solution.py:172
  63.1 16.3 %copy-start.1 = (bf16[512,4096]{1,0:T(8,128)(2,1)S(1)}, bf16[512,4096]{1,0:T(8,128)(2,1)}, u32[]{:S(2)}) copy-start(bf16[512,4096]{1,0:T(8,128)(2,1)} %refs_2_.3) | copy-start | bytes 12582916
  63.3 14.0 %collective-permute-start.17 = (bf16[512,512]{1,0:T(8,128)(2,1)S(1)}, bf16[512,512]{1,0:T(8,128)(2,1)S(1)}, u32[]{:S(2)}, u32[]{:S(2)}) collective-permute-start(bf16[512,512]{1,0:T(8,128)(2,1)S(1)} %shard_map.100.refs_5_), channel_id=1, source_target_pairs={{0,16},{16,0},{1,17},{17,1},{2,18},{18,2},{3,19},{19,3},{4,20},{20... | collective-permute-start | bytes 1572872 | tf_op jit(solution)/shard_map/ppermute | solution.py:164
  63.9 15.5 %collective-permute-start.13 = (bf16[1024,512]{1,0:T(8,128)(2,1)S(1)}, bf16[1024,512]{1,0:T(8,128)(2,1)S(1)}, u32[]{:S(2)}, u32[]{:S(2)}) collective-permute-start(bf16[1024,512]{1,0:T(8,128)(2,1)S(1)} %copy-done.2), channel_id=1, source_target_pairs={{0,1},{1,0},{2,3},{3,2},{4,5},{5,4},{6,7},{7,6},{8,9},{9,8},{10,11... | collective-permute-start | bytes 3145736 | tf_op jit(solution)/shard_map/ppermute | solution.py:164
  63.9 8.7 %collective-permute-start.10 = (bf16[4,256,128]{2,1,0:T(8,128)(2,1)S(1)}, bf16[4,256,128]{2,1,0:T(8,128)(2,1)S(1)}, u32[]{:S(2)}, u32[]{:S(2)}) collective-permute-start(bf16[4,256,128]{2,1,0:T(8,128)(2,1)S(1)} %pad_maximum_fusion.refs_3_.refs_1_), channel_id=1, source_target_pairs={{0,2},{2,0},{4,6},{6,4},{8,10},{10,8},{12,14},{14,12},{1,3},{3,1},... | collective-permute-start | bytes 786440 | tf_op jit(solution)/shard_map/ppermute | solution.py:164
  65.4 11.9 %collective-permute-start.11 = (bf16[4,256,128]{2,1,0:T(8,128)(2,1)S(1)}, bf16[4,256,128]{2,1,0:T(8,128)(2,1)S(1)}, u32[]{:S(2)}, u32[]{:S(2)}) collective-permute-start(bf16[4,256,128]{2,1,0:T(8,128)(2,1)S(1)} %pad_maximum_fusion.refs_3_.refs_1_), channel_id=1, source_target_pairs={{0,4},{2,6},{4,0},{6,2},{8,12},{10,14},{12,8},{14,10},{1,5},{3,7},... | collective-permute-start | bytes 786440 | tf_op jit(solution)/shard_map/ppermute | solution.py:164
  66.2 13.2 %collective-permute-start.12 = (bf16[4,256,128]{2,1,0:T(8,128)(2,1)S(1)}, bf16[4,256,128]{2,1,0:T(8,128)(2,1)S(1)}, u32[]{:S(2)}, u32[]{:S(2)}) collective-permute-start(bf16[4,256,128]{2,1,0:T(8,128)(2,1)S(1)} %pad_maximum_fusion.refs_3_.refs_1_), channel_id=1, source_target_pairs={{0,6},{2,4},{4,2},{6,0},{8,14},{10,12},{12,10},{14,8},{1,7},{3,5},... | collective-permute-start | bytes 786440 | tf_op jit(solution)/shard_map/ppermute | solution.py:164
  72.6 8.7 %collective-permute-start.16 = (bf16[512,512]{1,0:T(8,128)(2,1)S(1)}, bf16[512,512]{1,0:T(8,128)(2,1)S(1)}, u32[]{:S(2)}, u32[]{:S(2)}) collective-permute-start(bf16[512,512]{1,0:T(8,128)(2,1)S(1)} %shard_map.100.refs_5_), channel_id=1, source_target_pairs={{0,1},{1,0},{2,3},{3,2},{4,5},{5,4},{6,7},{7,6},{8,9},{9,8},{10,11... | collective-permute-start | bytes 1572872 | tf_op jit(solution)/shard_map/ppermute | solution.py:164
  79.4 1.9 %collective-permute-start.18 = (bf16[512,512]{1,0:T(8,128)(2,1)S(1)}, bf16[512,512]{1,0:T(8,128)(2,1)S(1)}, u32[]{:S(2)}, u32[]{:S(2)}) collective-permute-start(bf16[512,512]{1,0:T(8,128)(2,1)S(1)} %shard_map.103.refs_7_), channel_id=1, source_target_pairs={{0,1},{1,0},{2,3},{3,2},{4,5},{5,4},{6,7},{7,6},{8,9},{9,8},{10,11... | collective-permute-start | bytes 1572872 | tf_op jit(solution)/shard_map/ppermute | solution.py:164
  82.8 1.7 %collective-permute-start.19 = (bf16[256,512]{1,0:T(8,128)(2,1)S(1)}, bf16[256,512]{1,0:T(8,128)(2,1)S(1)}, u32[]{:S(2)}, u32[]{:S(2)}) collective-permute-start(bf16[256,512]{1,0:T(8,128)(2,1)S(1)} %get-tuple-element.43), channel_id=1, source_target_pairs={{0,1},{1,0},{2,3},{3,2},{4,5},{5,4},{6,7},{7,6},{8,9},{9,8},{10,11... | collective-permute-start | bytes 786440 | tf_op jit(solution)/shard_map/ppermute | solution.py:164
  84.5 5.8 %collective-permute-start.20 = (bf16[2,64,512]{2,1,0:T(8,128)(2,1)S(1)}, bf16[2,64,512]{2,1,0:T(8,128)(2,1)S(1)}, u32[]{:S(2)}, u32[]{:S(2)}) collective-permute-start(bf16[2,64,512]{2,1,0:T(8,128)(2,1)S(1)} %get-tuple-element.41), channel_id=1, source_target_pairs={{0,2},{2,0},{4,6},{6,4},{8,10},{10,8},{12,14},{14,12},{1,3},{3,1},... | collective-permute-start | bytes 393224 | tf_op jit(solution)/shard_map/ppermute | solution.py:164
  86.1 6.4 %collective-permute-start.21 = (bf16[2,64,512]{2,1,0:T(8,128)(2,1)S(1)}, bf16[2,64,512]{2,1,0:T(8,128)(2,1)S(1)}, u32[]{:S(2)}, u32[]{:S(2)}) collective-permute-start(bf16[2,64,512]{2,1,0:T(8,128)(2,1)S(1)} %get-tuple-element.42), channel_id=1, source_target_pairs={{0,4},{2,6},{4,0},{6,2},{8,12},{10,14},{12,8},{14,10},{1,5},{3,7},... | collective-permute-start | bytes 393224 | tf_op jit(solution)/shard_map/ppermute | solution.py:164
  86.9 7.5 %collective-permute-start.22 = (bf16[2,64,512]{2,1,0:T(8,128)(2,1)S(1)}, bf16[2,64,512]{2,1,0:T(8,128)(2,1)S(1)}, u32[]{:S(2)}, u32[]{:S(2)}) collective-permute-start(bf16[2,64,512]{2,1,0:T(8,128)(2,1)S(1)} %get-tuple-element.39), channel_id=1, source_target_pairs={{0,6},{2,4},{4,2},{6,0},{8,14},{10,12},{12,10},{14,8},{1,7},{3,5},... | collective-permute-start | bytes 393224 | tf_op jit(solution)/shard_map/ppermute | solution.py:164

commit v4 on v3

--- a/solution.py
+++ b/solution.py
@@ -192,8 +192,8 @@
     return pltpu.roll(value, LANES // 2, value.ndim - 1)
 
 
-def norm_kernel(place_ref, table_ref, gain_ref, part_ref, packed_ref, out_ref):
-    del place_ref, packed_ref
+def norm_kernel(place_ref, table_ref, gain_ref, part_ref, pair_ref, query_ref, out_ref):
+    del place_ref, pair_ref, query_ref
     widened = table_ref[...].astype(f32)
     mean = jnp.sum(widened * widened, axis=1, keepdims=True) / widened.shape[1]
     own = part_ref[...].astype(f32)
@@ -213,7 +213,7 @@
             copies.append(
                 pltpu.make_async_copy(
                     weight_ref.at[j, :, pl.ds(first, LANES)],
-                    out_refs[m].at[pl.ds(j * depth, depth), :],
+                    out_refs[m].at[pl.ds((j + 2) % 3 * depth, depth), :],
                     sems.at[m, j],
                 )
             )
@@ -319,23 +319,22 @@
     rows_ref[end : end + 1] = jnp.where(lane_half(upper.shape), upper, lower)
 
 
-def partial_kernel(place_ref, normed_ref, *refs):
+def partial_kernel(place_ref, normed_ref, *refs, begin, count):
     weight_refs, (keep_ref, send_ref) = refs[:-2], refs[-2:]
     quad, half = place_ref[0], place_ref[1]
     rows, features = normed_ref.shape
     depth = features // len(weight_refs)
-    count = weight_refs[0].shape[0] // depth
     total = jnp.zeros((rows, count * LANES), f32)
     tokens = jnp.zeros((SPARE, LANES), f32)
     for m, weight_ref in enumerate(weight_refs):
         first = pl.multiple_of((quad ^ m) * depth, depth)
         columns = jnp.concatenate(
-            [weight_ref[j * depth : (j + 1) * depth, :] for j in range(count)], axis=1
+            [weight_ref[j * depth : (j + 1) * depth, :] for j in range(begin, begin + count)], axis=1
         )
         total += jnp.dot(
             normed_ref[:, pl.ds(first, depth)], columns, preferred_element_type=f32
         )
-        tokens += weight_ref[count * depth :, :].astype(f32)
+        tokens += weight_ref[weight_ref.shape[0] - SPARE :, :].astype(f32)
     part = rows // 2
     for j in range(count):
         mine = total[:, j * LANES : (j + 1) * LANES]
@@ -344,7 +343,8 @@
         left = lane_half(top.shape)
         keep_ref[j * part : (j + 1) * part, :] = jnp.where(left, top, half_turn(bottom))
         send_ref[j * part : (j + 1) * part, :] = jnp.where(left, half_turn(top), bottom).astype(bf16)
-    send_ref[count * part :, :] = tokens.astype(bf16)
+    if send_ref.shape[0] > count * part:
+        send_ref[count * part :, :] = tokens.astype(bf16)
 
 
 def filtered_branch(group, picked, row, mine, theirs, rows_ref, branch):
@@ -365,17 +365,17 @@
 
 
 def conv_kernel(
-    place_ref, near_ref, far_ref, own_ref, other_ref, matrices_ref, rows_ref, *refs, genomes, rows
+    place_ref, near_ref, far_ref, own_ref, other_ref, matrices_ref, rows_ref, value_ref, picked_ref, *, genomes, rows
 ):
-    piece_refs, (mine_ref, picked_ref, held_ref) = refs[:4], refs[4:]
-    half, group, core = place_ref[1], place_ref[2], place_ref[3]
+    half, group = place_ref[1], place_ref[2]
     pick(half, near_ref, far_ref, picked_ref, genomes, rows)
     positions = picked_ref.shape[0]
     length = positions // genomes
     row = lax.broadcasted_iota(jnp.int32, (positions, LANES), 0) % length
     picked = picked_ref[...]
-    query, key, value = (
-        filtered_branch(group, picked, row, own_ref[j], other_ref[j], rows_ref, j) for j in range(3)
+    key, value = (
+        filtered_branch(group, picked, row, own_ref[j - 1], other_ref[j - 1], rows_ref, j)
+        for j in (1, 2)
     )
     product = key * value
     size = 16
@@ -385,8 +385,7 @@
     pole_row = lax.broadcasted_iota(jnp.int32, (LANES, width), 0)
     same = pole_row // size == (lax.broadcasted_iota(jnp.int32, (LANES, width), 1) % LANES) // size
     fade = jnp.concatenate([rows_ref[:LANES]] * genomes, axis=1)
-    end = LANES + 8 * own_ref.shape[0]
-    skip = rows_ref[end : end + 1]
+    skip = rows_ref[rows_ref.shape[0] - 8 : rows_ref.shape[0] - 7]
     across = (count + 1) * CHUNK
     high, low = matrices_ref[:, :across], matrices_ref[:, across : 2 * across]
     ends_high = matrices_ref[:, 2 * across : 2 * across + CHUNK]
@@ -401,11 +400,20 @@
         )
         conv = dot3(high, low, stacked)
         for b, span in enumerate(spans):
-            value = conv[:, b * LANES : (b + 1) * LANES] + skip * product[span]
-            held_ref[span, :] = (query[span] * value).astype(bf16)
+            value_ref[span, :] = conv[:, b * LANES : (b + 1) * LANES] + skip * product[span]
         if c < chunks - 1:
             ends = dot3(ends_high, ends_low, block)
             state = fade * state + jnp.where(same, ends, 0.0)
+
+
+def gate_kernel(place_ref, picked_ref, own_ref, other_ref, rows_ref, value_ref, *refs, genomes):
+    piece_refs, (mine_ref, held_ref) = refs[:4], refs[4:]
+    half, group, core = place_ref[1], place_ref[2], place_ref[3]
+    positions = picked_ref.shape[0]
+    length = positions // genomes
+    row = lax.broadcasted_iota(jnp.int32, (positions, LANES), 0) % length
+    query = filtered_branch(group, picked_ref[...], row, own_ref[0], other_ref[0], rows_ref, 0)
+    held_ref[...] = (query * value_ref[...]).astype(bf16)
     part = length // 2
     for r, piece_ref in enumerate(piece_refs):
         place = 2 * (core ^ (r % 2)) + (half ^ (r // 2))
@@ -592,13 +600,33 @@
                 pl.BlockSpec((1, part), lambda i, place: (0, place[1])),
                 pl.BlockSpec((step, part), lambda i, place: (i, place[1])),
                 anywhere,
+                anywhere,
             ],
             out_specs=pl.BlockSpec((step, part), lambda i, place: (i, 0)),
         ),
         compiler_params=pltpu.CompilerParams(vmem_limit_bytes=16 * MIB),
-    )(place, embed_table, norm_gain.reshape(1, features), embed_table, gathered[1])
+    )(place, embed_table, norm_gain.reshape(1, features), embed_table, gathered[1], packed[1])
 
     inner_fetched = [lax.ppermute(rows_part, "ctx", inner) for rows_part in offered]
+    def partials(begin, count, spare, earlier=()):
+        table_rows = count * (vocab // 2)
+        return called(
+            functools.partial(partial_kernel, begin=begin, count=count),
+            [shaped(table_rows, LANES), shaped(table_rows + spare, LANES, dtype=bf16)],
+            (place,),
+            normed,
+            *gathered,
+            earlier=earlier,
+        )
+
+    def finished(keep, arrived):
+        own = (keep + arrived[: keep.shape[0]].astype(f32)).astype(bf16)
+        return own.reshape(-1, vocab // 2, LANES)
+
+    pair_keep, pair_send = partials(0, 2, SPARE, tuple(inner_fetched))
+    query_keep, query_send = partials(2, 1, 0)
+    pair_arrived = swapped(pair_send, "ctx", members)
+    query_arrived = swapped(query_send, "ctx", members)
     amp = residue * jnp.sqrt(-jnp.expm1(-2.0 * pole_rate))
     across = (LANES // pole_rate.shape[1] + 1) * CHUNK
     matrices, lines = called(
@@ -612,34 +640,36 @@
         amp.T,
         short_filter.transpose(0, 2, 1),
         skip_gain.reshape(-1, LANES),
-        earlier=(gathered[1],),
-    )
-
-    table_rows = branches * (vocab // 2)
-    keep, send = called(
-        partial_kernel,
-        [shaped(table_rows, LANES), shaped(table_rows + SPARE, LANES, dtype=bf16)],
+        earlier=(pair_send,),
+    )
+
+    pair_own = after(finished(pair_keep, pair_arrived), matrices)
+    query_own = finished(query_keep, query_arrived)
+    pair_other = swapped(pair_own, "groups", 1)
+    query_other = swapped(query_own, "groups", 1)
+
+    span = length // 2
+    value, picked = called(
+        functools.partial(conv_kernel, genomes=genomes, rows=rows),
+        [shaped(genomes * length, LANES), shaped(genomes * length, vocab, dtype=bf16)],
         (place,),
-        normed,
-        *gathered,
-        earlier=(matrices, *inner_fetched),
-    )
-    arrived = swapped(send, "ctx", members)
-    own = (keep + arrived[:table_rows].astype(f32)).astype(bf16)
-    own = own.reshape(branches, vocab // 2, LANES)
-    other = swapped(own, "groups", 1)
-    span = length // 2
+        pair_send,
+        pair_arrived,
+        pair_own,
+        pair_other,
+        matrices,
+        lines,
+    )
     *pieces, picked = called(
-        functools.partial(conv_kernel, genomes=genomes, rows=rows),
+        functools.partial(gate_kernel, genomes=genomes),
         [shaped(span, LANES, dtype=bf16)] * 4 + [shaped(span, vocab, dtype=bf16)],
         (place,),
-        send,
-        arrived,
-        own,
-        other,
-        matrices,
+        picked,
+        query_own,
+        query_other,
         lines,
-        scratch=[pltpu.VMEM((genomes * length, vocab), bf16), pltpu.VMEM((genomes * length, LANES), bf16)],
+        value,
+        scratch=[pltpu.VMEM((genomes * length, LANES), bf16)],
     )
     core_piece = swapped(pieces[1], "chan", 1)
     piece = jnp.stack(
@@ -652,7 +682,7 @@
     )
     gated = [piece] + [swapped(piece, "ctx", m) for m in range(1, members)]
 
-    outer_fetched = [lax.ppermute(after(rows_part, own), "ctx", outer) for rows_part in offered]
+    outer_fetched = [lax.ppermute(after(rows_part, pair_own), "ctx", outer) for rows_part in offered]
     fetched = jnp.where(
         (ctx >= members // 2) & (ctx < members + members // 2),
         jnp.concatenate(inner_fetched),

time: 96 us -> 94.1 us (0.980)
  waiting for transfers between devices: 43.7 us -> 37.8 us
  starting transfers between devices: 28.8 us -> 30.4 us
  Pallas kernels: 19.4 us -> 20.6 us
  local copies, waits for them, and re-layouts: 3.26 us -> 4.26 us
    ppermute x18 -> x20, waiting for transfers between devices: 42.3 us -> 35.9 us  [swapped(): return lax.ppermute(value, axis, [(i, i ^ mask) for i in range(count)])]
    ppermute x18 -> x20, starting transfers between devices: 17.2 us -> 18.8 us  [swapped(): return lax.ppermute(value, axis, [(i, i ^ mask) for i in range(count)])]
    pallas_call x6 -> x8, Pallas kernels: 12.7 us -> 13.9 us  [called(): pl.pallas_call(body, out_shape=out_shape, in_specs=[smem] * len(scalars)...]
    unnamed x20 -> x22, local copies, waits for them, and re-layouts: 3.22 us -> 4.22 us
  transfers between devices with their start and end apart: 23 -> 25, of which waited for: 12 -> 13; matrix products, arithmetic and copies ran while one was open for 0% -> 0% of each run, Pallas kernels for 12% -> 14%
where the time goes in v4:
time: 94.1 us; the launch traced here: 93.8 us
  waiting for transfers between devices  37.8 us (40%)
  starting transfers between devices  30.4 us (32%)
  Pallas kernels  20.6 us (22%)
  local copies, waits for them, and re-layouts  4.26 us (5%)
    ppermute x20, waiting for transfers between devices, swapped(): return lax.ppermute(value, axis, [(i, i ^ mask) for i in range(count)])  35.9 us
    ppermute x20, starting transfers between devices, swapped(): return lax.ppermute(value, axis, [(i, i ^ mask) for i in range(count)])  18.8 us
    pallas_call x8, Pallas kernels, called(): pl.pallas_call(body, out_shape=out_shape, in_specs=[smem] * len(scalars)...  13.9 us
    ppermute x2, starting transfers between devices, quad_body(): lax.ppermute(after(rows_part, pair_own), 'ctx', outer)  7.63 us
    unnamed x22, local copies, waits for them, and re-layouts  4.22 us
    pallas_call x1, Pallas kernels, quad_body(): pl.pallas_call(pack_kernel, out_shape=[shaped(branches * depth + SPARE, L...  3.5 us
    ppermute x1, starting transfers between devices, swapped_both(): return lax.ppermute(value, ('ctx', 'chan'), pairs)  2.68 us
    pallas_call x1, Pallas kernels, quad_body(): pl.pallas_call(norm_kernel, out_shape=shaped(vocab, part, dtype=bf16), gr...  2.56 us
  transfers between devices with their start and end apart: 25, of which 13 were waited for; matrix products, arithmetic and copies ran while one was open for 0% of the time, Pallas kernels for 14%

profile of v4, /device:TPU:0, one launch (start us, length us, event | category | flops | bytes accessed | tf_op | source)
XLA Modules:
  0.0 93.8 jit_solution(5962307127079821979)
XLA Ops:
  0.0 3.5 %shard_map.91 = (bf16[1552,128]{1,0:T(8,128)(2,1)}, bf16[1552,128]{1,0:T(8,128)(2,1)}, bf16[1552,128]{1,0:T(8,128)(2,1)}, bf16[1552,128]{1,0:T(8,128)(2,1)}) custom-call(s32[2,64]{1,0:T(2,128)} %token_ref.1, bf16[3,512,1024]{2,1,0:T(8,128)(2,1)} %bitcast.27), custom_call_target="tpu_custom_call" | custom-call | tf_op jit(solution)/shard_map/pallas_call | solution.py:558
  3.5 3.0 %collective-permute-start = (bf16[1552,128]{1,0:T(8,128)(2,1)}, bf16[1552,128]{1,0:T(8,128)(2,1)S(1)}, u32[]{:S(2)}, u32[]{:S(2)}) collective-permute-start(bf16[1552,128]{1,0:T(8,128)(2,1)} %get-tuple-element.26.query_ref.packed_ref), channel_id=1, source_target_pairs={{0,2},{2,0},{4,6},{6,4},{8,10},{10,8},{12,14},{14,12},{1,3},{3,1},... | collective-permute-start | bytes 1191944 | tf_op jit(solution)/shard_map/ppermute | solution.py:164
  6.5 1.6 %collective-permute-start.1 = (bf16[1552,128]{1,0:T(8,128)(2,1)}, bf16[1552,128]{1,0:T(8,128)(2,1)S(1)}, u32[]{:S(2)}, u32[]{:S(2)}) collective-permute-start(bf16[1552,128]{1,0:T(8,128)(2,1)} %get-tuple-element.28), channel_id=1, source_target_pairs={{0,4},{2,6},{4,0},{6,2},{8,12},{10,14},{12,8},{14,10},{1,5},{3,7},... | collective-permute-start | bytes 1191944 | tf_op jit(solution)/shard_map/ppermute | solution.py:164
  8.1 0.1 pad_add_fusion.place_ref.refs_0_
  8.2 1.0 %copy-done.4 = bf16[1552,128]{1,0:T(8,128)(2,1)S(1)} copy-done((bf16[1552,128]{1,0:T(8,128)(2,1)S(1)}, bf16[1552,128]{1,0:T(8,128)(2,1)}, u32[]{:S(2)}) %copy-start.4) | copy-done | bytes 397336
  9.2 0.6 shard_map.93
  9.8 0.7 collective-permute-start.3
  10.5 0.7 collective-permute-start.4
  11.2 4.8 %collective-permute-done.pair_ref.refs_3_ = bf16[1552,128]{1,0:T(8,128)(2,1)S(1)} collective-permute-done((bf16[1552,128]{1,0:T(8,128)(2,1)}, bf16[1552,128]{1,0:T(8,128)(2,1)S(1)}, u32[]{:S(2)}, u32[]{:S(2)}) %collective-permute-start) | collective-permute-done | bytes 397344 | tf_op jit(solution)/shard_map/ppermute | solution.py:164
  16.0 2.2 %copy-done = bf16[512,4096]{1,0:T(8,128)(2,1)S(1)} copy-done((bf16[512,4096]{1,0:T(8,128)(2,1)S(1)}, bf16[512,4096]{1,0:T(8,128)(2,1)}, u32[]{:S(2)}) %copy-start) | copy-done | bytes 4194328
  18.1 1.0 %copy-done.5 = bf16[1552,128]{1,0:T(8,128)(2,1)S(1)} copy-done((bf16[1552,128]{1,0:T(8,128)(2,1)S(1)}, bf16[1552,128]{1,0:T(8,128)(2,1)}, u32[]{:S(2)}) %copy-start.5) | copy-done | bytes 397336
  19.1 2.6 %shard_map.92.refs_1_ = bf16[512,2048]{1,0:T(8,128)(2,1)S(1)} custom-call(s32[4]{0:T(128)S(1)} %pad_add_fusion.place_ref.refs_0_, bf16[512,4096]{1,0:T(8,128)(2,1)S(1)} %copy-done, f32[1,4096]{1,0:T(1,128)S(1)} %bitcast.24, bf16[512,4096]{1,0:T(8,128)(2,1)S(1)} %copy-done, bf16[1552,128]{1,0:T(8,128)(2,1)S(1)} %collective-permute-done.pair_ref.refs_3_, ...), custom_call_target="tpu_custom_call" | custom-call | tf_op jit(solution)/shard_map/pallas_call | solution.py:592
  21.8 4.0 %collective-permute-done.2.refs_5_ = bf16[1552,128]{1,0:T(8,128)(2,1)S(1)} collective-permute-done((bf16[1552,128]{1,0:T(8,128)(2,1)}, bf16[1552,128]{1,0:T(8,128)(2,1)S(1)}, u32[]{:S(2)}, u32[]{:S(2)}) %collective-permute-start.2) | collective-permute-done | bytes 397344 | tf_op jit(solution)/shard_map/ppermute | solution.py:164
  25.7 1.4 %shard_map.94 = (f32[512,128]{1,0:T(8,128)S(1)}, bf16[528,128]{1,0:T(8,128)(2,1)S(1)}) custom-call(s32[4]{0:T(128)S(1)} %pad_add_fusion.place_ref.refs_0_, bf16[512,2048]{1,0:T(8,128)(2,1)S(1)} %shard_map.92.refs_1_, bf16[1552,128]{1,0:T(8,128)(2,1)S(1)} %copy-done.3, bf16[1552,128]{1,0:T(8,128)(2,1)S(1)} %collective-permute-done.pair_ref.refs_3_, ...), custom_call_target="tpu_custom_call" | custom-call | tf_op jit(solution)/shard_map/pallas_call | solution.py:507
  27.2 2.8 %collective-permute-start.5 = (bf16[528,128]{1,0:T(8,128)(2,1)S(1)}, bf16[528,128]{1,0:T(8,128)(2,1)S(1)}, u32[]{:S(2)}, u32[]{:S(2)}) collective-permute-start(bf16[528,128]{1,0:T(8,128)(2,1)S(1)} %get-tuple-element.32.refs_5_.refs_1_), channel_id=1, source_target_pairs={{0,8},{2,10},{4,12},{6,14},{8,0},{10,2},{12,4},{14,6},{1,9},{3,11}... | collective-permute-start | bytes 405512 | tf_op jit(solution)/shard_map/ppermute | solution.py:164
  30.0 1.4 %shard_map.98 = (f32[256,128]{1,0:T(8,128)S(1)}, bf16[256,128]{1,0:T(8,128)(2,1)S(1)}) custom-call(s32[4]{0:T(128)S(1)} %pad_add_fusion.place_ref.refs_0_, bf16[512,2048]{1,0:T(8,128)(2,1)S(1)} %shard_map.92.refs_1_, bf16[1552,128]{1,0:T(8,128)(2,1)S(1)} %copy-done.3, bf16[1552,128]{1,0:T(8,128)(2,1)S(1)} %collective-permute-done.pair_ref.refs_3_, ...), custom_call_target="tpu_custom_call" | custom-call | tf_op jit(solution)/shard_map/pallas_call | solution.py:507
  31.4 0.2 collective-permute-start.7
  31.7 2.1 %shard_map.95 = (bf16[128,2560]{1,0:T(8,128)(2,1)S(1)}, f32[160,128]{1,0:T(8,128)S(1)}) custom-call(s32[4]{0:T(128)S(1)} %pad_add_fusion.place_ref.refs_0_, f32[16,64]{1,0:T(8,128)S(1)} %bitcast.23, f32[16,64]{1,0:T(8,128)S(1)} %multiply_bitcast_fusion.refs_2_, f32[3,3,64]{2,1,0:T(4,128)S(1)} %bitcast.25, f32[8,128]{1,0:T(8,128)S(1)} %bitcast.26, ...), custom_call_target="tpu_custom_call" | custom-call | tf_op jit(solution)/shard_map/pallas_call | solution.py:507
  33.7 3.2 %collective-permute-done.5.refs_2_ = bf16[528,128]{1,0:T(8,128)(2,1)S(1)} collective-permute-done((bf16[528,128]{1,0:T(8,128)(2,1)S(1)}, bf16[528,128]{1,0:T(8,128)(2,1)S(1)}, u32[]{:S(2)}, u32[]{:S(2)}) %collective-permute-start.5) | collective-permute-done | bytes 135200 | tf_op jit(solution)/shard_map/ppermute | solution.py:164
  37.0 1.4 %collective-permute-start.6 = (bf16[2,256,128]{2,1,0:T(8,128)(2,1)S(1)}, bf16[2,256,128]{2,1,0:T(8,128)(2,1)S(1)}, u32[]{:S(2)}, u32[]{:S(2)}) collective-permute-start(bf16[2,256,128]{2,1,0:T(8,128)(2,1)S(1)} %shard_map.96.refs_3_.refs_1_), channel_id=1, source_target_pairs={{0,16},{16,0},{1,17},{17,1},{2,18},{18,2},{3,19},{19,3},{4,20},{20... | collective-permute-start | bytes 393224 | tf_op jit(solution)/shard_map/ppermute | solution.py:164
  38.3 5.6 %collective-permute-start.16 = (bf16[256,512]{1,0:T(8,128)(2,1)S(1)}, bf16[256,512]{1,0:T(8,128)(2,1)S(1)}, u32[]{:S(2)}, u32[]{:S(2)}) collective-permute-start(bf16[256,512]{1,0:T(8,128)(2,1)S(1)} %shard_map.101), channel_id=1, source_target_pairs={{0,12},{2,14},{12,0},{14,2},{1,13},{3,15},{13,1},{15,3},{16,28},{1... | collective-permute-start | bytes 786440 | tf_op jit(solution)/shard_map/ppermute | solution.py:685
  43.9 2.1 %collective-permute-start.17 = (bf16[256,512]{1,0:T(8,128)(2,1)S(1)}, bf16[256,512]{1,0:T(8,128)(2,1)S(1)}, u32[]{:S(2)}, u32[]{:S(2)}) collective-permute-start(bf16[256,512]{1,0:T(8,128)(2,1)S(1)} %shard_map.102), channel_id=1, source_target_pairs={{0,12},{2,14},{12,0},{14,2},{1,13},{3,15},{13,1},{15,3},{16,28},{1... | collective-permute-start | bytes 786440 | tf_op jit(solution)/shard_map/ppermute | solution.py:685
  46.0 0.8 collective-permute-start.8
  46.8 3.3 %shard_map.97 = (f32[1024,128]{1,0:T(8,128)S(1)}, bf16[1024,512]{1,0:T(8,128)(2,1)S(1)}) custom-call(s32[4]{0:T(128)S(1)} %pad_add_fusion.place_ref.refs_0_, bf16[528,128]{1,0:T(8,128)(2,1)S(1)} %get-tuple-element.32.refs_5_.refs_1_, bf16[528,128]{1,0:T(8,128)(2,1)S(1)} %collective-permute-done.5.refs_2_, ...), custom_call_target="tpu_custom_call" | custom-call | tf_op jit(solution)/shard_map/pallas_call | solution.py:507
  50.1 0.2 collective-permute-done.8.refs_3_
  50.3 1.1 %shard_map.99 = (bf16[256,128]{1,0:T(8,128)(2,1)S(1)}, bf16[256,128]{1,0:T(8,128)(2,1)S(1)}, bf16[256,128]{1,0:T(8,128)(2,1)S(1)}, bf16[256,128]{1,0:T(8,128)(2,1)S(1)}, bf16[256,512]{1,0:T(8,128)(2,1)S(1)}) custom-call(s32[4]{0:T(128)S(1)} %pad_add_fusion.place_ref.refs_0_, bf16[1024,512]{1,0:T(8,128)(2,1)S(1)} %get-tuple-element.36.refs_1_, ...), custom_call_target="tpu_custom_call" | custom-call | tf_op jit(solution)/shard_map/pallas_call | solution.py:507
  51.6 2.7 %collective-permute-start.11 = (bf16[256,128]{1,0:T(8,128)(2,1)S(1)}, bf16[256,128]{1,0:T(8,128)(2,1)S(1)}, u32[]{:S(2)}, u32[]{:S(2)}) collective-permute-start(bf16[256,128]{1,0:T(8,128)(2,1)S(1)} %get-tuple-element.44), channel_id=1, source_target_pairs={{0,9},{1,8},{2,11},{3,10},{4,13},{5,12},{6,15},{7,14},{8,1},{9,0},... | collective-permute-start | bytes 196616 | tf_op jit(solution)/shard_map/ppermute | solution.py:172
  54.3 4.5 %collective-permute-done.10 = bf16[256,128]{1,0:T(8,128)(2,1)S(1)} collective-permute-done((bf16[256,128]{1,0:T(8,128)(2,1)S(1)}, bf16[256,128]{1,0:T(8,128)(2,1)S(1)}, u32[]{:S(2)}, u32[]{:S(2)}) %collective-permute-start.10) | collective-permute-done | bytes 65568 | tf_op jit(solution)/shard_map/ppermute | solution.py:164
  58.8 1.9 %collective-permute-done.11 = bf16[256,128]{1,0:T(8,128)(2,1)S(1)} collective-permute-done((bf16[256,128]{1,0:T(8,128)(2,1)S(1)}, bf16[256,128]{1,0:T(8,128)(2,1)S(1)}, u32[]{:S(2)}, u32[]{:S(2)}) %collective-permute-start.11) | collective-permute-done | bytes 65568 | tf_op jit(solution)/shard_map/ppermute | solution.py:172
  60.8 0.1 maximum_select_fusion.refs_0_
  60.9 1.2 %collective-permute-start.19 = (bf16[512,512]{1,0:T(8,128)(2,1)S(1)}, bf16[512,512]{1,0:T(8,128)(2,1)S(1)}, u32[]{:S(2)}, u32[]{:S(2)}) collective-permute-start(bf16[512,512]{1,0:T(8,128)(2,1)S(1)} %shard_map.103.refs_5_), channel_id=1, source_target_pairs={{0,16},{16,0},{1,17},{17,1},{2,18},{18,2},{3,19},{19,3},{4,20},{20... | collective-permute-start | bytes 1572872 | tf_op jit(solution)/shard_map/ppermute | solution.py:164
  62.1 1.5 %collective-permute-start.12 = (bf16[4,256,128]{2,1,0:T(8,128)(2,1)S(1)}, bf16[4,256,128]{2,1,0:T(8,128)(2,1)S(1)}, u32[]{:S(2)}, u32[]{:S(2)}) collective-permute-start(bf16[4,256,128]{2,1,0:T(8,128)(2,1)S(1)} %pad_maximum_fusion.refs_3_.refs_1_), channel_id=1, source_target_pairs={{0,2},{2,0},{4,6},{6,4},{8,10},{10,8},{12,14},{14,12},{1,3},{3,1},... | collective-permute-start | bytes 786440 | tf_op jit(solution)/shard_map/ppermute | solution.py:164
  63.6 0.5 collective-permute-start.13
  64.2 1.4 %collective-permute-start.14 = (bf16[4,256,128]{2,1,0:T(8,128)(2,1)S(1)}, bf16[4,256,128]{2,1,0:T(8,128)(2,1)S(1)}, u32[]{:S(2)}, u32[]{:S(2)}) collective-permute-start(bf16[4,256,128]{2,1,0:T(8,128)(2,1)S(1)} %pad_maximum_fusion.refs_3_.refs_1_), channel_id=1, source_target_pairs={{0,6},{2,4},{4,2},{6,0},{8,14},{10,12},{12,10},{14,8},{1,7},{3,5},... | collective-permute-start | bytes 786440 | tf_op jit(solution)/shard_map/ppermute | solution.py:164
  65.6 5.2 %collective-permute-done.12.refs_4_.refs_1_ = bf16[4,256,128]{2,1,0:T(8,128)(2,1)S(1)} collective-permute-done((bf16[4,256,128]{2,1,0:T(8,128)(2,1)S(1)}, bf16[4,256,128]{2,1,0:T(8,128)(2,1)S(1)}, u32[]{:S(2)}, u32[]{:S(2)}) %collective-permute-start.12) | collective-permute-done | bytes 262176 | tf_op jit(solution)/shard_map/ppermute | solution.py:164
  70.8 4.3 %collective-permute-done.19.refs_0_ = bf16[512,512]{1,0:T(8,128)(2,1)S(1)} collective-permute-done((bf16[512,512]{1,0:T(8,128)(2,1)S(1)}, bf16[512,512]{1,0:T(8,128)(2,1)S(1)}, u32[]{:S(2)}, u32[]{:S(2)}) %collective-permute-start.19) | collective-permute-done | bytes 524320 | tf_op jit(solution)/shard_map/ppermute | solution.py:164
  75.1 2.5 %collective-permute-done.14.refs_6_.refs_1_ = bf16[4,256,128]{2,1,0:T(8,128)(2,1)S(1)} collective-permute-done((bf16[4,256,128]{2,1,0:T(8,128)(2,1)S(1)}, bf16[4,256,128]{2,1,0:T(8,128)(2,1)S(1)}, u32[]{:S(2)}, u32[]{:S(2)}) %collective-permute-start.14) | collective-permute-done | bytes 262176 | tf_op jit(solution)/shard_map/ppermute | solution.py:164
  77.6 1.9 %shard_map.100 = (bf16[256,512]{1,0:T(8,128)(2,1)S(1)}, bf16[8,256,256]{2,1,0:T(8,128)(2,1)S(1)}) custom-call(s32[4]{0:T(128)S(1)} %pad_add_fusion.place_ref.refs_0_, bf16[256,512]{1,0:T(8,128)(2,1)S(1)} %get-tuple-element.40.refs_1_, bf16[512,4096]{1,0:T(8,128)(2,1)S(1)} %copy-done.1, bf16[4,256,128]{2,1,0:T(8,128)(2,1)S(1)} %pad_maximum_fusion.refs_3_.refs_1_, ...), custom_call_target="tpu_custom_call" | custom-call | tf_op jit(solution)/shard_map/pallas_call | solution.py:507
  79.5 1.4 %shard_map.107 = bf16[2,256,512]{2,1,0:T(8,128)(2,1)S(1)} custom-call(s32[4]{0:T(128)S(1)} %pad_add_fusion.place_ref.refs_0_, bf16[256,512]{1,0:T(8,128)(2,1)S(1)} %get-tuple-element.40.refs_1_, bf16[512,4096]{1,0:T(8,128)(2,1)S(1)} %copy-done.1, bf16[256,512]{1,0:T(8,128)(2,1)S(1)} %get-tuple-element.45.refs_3_, ...), custom_call_target="tpu_custom_call" | custom-call | tf_op jit(solution)/shard_map/pallas_call | solution.py:507
  81.0 0.6 collective-permute-start.21
  81.5 1.2 %collective-permute-done.21 = bf16[256,512]{1,0:T(8,128)(2,1)S(1)} collective-permute-done((bf16[256,512]{1,0:T(8,128)(2,1)S(1)}, bf16[256,512]{1,0:T(8,128)(2,1)S(1)}, u32[]{:S(2)}, u32[]{:S(2)}) %collective-permute-start.21) | collective-permute-done | bytes 262176 | tf_op jit(solution)/shard_map/ppermute | solution.py:164
  82.7 1.6 %collective-permute-start.24 = (bf16[2,64,512]{2,1,0:T(8,128)(2,1)S(1)}, bf16[2,64,512]{2,1,0:T(8,128)(2,1)S(1)}, u32[]{:S(2)}, u32[]{:S(2)}) collective-permute-start(bf16[2,64,512]{2,1,0:T(8,128)(2,1)S(1)} %get-tuple-element.47), channel_id=1, source_target_pairs={{0,6},{2,4},{4,2},{6,0},{8,14},{10,12},{12,10},{14,8},{1,7},{3,5},... | collective-permute-start | bytes 393224 | tf_op jit(solution)/shard_map/ppermute | solution.py:164
  84.3 0.4 collective-permute-start.22
  84.7 1.6 %collective-permute-start.23 = (bf16[2,64,512]{2,1,0:T(8,128)(2,1)S(1)}, bf16[2,64,512]{2,1,0:T(8,128)(2,1)S(1)}, u32[]{:S(2)}, u32[]{:S(2)}) collective-permute-start(bf16[2,64,512]{2,1,0:T(8,128)(2,1)S(1)} %get-tuple-element.50), channel_id=1, source_target_pairs={{0,4},{2,6},{4,0},{6,2},{8,12},{10,14},{12,8},{14,10},{1,5},{3,7},... | collective-permute-start | bytes 393224 | tf_op jit(solution)/shard_map/ppermute | solution.py:164
  86.3 3.8 %collective-permute-done.24.refs_4_ = bf16[2,64,512]{2,1,0:T(8,128)(2,1)S(1)} collective-permute-done((bf16[2,64,512]{2,1,0:T(8,128)(2,1)S(1)}, bf16[2,64,512]{2,1,0:T(8,128)(2,1)S(1)}, u32[]{:S(2)}, u32[]{:S(2)}) %collective-permute-start.24) | collective-permute-done | bytes 131104 | tf_op jit(solution)/shard_map/ppermute | solution.py:164
  90.1 2.2 %collective-permute-done.22.refs_2_ = bf16[2,64,512]{2,1,0:T(8,128)(2,1)S(1)} collective-permute-done((bf16[2,64,512]{2,1,0:T(8,128)(2,1)S(1)}, bf16[2,64,512]{2,1,0:T(8,128)(2,1)S(1)}, u32[]{:S(2)}, u32[]{:S(2)}) %collective-permute-start.22) | collective-permute-done | bytes 131104 | tf_op jit(solution)/shard_map/ppermute | solution.py:164
  92.3 0.1 collective-permute-done.23.refs_3_
  92.4 1.4 %shard_map.108 = bf16[2,64,2048]{2,1,0:T(8,128)(2,1)} custom-call(s32[4]{0:T(128)S(1)} %pad_add_fusion.place_ref.refs_0_, bf16[2,64,512]{2,1,0:T(8,128)(2,1)S(1)} %get-tuple-element.48.refs_1_, bf16[2,64,512]{2,1,0:T(8,128)(2,1)S(1)} %collective-permute-done.22.refs_2_, bf16[2,64,512]{2,1,0:T(8,128)(2,1)S(1)} %collective-permute-done.23.refs_3_, ...), custom_call_target="tpu_custom_call" | custom-call | tf_op jit(solution)/shard_map/pallas_call | solution.py:507
  (50 shorter events, 0.4 us)
Async XLA Ops:
  0.0 8.2 %copy-start.2 = (bf16[1024,512]{1,0:T(8,128)(2,1)S(1)}, bf16[1024,512]{1,0:T(8,128)(2,1)}, u32[]{:S(2)}) copy-start(bf16[1024,512]{1,0:T(8,128)(2,1)} %refs_7_.1) | copy-start | bytes 3145732
  0.0 16.0 %copy-start.7 = (f32[4096]{0:T(1024)S(1)}, f32[4096]{0:T(1024)}, u32[]{:S(2)}) copy-start(f32[4096]{0:T(1024)} %param.11) | copy-start | bytes 49156
  3.5 12.4 %collective-permute-start = (bf16[1552,128]{1,0:T(8,128)(2,1)}, bf16[1552,128]{1,0:T(8,128)(2,1)S(1)}, u32[]{:S(2)}, u32[]{:S(2)}) collective-permute-start(bf16[1552,128]{1,0:T(8,128)(2,1)} %get-tuple-element.26.query_ref.packed_ref), channel_id=1, source_target_pairs={{0,2},{2,0},{4,6},{6,4},{8,10},{10,8},{12,14},{14,12},{1,3},{3,1},... | collective-permute-start | bytes 1191944 | tf_op jit(solution)/shard_map/ppermute | solution.py:164
  6.5 15.2 %collective-permute-start.1 = (bf16[1552,128]{1,0:T(8,128)(2,1)}, bf16[1552,128]{1,0:T(8,128)(2,1)S(1)}, u32[]{:S(2)}, u32[]{:S(2)}) collective-permute-start(bf16[1552,128]{1,0:T(8,128)(2,1)} %get-tuple-element.28), channel_id=1, source_target_pairs={{0,4},{2,6},{4,0},{6,2},{8,12},{10,14},{12,8},{14,10},{1,5},{3,7},... | collective-permute-start | bytes 1191944 | tf_op jit(solution)/shard_map/ppermute | solution.py:164
  8.1 17.6 %collective-permute-start.2 = (bf16[1552,128]{1,0:T(8,128)(2,1)}, bf16[1552,128]{1,0:T(8,128)(2,1)S(1)}, u32[]{:S(2)}, u32[]{:S(2)}) collective-permute-start(bf16[1552,128]{1,0:T(8,128)(2,1)} %get-tuple-element.29), channel_id=1, source_target_pairs={{0,6},{2,4},{4,2},{6,0},{8,14},{10,12},{12,10},{14,8},{1,7},{3,5},... | collective-permute-start | bytes 1191944 | tf_op jit(solution)/shard_map/ppermute | solution.py:164
  8.2 1.0 %copy-start.4 = (bf16[1552,128]{1,0:T(8,128)(2,1)S(1)}, bf16[1552,128]{1,0:T(8,128)(2,1)}, u32[]{:S(2)}) copy-start(bf16[1552,128]{1,0:T(8,128)(2,1)} %get-tuple-element.26.query_ref.packed_ref) | copy-start | bytes 1191940
  9.8 12.0 %collective-permute-start.3 = (bf16[256,512]{1,0:T(8,128)(2,1)S(1)}, bf16[256,512]{1,0:T(8,128)(2,1)S(1)}, u32[]{:S(2)}, u32[]{:S(2)}) collective-permute-start(bf16[256,512]{1,0:T(8,128)(2,1)S(1)} %get-tuple-element.30.refs_0_), channel_id=1, source_target_pairs={{4,8},{6,10},{8,4},{10,6},{5,9},{7,11},{9,5},{11,7},{20,24},{22,26... | collective-permute-start | bytes 786440 | tf_op jit(solution)/shard_map/ppermute | solution.py:610
  10.5 11.3 %collective-permute-start.4 = (bf16[256,512]{1,0:T(8,128)(2,1)S(1)}, bf16[256,512]{1,0:T(8,128)(2,1)S(1)}, u32[]{:S(2)}, u32[]{:S(2)}) collective-permute-start(bf16[256,512]{1,0:T(8,128)(2,1)S(1)} %get-tuple-element.31.refs_0_), channel_id=1, source_target_pairs={{4,8},{6,10},{8,4},{10,6},{5,9},{7,11},{9,5},{11,7},{20,24},{22,26... | collective-permute-start | bytes 786440 | tf_op jit(solution)/shard_map/ppermute | solution.py:610
  16.0 2.2 %copy-start = (bf16[512,4096]{1,0:T(8,128)(2,1)S(1)}, bf16[512,4096]{1,0:T(8,128)(2,1)}, u32[]{:S(2)}) copy-start(bf16[512,4096]{1,0:T(8,128)(2,1)} %refs_2_.3) | copy-start | bytes 12582916
  18.1 1.0 %copy-start.5 = (bf16[1552,128]{1,0:T(8,128)(2,1)S(1)}, bf16[1552,128]{1,0:T(8,128)(2,1)}, u32[]{:S(2)}) copy-start(bf16[1552,128]{1,0:T(8,128)(2,1)} %get-tuple-element.26.query_ref.packed_ref) | copy-start | bytes 1191940
  19.1 6.6 %copy-start.3 = (bf16[1552,128]{1,0:T(8,128)(2,1)S(1)}, bf16[1552,128]{1,0:T(8,128)(2,1)}, u32[]{:S(2)}) copy-start(bf16[1552,128]{1,0:T(8,128)(2,1)} %get-tuple-element.27.refs_2_) | copy-start | bytes 1191940
  21.7 8.3 %copy-start.6 = (f32[64,16]{0,1:T(8,128)S(1)}, f32[64,16]{0,1:T(8,128)}, u32[]{:S(2)}) copy-start(f32[64,16]{0,1:T(8,128)} %param.14) | copy-start | bytes 12292
  21.7 8.3 %copy-start.10 = (f32[64,16]{0,1:T(8,128)S(1)}, f32[64,16]{0,1:T(8,128)}, u32[]{:S(2)}) copy-start(f32[64,16]{0,1:T(8,128)} %param.15) | copy-start | bytes 12292
  25.7 5.9 %copy-start.8 = (f32[3,64,3]{1,2,0:T(4,128)S(1)}, f32[3,64,3]{1,2,0:T(4,128)}, u32[]{:S(2)}) copy-start(f32[3,64,3]{1,2,0:T(4,128)} %param.13) | copy-start | bytes 6916
  25.7 5.9 %copy-start.9 = (f32[1024]{0:T(1024)S(1)}, f32[1024]{0:T(1024)}, u32[]{:S(2)}) copy-start(f32[1024]{0:T(1024)} %param.16) | copy-start | bytes 12292
  27.2 9.7 %collective-permute-start.5 = (bf16[528,128]{1,0:T(8,128)(2,1)S(1)}, bf16[528,128]{1,0:T(8,128)(2,1)S(1)}, u32[]{:S(2)}, u32[]{:S(2)}) collective-permute-start(bf16[528,128]{1,0:T(8,128)(2,1)S(1)} %get-tuple-element.32.refs_5_.refs_1_), channel_id=1, source_target_pairs={{0,8},{2,10},{4,12},{6,14},{8,0},{10,2},{12,4},{14,6},{1,9},{3,11}... | collective-permute-start | bytes 405512 | tf_op jit(solution)/shard_map/ppermute | solution.py:164
  31.4 14.6 %collective-permute-start.7 = (bf16[256,128]{1,0:T(8,128)(2,1)S(1)}, bf16[256,128]{1,0:T(8,128)(2,1)S(1)}, u32[]{:S(2)}, u32[]{:S(2)}) collective-permute-start(bf16[256,128]{1,0:T(8,128)(2,1)S(1)} %get-tuple-element.38), channel_id=1, source_target_pairs={{0,8},{2,10},{4,12},{6,14},{8,0},{10,2},{12,4},{14,6},{1,9},{3,11}... | collective-permute-start | bytes 196616 | tf_op jit(solution)/shard_map/ppermute | solution.py:164
  37.0 9.8 %collective-permute-start.6 = (bf16[2,256,128]{2,1,0:T(8,128)(2,1)S(1)}, bf16[2,256,128]{2,1,0:T(8,128)(2,1)S(1)}, u32[]{:S(2)}, u32[]{:S(2)}) collective-permute-start(bf16[2,256,128]{2,1,0:T(8,128)(2,1)S(1)} %shard_map.96.refs_3_.refs_1_), channel_id=1, source_target_pairs={{0,16},{16,0},{1,17},{17,1},{2,18},{18,2},{3,19},{19,3},{4,20},{20... | collective-permute-start | bytes 393224 | tf_op jit(solution)/shard_map/ppermute | solution.py:164
  38.3 22.4 %collective-permute-start.16 = (bf16[256,512]{1,0:T(8,128)(2,1)S(1)}, bf16[256,512]{1,0:T(8,128)(2,1)S(1)}, u32[]{:S(2)}, u32[]{:S(2)}) collective-permute-start(bf16[256,512]{1,0:T(8,128)(2,1)S(1)} %shard_map.101), channel_id=1, source_target_pairs={{0,12},{2,14},{12,0},{14,2},{1,13},{3,15},{13,1},{15,3},{16,28},{1... | collective-permute-start | bytes 786440 | tf_op jit(solution)/shard_map/ppermute | solution.py:685
  43.9 16.9 %collective-permute-start.17 = (bf16[256,512]{1,0:T(8,128)(2,1)S(1)}, bf16[256,512]{1,0:T(8,128)(2,1)S(1)}, u32[]{:S(2)}, u32[]{:S(2)}) collective-permute-start(bf16[256,512]{1,0:T(8,128)(2,1)S(1)} %shard_map.102), channel_id=1, source_target_pairs={{0,12},{2,14},{12,0},{14,2},{1,13},{3,15},{13,1},{15,3},{16,28},{1... | collective-permute-start | bytes 786440 | tf_op jit(solution)/shard_map/ppermute | solution.py:685
  46.0 4.3 %collective-permute-start.8 = (bf16[1,256,128]{2,1,0:T(8,128)(2,1)S(1)}, bf16[1,256,128]{2,1,0:T(8,128)(2,1)S(1)}, u32[]{:S(2)}, u32[]{:S(2)}) collective-permute-start(bf16[1,256,128]{2,1,0:T(8,128)(2,1)S(1)} %fusion.4.refs_2_), channel_id=1, source_target_pairs={{0,16},{16,0},{1,17},{17,1},{2,18},{18,2},{3,19},{19,3},{4,20},{20... | collective-permute-start | bytes 196616 | tf_op jit(solution)/shard_map/ppermute | solution.py:164
  51.4 2.8 %collective-permute-start.9 = (bf16[256,128]{1,0:T(8,128)(2,1)S(1)}, bf16[256,128]{1,0:T(8,128)(2,1)S(1)}, u32[]{:S(2)}, u32[]{:S(2)}) collective-permute-start(bf16[256,128]{1,0:T(8,128)(2,1)S(1)} %get-tuple-element.42), channel_id=1, source_target_pairs={{0,1},{1,0},{2,3},{3,2},{4,5},{5,4},{6,7},{7,6},{8,9},{9,8},{10,11... | collective-permute-start | bytes 196616 | tf_op jit(solution)/shard_map/ppermute | solution.py:164
  51.5 7.3 %collective-permute-start.10 = (bf16[256,128]{1,0:T(8,128)(2,1)S(1)}, bf16[256,128]{1,0:T(8,128)(2,1)S(1)}, u32[]{:S(2)}, u32[]{:S(2)}) collective-permute-start(bf16[256,128]{1,0:T(8,128)(2,1)S(1)} %get-tuple-element.43), channel_id=1, source_target_pairs={{0,8},{2,10},{4,12},{6,14},{8,0},{10,2},{12,4},{14,6},{1,9},{3,11}... | collective-permute-start | bytes 196616 | tf_op jit(solution)/shard_map/ppermute | solution.py:164
  51.6 9.1 %collective-permute-start.11 = (bf16[256,128]{1,0:T(8,128)(2,1)S(1)}, bf16[256,128]{1,0:T(8,128)(2,1)S(1)}, u32[]{:S(2)}, u32[]{:S(2)}) collective-permute-start(bf16[256,128]{1,0:T(8,128)(2,1)S(1)} %get-tuple-element.44), channel_id=1, source_target_pairs={{0,9},{1,8},{2,11},{3,10},{4,13},{5,12},{6,15},{7,14},{8,1},{9,0},... | collective-permute-start | bytes 196616 | tf_op jit(solution)/shard_map/ppermute | solution.py:172
  60.7 16.9 %copy-start.1 = (bf16[512,4096]{1,0:T(8,128)(2,1)S(1)}, bf16[512,4096]{1,0:T(8,128)(2,1)}, u32[]{:S(2)}) copy-start(bf16[512,4096]{1,0:T(8,128)(2,1)} %refs_2_.3) | copy-start | bytes 12582916
  60.9 14.2 %collective-permute-start.19 = (bf16[512,512]{1,0:T(8,128)(2,1)S(1)}, bf16[512,512]{1,0:T(8,128)(2,1)S(1)}, u32[]{:S(2)}, u32[]{:S(2)}) collective-permute-start(bf16[512,512]{1,0:T(8,128)(2,1)S(1)} %shard_map.103.refs_5_), channel_id=1, source_target_pairs={{0,16},{16,0},{1,17},{17,1},{2,18},{18,2},{3,19},{19,3},{4,20},{20... | collective-permute-start | bytes 1572872 | tf_op jit(solution)/shard_map/ppermute | solution.py:164
  62.1 15.5 %collective-permute-start.15 = (bf16[1024,512]{1,0:T(8,128)(2,1)S(1)}, bf16[1024,512]{1,0:T(8,128)(2,1)S(1)}, u32[]{:S(2)}, u32[]{:S(2)}) collective-permute-start(bf16[1024,512]{1,0:T(8,128)(2,1)S(1)} %copy-done.2), channel_id=1, source_target_pairs={{0,1},{1,0},{2,3},{3,2},{4,5},{5,4},{6,7},{7,6},{8,9},{9,8},{10,11... | collective-permute-start | bytes 3145736 | tf_op jit(solution)/shard_map/ppermute | solution.py:164
  62.1 8.7 %collective-permute-start.12 = (bf16[4,256,128]{2,1,0:T(8,128)(2,1)S(1)}, bf16[4,256,128]{2,1,0:T(8,128)(2,1)S(1)}, u32[]{:S(2)}, u32[]{:S(2)}) collective-permute-start(bf16[4,256,128]{2,1,0:T(8,128)(2,1)S(1)} %pad_maximum_fusion.refs_3_.refs_1_), channel_id=1, source_target_pairs={{0,2},{2,0},{4,6},{6,4},{8,10},{10,8},{12,14},{14,12},{1,3},{3,1},... | collective-permute-start | bytes 786440 | tf_op jit(solution)/shard_map/ppermute | solution.py:164
  63.6 11.5 %collective-permute-start.13 = (bf16[4,256,128]{2,1,0:T(8,128)(2,1)S(1)}, bf16[4,256,128]{2,1,0:T(8,128)(2,1)S(1)}, u32[]{:S(2)}, u32[]{:S(2)}) collective-permute-start(bf16[4,256,128]{2,1,0:T(8,128)(2,1)S(1)} %pad_maximum_fusion.refs_3_.refs_1_), channel_id=1, source_target_pairs={{0,4},{2,6},{4,0},{6,2},{8,12},{10,14},{12,8},{14,10},{1,5},{3,7},... | collective-permute-start | bytes 786440 | tf_op jit(solution)/shard_map/ppermute | solution.py:164
  64.2 13.5 %collective-permute-start.14 = (bf16[4,256,128]{2,1,0:T(8,128)(2,1)S(1)}, bf16[4,256,128]{2,1,0:T(8,128)(2,1)S(1)}, u32[]{:S(2)}, u32[]{:S(2)}) collective-permute-start(bf16[4,256,128]{2,1,0:T(8,128)(2,1)S(1)} %pad_maximum_fusion.refs_3_.refs_1_), channel_id=1, source_target_pairs={{0,6},{2,4},{4,2},{6,0},{8,14},{10,12},{12,10},{14,8},{1,7},{3,5},... | collective-permute-start | bytes 786440 | tf_op jit(solution)/shard_map/ppermute | solution.py:164
  70.8 8.7 %collective-permute-start.18 = (bf16[512,512]{1,0:T(8,128)(2,1)S(1)}, bf16[512,512]{1,0:T(8,128)(2,1)S(1)}, u32[]{:S(2)}, u32[]{:S(2)}) collective-permute-start(bf16[512,512]{1,0:T(8,128)(2,1)S(1)} %shard_map.103.refs_5_), channel_id=1, source_target_pairs={{0,1},{1,0},{2,3},{3,2},{4,5},{5,4},{6,7},{7,6},{8,9},{9,8},{10,11... | collective-permute-start | bytes 1572872 | tf_op jit(solution)/shard_map/ppermute | solution.py:164
  77.6 1.9 %collective-permute-start.20 = (bf16[512,512]{1,0:T(8,128)(2,1)S(1)}, bf16[512,512]{1,0:T(8,128)(2,1)S(1)}, u32[]{:S(2)}, u32[]{:S(2)}) collective-permute-start(bf16[512,512]{1,0:T(8,128)(2,1)S(1)} %shard_map.106.refs_7_), channel_id=1, source_target_pairs={{0,1},{1,0},{2,3},{3,2},{4,5},{5,4},{6,7},{7,6},{8,9},{9,8},{10,11... | collective-permute-start | bytes 1572872 | tf_op jit(solution)/shard_map/ppermute | solution.py:164
  81.0 1.7 %collective-permute-start.21 = (bf16[256,512]{1,0:T(8,128)(2,1)S(1)}, bf16[256,512]{1,0:T(8,128)(2,1)S(1)}, u32[]{:S(2)}, u32[]{:S(2)}) collective-permute-start(bf16[256,512]{1,0:T(8,128)(2,1)S(1)} %get-tuple-element.51), channel_id=1, source_target_pairs={{0,1},{1,0},{2,3},{3,2},{4,5},{5,4},{6,7},{7,6},{8,9},{9,8},{10,11... | collective-permute-start | bytes 786440 | tf_op jit(solution)/shard_map/ppermute | solution.py:164
  82.7 7.3 %collective-permute-start.24 = (bf16[2,64,512]{2,1,0:T(8,128)(2,1)S(1)}, bf16[2,64,512]{2,1,0:T(8,128)(2,1)S(1)}, u32[]{:S(2)}, u32[]{:S(2)}) collective-permute-start(bf16[2,64,512]{2,1,0:T(8,128)(2,1)S(1)} %get-tuple-element.47), channel_id=1, source_target_pairs={{0,6},{2,4},{4,2},{6,0},{8,14},{10,12},{12,10},{14,8},{1,7},{3,5},... | collective-permute-start | bytes 393224 | tf_op jit(solution)/shard_map/ppermute | solution.py:164
  84.3 8.0 %collective-permute-start.22 = (bf16[2,64,512]{2,1,0:T(8,128)(2,1)S(1)}, bf16[2,64,512]{2,1,0:T(8,128)(2,1)S(1)}, u32[]{:S(2)}, u32[]{:S(2)}) collective-permute-start(bf16[2,64,512]{2,1,0:T(8,128)(2,1)S(1)} %get-tuple-element.49), channel_id=1, source_target_pairs={{0,2},{2,0},{4,6},{6,4},{8,10},{10,8},{12,14},{14,12},{1,3},{3,1},... | collective-permute-start | bytes 393224 | tf_op jit(solution)/shard_map/ppermute | solution.py:164
  84.7 7.7 %collective-permute-start.23 = (bf16[2,64,512]{2,1,0:T(8,128)(2,1)S(1)}, bf16[2,64,512]{2,1,0:T(8,128)(2,1)S(1)}, u32[]{:S(2)}, u32[]{:S(2)}) collective-permute-start(bf16[2,64,512]{2,1,0:T(8,128)(2,1)S(1)} %get-tuple-element.50), channel_id=1, source_target_pairs={{0,4},{2,6},{4,0},{6,2},{8,12},{10,14},{12,8},{14,10},{1,5},{3,7},... | collective-permute-start | bytes 393224 | tf_op jit(solution)/shard_map/ppermute | solution.py:164

commit v5 on v4

--- a/solution.py
+++ b/solution.py
@@ -200,34 +200,48 @@
     out_ref[...] = (own * lax.rsqrt(mean + epsilon) * gain_ref[...]).astype(bf16)
 
 
-def pack_kernel(token_ref, weight_ref, *refs):
-    out_refs, sems = refs[:-1], refs[-1]
+def pack_kernel(tokens_ref, weight_ref, *refs):
+    out_refs, (held_ref, token_ref, token_sem, in_sems, out_sems) = refs[:-5], refs[-5:]
     branches, depth, channels = weight_ref.shape
     members = len(out_refs)
     quad, group = lax.axis_index("ctx") % members, lax.axis_index("groups")
     block = channels // members
-    copies = []
-    for m in (1, 2, 3, 0):
+    order = (1, 2, 3, 0)
+    fetch = pltpu.make_async_copy(tokens_ref, token_ref, token_sem)
+    fetch.start()
+    copies = {}
+    for m in order:
         first = pl.multiple_of((quad ^ m) * block + group * LANES, LANES)
-        for j in range(branches):
-            copies.append(
-                pltpu.make_async_copy(
-                    weight_ref.at[j, :, pl.ds(first, LANES)],
-                    out_refs[m].at[pl.ds((j + 2) % 3 * depth, depth), :],
-                    sems.at[m, j],
-                )
+        for i, j in enumerate((1, 2, 0)):
+            copies[m, i] = pltpu.make_async_copy(
+                weight_ref.at[j, :, pl.ds(first, LANES)],
+                held_ref.at[m, pl.ds(i * depth, depth), :],
+                in_sems.at[m, i],
             )
-            copies[-1].start()
+            copies[m, i].start()
     rows = token_ref.shape[1]
     row = lax.broadcasted_iota(jnp.int32, (SPARE, rows), 0)
+    fetch.wait()
     token = jnp.where(row % 4 < 2, token_ref[0:1, :], token_ref[1:2, :])
     token = jnp.where(row % 2 == 0, token >> 8, token & 255)
     token = jnp.where(row // 4 == quad, token, 0).astype(f32).astype(bf16)
-    for out_ref in out_refs:
-        out_ref[branches * depth :, :] = jnp.zeros((SPARE, LANES), bf16)
-        out_ref[branches * depth :, :rows] = token
-    for copy in copies:
-        copy.wait()
+    for m in order:
+        held_ref[m, branches * depth :, :] = jnp.zeros((SPARE, LANES), bf16)
+        held_ref[m, branches * depth :, :rows] = token
+    results = []
+    for m in order:
+        for i in range(branches):
+            copies[m, i].wait()
+        results.append(pltpu.make_async_copy(held_ref.at[m], out_refs[m], out_sems.at[m]))
+        results[-1].start()
+    for result in results:
+        result.wait()
+
+
+def here():
+    members = lax.axis_size("ctx") // 2
+    ctx = lax.axis_index("ctx")
+    return ctx % members, ctx // members, lax.axis_index("groups"), lax.axis_index("chan")
 
 
 def pick(half, near_ref, far_ref, picked_ref, genomes, rows):
@@ -251,8 +265,8 @@
                 )
 
 
-def prepare_kernel(place_ref, rate_ref, amp_ref, taps_ref, skip_ref, matrices_ref, rows_ref):
-    quad, half = place_ref[0], place_ref[1]
+def prepare_kernel(rate_ref, amp_ref, taps_ref, skip_ref, matrices_ref, rows_ref):
+    quad, half, _, _ = here()
 
     group_count = rate_ref.shape[1]
     poles = rate_ref.shape[0]
@@ -319,9 +333,9 @@
     rows_ref[end : end + 1] = jnp.where(lane_half(upper.shape), upper, lower)
 
 
-def partial_kernel(place_ref, normed_ref, *refs, begin, count):
+def partial_kernel(normed_ref, *refs, begin, count):
     weight_refs, (keep_ref, send_ref) = refs[:-2], refs[-2:]
-    quad, half = place_ref[0], place_ref[1]
+    quad, half, _, _ = here()
     rows, features = normed_ref.shape
     depth = features // len(weight_refs)
     total = jnp.zeros((rows, count * LANES), f32)
@@ -365,9 +379,9 @@
 
 
 def conv_kernel(
-    place_ref, near_ref, far_ref, own_ref, other_ref, matrices_ref, rows_ref, value_ref, picked_ref, *, genomes, rows
+    near_ref, far_ref, own_ref, other_ref, matrices_ref, rows_ref, value_ref, picked_ref, *, genomes, rows
 ):
-    half, group = place_ref[1], place_ref[2]
+    _, half, group, _ = here()
     pick(half, near_ref, far_ref, picked_ref, genomes, rows)
     positions = picked_ref.shape[0]
     length = positions // genomes
@@ -406,9 +420,9 @@
             state = fade * state + jnp.where(same, ends, 0.0)
 
 
-def gate_kernel(place_ref, picked_ref, own_ref, other_ref, rows_ref, value_ref, *refs, genomes):
+def gate_kernel(picked_ref, own_ref, other_ref, rows_ref, value_ref, *refs, genomes):
     piece_refs, (mine_ref, held_ref) = refs[:4], refs[4:]
-    half, group, core = place_ref[1], place_ref[2], place_ref[3]
+    _, half, group, core = here()
     positions = picked_ref.shape[0]
     length = positions // genomes
     row = lax.broadcasted_iota(jnp.int32, (positions, LANES), 0) % length
@@ -436,9 +450,9 @@
     )
 
 
-def near_kernel(place_ref, picked_ref, table_ref, *refs):
+def near_kernel(picked_ref, table_ref, *refs):
     piece_refs, (own_ref, core_ref, out_ref, joined_ref) = refs[:4], refs[4:]
-    quad, half = place_ref[0], place_ref[1]
+    quad, half, _, _ = here()
     block = 2 * LANES
     for m, piece_ref in enumerate(piece_refs):
         for other_core in (0, 1):
@@ -464,9 +478,9 @@
     out_ref[...] = total.astype(bf16)
 
 
-def far_kernel(place_ref, picked_ref, table_ref, near_ref, joined_ref, *refs):
+def far_kernel(picked_ref, table_ref, near_ref, joined_ref, *refs):
     far_refs, out_ref = (refs[:2], refs[2:4]), refs[4]
-    quad, half, group, core = (place_ref[i] for i in range(4))
+    quad, half, group, core = here()
     block = 2 * LANES
     width = near_ref.shape[1]
     total = jnp.zeros(near_ref.shape, f32)
@@ -484,14 +498,22 @@
     out_ref[half ^ 1 ^ core] = total.astype(bf16)
 
 
-def place_kernel(place_ref, *refs):
-    piece_refs, out_ref = refs[:4], refs[4]
-    quad, half, core = place_ref[0], place_ref[1], place_ref[3]
+def place_kernel(*refs):
+    piece_refs, (out_ref, sems) = refs[:4], refs[4:]
+    quad, half, _, core = here()
     width = piece_refs[0].shape[2]
+    copies = []
     for m, piece_ref in enumerate(piece_refs):
         first = pl.multiple_of((quad ^ m ^ (2 * (half ^ core))) * width, width)
         for g in (0, 1):
-            out_ref[core ^ g, :, pl.ds(first, width)] = piece_ref[g]
+            copies.append(
+                pltpu.make_async_copy(
+                    piece_ref.at[g], out_ref.at[core ^ g, :, pl.ds(first, width)], sems.at[m, g]
+                )
+            )
+            copies[-1].start()
+    for copy in copies:
+        copy.wait()
 
 
 def called(kernel, out_shape, scalars, *operands, scratch=(), mib=16, earlier=()):
@@ -558,9 +580,15 @@
     packed = pl.pallas_call(
         pack_kernel,
         out_shape=[shaped(branches * depth + SPARE, LANES, dtype=bf16)] * members,
-        in_specs=[pl.BlockSpec(memory_space=pltpu.VMEM), anywhere],
-        out_specs=[pl.BlockSpec(memory_space=pltpu.VMEM)] * members,
-        scratch_shapes=[pltpu.SemaphoreType.DMA((members, branches))],
+        in_specs=[anywhere, anywhere],
+        out_specs=[anywhere] * members,
+        scratch_shapes=[
+            pltpu.VMEM((members, branches * depth + SPARE, LANES), bf16),
+            pltpu.VMEM((genomes, rows), jnp.int32),
+            pltpu.SemaphoreType.DMA,
+            pltpu.SemaphoreType.DMA((members, branches)),
+            pltpu.SemaphoreType.DMA((members,)),
+        ],
         compiler_params=pltpu.CompilerParams(vmem_limit_bytes=61 * MIB),
     )(tokens, weights)
     gathered = [packed[0]] + [swapped(packed[m], "ctx", m) for m in range(1, members)]
@@ -613,7 +641,7 @@
         return called(
             functools.partial(partial_kernel, begin=begin, count=count),
             [shaped(table_rows, LANES), shaped(table_rows + spare, LANES, dtype=bf16)],
-            (place,),
+            (),
             normed,
             *gathered,
             earlier=earlier,
@@ -635,7 +663,7 @@
             shaped(CHUNK, 2 * across + 2 * CHUNK, dtype=bf16),
             shaped(LANES + 8 * (branches + 1), LANES),
         ],
-        (place,),
+        (),
         pole_rate.T,
         amp.T,
         short_filter.transpose(0, 2, 1),
@@ -652,7 +680,7 @@
     value, picked = called(
         functools.partial(conv_kernel, genomes=genomes, rows=rows),
         [shaped(genomes * length, LANES), shaped(genomes * length, vocab, dtype=bf16)],
-        (place,),
+        (),
         pair_send,
         pair_arrived,
         pair_own,
@@ -663,7 +691,7 @@
     *pieces, picked = called(
         functools.partial(gate_kernel, genomes=genomes),
         [shaped(span, LANES, dtype=bf16)] * 4 + [shaped(span, vocab, dtype=bf16)],
-        (place,),
+        (),
         picked,
         query_own,
         query_other,
@@ -695,7 +723,7 @@
     near, joined = called(
         near_kernel,
         [shaped(span, width, dtype=bf16), shaped(4 * 2, span, 2 * LANES, dtype=bf16)],
-        (place,),
+        (),
         picked,
         embed_table,
         *gated,
@@ -706,7 +734,7 @@
     results = called(
         far_kernel,
         shaped(2, span, width, dtype=bf16),
-        (place,),
+        (),
         picked,
         embed_table,
         near,
@@ -723,9 +751,14 @@
         return lax.dynamic_slice_in_dim(both, member * rows, rows, 1)
 
     arrived = [rows_of(quad)] + [swapped(rows_of(quad ^ m), "ctx", m) for m in range(1, members)]
-    return called(
-        place_kernel, shaped(genomes, rows, members * width, dtype=bf16), (place,), *arrived
-    )
+    return pl.pallas_call(
+        place_kernel,
+        out_shape=shaped(genomes, rows, members * width, dtype=bf16),
+        in_specs=[pl.BlockSpec(memory_space=pltpu.VMEM)] * members,
+        out_specs=anywhere,
+        scratch_shapes=[pltpu.SemaphoreType.DMA((members, 2))],
+        compiler_params=pltpu.CompilerParams(vmem_limit_bytes=4 * MIB),
+    )(*arrived)
 
 
 def solution(mesh):

time: 94.1 us -> 91.1 us (0.968)
  Pallas kernels: 20.6 us -> 15.3 us
  waiting for transfers between devices: 37.8 us -> 40.8 us
    pallas_call x8 -> x7, Pallas kernels: 13.9 us -> 8.67 us  [called(): pl.pallas_call(body, out_shape=out_shape, in_specs=[smem] * len(scalars)...]
    ppermute x20, waiting for transfers between devices: 35.9 us -> 40.1 us  [swapped(): return lax.ppermute(value, axis, [(i, i ^ mask) for i in range(count)])]
    ppermute x1, waiting for transfers between devices: 1.9 us -> 0.73 us  [swapped_both(): return lax.ppermute(value, ('ctx', 'chan'), pairs)]
  transfers between devices with their start and end apart: 25 -> 25, of which waited for: 13 -> 13; matrix products, arithmetic and copies ran while one was open for 0% -> 0% of each run, Pallas kernels for 14% -> 11%
where the time goes in v5:
time: 91.1 us; the launch traced here: 90.8 us
  waiting for transfers between devices  40.8 us (45%)
  starting transfers between devices  29.8 us (33%)
  Pallas kernels  15.3 us (17%)
  local copies, waits for them, and re-layouts  4.26 us (5%)
    ppermute x20, waiting for transfers between devices, swapped(): return lax.ppermute(value, axis, [(i, i ^ mask) for i in range(count)])  40.1 us
    ppermute x20, starting transfers between devices, swapped(): return lax.ppermute(value, axis, [(i, i ^ mask) for i in range(count)])  18.1 us
    pallas_call x7, Pallas kernels, called(): pl.pallas_call(body, out_shape=out_shape, in_specs=[smem] * len(scalars)...  8.67 us
    ppermute x2, starting transfers between devices, quad_body(): lax.ppermute(after(rows_part, pair_own), 'ctx', outer)  7.63 us
    unnamed x22, local copies, waits for them, and re-layouts  4.22 us
    ppermute x1, starting transfers between devices, swapped_both(): return lax.ppermute(value, ('ctx', 'chan'), pairs)  2.68 us
    pallas_call x1, Pallas kernels, quad_body(): pl.pallas_call(pack_kernel, out_shape=[shaped(branches * depth + SPARE, L...  2.64 us
    pallas_call x1, Pallas kernels, quad_body(): pl.pallas_call(norm_kernel, out_shape=shaped(vocab, part, dtype=bf16), gr...  2.56 us
  transfers between devices with their start and end apart: 25, of which 13 were waited for; matrix products, arithmetic and copies ran while one was open for 0% of the time, Pallas kernels for 11%

profile of v5, /device:TPU:0, one launch (start us, length us, event | category | flops | bytes accessed | tf_op | source)
XLA Modules:
  0.0 90.8 jit_solution(13061662751360236224)
XLA Ops:
  0.0 2.6 %shard_map.91 = (bf16[1552,128]{1,0:T(8,128)(2,1)}, bf16[1552,128]{1,0:T(8,128)(2,1)}, bf16[1552,128]{1,0:T(8,128)(2,1)}, bf16[1552,128]{1,0:T(8,128)(2,1)}) custom-call(s32[2,64]{1,0:T(2,128)} %tokens_ref.1, bf16[3,512,1024]{2,1,0:T(8,128)(2,1)} %bitcast.27), custom_call_target="tpu_custom_call" | custom-call | tf_op jit(solution)/shard_map/pallas_call | solution.py:580
  2.7 3.0 %collective-permute-start = (bf16[1552,128]{1,0:T(8,128)(2,1)}, bf16[1552,128]{1,0:T(8,128)(2,1)S(1)}, u32[]{:S(2)}, u32[]{:S(2)}) collective-permute-start(bf16[1552,128]{1,0:T(8,128)(2,1)} %get-tuple-element.26.query_ref.packed_ref), channel_id=1, source_target_pairs={{0,2},{2,0},{4,6},{6,4},{8,10},{10,8},{12,14},{14,12},{1,3},{3,1},... | collective-permute-start | bytes 1191944 | tf_op jit(solution)/shard_map/ppermute | solution.py:164
  5.7 1.6 %collective-permute-start.1 = (bf16[1552,128]{1,0:T(8,128)(2,1)}, bf16[1552,128]{1,0:T(8,128)(2,1)S(1)}, u32[]{:S(2)}, u32[]{:S(2)}) collective-permute-start(bf16[1552,128]{1,0:T(8,128)(2,1)} %get-tuple-element.28), channel_id=1, source_target_pairs={{0,4},{2,6},{4,0},{6,2},{8,12},{10,14},{12,8},{14,10},{1,5},{3,7},... | collective-permute-start | bytes 1191944 | tf_op jit(solution)/shard_map/ppermute | solution.py:164
  7.3 0.1 pad_add_fusion.place_ref
  7.4 1.0 %copy-done.4 = bf16[1552,128]{1,0:T(8,128)(2,1)S(1)} copy-done((bf16[1552,128]{1,0:T(8,128)(2,1)S(1)}, bf16[1552,128]{1,0:T(8,128)(2,1)}, u32[]{:S(2)}) %copy-start.4) | copy-done | bytes 397336
  8.4 0.6 shard_map.93
  8.9 0.7 collective-permute-start.3
  9.6 0.7 collective-permute-start.4
  10.3 4.8 %collective-permute-done.pair_ref.refs_2_ = bf16[1552,128]{1,0:T(8,128)(2,1)S(1)} collective-permute-done((bf16[1552,128]{1,0:T(8,128)(2,1)}, bf16[1552,128]{1,0:T(8,128)(2,1)S(1)}, u32[]{:S(2)}, u32[]{:S(2)}) %collective-permute-start) | collective-permute-done | bytes 397344 | tf_op jit(solution)/shard_map/ppermute | solution.py:164
  15.1 2.2 %copy-done = bf16[512,4096]{1,0:T(8,128)(2,1)S(1)} copy-done((bf16[512,4096]{1,0:T(8,128)(2,1)S(1)}, bf16[512,4096]{1,0:T(8,128)(2,1)}, u32[]{:S(2)}) %copy-start) | copy-done | bytes 4194328
  17.3 1.0 %copy-done.5 = bf16[1552,128]{1,0:T(8,128)(2,1)S(1)} copy-done((bf16[1552,128]{1,0:T(8,128)(2,1)S(1)}, bf16[1552,128]{1,0:T(8,128)(2,1)}, u32[]{:S(2)}) %copy-start.5) | copy-done | bytes 397336
  18.3 2.6 %shard_map.92.refs_0_ = bf16[512,2048]{1,0:T(8,128)(2,1)S(1)} custom-call(s32[4]{0:T(128)S(1)} %pad_add_fusion.place_ref, bf16[512,4096]{1,0:T(8,128)(2,1)S(1)} %copy-done, f32[1,4096]{1,0:T(1,128)S(1)} %bitcast.24, bf16[512,4096]{1,0:T(8,128)(2,1)S(1)} %copy-done, bf16[1552,128]{1,0:T(8,128)(2,1)S(1)} %collective-permute-done.pair_ref.refs_2_, ...), custom_call_target="tpu_custom_call" | custom-call | tf_op jit(solution)/shard_map/pallas_call | solution.py:620
  20.9 4.0 %collective-permute-done.2.refs_4_ = bf16[1552,128]{1,0:T(8,128)(2,1)S(1)} collective-permute-done((bf16[1552,128]{1,0:T(8,128)(2,1)}, bf16[1552,128]{1,0:T(8,128)(2,1)S(1)}, u32[]{:S(2)}, u32[]{:S(2)}) %collective-permute-start.2) | collective-permute-done | bytes 397344 | tf_op jit(solution)/shard_map/ppermute | solution.py:164
  24.9 0.9 shard_map.94
  25.8 2.8 %collective-permute-start.5 = (bf16[528,128]{1,0:T(8,128)(2,1)S(1)}, bf16[528,128]{1,0:T(8,128)(2,1)S(1)}, u32[]{:S(2)}, u32[]{:S(2)}) collective-permute-start(bf16[528,128]{1,0:T(8,128)(2,1)S(1)} %get-tuple-element.32.refs_4_.refs_0_), channel_id=1, source_target_pairs={{0,8},{2,10},{4,12},{6,14},{8,0},{10,2},{12,4},{14,6},{1,9},{3,11}... | collective-permute-start | bytes 405512 | tf_op jit(solution)/shard_map/ppermute | solution.py:164
  28.6 0.8 shard_map.98
  29.5 0.3 collective-permute-start.7
  29.7 1.5 %shard_map.95 = (bf16[128,2560]{1,0:T(8,128)(2,1)S(1)}, f32[160,128]{1,0:T(8,128)S(1)}) custom-call(f32[16,64]{1,0:T(8,128)S(1)} %bitcast.23, f32[16,64]{1,0:T(8,128)S(1)} %multiply_bitcast_fusion.refs_1_, f32[3,3,64]{2,1,0:T(4,128)S(1)} %bitcast.25, f32[8,128]{1,0:T(8,128)S(1)} %bitcast.26, bf16[528,128]{1,0:T(8,128)(2,1)S(1)} %get-tuple-element.32.refs_4_.refs_0_), custom_call_target="tpu_custom_call" | custom-call | tf_op jit(solution)/shard_map/pallas_call | solution.py:529
  31.3 4.9 %collective-permute-done.5.refs_1_ = bf16[528,128]{1,0:T(8,128)(2,1)S(1)} collective-permute-done((bf16[528,128]{1,0:T(8,128)(2,1)S(1)}, bf16[528,128]{1,0:T(8,128)(2,1)S(1)}, u32[]{:S(2)}, u32[]{:S(2)}) %collective-permute-start.5) | collective-permute-done | bytes 135200 | tf_op jit(solution)/shard_map/ppermute | solution.py:164
  36.3 1.4 %collective-permute-start.6 = (bf16[2,256,128]{2,1,0:T(8,128)(2,1)S(1)}, bf16[2,256,128]{2,1,0:T(8,128)(2,1)S(1)}, u32[]{:S(2)}, u32[]{:S(2)}) collective-permute-start(bf16[2,256,128]{2,1,0:T(8,128)(2,1)S(1)} %shard_map.96.refs_2_.refs_1_), channel_id=1, source_target_pairs={{0,16},{16,0},{1,17},{17,1},{2,18},{18,2},{3,19},{19,3},{4,20},{20... | collective-permute-start | bytes 393224 | tf_op jit(solution)/shard_map/ppermute | solution.py:164
  37.7 4.9 %collective-permute-start.16 = (bf16[256,512]{1,0:T(8,128)(2,1)S(1)}, bf16[256,512]{1,0:T(8,128)(2,1)S(1)}, u32[]{:S(2)}, u32[]{:S(2)}) collective-permute-start(bf16[256,512]{1,0:T(8,128)(2,1)S(1)} %shard_map.101), channel_id=1, source_target_pairs={{0,12},{2,14},{12,0},{14,2},{1,13},{3,15},{13,1},{15,3},{16,28},{1... | collective-permute-start | bytes 786440 | tf_op jit(solution)/shard_map/ppermute | solution.py:713
  42.5 2.8 %collective-permute-start.17 = (bf16[256,512]{1,0:T(8,128)(2,1)S(1)}, bf16[256,512]{1,0:T(8,128)(2,1)S(1)}, u32[]{:S(2)}, u32[]{:S(2)}) collective-permute-start(bf16[256,512]{1,0:T(8,128)(2,1)S(1)} %shard_map.102), channel_id=1, source_target_pairs={{0,12},{2,14},{12,0},{14,2},{1,13},{3,15},{13,1},{15,3},{16,28},{1... | collective-permute-start | bytes 786440 | tf_op jit(solution)/shard_map/ppermute | solution.py:713
  45.3 0.8 collective-permute-start.8
  46.1 2.7 %shard_map.97 = (f32[1024,128]{1,0:T(8,128)S(1)}, bf16[1024,512]{1,0:T(8,128)(2,1)S(1)}) custom-call(bf16[528,128]{1,0:T(8,128)(2,1)S(1)} %get-tuple-element.32.refs_4_.refs_0_, bf16[528,128]{1,0:T(8,128)(2,1)S(1)} %collective-permute-done.5.refs_1_, bf16[2,256,128]{2,1,0:T(8,128)(2,1)S(1)} %shard_map.96.refs_2_.refs_1_, ...), custom_call_target="tpu_custom_call" | custom-call | tf_op jit(solution)/shard_map/pallas_call | solution.py:529
  48.8 0.8 collective-permute-done.8.refs_2_
  49.7 0.5 shard_map.99
  50.4 2.7 %collective-permute-start.11 = (bf16[256,128]{1,0:T(8,128)(2,1)S(1)}, bf16[256,128]{1,0:T(8,128)(2,1)S(1)}, u32[]{:S(2)}, u32[]{:S(2)}) collective-permute-start(bf16[256,128]{1,0:T(8,128)(2,1)S(1)} %get-tuple-element.44), channel_id=1, source_target_pairs={{0,9},{1,8},{2,11},{3,10},{4,13},{5,12},{6,15},{7,14},{8,1},{9,0},... | collective-permute-start | bytes 196616 | tf_op jit(solution)/shard_map/ppermute | solution.py:172
  53.1 5.8 %collective-permute-done.10 = bf16[256,128]{1,0:T(8,128)(2,1)S(1)} collective-permute-done((bf16[256,128]{1,0:T(8,128)(2,1)S(1)}, bf16[256,128]{1,0:T(8,128)(2,1)S(1)}, u32[]{:S(2)}, u32[]{:S(2)}) %collective-permute-start.10) | collective-permute-done | bytes 65568 | tf_op jit(solution)/shard_map/ppermute | solution.py:164
  58.8 0.7 collective-permute-done.11
  59.6 0.1 maximum_select_fusion.refs_0_
  59.8 0.9 collective-permute-start.19
  60.7 1.2 %collective-permute-start.12 = (bf16[4,256,128]{2,1,0:T(8,128)(2,1)S(1)}, bf16[4,256,128]{2,1,0:T(8,128)(2,1)S(1)}, u32[]{:S(2)}, u32[]{:S(2)}) collective-permute-start(bf16[4,256,128]{2,1,0:T(8,128)(2,1)S(1)} %pad_maximum_fusion.refs_2_.refs_1_), channel_id=1, source_target_pairs={{0,2},{2,0},{4,6},{6,4},{8,10},{10,8},{12,14},{14,12},{1,3},{3,1},... | collective-permute-start | bytes 786440 | tf_op jit(solution)/shard_map/ppermute | solution.py:164
  61.9 0.8 collective-permute-start.13
  62.8 1.4 %collective-permute-start.14 = (bf16[4,256,128]{2,1,0:T(8,128)(2,1)S(1)}, bf16[4,256,128]{2,1,0:T(8,128)(2,1)S(1)}, u32[]{:S(2)}, u32[]{:S(2)}) collective-permute-start(bf16[4,256,128]{2,1,0:T(8,128)(2,1)S(1)} %pad_maximum_fusion.refs_2_.refs_1_), channel_id=1, source_target_pairs={{0,6},{2,4},{4,2},{6,0},{8,14},{10,12},{12,10},{14,8},{1,7},{3,5},... | collective-permute-start | bytes 786440 | tf_op jit(solution)/shard_map/ppermute | solution.py:164
  64.2 5.2 %collective-permute-done.12.refs_3_.refs_1_ = bf16[4,256,128]{2,1,0:T(8,128)(2,1)S(1)} collective-permute-done((bf16[4,256,128]{2,1,0:T(8,128)(2,1)S(1)}, bf16[4,256,128]{2,1,0:T(8,128)(2,1)S(1)}, u32[]{:S(2)}, u32[]{:S(2)}) %collective-permute-start.12) | collective-permute-done | bytes 262176 | tf_op jit(solution)/shard_map/ppermute | solution.py:164
  69.4 4.4 %collective-permute-done.19.refs_0_ = bf16[512,512]{1,0:T(8,128)(2,1)S(1)} collective-permute-done((bf16[512,512]{1,0:T(8,128)(2,1)S(1)}, bf16[512,512]{1,0:T(8,128)(2,1)S(1)}, u32[]{:S(2)}, u32[]{:S(2)}) %collective-permute-start.19) | collective-permute-done | bytes 524320 | tf_op jit(solution)/shard_map/ppermute | solution.py:164
  73.9 2.4 %collective-permute-done.14.refs_5_.refs_1_ = bf16[4,256,128]{2,1,0:T(8,128)(2,1)S(1)} collective-permute-done((bf16[4,256,128]{2,1,0:T(8,128)(2,1)S(1)}, bf16[4,256,128]{2,1,0:T(8,128)(2,1)S(1)}, u32[]{:S(2)}, u32[]{:S(2)}) %collective-permute-start.14) | collective-permute-done | bytes 262176 | tf_op jit(solution)/shard_map/ppermute | solution.py:164
  76.2 1.3 %shard_map.100 = (bf16[256,512]{1,0:T(8,128)(2,1)S(1)}, bf16[8,256,256]{2,1,0:T(8,128)(2,1)S(1)}) custom-call(bf16[256,512]{1,0:T(8,128)(2,1)S(1)} %get-tuple-element.40.refs_0_, bf16[512,4096]{1,0:T(8,128)(2,1)S(1)} %copy-done.1, bf16[4,256,128]{2,1,0:T(8,128)(2,1)S(1)} %pad_maximum_fusion.refs_2_.refs_1_, ...), custom_call_target="tpu_custom_call" | custom-call | tf_op jit(solution)/shard_map/pallas_call | solution.py:529
  77.5 0.6 collective-permute-done.20.refs_7_
  78.1 0.8 shard_map.107
  79.0 0.2 collective-permute-start.21
  79.2 1.4 %collective-permute-done.21 = bf16[256,512]{1,0:T(8,128)(2,1)S(1)} collective-permute-done((bf16[256,512]{1,0:T(8,128)(2,1)S(1)}, bf16[256,512]{1,0:T(8,128)(2,1)S(1)}, u32[]{:S(2)}, u32[]{:S(2)}) %collective-permute-start.21) | collective-permute-done | bytes 262176 | tf_op jit(solution)/shard_map/ppermute | solution.py:164
  80.7 1.6 %collective-permute-start.24 = (bf16[2,64,512]{2,1,0:T(8,128)(2,1)S(1)}, bf16[2,64,512]{2,1,0:T(8,128)(2,1)S(1)}, u32[]{:S(2)}, u32[]{:S(2)}) collective-permute-start(bf16[2,64,512]{2,1,0:T(8,128)(2,1)S(1)} %get-tuple-element.47), channel_id=1, source_target_pairs={{0,6},{2,4},{4,2},{6,0},{8,14},{10,12},{12,10},{14,8},{1,7},{3,5},... | collective-permute-start | bytes 393224 | tf_op jit(solution)/shard_map/ppermute | solution.py:164
  82.2 0.5 collective-permute-start.22
  82.8 1.5 %collective-permute-start.23 = (bf16[2,64,512]{2,1,0:T(8,128)(2,1)S(1)}, bf16[2,64,512]{2,1,0:T(8,128)(2,1)S(1)}, u32[]{:S(2)}, u32[]{:S(2)}) collective-permute-start(bf16[2,64,512]{2,1,0:T(8,128)(2,1)S(1)} %get-tuple-element.50), channel_id=1, source_target_pairs={{0,4},{2,6},{4,0},{6,2},{8,12},{10,14},{12,8},{14,10},{1,5},{3,7},... | collective-permute-start | bytes 393224 | tf_op jit(solution)/shard_map/ppermute | solution.py:164
  84.2 3.8 %collective-permute-done.24.refs_3_ = bf16[2,64,512]{2,1,0:T(8,128)(2,1)S(1)} collective-permute-done((bf16[2,64,512]{2,1,0:T(8,128)(2,1)S(1)}, bf16[2,64,512]{2,1,0:T(8,128)(2,1)S(1)}, u32[]{:S(2)}, u32[]{:S(2)}) %collective-permute-start.24) | collective-permute-done | bytes 131104 | tf_op jit(solution)/shard_map/ppermute | solution.py:164
  88.0 2.0 %collective-permute-done.22.refs_1_ = bf16[2,64,512]{2,1,0:T(8,128)(2,1)S(1)} collective-permute-done((bf16[2,64,512]{2,1,0:T(8,128)(2,1)S(1)}, bf16[2,64,512]{2,1,0:T(8,128)(2,1)S(1)}, u32[]{:S(2)}, u32[]{:S(2)}) %collective-permute-start.22) | collective-permute-done | bytes 131104 | tf_op jit(solution)/shard_map/ppermute | solution.py:164
  90.0 0.8 shard_map.108
  (50 shorter events, 0.4 us)
Async XLA Ops:
  0.0 7.4 %copy-start.2 = (bf16[1024,512]{1,0:T(8,128)(2,1)S(1)}, bf16[1024,512]{1,0:T(8,128)(2,1)}, u32[]{:S(2)}) copy-start(bf16[1024,512]{1,0:T(8,128)(2,1)} %refs_6_.1) | copy-start | bytes 3145732
  0.0 15.1 %copy-start.7 = (f32[4096]{0:T(1024)S(1)}, f32[4096]{0:T(1024)}, u32[]{:S(2)}) copy-start(f32[4096]{0:T(1024)} %param.11) | copy-start | bytes 49156
  2.7 12.5 %collective-permute-start = (bf16[1552,128]{1,0:T(8,128)(2,1)}, bf16[1552,128]{1,0:T(8,128)(2,1)S(1)}, u32[]{:S(2)}, u32[]{:S(2)}) collective-permute-start(bf16[1552,128]{1,0:T(8,128)(2,1)} %get-tuple-element.26.query_ref.packed_ref), channel_id=1, source_target_pairs={{0,2},{2,0},{4,6},{6,4},{8,10},{10,8},{12,14},{14,12},{1,3},{3,1},... | collective-permute-start | bytes 1191944 | tf_op jit(solution)/shard_map/ppermute | solution.py:164
  5.7 15.2 %collective-permute-start.1 = (bf16[1552,128]{1,0:T(8,128)(2,1)}, bf16[1552,128]{1,0:T(8,128)(2,1)S(1)}, u32[]{:S(2)}, u32[]{:S(2)}) collective-permute-start(bf16[1552,128]{1,0:T(8,128)(2,1)} %get-tuple-element.28), channel_id=1, source_target_pairs={{0,4},{2,6},{4,0},{6,2},{8,12},{10,14},{12,8},{14,10},{1,5},{3,7},... | collective-permute-start | bytes 1191944 | tf_op jit(solution)/shard_map/ppermute | solution.py:164
  7.3 17.6 %collective-permute-start.2 = (bf16[1552,128]{1,0:T(8,128)(2,1)}, bf16[1552,128]{1,0:T(8,128)(2,1)S(1)}, u32[]{:S(2)}, u32[]{:S(2)}) collective-permute-start(bf16[1552,128]{1,0:T(8,128)(2,1)} %get-tuple-element.29), channel_id=1, source_target_pairs={{0,6},{2,4},{4,2},{6,0},{8,14},{10,12},{12,10},{14,8},{1,7},{3,5},... | collective-permute-start | bytes 1191944 | tf_op jit(solution)/shard_map/ppermute | solution.py:164
  7.4 1.0 %copy-start.4 = (bf16[1552,128]{1,0:T(8,128)(2,1)S(1)}, bf16[1552,128]{1,0:T(8,128)(2,1)}, u32[]{:S(2)}) copy-start(bf16[1552,128]{1,0:T(8,128)(2,1)} %get-tuple-element.26.query_ref.packed_ref) | copy-start | bytes 1191940
  8.9 11.9 %collective-permute-start.3 = (bf16[256,512]{1,0:T(8,128)(2,1)S(1)}, bf16[256,512]{1,0:T(8,128)(2,1)S(1)}, u32[]{:S(2)}, u32[]{:S(2)}) collective-permute-start(bf16[256,512]{1,0:T(8,128)(2,1)S(1)} %get-tuple-element.30.refs_0_), channel_id=1, source_target_pairs={{4,8},{6,10},{8,4},{10,6},{5,9},{7,11},{9,5},{11,7},{20,24},{22,26... | collective-permute-start | bytes 786440 | tf_op jit(solution)/shard_map/ppermute | solution.py:638
  9.6 11.3 %collective-permute-start.4 = (bf16[256,512]{1,0:T(8,128)(2,1)S(1)}, bf16[256,512]{1,0:T(8,128)(2,1)S(1)}, u32[]{:S(2)}, u32[]{:S(2)}) collective-permute-start(bf16[256,512]{1,0:T(8,128)(2,1)S(1)} %get-tuple-element.31.refs_0_), channel_id=1, source_target_pairs={{4,8},{6,10},{8,4},{10,6},{5,9},{7,11},{9,5},{11,7},{20,24},{22,26... | collective-permute-start | bytes 786440 | tf_op jit(solution)/shard_map/ppermute | solution.py:638
  15.1 2.2 %copy-start = (bf16[512,4096]{1,0:T(8,128)(2,1)S(1)}, bf16[512,4096]{1,0:T(8,128)(2,1)}, u32[]{:S(2)}) copy-start(bf16[512,4096]{1,0:T(8,128)(2,1)} %refs_1_.3) | copy-start | bytes 12582916
  17.3 1.0 %copy-start.5 = (bf16[1552,128]{1,0:T(8,128)(2,1)S(1)}, bf16[1552,128]{1,0:T(8,128)(2,1)}, u32[]{:S(2)}) copy-start(bf16[1552,128]{1,0:T(8,128)(2,1)} %get-tuple-element.26.query_ref.packed_ref) | copy-start | bytes 1191940
  18.3 6.6 %copy-start.3 = (bf16[1552,128]{1,0:T(8,128)(2,1)S(1)}, bf16[1552,128]{1,0:T(8,128)(2,1)}, u32[]{:S(2)}) copy-start(bf16[1552,128]{1,0:T(8,128)(2,1)} %get-tuple-element.27.refs_1_) | copy-start | bytes 1191940
  20.9 7.7 %copy-start.6 = (f32[64,16]{0,1:T(8,128)S(1)}, f32[64,16]{0,1:T(8,128)}, u32[]{:S(2)}) copy-start(f32[64,16]{0,1:T(8,128)} %param.14) | copy-start | bytes 12292
  20.9 7.7 %copy-start.10 = (f32[64,16]{0,1:T(8,128)S(1)}, f32[64,16]{0,1:T(8,128)}, u32[]{:S(2)}) copy-start(f32[64,16]{0,1:T(8,128)} %param.15) | copy-start | bytes 12292
  24.9 4.8 %copy-start.8 = (f32[3,64,3]{1,2,0:T(4,128)S(1)}, f32[3,64,3]{1,2,0:T(4,128)}, u32[]{:S(2)}) copy-start(f32[3,64,3]{1,2,0:T(4,128)} %param.13) | copy-start | bytes 6916
  24.9 4.8 %copy-start.9 = (f32[1024]{0:T(1024)S(1)}, f32[1024]{0:T(1024)}, u32[]{:S(2)}) copy-start(f32[1024]{0:T(1024)} %param.16) | copy-start | bytes 12292
  25.8 10.4 %collective-permute-start.5 = (bf16[528,128]{1,0:T(8,128)(2,1)S(1)}, bf16[528,128]{1,0:T(8,128)(2,1)S(1)}, u32[]{:S(2)}, u32[]{:S(2)}) collective-permute-start(bf16[528,128]{1,0:T(8,128)(2,1)S(1)} %get-tuple-element.32.refs_4_.refs_0_), channel_id=1, source_target_pairs={{0,8},{2,10},{4,12},{6,14},{8,0},{10,2},{12,4},{14,6},{1,9},{3,11}... | collective-permute-start | bytes 405512 | tf_op jit(solution)/shard_map/ppermute | solution.py:164
  29.5 15.8 %collective-permute-start.7 = (bf16[256,128]{1,0:T(8,128)(2,1)S(1)}, bf16[256,128]{1,0:T(8,128)(2,1)S(1)}, u32[]{:S(2)}, u32[]{:S(2)}) collective-permute-start(bf16[256,128]{1,0:T(8,128)(2,1)S(1)} %get-tuple-element.38), channel_id=1, source_target_pairs={{0,8},{2,10},{4,12},{6,14},{8,0},{10,2},{12,4},{14,6},{1,9},{3,11}... | collective-permute-start | bytes 196616 | tf_op jit(solution)/shard_map/ppermute | solution.py:164
  36.3 9.8 %collective-permute-start.6 = (bf16[2,256,128]{2,1,0:T(8,128)(2,1)S(1)}, bf16[2,256,128]{2,1,0:T(8,128)(2,1)S(1)}, u32[]{:S(2)}, u32[]{:S(2)}) collective-permute-start(bf16[2,256,128]{2,1,0:T(8,128)(2,1)S(1)} %shard_map.96.refs_2_.refs_1_), channel_id=1, source_target_pairs={{0,16},{16,0},{1,17},{17,1},{2,18},{18,2},{3,19},{19,3},{4,20},{20... | collective-permute-start | bytes 393224 | tf_op jit(solution)/shard_map/ppermute | solution.py:164
  37.7 22.0 %collective-permute-start.16 = (bf16[256,512]{1,0:T(8,128)(2,1)S(1)}, bf16[256,512]{1,0:T(8,128)(2,1)S(1)}, u32[]{:S(2)}, u32[]{:S(2)}) collective-permute-start(bf16[256,512]{1,0:T(8,128)(2,1)S(1)} %shard_map.101), channel_id=1, source_target_pairs={{0,12},{2,14},{12,0},{14,2},{1,13},{3,15},{13,1},{15,3},{16,28},{1... | collective-permute-start | bytes 786440 | tf_op jit(solution)/shard_map/ppermute | solution.py:713
  42.5 17.1 %collective-permute-start.17 = (bf16[256,512]{1,0:T(8,128)(2,1)S(1)}, bf16[256,512]{1,0:T(8,128)(2,1)S(1)}, u32[]{:S(2)}, u32[]{:S(2)}) collective-permute-start(bf16[256,512]{1,0:T(8,128)(2,1)S(1)} %shard_map.102), channel_id=1, source_target_pairs={{0,12},{2,14},{12,0},{14,2},{1,13},{3,15},{13,1},{15,3},{16,28},{1... | collective-permute-start | bytes 786440 | tf_op jit(solution)/shard_map/ppermute | solution.py:713
  45.3 4.3 %collective-permute-start.8 = (bf16[1,256,128]{2,1,0:T(8,128)(2,1)S(1)}, bf16[1,256,128]{2,1,0:T(8,128)(2,1)S(1)}, u32[]{:S(2)}, u32[]{:S(2)}) collective-permute-start(bf16[1,256,128]{2,1,0:T(8,128)(2,1)S(1)} %fusion.4.refs_1_), channel_id=1, source_target_pairs={{0,16},{16,0},{1,17},{17,1},{2,18},{18,2},{3,19},{19,3},{4,20},{20... | collective-permute-start | bytes 196616 | tf_op jit(solution)/shard_map/ppermute | solution.py:164
  50.2 2.8 %collective-permute-start.9 = (bf16[256,128]{1,0:T(8,128)(2,1)S(1)}, bf16[256,128]{1,0:T(8,128)(2,1)S(1)}, u32[]{:S(2)}, u32[]{:S(2)}) collective-permute-start(bf16[256,128]{1,0:T(8,128)(2,1)S(1)} %get-tuple-element.42), channel_id=1, source_target_pairs={{0,1},{1,0},{2,3},{3,2},{4,5},{5,4},{6,7},{7,6},{8,9},{9,8},{10,11... | collective-permute-start | bytes 196616 | tf_op jit(solution)/shard_map/ppermute | solution.py:164
  50.3 8.6 %collective-permute-start.10 = (bf16[256,128]{1,0:T(8,128)(2,1)S(1)}, bf16[256,128]{1,0:T(8,128)(2,1)S(1)}, u32[]{:S(2)}, u32[]{:S(2)}) collective-permute-start(bf16[256,128]{1,0:T(8,128)(2,1)S(1)} %get-tuple-element.43), channel_id=1, source_target_pairs={{0,8},{2,10},{4,12},{6,14},{8,0},{10,2},{12,4},{14,6},{1,9},{3,11}... | collective-permute-start | bytes 196616 | tf_op jit(solution)/shard_map/ppermute | solution.py:164
  50.4 9.2 %collective-permute-start.11 = (bf16[256,128]{1,0:T(8,128)(2,1)S(1)}, bf16[256,128]{1,0:T(8,128)(2,1)S(1)}, u32[]{:S(2)}, u32[]{:S(2)}) collective-permute-start(bf16[256,128]{1,0:T(8,128)(2,1)S(1)} %get-tuple-element.44), channel_id=1, source_target_pairs={{0,9},{1,8},{2,11},{3,10},{4,13},{5,12},{6,15},{7,14},{8,1},{9,0},... | collective-permute-start | bytes 196616 | tf_op jit(solution)/shard_map/ppermute | solution.py:172
  59.6 16.6 %copy-start.1 = (bf16[512,4096]{1,0:T(8,128)(2,1)S(1)}, bf16[512,4096]{1,0:T(8,128)(2,1)}, u32[]{:S(2)}) copy-start(bf16[512,4096]{1,0:T(8,128)(2,1)} %refs_1_.3) | copy-start | bytes 12582916
  59.8 14.1 %collective-permute-start.19 = (bf16[512,512]{1,0:T(8,128)(2,1)S(1)}, bf16[512,512]{1,0:T(8,128)(2,1)S(1)}, u32[]{:S(2)}, u32[]{:S(2)}) collective-permute-start(bf16[512,512]{1,0:T(8,128)(2,1)S(1)} %shard_map.103.refs_4_), channel_id=1, source_target_pairs={{0,16},{16,0},{1,17},{17,1},{2,18},{18,2},{3,19},{19,3},{4,20},{20... | collective-permute-start | bytes 1572872 | tf_op jit(solution)/shard_map/ppermute | solution.py:164
  60.7 15.5 %collective-permute-start.15 = (bf16[1024,512]{1,0:T(8,128)(2,1)S(1)}, bf16[1024,512]{1,0:T(8,128)(2,1)S(1)}, u32[]{:S(2)}, u32[]{:S(2)}) collective-permute-start(bf16[1024,512]{1,0:T(8,128)(2,1)S(1)} %copy-done.2), channel_id=1, source_target_pairs={{0,1},{1,0},{2,3},{3,2},{4,5},{5,4},{6,7},{7,6},{8,9},{9,8},{10,11... | collective-permute-start | bytes 3145736 | tf_op jit(solution)/shard_map/ppermute | solution.py:164
  60.7 8.7 %collective-permute-start.12 = (bf16[4,256,128]{2,1,0:T(8,128)(2,1)S(1)}, bf16[4,256,128]{2,1,0:T(8,128)(2,1)S(1)}, u32[]{:S(2)}, u32[]{:S(2)}) collective-permute-start(bf16[4,256,128]{2,1,0:T(8,128)(2,1)S(1)} %pad_maximum_fusion.refs_2_.refs_1_), channel_id=1, source_target_pairs={{0,2},{2,0},{4,6},{6,4},{8,10},{10,8},{12,14},{14,12},{1,3},{3,1},... | collective-permute-start | bytes 786440 | tf_op jit(solution)/shard_map/ppermute | solution.py:164
  61.9 11.9 %collective-permute-start.13 = (bf16[4,256,128]{2,1,0:T(8,128)(2,1)S(1)}, bf16[4,256,128]{2,1,0:T(8,128)(2,1)S(1)}, u32[]{:S(2)}, u32[]{:S(2)}) collective-permute-start(bf16[4,256,128]{2,1,0:T(8,128)(2,1)S(1)} %pad_maximum_fusion.refs_2_.refs_1_), channel_id=1, source_target_pairs={{0,4},{2,6},{4,0},{6,2},{8,12},{10,14},{12,8},{14,10},{1,5},{3,7},... | collective-permute-start | bytes 786440 | tf_op jit(solution)/shard_map/ppermute | solution.py:164
  62.8 13.4 %collective-permute-start.14 = (bf16[4,256,128]{2,1,0:T(8,128)(2,1)S(1)}, bf16[4,256,128]{2,1,0:T(8,128)(2,1)S(1)}, u32[]{:S(2)}, u32[]{:S(2)}) collective-permute-start(bf16[4,256,128]{2,1,0:T(8,128)(2,1)S(1)} %pad_maximum_fusion.refs_2_.refs_1_), channel_id=1, source_target_pairs={{0,6},{2,4},{4,2},{6,0},{8,14},{10,12},{12,10},{14,8},{1,7},{3,5},... | collective-permute-start | bytes 786440 | tf_op jit(solution)/shard_map/ppermute | solution.py:164
  69.4 8.1 %collective-permute-start.18 = (bf16[512,512]{1,0:T(8,128)(2,1)S(1)}, bf16[512,512]{1,0:T(8,128)(2,1)S(1)}, u32[]{:S(2)}, u32[]{:S(2)}) collective-permute-start(bf16[512,512]{1,0:T(8,128)(2,1)S(1)} %shard_map.103.refs_4_), channel_id=1, source_target_pairs={{0,1},{1,0},{2,3},{3,2},{4,5},{5,4},{6,7},{7,6},{8,9},{9,8},{10,11... | collective-permute-start | bytes 1572872 | tf_op jit(solution)/shard_map/ppermute | solution.py:164
  76.2 1.9 %collective-permute-start.20 = (bf16[512,512]{1,0:T(8,128)(2,1)S(1)}, bf16[512,512]{1,0:T(8,128)(2,1)S(1)}, u32[]{:S(2)}, u32[]{:S(2)}) collective-permute-start(bf16[512,512]{1,0:T(8,128)(2,1)S(1)} %shard_map.106.refs_6_), channel_id=1, source_target_pairs={{0,1},{1,0},{2,3},{3,2},{4,5},{5,4},{6,7},{7,6},{8,9},{9,8},{10,11... | collective-permute-start | bytes 1572872 | tf_op jit(solution)/shard_map/ppermute | solution.py:164
  79.0 1.6 %collective-permute-start.21 = (bf16[256,512]{1,0:T(8,128)(2,1)S(1)}, bf16[256,512]{1,0:T(8,128)(2,1)S(1)}, u32[]{:S(2)}, u32[]{:S(2)}) collective-permute-start(bf16[256,512]{1,0:T(8,128)(2,1)S(1)} %get-tuple-element.51), channel_id=1, source_target_pairs={{0,1},{1,0},{2,3},{3,2},{4,5},{5,4},{6,7},{7,6},{8,9},{9,8},{10,11... | collective-permute-start | bytes 786440 | tf_op jit(solution)/shard_map/ppermute | solution.py:164
  80.7 7.3 %collective-permute-start.24 = (bf16[2,64,512]{2,1,0:T(8,128)(2,1)S(1)}, bf16[2,64,512]{2,1,0:T(8,128)(2,1)S(1)}, u32[]{:S(2)}, u32[]{:S(2)}) collective-permute-start(bf16[2,64,512]{2,1,0:T(8,128)(2,1)S(1)} %get-tuple-element.47), channel_id=1, source_target_pairs={{0,6},{2,4},{4,2},{6,0},{8,14},{10,12},{12,10},{14,8},{1,7},{3,5},... | collective-permute-start | bytes 393224 | tf_op jit(solution)/shard_map/ppermute | solution.py:164
  82.2 7.7 %collective-permute-start.22 = (bf16[2,64,512]{2,1,0:T(8,128)(2,1)S(1)}, bf16[2,64,512]{2,1,0:T(8,128)(2,1)S(1)}, u32[]{:S(2)}, u32[]{:S(2)}) collective-permute-start(bf16[2,64,512]{2,1,0:T(8,128)(2,1)S(1)} %get-tuple-element.49), channel_id=1, source_target_pairs={{0,2},{2,0},{4,6},{6,4},{8,10},{10,8},{12,14},{14,12},{1,3},{3,1},... | collective-permute-start | bytes 393224 | tf_op jit(solution)/shard_map/ppermute | solution.py:164
  82.8 7.2 %collective-permute-start.23 = (bf16[2,64,512]{2,1,0:T(8,128)(2,1)S(1)}, bf16[2,64,512]{2,1,0:T(8,128)(2,1)S(1)}, u32[]{:S(2)}, u32[]{:S(2)}) collective-permute-start(bf16[2,64,512]{2,1,0:T(8,128)(2,1)S(1)} %get-tuple-element.50), channel_id=1, source_target_pairs={{0,4},{2,6},{4,0},{6,2},{8,12},{10,14},{12,8},{14,10},{1,5},{3,7},... | collective-permute-start | bytes 393224 | tf_op jit(solution)/shard_map/ppermute | solution.py:164

commit v6 on v5

--- a/solution.py
+++ b/solution.py
@@ -479,7 +479,7 @@
 
 
 def far_kernel(picked_ref, table_ref, near_ref, joined_ref, *refs):
-    far_refs, out_ref = (refs[:2], refs[2:4]), refs[4]
+    far_refs, (kept_ref, sent_ref) = (refs[:2], refs[2:4]), refs[4:]
     quad, half, group, core = here()
     block = 2 * LANES
     width = near_ref.shape[1]
@@ -494,26 +494,19 @@
                 preferred_element_type=f32,
             )
     total += residual(picked_ref, table_ref, (4 * (half ^ 1) + (quad ^ 2)) * width, width)
-    out_ref[half ^ core] = near_ref[...]
-    out_ref[half ^ 1 ^ core] = total.astype(bf16)
+    near, far = near_ref[...], total.astype(bf16)
+    kept_ref[...] = jnp.where(half == core, near, far)
+    sent_ref[...] = jnp.where(half == core, far, near)
 
 
 def place_kernel(*refs):
-    piece_refs, (out_ref, sems) = refs[:4], refs[4:]
+    part_refs, out_ref = refs[:8], refs[8]
     quad, half, _, core = here()
-    width = piece_refs[0].shape[2]
-    copies = []
-    for m, piece_ref in enumerate(piece_refs):
-        first = pl.multiple_of((quad ^ m ^ (2 * (half ^ core))) * width, width)
-        for g in (0, 1):
-            copies.append(
-                pltpu.make_async_copy(
-                    piece_ref.at[g], out_ref.at[core ^ g, :, pl.ds(first, width)], sems.at[m, g]
-                )
-            )
-            copies[-1].start()
-    for copy in copies:
-        copy.wait()
+    width = part_refs[0].shape[1]
+    for g in (0, 1):
+        for m in range(4):
+            first = pl.multiple_of((quad ^ m ^ (2 * (half ^ core))) * width, width)
+            out_ref[core ^ g, :, pl.ds(first, width)] = part_refs[4 * g + m][...]
 
 
 def called(kernel, out_shape, scalars, *operands, scratch=(), mib=16, earlier=()):
@@ -633,7 +626,7 @@
             out_specs=pl.BlockSpec((step, part), lambda i, place: (i, 0)),
         ),
         compiler_params=pltpu.CompilerParams(vmem_limit_bytes=16 * MIB),
-    )(place, embed_table, norm_gain.reshape(1, features), embed_table, gathered[1], packed[1])
+    )(place, embed_table, norm_gain.reshape(1, features), embed_table, gathered[2], packed[1])
 
     inner_fetched = [lax.ppermute(rows_part, "ctx", inner) for rows_part in offered]
     def partials(begin, count, spare, earlier=()):
@@ -733,7 +726,7 @@
     )
     results = called(
         far_kernel,
-        shaped(2, span, width, dtype=bf16),
+        [shaped(span, width, dtype=bf16)] * 2,
         (),
         picked,
         embed_table,
@@ -745,20 +738,25 @@
         swapped(shared, "chan", 1),
         mib=24,
     )
-    both = jnp.stack([results[0], swapped(results[1], "chan", 1)])
-
-    def rows_of(member):
-        return lax.dynamic_slice_in_dim(both, member * rows, rows, 1)
-
-    arrived = [rows_of(quad)] + [swapped(rows_of(quad ^ m), "ctx", m) for m in range(1, members)]
-    return pl.pallas_call(
+    kept, sent = results
+    received = swapped(sent, "chan", 1)
+
+    def rows_of(array, member):
+        return lax.dynamic_slice_in_dim(array, member * rows, rows, 0)
+
+    kept_parts = [rows_of(kept, quad)] + [
+        swapped(rows_of(kept, quad ^ m), "ctx", m) for m in range(1, members)
+    ]
+    received_parts = [rows_of(received, quad)] + [
+        swapped(rows_of(received, quad ^ m), "ctx", m) for m in range(1, members)
+    ]
+    return called(
         place_kernel,
-        out_shape=shaped(genomes, rows, members * width, dtype=bf16),
-        in_specs=[pl.BlockSpec(memory_space=pltpu.VMEM)] * members,
-        out_specs=anywhere,
-        scratch_shapes=[pltpu.SemaphoreType.DMA((members, 2))],
-        compiler_params=pltpu.CompilerParams(vmem_limit_bytes=4 * MIB),
-    )(*arrived)
+        shaped(genomes, rows, members * width, dtype=bf16),
+        (),
+        *kept_parts,
+        *received_parts,
+    )
 
 
 def solution(mesh):

time: 91.1 us -> 89.4 us (0.981)
  waiting for transfers between devices: 40.8 us -> 34.7 us
  starting transfers between devices: 29.8 us -> 34.2 us
    ppermute x20 -> x23, waiting for transfers between devices: 40.1 us -> 34.2 us  [swapped(): return lax.ppermute(value, axis, [(i, i ^ mask) for i in range(count)])]
    ppermute x20 -> x23, starting transfers between devices: 18.1 us -> 22.5 us  [swapped(): return lax.ppermute(value, axis, [(i, i ^ mask) for i in range(count)])]
    pallas_call x7 -> x8, Pallas kernels: 8.67 us -> 9.51 us  [called(): pl.pallas_call(body, out_shape=out_shape, in_specs=[smem] * len(scalars)...]
  transfers between devices with their start and end apart: 25 -> 28, of which waited for: 13 -> 14; matrix products, arithmetic and copies ran while one was open for 0% -> 0% of each run, Pallas kernels for 11% -> 11%
where the time goes in v6:
time: 89.4 us; the launch traced here: 89.1 us
  waiting for transfers between devices  34.7 us (39%)
  starting transfers between devices  34.2 us (38%)
  Pallas kernels  15.3 us (17%)
  local copies, waits for them, and re-layouts  4.26 us (5%)
    ppermute x23, waiting for transfers between devices, swapped(): return lax.ppermute(value, axis, [(i, i ^ mask) for i in range(count)])  34.2 us
    ppermute x23, starting transfers between devices, swapped(): return lax.ppermute(value, axis, [(i, i ^ mask) for i in range(count)])  22.5 us
    pallas_call x8, Pallas kernels, called(): pl.pallas_call(body, out_shape=out_shape, in_specs=[smem] * len(scalars)...  9.51 us
    ppermute x2, starting transfers between devices, quad_body(): lax.ppermute(after(rows_part, pair_own), 'ctx', outer)  7.65 us
    unnamed x22, local copies, waits for them, and re-layouts  4.22 us
    ppermute x1, starting transfers between devices, swapped_both(): return lax.ppermute(value, ('ctx', 'chan'), pairs)  2.68 us
    pallas_call x1, Pallas kernels, quad_body(): pl.pallas_call(pack_kernel, out_shape=[shaped(branches * depth + SPARE, L...  2.64 us
    pallas_call x1, Pallas kernels, quad_body(): pl.pallas_call(norm_kernel, out_shape=shaped(vocab, part, dtype=bf16), gr...  2.56 us
  transfers between devices with their start and end apart: 28, of which 14 were waited for; matrix products, arithmetic and copies ran while one was open for 0% of the time, Pallas kernels for 11%

profile of v6, /device:TPU:0, one launch (start us, length us, event | category | flops | bytes accessed | tf_op | source)
XLA Modules:
  0.0 89.1 jit_solution(4703502372281908480)
XLA Ops:
  0.0 2.6 %shard_map.91 = (bf16[1552,128]{1,0:T(8,128)(2,1)}, bf16[1552,128]{1,0:T(8,128)(2,1)}, bf16[1552,128]{1,0:T(8,128)(2,1)}, bf16[1552,128]{1,0:T(8,128)(2,1)}) custom-call(s32[2,64]{1,0:T(2,128)} %tokens_ref.1, bf16[3,512,1024]{2,1,0:T(8,128)(2,1)} %bitcast.24), custom_call_target="tpu_custom_call" | custom-call | tf_op jit(solution)/shard_map/pallas_call | solution.py:573
  2.7 3.1 %collective-permute-start = (bf16[1552,128]{1,0:T(8,128)(2,1)}, bf16[1552,128]{1,0:T(8,128)(2,1)S(1)}, u32[]{:S(2)}, u32[]{:S(2)}) collective-permute-start(bf16[1552,128]{1,0:T(8,128)(2,1)} %get-tuple-element.28), channel_id=1, source_target_pairs={{0,4},{2,6},{4,0},{6,2},{8,12},{10,14},{12,8},{14,10},{1,5},{3,7},... | collective-permute-start | bytes 1191944 | tf_op jit(solution)/shard_map/ppermute | solution.py:164
  5.8 1.4 %collective-permute-start.2 = (bf16[1552,128]{1,0:T(8,128)(2,1)}, bf16[1552,128]{1,0:T(8,128)(2,1)S(1)}, u32[]{:S(2)}, u32[]{:S(2)}) collective-permute-start(bf16[1552,128]{1,0:T(8,128)(2,1)} %get-tuple-element.31), channel_id=1, source_target_pairs={{0,6},{2,4},{4,2},{6,0},{8,14},{10,12},{12,10},{14,8},{1,7},{3,5},... | collective-permute-start | bytes 1191944 | tf_op jit(solution)/shard_map/ppermute | solution.py:164
  7.4 1.0 %copy-done.4 = bf16[1552,128]{1,0:T(8,128)(2,1)S(1)} copy-done((bf16[1552,128]{1,0:T(8,128)(2,1)S(1)}, bf16[1552,128]{1,0:T(8,128)(2,1)}, u32[]{:S(2)}) %copy-start.4) | copy-done | bytes 397336
  8.4 0.6 shard_map.93
  9.0 0.7 collective-permute-start.3
  9.6 0.7 collective-permute-start.4
  10.3 5.7 %collective-permute-done.pair_ref.refs_3_ = bf16[1552,128]{1,0:T(8,128)(2,1)S(1)} collective-permute-done((bf16[1552,128]{1,0:T(8,128)(2,1)}, bf16[1552,128]{1,0:T(8,128)(2,1)S(1)}, u32[]{:S(2)}, u32[]{:S(2)}) %collective-permute-start) | collective-permute-done | bytes 397344 | tf_op jit(solution)/shard_map/ppermute | solution.py:164
  16.0 2.2 %copy-done = bf16[512,4096]{1,0:T(8,128)(2,1)S(1)} copy-done((bf16[512,4096]{1,0:T(8,128)(2,1)S(1)}, bf16[512,4096]{1,0:T(8,128)(2,1)}, u32[]{:S(2)}) %copy-start) | copy-done | bytes 4194328
  18.2 1.0 %copy-done.5 = bf16[1552,128]{1,0:T(8,128)(2,1)S(1)} copy-done((bf16[1552,128]{1,0:T(8,128)(2,1)S(1)}, bf16[1552,128]{1,0:T(8,128)(2,1)}, u32[]{:S(2)}) %copy-start.5) | copy-done | bytes 397336
  19.2 2.6 %shard_map.92.refs_0_ = bf16[512,2048]{1,0:T(8,128)(2,1)S(1)} custom-call(s32[4]{0:T(128)S(1)} %pad_add_fusion.place_ref, bf16[512,4096]{1,0:T(8,128)(2,1)S(1)} %copy-done, f32[1,4096]{1,0:T(1,128)S(1)} %bitcast.21, bf16[512,4096]{1,0:T(8,128)(2,1)S(1)} %copy-done, bf16[1552,128]{1,0:T(8,128)(2,1)S(1)} %collective-permute-done.pair_ref.refs_3_, ...), custom_call_target="tpu_custom_call" | custom-call | tf_op jit(solution)/shard_map/pallas_call | solution.py:613
  21.8 3.1 %collective-permute-done.2.refs_4_ = bf16[1552,128]{1,0:T(8,128)(2,1)S(1)} collective-permute-done((bf16[1552,128]{1,0:T(8,128)(2,1)}, bf16[1552,128]{1,0:T(8,128)(2,1)S(1)}, u32[]{:S(2)}, u32[]{:S(2)}) %collective-permute-start.2) | collective-permute-done | bytes 397344 | tf_op jit(solution)/shard_map/ppermute | solution.py:164
  24.9 1.4 %collective-permute-done.1.refs_2_ = bf16[1552,128]{1,0:T(8,128)(2,1)S(1)} collective-permute-done((bf16[1552,128]{1,0:T(8,128)(2,1)}, bf16[1552,128]{1,0:T(8,128)(2,1)S(1)}, u32[]{:S(2)}, u32[]{:S(2)}) %collective-permute-start.1) | collective-permute-done | bytes 397344 | tf_op jit(solution)/shard_map/ppermute | solution.py:164
  26.3 0.9 %shard_map.94 = (f32[512,128]{1,0:T(8,128)S(1)}, bf16[528,128]{1,0:T(8,128)(2,1)S(1)}) custom-call(bf16[512,2048]{1,0:T(8,128)(2,1)S(1)} %shard_map.92.refs_0_, bf16[1552,128]{1,0:T(8,128)(2,1)S(1)} %copy-done.3, bf16[1552,128]{1,0:T(8,128)(2,1)S(1)} %collective-permute-done.1.refs_2_, bf16[1552,128]{1,0:T(8,128)(2,1)S(1)} %collective-permute-done.pair_ref.refs_3_, ...), custom_call_target="tpu_custom_call" | custom-call | tf_op jit(solution)/shard_map/pallas_call | solution.py:522
  27.2 2.7 %collective-permute-start.5 = (bf16[528,128]{1,0:T(8,128)(2,1)S(1)}, bf16[528,128]{1,0:T(8,128)(2,1)S(1)}, u32[]{:S(2)}, u32[]{:S(2)}) collective-permute-start(bf16[528,128]{1,0:T(8,128)(2,1)S(1)} %get-tuple-element.34.refs_4_.refs_0_), channel_id=1, source_target_pairs={{0,8},{2,10},{4,12},{6,14},{8,0},{10,2},{12,4},{14,6},{1,9},{3,11}... | collective-permute-start | bytes 405512 | tf_op jit(solution)/shard_map/ppermute | solution.py:164
  29.9 0.8 shard_map.98
  30.7 0.4 collective-permute-start.7
  31.1 1.5 %shard_map.95 = (bf16[128,2560]{1,0:T(8,128)(2,1)S(1)}, f32[160,128]{1,0:T(8,128)S(1)}) custom-call(f32[16,64]{1,0:T(8,128)S(1)} %bitcast.20, f32[16,64]{1,0:T(8,128)S(1)} %multiply_bitcast_fusion.refs_1_, f32[3,3,64]{2,1,0:T(4,128)S(1)} %bitcast.22, f32[8,128]{1,0:T(8,128)S(1)} %bitcast.23, bf16[528,128]{1,0:T(8,128)(2,1)S(1)} %get-tuple-element.34.refs_4_.refs_0_), custom_call_target="tpu_custom_call" | custom-call | tf_op jit(solution)/shard_map/pallas_call | solution.py:522
  32.7 3.2 %collective-permute-done.5.refs_1_ = bf16[528,128]{1,0:T(8,128)(2,1)S(1)} collective-permute-done((bf16[528,128]{1,0:T(8,128)(2,1)S(1)}, bf16[528,128]{1,0:T(8,128)(2,1)S(1)}, u32[]{:S(2)}, u32[]{:S(2)}) %collective-permute-start.5) | collective-permute-done | bytes 135200 | tf_op jit(solution)/shard_map/ppermute | solution.py:164
  35.9 1.6 %collective-permute-start.6 = (bf16[2,256,128]{2,1,0:T(8,128)(2,1)S(1)}, bf16[2,256,128]{2,1,0:T(8,128)(2,1)S(1)}, u32[]{:S(2)}, u32[]{:S(2)}) collective-permute-start(bf16[2,256,128]{2,1,0:T(8,128)(2,1)S(1)} %shard_map.96.refs_2_.refs_1_), channel_id=1, source_target_pairs={{0,16},{16,0},{1,17},{17,1},{2,18},{18,2},{3,19},{19,3},{4,20},{20... | collective-permute-start | bytes 393224 | tf_op jit(solution)/shard_map/ppermute | solution.py:164
  37.5 5.7 %collective-permute-start.16 = (bf16[256,512]{1,0:T(8,128)(2,1)S(1)}, bf16[256,512]{1,0:T(8,128)(2,1)S(1)}, u32[]{:S(2)}, u32[]{:S(2)}) collective-permute-start(bf16[256,512]{1,0:T(8,128)(2,1)S(1)} %shard_map.101), channel_id=1, source_target_pairs={{0,12},{2,14},{12,0},{14,2},{1,13},{3,15},{13,1},{15,3},{16,28},{1... | collective-permute-start | bytes 786440 | tf_op jit(solution)/shard_map/ppermute | solution.py:706
  43.2 1.9 %collective-permute-start.17 = (bf16[256,512]{1,0:T(8,128)(2,1)S(1)}, bf16[256,512]{1,0:T(8,128)(2,1)S(1)}, u32[]{:S(2)}, u32[]{:S(2)}) collective-permute-start(bf16[256,512]{1,0:T(8,128)(2,1)S(1)} %shard_map.102), channel_id=1, source_target_pairs={{0,12},{2,14},{12,0},{14,2},{1,13},{3,15},{13,1},{15,3},{16,28},{1... | collective-permute-start | bytes 786440 | tf_op jit(solution)/shard_map/ppermute | solution.py:706
  45.2 0.6 collective-permute-start.8
  45.8 2.7 %shard_map.97 = (f32[1024,128]{1,0:T(8,128)S(1)}, bf16[1024,512]{1,0:T(8,128)(2,1)S(1)}) custom-call(bf16[528,128]{1,0:T(8,128)(2,1)S(1)} %get-tuple-element.34.refs_4_.refs_0_, bf16[528,128]{1,0:T(8,128)(2,1)S(1)} %collective-permute-done.5.refs_1_, bf16[2,256,128]{2,1,0:T(8,128)(2,1)S(1)} %shard_map.96.refs_2_.refs_1_, ...), custom_call_target="tpu_custom_call" | custom-call | tf_op jit(solution)/shard_map/pallas_call | solution.py:522
  48.5 1.0 %collective-permute-done.8.refs_2_ = bf16[1,256,128]{2,1,0:T(8,128)(2,1)S(1)} collective-permute-done((bf16[1,256,128]{2,1,0:T(8,128)(2,1)S(1)}, bf16[1,256,128]{2,1,0:T(8,128)(2,1)S(1)}, u32[]{:S(2)}, u32[]{:S(2)}) %collective-permute-start.8) | collective-permute-done | bytes 65568 | tf_op jit(solution)/shard_map/ppermute | solution.py:164
  49.5 0.5 shard_map.99
  50.2 2.7 %collective-permute-start.11 = (bf16[256,128]{1,0:T(8,128)(2,1)S(1)}, bf16[256,128]{1,0:T(8,128)(2,1)S(1)}, u32[]{:S(2)}, u32[]{:S(2)}) collective-permute-start(bf16[256,128]{1,0:T(8,128)(2,1)S(1)} %get-tuple-element.46), channel_id=1, source_target_pairs={{0,9},{1,8},{2,11},{3,10},{4,13},{5,12},{6,15},{7,14},{8,1},{9,0},... | collective-permute-start | bytes 196616 | tf_op jit(solution)/shard_map/ppermute | solution.py:172
  52.9 4.5 %collective-permute-done.10 = bf16[256,128]{1,0:T(8,128)(2,1)S(1)} collective-permute-done((bf16[256,128]{1,0:T(8,128)(2,1)S(1)}, bf16[256,128]{1,0:T(8,128)(2,1)S(1)}, u32[]{:S(2)}, u32[]{:S(2)}) %collective-permute-start.10) | collective-permute-done | bytes 65568 | tf_op jit(solution)/shard_map/ppermute | solution.py:164
  57.4 0.5 collective-permute-done.11
  58.1 0.6 collective-permute-start.19
  58.7 1.4 %collective-permute-start.15 = (bf16[1024,512]{1,0:T(8,128)(2,1)S(1)}, bf16[1024,512]{1,0:T(8,128)(2,1)S(1)}, u32[]{:S(2)}, u32[]{:S(2)}) collective-permute-start(bf16[1024,512]{1,0:T(8,128)(2,1)S(1)} %copy-done.2), channel_id=1, source_target_pairs={{0,1},{1,0},{2,3},{3,2},{4,5},{5,4},{6,7},{7,6},{8,9},{9,8},{10,11... | collective-permute-start | bytes 3145736 | tf_op jit(solution)/shard_map/ppermute | solution.py:164
  60.1 0.5 collective-permute-start.12
  61.0 2.7 %collective-permute-start.14 = (bf16[4,256,128]{2,1,0:T(8,128)(2,1)S(1)}, bf16[4,256,128]{2,1,0:T(8,128)(2,1)S(1)}, u32[]{:S(2)}, u32[]{:S(2)}) collective-permute-start(bf16[4,256,128]{2,1,0:T(8,128)(2,1)S(1)} %pad_maximum_fusion.refs_2_.refs_1_), channel_id=1, source_target_pairs={{0,6},{2,4},{4,2},{6,0},{8,14},{10,12},{12,10},{14,8},{1,7},{3,5},... | collective-permute-start | bytes 786440 | tf_op jit(solution)/shard_map/ppermute | solution.py:164
  63.6 4.8 %collective-permute-done.12.refs_3_.refs_1_ = bf16[4,256,128]{2,1,0:T(8,128)(2,1)S(1)} collective-permute-done((bf16[4,256,128]{2,1,0:T(8,128)(2,1)S(1)}, bf16[4,256,128]{2,1,0:T(8,128)(2,1)S(1)}, u32[]{:S(2)}, u32[]{:S(2)}) %collective-permute-start.12) | collective-permute-done | bytes 262176 | tf_op jit(solution)/shard_map/ppermute | solution.py:164
  68.4 3.9 %collective-permute-done.19.refs_0_ = bf16[512,512]{1,0:T(8,128)(2,1)S(1)} collective-permute-done((bf16[512,512]{1,0:T(8,128)(2,1)S(1)}, bf16[512,512]{1,0:T(8,128)(2,1)S(1)}, u32[]{:S(2)}, u32[]{:S(2)}) %collective-permute-start.19) | collective-permute-done | bytes 524320 | tf_op jit(solution)/shard_map/ppermute | solution.py:164
  72.3 2.8 %collective-permute-done.14.refs_5_.refs_1_ = bf16[4,256,128]{2,1,0:T(8,128)(2,1)S(1)} collective-permute-done((bf16[4,256,128]{2,1,0:T(8,128)(2,1)S(1)}, bf16[4,256,128]{2,1,0:T(8,128)(2,1)S(1)}, u32[]{:S(2)}, u32[]{:S(2)}) %collective-permute-start.14) | collective-permute-done | bytes 262176 | tf_op jit(solution)/shard_map/ppermute | solution.py:164
  75.2 1.3 %shard_map.100 = (bf16[256,512]{1,0:T(8,128)(2,1)S(1)}, bf16[8,256,256]{2,1,0:T(8,128)(2,1)S(1)}) custom-call(bf16[256,512]{1,0:T(8,128)(2,1)S(1)} %get-tuple-element.42.refs_0_, bf16[512,4096]{1,0:T(8,128)(2,1)S(1)} %copy-done.1, bf16[4,256,128]{2,1,0:T(8,128)(2,1)S(1)} %pad_maximum_fusion.refs_2_.refs_1_, ...), custom_call_target="tpu_custom_call" | custom-call | tf_op jit(solution)/shard_map/pallas_call | solution.py:522
  76.5 0.6 collective-permute-done.20.refs_7_
  77.1 0.8 shard_map.107
  78.1 0.8 collective-permute-start.23
  79.0 1.2 %collective-permute-start.22 = (bf16[64,512]{1,0:T(8,128)(2,1)S(1)}, bf16[64,512]{1,0:T(8,128)(2,1)S(1)}, u32[]{:S(2)}, u32[]{:S(2)}) collective-permute-start(bf16[64,512]{1,0:T(8,128)(2,1)S(1)} %get-tuple-element.56), channel_id=1, source_target_pairs={{0,4},{2,6},{4,0},{6,2},{8,12},{10,14},{12,8},{14,10},{1,5},{3,7},... | collective-permute-start | bytes 196616 | tf_op jit(solution)/shard_map/ppermute | solution.py:164
  80.2 1.5 %collective-permute-start.21 = (bf16[64,512]{1,0:T(8,128)(2,1)S(1)}, bf16[64,512]{1,0:T(8,128)(2,1)S(1)}, u32[]{:S(2)}, u32[]{:S(2)}) collective-permute-start(bf16[64,512]{1,0:T(8,128)(2,1)S(1)} %get-tuple-element.57), channel_id=1, source_target_pairs={{0,2},{2,0},{4,6},{6,4},{8,10},{10,8},{12,14},{14,12},{1,3},{3,1},... | collective-permute-start | bytes 196616 | tf_op jit(solution)/shard_map/ppermute | solution.py:164
  81.7 0.8 collective-permute-start.27
  82.6 1.2 %collective-permute-start.26 = (bf16[64,512]{1,0:T(8,128)(2,1)S(1)}, bf16[64,512]{1,0:T(8,128)(2,1)S(1)}, u32[]{:S(2)}, u32[]{:S(2)}) collective-permute-start(bf16[64,512]{1,0:T(8,128)(2,1)S(1)} %get-tuple-element.52), channel_id=1, source_target_pairs={{0,4},{2,6},{4,0},{6,2},{8,12},{10,14},{12,8},{14,10},{1,5},{3,7},... | collective-permute-start | bytes 196616 | tf_op jit(solution)/shard_map/ppermute | solution.py:164
  84.0 1.3 %collective-permute-start.25 = (bf16[64,512]{1,0:T(8,128)(2,1)S(1)}, bf16[64,512]{1,0:T(8,128)(2,1)S(1)}, u32[]{:S(2)}, u32[]{:S(2)}) collective-permute-start(bf16[64,512]{1,0:T(8,128)(2,1)S(1)} %get-tuple-element.53), channel_id=1, source_target_pairs={{0,2},{2,0},{4,6},{6,4},{8,10},{10,8},{12,14},{14,12},{1,3},{3,1},... | collective-permute-start | bytes 196616 | tf_op jit(solution)/shard_map/ppermute | solution.py:164
  85.3 1.7 %collective-permute-done.27.refs_7_ = bf16[64,512]{1,0:T(8,128)(2,1)S(1)} collective-permute-done((bf16[64,512]{1,0:T(8,128)(2,1)S(1)}, bf16[64,512]{1,0:T(8,128)(2,1)S(1)}, u32[]{:S(2)}, u32[]{:S(2)}) %collective-permute-start.27) | collective-permute-done | bytes 65568 | tf_op jit(solution)/shard_map/ppermute | solution.py:164
  87.0 1.3 %collective-permute-done.25.refs_5_ = bf16[64,512]{1,0:T(8,128)(2,1)S(1)} collective-permute-done((bf16[64,512]{1,0:T(8,128)(2,1)S(1)}, bf16[64,512]{1,0:T(8,128)(2,1)S(1)}, u32[]{:S(2)}, u32[]{:S(2)}) %collective-permute-start.25) | collective-permute-done | bytes 65568 | tf_op jit(solution)/shard_map/ppermute | solution.py:164
  88.3 0.8 shard_map.108
  (56 shorter events, 1.5 us)
Async XLA Ops:
  0.0 7.4 %copy-start.2 = (bf16[1024,512]{1,0:T(8,128)(2,1)S(1)}, bf16[1024,512]{1,0:T(8,128)(2,1)}, u32[]{:S(2)}) copy-start(bf16[1024,512]{1,0:T(8,128)(2,1)} %refs_6_.1) | copy-start | bytes 3145732
  0.0 16.0 %copy-start.7 = (f32[4096]{0:T(1024)S(1)}, f32[4096]{0:T(1024)}, u32[]{:S(2)}) copy-start(f32[4096]{0:T(1024)} %param.11) | copy-start | bytes 49156
  2.7 13.3 %collective-permute-start = (bf16[1552,128]{1,0:T(8,128)(2,1)}, bf16[1552,128]{1,0:T(8,128)(2,1)S(1)}, u32[]{:S(2)}, u32[]{:S(2)}) collective-permute-start(bf16[1552,128]{1,0:T(8,128)(2,1)} %get-tuple-element.28), channel_id=1, source_target_pairs={{0,4},{2,6},{4,0},{6,2},{8,12},{10,14},{12,8},{14,10},{1,5},{3,7},... | collective-permute-start | bytes 1191944 | tf_op jit(solution)/shard_map/ppermute | solution.py:164
  5.8 19.2 %collective-permute-start.2 = (bf16[1552,128]{1,0:T(8,128)(2,1)}, bf16[1552,128]{1,0:T(8,128)(2,1)S(1)}, u32[]{:S(2)}, u32[]{:S(2)}) collective-permute-start(bf16[1552,128]{1,0:T(8,128)(2,1)} %get-tuple-element.31), channel_id=1, source_target_pairs={{0,6},{2,4},{4,2},{6,0},{8,14},{10,12},{12,10},{14,8},{1,7},{3,5},... | collective-permute-start | bytes 1191944 | tf_op jit(solution)/shard_map/ppermute | solution.py:164
  7.2 19.1 %collective-permute-start.1 = (bf16[1552,128]{1,0:T(8,128)(2,1)}, bf16[1552,128]{1,0:T(8,128)(2,1)S(1)}, u32[]{:S(2)}, u32[]{:S(2)}) collective-permute-start(bf16[1552,128]{1,0:T(8,128)(2,1)} %get-tuple-element.29.query_ref.packed_ref), channel_id=1, source_target_pairs={{0,2},{2,0},{4,6},{6,4},{8,10},{10,8},{12,14},{14,12},{1,3},{3,1},... | collective-permute-start | bytes 1191944 | tf_op jit(solution)/shard_map/ppermute | solution.py:164
  7.4 1.0 %copy-start.4 = (bf16[1552,128]{1,0:T(8,128)(2,1)S(1)}, bf16[1552,128]{1,0:T(8,128)(2,1)}, u32[]{:S(2)}) copy-start(bf16[1552,128]{1,0:T(8,128)(2,1)} %get-tuple-element.29.query_ref.packed_ref) | copy-start | bytes 1191940
  9.0 12.8 %collective-permute-start.3 = (bf16[256,512]{1,0:T(8,128)(2,1)S(1)}, bf16[256,512]{1,0:T(8,128)(2,1)S(1)}, u32[]{:S(2)}, u32[]{:S(2)}) collective-permute-start(bf16[256,512]{1,0:T(8,128)(2,1)S(1)} %get-tuple-element.32.refs_0_), channel_id=1, source_target_pairs={{4,8},{6,10},{8,4},{10,6},{5,9},{7,11},{9,5},{11,7},{20,24},{22,26... | collective-permute-start | bytes 786440 | tf_op jit(solution)/shard_map/ppermute | solution.py:631
  9.6 12.1 %collective-permute-start.4 = (bf16[256,512]{1,0:T(8,128)(2,1)S(1)}, bf16[256,512]{1,0:T(8,128)(2,1)S(1)}, u32[]{:S(2)}, u32[]{:S(2)}) collective-permute-start(bf16[256,512]{1,0:T(8,128)(2,1)S(1)} %get-tuple-element.33.refs_0_), channel_id=1, source_target_pairs={{4,8},{6,10},{8,4},{10,6},{5,9},{7,11},{9,5},{11,7},{20,24},{22,26... | collective-permute-start | bytes 786440 | tf_op jit(solution)/shard_map/ppermute | solution.py:631
  16.0 2.2 %copy-start = (bf16[512,4096]{1,0:T(8,128)(2,1)S(1)}, bf16[512,4096]{1,0:T(8,128)(2,1)}, u32[]{:S(2)}) copy-start(bf16[512,4096]{1,0:T(8,128)(2,1)} %refs_1_.3) | copy-start | bytes 12582916
  18.2 1.0 %copy-start.5 = (bf16[1552,128]{1,0:T(8,128)(2,1)S(1)}, bf16[1552,128]{1,0:T(8,128)(2,1)}, u32[]{:S(2)}) copy-start(bf16[1552,128]{1,0:T(8,128)(2,1)} %get-tuple-element.29.query_ref.packed_ref) | copy-start | bytes 1191940
  19.2 7.1 %copy-start.3 = (bf16[1552,128]{1,0:T(8,128)(2,1)S(1)}, bf16[1552,128]{1,0:T(8,128)(2,1)}, u32[]{:S(2)}) copy-start(bf16[1552,128]{1,0:T(8,128)(2,1)} %get-tuple-element.30.refs_1_) | copy-start | bytes 1191940
  21.7 8.1 %copy-start.6 = (f32[64,16]{0,1:T(8,128)S(1)}, f32[64,16]{0,1:T(8,128)}, u32[]{:S(2)}) copy-start(f32[64,16]{0,1:T(8,128)} %param.14) | copy-start | bytes 12292
  21.8 8.1 %copy-start.10 = (f32[64,16]{0,1:T(8,128)S(1)}, f32[64,16]{0,1:T(8,128)}, u32[]{:S(2)}) copy-start(f32[64,16]{0,1:T(8,128)} %param.15) | copy-start | bytes 12292
  26.3 4.8 %copy-start.8 = (f32[3,64,3]{1,2,0:T(4,128)S(1)}, f32[3,64,3]{1,2,0:T(4,128)}, u32[]{:S(2)}) copy-start(f32[3,64,3]{1,2,0:T(4,128)} %param.13) | copy-start | bytes 6916
  26.3 4.8 %copy-start.9 = (f32[1024]{0:T(1024)S(1)}, f32[1024]{0:T(1024)}, u32[]{:S(2)}) copy-start(f32[1024]{0:T(1024)} %param.16) | copy-start | bytes 12292
  27.2 8.7 %collective-permute-start.5 = (bf16[528,128]{1,0:T(8,128)(2,1)S(1)}, bf16[528,128]{1,0:T(8,128)(2,1)S(1)}, u32[]{:S(2)}, u32[]{:S(2)}) collective-permute-start(bf16[528,128]{1,0:T(8,128)(2,1)S(1)} %get-tuple-element.34.refs_4_.refs_0_), channel_id=1, source_target_pairs={{0,8},{2,10},{4,12},{6,14},{8,0},{10,2},{12,4},{14,6},{1,9},{3,11}... | collective-permute-start | bytes 405512 | tf_op jit(solution)/shard_map/ppermute | solution.py:164
  30.7 14.4 %collective-permute-start.7 = (bf16[256,128]{1,0:T(8,128)(2,1)S(1)}, bf16[256,128]{1,0:T(8,128)(2,1)S(1)}, u32[]{:S(2)}, u32[]{:S(2)}) collective-permute-start(bf16[256,128]{1,0:T(8,128)(2,1)S(1)} %get-tuple-element.40), channel_id=1, source_target_pairs={{0,8},{2,10},{4,12},{6,14},{8,0},{10,2},{12,4},{14,6},{1,9},{3,11}... | collective-permute-start | bytes 196616 | tf_op jit(solution)/shard_map/ppermute | solution.py:164
  35.9 9.9 %collective-permute-start.6 = (bf16[2,256,128]{2,1,0:T(8,128)(2,1)S(1)}, bf16[2,256,128]{2,1,0:T(8,128)(2,1)S(1)}, u32[]{:S(2)}, u32[]{:S(2)}) collective-permute-start(bf16[2,256,128]{2,1,0:T(8,128)(2,1)S(1)} %shard_map.96.refs_2_.refs_1_), channel_id=1, source_target_pairs={{0,16},{16,0},{1,17},{17,1},{2,18},{18,2},{3,19},{19,3},{4,20},{20... | collective-permute-start | bytes 393224 | tf_op jit(solution)/shard_map/ppermute | solution.py:164
  37.5 20.5 %collective-permute-start.16 = (bf16[256,512]{1,0:T(8,128)(2,1)S(1)}, bf16[256,512]{1,0:T(8,128)(2,1)S(1)}, u32[]{:S(2)}, u32[]{:S(2)}) collective-permute-start(bf16[256,512]{1,0:T(8,128)(2,1)S(1)} %shard_map.101), channel_id=1, source_target_pairs={{0,12},{2,14},{12,0},{14,2},{1,13},{3,15},{13,1},{15,3},{16,28},{1... | collective-permute-start | bytes 786440 | tf_op jit(solution)/shard_map/ppermute | solution.py:706
  43.2 14.8 %collective-permute-start.17 = (bf16[256,512]{1,0:T(8,128)(2,1)S(1)}, bf16[256,512]{1,0:T(8,128)(2,1)S(1)}, u32[]{:S(2)}, u32[]{:S(2)}) collective-permute-start(bf16[256,512]{1,0:T(8,128)(2,1)S(1)} %shard_map.102), channel_id=1, source_target_pairs={{0,12},{2,14},{12,0},{14,2},{1,13},{3,15},{13,1},{15,3},{16,28},{1... | collective-permute-start | bytes 786440 | tf_op jit(solution)/shard_map/ppermute | solution.py:706
  45.2 4.3 %collective-permute-start.8 = (bf16[1,256,128]{2,1,0:T(8,128)(2,1)S(1)}, bf16[1,256,128]{2,1,0:T(8,128)(2,1)S(1)}, u32[]{:S(2)}, u32[]{:S(2)}) collective-permute-start(bf16[1,256,128]{2,1,0:T(8,128)(2,1)S(1)} %fusion.refs_1_), channel_id=1, source_target_pairs={{0,16},{16,0},{1,17},{17,1},{2,18},{18,2},{3,19},{19,3},{4,20},{20... | collective-permute-start | bytes 196616 | tf_op jit(solution)/shard_map/ppermute | solution.py:164
  50.1 2.8 %collective-permute-start.9 = (bf16[256,128]{1,0:T(8,128)(2,1)S(1)}, bf16[256,128]{1,0:T(8,128)(2,1)S(1)}, u32[]{:S(2)}, u32[]{:S(2)}) collective-permute-start(bf16[256,128]{1,0:T(8,128)(2,1)S(1)} %get-tuple-element.44), channel_id=1, source_target_pairs={{0,1},{1,0},{2,3},{3,2},{4,5},{5,4},{6,7},{7,6},{8,9},{9,8},{10,11... | collective-permute-start | bytes 196616 | tf_op jit(solution)/shard_map/ppermute | solution.py:164
  50.1 7.3 %collective-permute-start.10 = (bf16[256,128]{1,0:T(8,128)(2,1)S(1)}, bf16[256,128]{1,0:T(8,128)(2,1)S(1)}, u32[]{:S(2)}, u32[]{:S(2)}) collective-permute-start(bf16[256,128]{1,0:T(8,128)(2,1)S(1)} %get-tuple-element.45), channel_id=1, source_target_pairs={{0,8},{2,10},{4,12},{6,14},{8,0},{10,2},{12,4},{14,6},{1,9},{3,11}... | collective-permute-start | bytes 196616 | tf_op jit(solution)/shard_map/ppermute | solution.py:164
  50.2 7.7 %collective-permute-start.11 = (bf16[256,128]{1,0:T(8,128)(2,1)S(1)}, bf16[256,128]{1,0:T(8,128)(2,1)S(1)}, u32[]{:S(2)}, u32[]{:S(2)}) collective-permute-start(bf16[256,128]{1,0:T(8,128)(2,1)S(1)} %get-tuple-element.46), channel_id=1, source_target_pairs={{0,9},{1,8},{2,11},{3,10},{4,13},{5,12},{6,15},{7,14},{8,1},{9,0},... | collective-permute-start | bytes 196616 | tf_op jit(solution)/shard_map/ppermute | solution.py:172
  57.9 17.2 %copy-start.1 = (bf16[512,4096]{1,0:T(8,128)(2,1)S(1)}, bf16[512,4096]{1,0:T(8,128)(2,1)}, u32[]{:S(2)}) copy-start(bf16[512,4096]{1,0:T(8,128)(2,1)} %refs_1_.3) | copy-start | bytes 12582916
  58.1 14.2 %collective-permute-start.19 = (bf16[512,512]{1,0:T(8,128)(2,1)S(1)}, bf16[512,512]{1,0:T(8,128)(2,1)S(1)}, u32[]{:S(2)}, u32[]{:S(2)}) collective-permute-start(bf16[512,512]{1,0:T(8,128)(2,1)S(1)} %shard_map.103.refs_4_), channel_id=1, source_target_pairs={{0,16},{16,0},{1,17},{17,1},{2,18},{18,2},{3,19},{19,3},{4,20},{20... | collective-permute-start | bytes 1572872 | tf_op jit(solution)/shard_map/ppermute | solution.py:164
  58.7 16.4 %collective-permute-start.15 = (bf16[1024,512]{1,0:T(8,128)(2,1)S(1)}, bf16[1024,512]{1,0:T(8,128)(2,1)S(1)}, u32[]{:S(2)}, u32[]{:S(2)}) collective-permute-start(bf16[1024,512]{1,0:T(8,128)(2,1)S(1)} %copy-done.2), channel_id=1, source_target_pairs={{0,1},{1,0},{2,3},{3,2},{4,5},{5,4},{6,7},{7,6},{8,9},{9,8},{10,11... | collective-permute-start | bytes 3145736 | tf_op jit(solution)/shard_map/ppermute | solution.py:164
  60.1 8.3 %collective-permute-start.12 = (bf16[4,256,128]{2,1,0:T(8,128)(2,1)S(1)}, bf16[4,256,128]{2,1,0:T(8,128)(2,1)S(1)}, u32[]{:S(2)}, u32[]{:S(2)}) collective-permute-start(bf16[4,256,128]{2,1,0:T(8,128)(2,1)S(1)} %pad_maximum_fusion.refs_2_.refs_1_), channel_id=1, source_target_pairs={{0,2},{2,0},{4,6},{6,4},{8,10},{10,8},{12,14},{14,12},{1,3},{3,1},... | collective-permute-start | bytes 786440 | tf_op jit(solution)/shard_map/ppermute | solution.py:164
  60.6 11.7 %collective-permute-start.13 = (bf16[4,256,128]{2,1,0:T(8,128)(2,1)S(1)}, bf16[4,256,128]{2,1,0:T(8,128)(2,1)S(1)}, u32[]{:S(2)}, u32[]{:S(2)}) collective-permute-start(bf16[4,256,128]{2,1,0:T(8,128)(2,1)S(1)} %pad_maximum_fusion.refs_2_.refs_1_), channel_id=1, source_target_pairs={{0,4},{2,6},{4,0},{6,2},{8,12},{10,14},{12,8},{14,10},{1,5},{3,7},... | collective-permute-start | bytes 786440 | tf_op jit(solution)/shard_map/ppermute | solution.py:164
  61.0 14.2 %collective-permute-start.14 = (bf16[4,256,128]{2,1,0:T(8,128)(2,1)S(1)}, bf16[4,256,128]{2,1,0:T(8,128)(2,1)S(1)}, u32[]{:S(2)}, u32[]{:S(2)}) collective-permute-start(bf16[4,256,128]{2,1,0:T(8,128)(2,1)S(1)} %pad_maximum_fusion.refs_2_.refs_1_), channel_id=1, source_target_pairs={{0,6},{2,4},{4,2},{6,0},{8,14},{10,12},{12,10},{14,8},{1,7},{3,5},... | collective-permute-start | bytes 786440 | tf_op jit(solution)/shard_map/ppermute | solution.py:164
  68.4 8.0 %collective-permute-start.18 = (bf16[512,512]{1,0:T(8,128)(2,1)S(1)}, bf16[512,512]{1,0:T(8,128)(2,1)S(1)}, u32[]{:S(2)}, u32[]{:S(2)}) collective-permute-start(bf16[512,512]{1,0:T(8,128)(2,1)S(1)} %shard_map.103.refs_4_), channel_id=1, source_target_pairs={{0,1},{1,0},{2,3},{3,2},{4,5},{5,4},{6,7},{7,6},{8,9},{9,8},{10,11... | collective-permute-start | bytes 1572872 | tf_op jit(solution)/shard_map/ppermute | solution.py:164
  75.1 1.9 %collective-permute-start.20 = (bf16[512,512]{1,0:T(8,128)(2,1)S(1)}, bf16[512,512]{1,0:T(8,128)(2,1)S(1)}, u32[]{:S(2)}, u32[]{:S(2)}) collective-permute-start(bf16[512,512]{1,0:T(8,128)(2,1)S(1)} %shard_map.106.refs_6_), channel_id=1, source_target_pairs={{0,1},{1,0},{2,3},{3,2},{4,5},{5,4},{6,7},{7,6},{8,9},{9,8},{10,11... | collective-permute-start | bytes 1572872 | tf_op jit(solution)/shard_map/ppermute | solution.py:164
  77.9 3.8 %collective-permute-start.24 = (bf16[256,512]{1,0:T(8,128)(2,1)S(1)}, bf16[256,512]{1,0:T(8,128)(2,1)S(1)}, u32[]{:S(2)}, u32[]{:S(2)}) collective-permute-start(bf16[256,512]{1,0:T(8,128)(2,1)S(1)} %get-tuple-element.50), channel_id=1, source_target_pairs={{0,1},{1,0},{2,3},{3,2},{4,5},{5,4},{6,7},{7,6},{8,9},{9,8},{10,11... | collective-permute-start | bytes 786440 | tf_op jit(solution)/shard_map/ppermute | solution.py:164
  78.1 5.9 %collective-permute-start.23 = (bf16[64,512]{1,0:T(8,128)(2,1)S(1)}, bf16[64,512]{1,0:T(8,128)(2,1)S(1)}, u32[]{:S(2)}, u32[]{:S(2)}) collective-permute-start(bf16[64,512]{1,0:T(8,128)(2,1)S(1)} %get-tuple-element.55), channel_id=1, source_target_pairs={{0,6},{2,4},{4,2},{6,0},{8,14},{10,12},{12,10},{14,8},{1,7},{3,5},... | collective-permute-start | bytes 196616 | tf_op jit(solution)/shard_map/ppermute | solution.py:164
  79.0 6.3 %collective-permute-start.22 = (bf16[64,512]{1,0:T(8,128)(2,1)S(1)}, bf16[64,512]{1,0:T(8,128)(2,1)S(1)}, u32[]{:S(2)}, u32[]{:S(2)}) collective-permute-start(bf16[64,512]{1,0:T(8,128)(2,1)S(1)} %get-tuple-element.56), channel_id=1, source_target_pairs={{0,4},{2,6},{4,0},{6,2},{8,12},{10,14},{12,8},{14,10},{1,5},{3,7},... | collective-permute-start | bytes 196616 | tf_op jit(solution)/shard_map/ppermute | solution.py:164
  80.2 5.1 %collective-permute-start.21 = (bf16[64,512]{1,0:T(8,128)(2,1)S(1)}, bf16[64,512]{1,0:T(8,128)(2,1)S(1)}, u32[]{:S(2)}, u32[]{:S(2)}) collective-permute-start(bf16[64,512]{1,0:T(8,128)(2,1)S(1)} %get-tuple-element.57), channel_id=1, source_target_pairs={{0,2},{2,0},{4,6},{6,4},{8,10},{10,8},{12,14},{14,12},{1,3},{3,1},... | collective-permute-start | bytes 196616 | tf_op jit(solution)/shard_map/ppermute | solution.py:164
  81.7 5.3 %collective-permute-start.27 = (bf16[64,512]{1,0:T(8,128)(2,1)S(1)}, bf16[64,512]{1,0:T(8,128)(2,1)S(1)}, u32[]{:S(2)}, u32[]{:S(2)}) collective-permute-start(bf16[64,512]{1,0:T(8,128)(2,1)S(1)} %get-tuple-element.51), channel_id=1, source_target_pairs={{0,6},{2,4},{4,2},{6,0},{8,14},{10,12},{12,10},{14,8},{1,7},{3,5},... | collective-permute-start | bytes 196616 | tf_op jit(solution)/shard_map/ppermute | solution.py:164
  82.6 4.5 %collective-permute-start.26 = (bf16[64,512]{1,0:T(8,128)(2,1)S(1)}, bf16[64,512]{1,0:T(8,128)(2,1)S(1)}, u32[]{:S(2)}, u32[]{:S(2)}) collective-permute-start(bf16[64,512]{1,0:T(8,128)(2,1)S(1)} %get-tuple-element.52), channel_id=1, source_target_pairs={{0,4},{2,6},{4,0},{6,2},{8,12},{10,14},{12,8},{14,10},{1,5},{3,7},... | collective-permute-start | bytes 196616 | tf_op jit(solution)/shard_map/ppermute | solution.py:164
  84.0 4.3 %collective-permute-start.25 = (bf16[64,512]{1,0:T(8,128)(2,1)S(1)}, bf16[64,512]{1,0:T(8,128)(2,1)S(1)}, u32[]{:S(2)}, u32[]{:S(2)}) collective-permute-start(bf16[64,512]{1,0:T(8,128)(2,1)S(1)} %get-tuple-element.53), channel_id=1, source_target_pairs={{0,2},{2,0},{4,6},{6,4},{8,10},{10,8},{12,14},{14,12},{1,3},{3,1},... | collective-permute-start | bytes 196616 | tf_op jit(solution)/shard_map/ppermute | solution.py:164

commit v7 on v6

--- a/solution.py
+++ b/solution.py
@@ -451,8 +451,9 @@
 
 
 def near_kernel(picked_ref, table_ref, *refs):
-    piece_refs, (own_ref, core_ref, out_ref, joined_ref) = refs[:4], refs[4:]
-    quad, half, _, _ = here()
+    piece_refs, refs = refs[:4], refs[4:]
+    own_ref, core_ref, fetched_ref, core_fetched_ref, out_ref, part_ref, joined_ref = refs
+    quad, half, group, _ = here()
     block = 2 * LANES
     for m, piece_ref in enumerate(piece_refs):
         for other_core in (0, 1):
@@ -476,24 +477,30 @@
             )
     total += residual(picked_ref, table_ref, (4 * half + quad) * width, width)
     out_ref[...] = total.astype(bf16)
-
-
-def far_kernel(picked_ref, table_ref, near_ref, joined_ref, *refs):
-    far_refs, (kept_ref, sent_ref) = (refs[:2], refs[2:4]), refs[4:]
-    quad, half, group, core = here()
-    block = 2 * LANES
-    width = near_ref.shape[1]
-    total = jnp.zeros(near_ref.shape, f32)
-    for member in range(4):
-        rows = slice((member % 2) * block, (member % 2 + 1) * block)
-        for other_core in (0, 1):
-            source = 2 * (2 * (group ^ (member // 2)) + member % 2) + other_core
-            total += jnp.dot(
-                joined_ref[source],
-                far_refs[member // 2][other_core][rows, :],
+    part = residual(picked_ref, table_ref, (4 * (half ^ 1) + (quad ^ 2)) * width, width)
+    for i in (0, 1):
+        rows = slice(i * block, (i + 1) * block)
+        for other_core, ref in enumerate((fetched_ref, core_fetched_ref)):
+            part += jnp.dot(
+                joined_ref[2 * (2 * group + i) + other_core],
+                ref[rows, :],
                 preferred_element_type=f32,
             )
-    total += residual(picked_ref, table_ref, (4 * (half ^ 1) + (quad ^ 2)) * width, width)
+    part_ref[...] = part
+
+
+def far_kernel(near_ref, part_ref, joined_ref, shared_ref, core_shared_ref, kept_ref, sent_ref):
+    _, half, group, core = here()
+    block = 2 * LANES
+    total = part_ref[...]
+    for i in (0, 1):
+        rows = slice(i * block, (i + 1) * block)
+        for other_core, ref in enumerate((shared_ref, core_shared_ref)):
+            total += jnp.dot(
+                joined_ref[2 * (2 * (group ^ 1) + i) + other_core],
+                ref[rows, :],
+                preferred_element_type=f32,
+            )
     near, far = near_ref[...], total.astype(bf16)
     kept_ref[...] = jnp.where(half == core, near, far)
     sent_ref[...] = jnp.where(half == core, far, near)
@@ -713,27 +720,30 @@
     shared = swapped(fetched, "groups", 1)
     for ready in gated[1:]:
         shared = after(shared, ready)
-    near, joined = called(
+    near, part_far, joined = called(
         near_kernel,
-        [shaped(span, width, dtype=bf16), shaped(4 * 2, span, 2 * LANES, dtype=bf16)],
+        [
+            shaped(span, width, dtype=bf16),
+            shaped(span, width),
+            shaped(4 * 2, span, 2 * LANES, dtype=bf16),
+        ],
         (),
         picked,
         embed_table,
         *gated,
         output_proj,
         swapped(output_proj, "chan", 1),
+        fetched,
+        swapped(fetched, "chan", 1),
         mib=24,
     )
     results = called(
         far_kernel,
         [shaped(span, width, dtype=bf16)] * 2,
         (),
-        picked,
-        embed_table,
         near,
+        part_far,
         joined,
-        fetched,
-        swapped(fetched, "chan", 1),
         shared,
         swapped(shared, "chan", 1),
         mib=24,

time: 89.4 us -> 89.2 us (level)
  transfers between devices with their start and end apart: 28 -> 28, of which waited for: 14 -> 14; matrix products, arithmetic and copies ran while one was open for 0% -> 0% of each run, Pallas kernels for 11% -> 12%
where the time goes in v7:
time: 89.2 us; the launch traced here: 88.9 us
  starting transfers between devices  34.5 us (39%)
  waiting for transfers between devices  34.3 us (38%)
  Pallas kernels  15.3 us (17%)
  local copies, waits for them, and re-layouts  4.26 us (5%)
    ppermute x23, waiting for transfers between devices, swapped(): return lax.ppermute(value, axis, [(i, i ^ mask) for i in range(count)])  33.7 us
    ppermute x23, starting transfers between devices, swapped(): return lax.ppermute(value, axis, [(i, i ^ mask) for i in range(count)])  22.8 us
    pallas_call x8, Pallas kernels, called(): pl.pallas_call(body, out_shape=out_shape, in_specs=[smem] * len(scalars)...  9.52 us
    ppermute x2, starting transfers between devices, quad_body(): lax.ppermute(after(rows_part, pair_own), 'ctx', outer)  7.65 us
    unnamed x22, local copies, waits for them, and re-layouts  4.22 us
    ppermute x1, starting transfers between devices, swapped_both(): return lax.ppermute(value, ('ctx', 'chan'), pairs)  2.68 us
    pallas_call x1, Pallas kernels, quad_body(): pl.pallas_call(pack_kernel, out_shape=[shaped(branches * depth + SPARE, L...  2.64 us
    pallas_call x1, Pallas kernels, quad_body(): pl.pallas_call(norm_kernel, out_shape=shaped(vocab, part, dtype=bf16), gr...  2.56 us
  transfers between devices with their start and end apart: 28, of which 14 were waited for; matrix products, arithmetic and copies ran while one was open for 0% of the time, Pallas kernels for 12%

profile of v7, /device:TPU:0, one launch (start us, length us, event | category | flops | bytes accessed | tf_op | source)
XLA Modules:
  0.0 88.9 jit_solution(4558959370968849775)
XLA Ops:
  0.0 2.6 %shard_map.91 = (bf16[1552,128]{1,0:T(8,128)(2,1)}, bf16[1552,128]{1,0:T(8,128)(2,1)}, bf16[1552,128]{1,0:T(8,128)(2,1)}, bf16[1552,128]{1,0:T(8,128)(2,1)}) custom-call(s32[2,64]{1,0:T(2,128)} %tokens_ref.1, bf16[3,512,1024]{2,1,0:T(8,128)(2,1)} %bitcast.24), custom_call_target="tpu_custom_call" | custom-call | tf_op jit(solution)/shard_map/pallas_call | solution.py:580
  2.7 3.1 %collective-permute-start = (bf16[1552,128]{1,0:T(8,128)(2,1)}, bf16[1552,128]{1,0:T(8,128)(2,1)S(1)}, u32[]{:S(2)}, u32[]{:S(2)}) collective-permute-start(bf16[1552,128]{1,0:T(8,128)(2,1)} %get-tuple-element.29), channel_id=1, source_target_pairs={{0,4},{2,6},{4,0},{6,2},{8,12},{10,14},{12,8},{14,10},{1,5},{3,7},... | collective-permute-start | bytes 1191944 | tf_op jit(solution)/shard_map/ppermute | solution.py:164
  5.8 1.4 %collective-permute-start.2 = (bf16[1552,128]{1,0:T(8,128)(2,1)}, bf16[1552,128]{1,0:T(8,128)(2,1)S(1)}, u32[]{:S(2)}, u32[]{:S(2)}) collective-permute-start(bf16[1552,128]{1,0:T(8,128)(2,1)} %get-tuple-element.32), channel_id=1, source_target_pairs={{0,6},{2,4},{4,2},{6,0},{8,14},{10,12},{12,10},{14,8},{1,7},{3,5},... | collective-permute-start | bytes 1191944 | tf_op jit(solution)/shard_map/ppermute | solution.py:164
  7.4 1.0 %copy-done.4 = bf16[1552,128]{1,0:T(8,128)(2,1)S(1)} copy-done((bf16[1552,128]{1,0:T(8,128)(2,1)S(1)}, bf16[1552,128]{1,0:T(8,128)(2,1)}, u32[]{:S(2)}) %copy-start.4) | copy-done | bytes 397336
  8.4 0.6 shard_map.93
  9.0 0.7 collective-permute-start.3
  9.6 0.7 collective-permute-start.4
  10.3 5.7 %collective-permute-done.pair_ref.refs_3_ = bf16[1552,128]{1,0:T(8,128)(2,1)S(1)} collective-permute-done((bf16[1552,128]{1,0:T(8,128)(2,1)}, bf16[1552,128]{1,0:T(8,128)(2,1)S(1)}, u32[]{:S(2)}, u32[]{:S(2)}) %collective-permute-start) | collective-permute-done | bytes 397344 | tf_op jit(solution)/shard_map/ppermute | solution.py:164
  16.0 2.2 %copy-done = bf16[512,4096]{1,0:T(8,128)(2,1)S(1)} copy-done((bf16[512,4096]{1,0:T(8,128)(2,1)S(1)}, bf16[512,4096]{1,0:T(8,128)(2,1)}, u32[]{:S(2)}) %copy-start) | copy-done | bytes 4194328
  18.2 1.0 %copy-done.5 = bf16[1552,128]{1,0:T(8,128)(2,1)S(1)} copy-done((bf16[1552,128]{1,0:T(8,128)(2,1)S(1)}, bf16[1552,128]{1,0:T(8,128)(2,1)}, u32[]{:S(2)}) %copy-start.5) | copy-done | bytes 397336
  19.2 2.6 %shard_map.92.refs_0_ = bf16[512,2048]{1,0:T(8,128)(2,1)S(1)} custom-call(s32[4]{0:T(128)S(1)} %pad_add_fusion.place_ref, bf16[512,4096]{1,0:T(8,128)(2,1)S(1)} %copy-done, f32[1,4096]{1,0:T(1,128)S(1)} %bitcast.21, bf16[512,4096]{1,0:T(8,128)(2,1)S(1)} %copy-done, bf16[1552,128]{1,0:T(8,128)(2,1)S(1)} %collective-permute-done.pair_ref.refs_3_, ...), custom_call_target="tpu_custom_call" | custom-call | tf_op jit(solution)/shard_map/pallas_call | solution.py:620
  21.8 3.1 %collective-permute-done.2.refs_4_ = bf16[1552,128]{1,0:T(8,128)(2,1)S(1)} collective-permute-done((bf16[1552,128]{1,0:T(8,128)(2,1)}, bf16[1552,128]{1,0:T(8,128)(2,1)S(1)}, u32[]{:S(2)}, u32[]{:S(2)}) %collective-permute-start.2) | collective-permute-done | bytes 397344 | tf_op jit(solution)/shard_map/ppermute | solution.py:164
  24.9 1.4 %collective-permute-done.1.refs_2_ = bf16[1552,128]{1,0:T(8,128)(2,1)S(1)} collective-permute-done((bf16[1552,128]{1,0:T(8,128)(2,1)}, bf16[1552,128]{1,0:T(8,128)(2,1)S(1)}, u32[]{:S(2)}, u32[]{:S(2)}) %collective-permute-start.1) | collective-permute-done | bytes 397344 | tf_op jit(solution)/shard_map/ppermute | solution.py:164
  26.3 0.9 %shard_map.94 = (f32[512,128]{1,0:T(8,128)S(1)}, bf16[528,128]{1,0:T(8,128)(2,1)S(1)}) custom-call(bf16[512,2048]{1,0:T(8,128)(2,1)S(1)} %shard_map.92.refs_0_, bf16[1552,128]{1,0:T(8,128)(2,1)S(1)} %copy-done.3, bf16[1552,128]{1,0:T(8,128)(2,1)S(1)} %collective-permute-done.1.refs_2_, bf16[1552,128]{1,0:T(8,128)(2,1)S(1)} %collective-permute-done.pair_ref.refs_3_, ...), custom_call_target="tpu_custom_call" | custom-call | tf_op jit(solution)/shard_map/pallas_call | solution.py:529
  27.2 2.7 %collective-permute-start.5 = (bf16[528,128]{1,0:T(8,128)(2,1)S(1)}, bf16[528,128]{1,0:T(8,128)(2,1)S(1)}, u32[]{:S(2)}, u32[]{:S(2)}) collective-permute-start(bf16[528,128]{1,0:T(8,128)(2,1)S(1)} %get-tuple-element.35.refs_4_.refs_0_), channel_id=1, source_target_pairs={{0,8},{2,10},{4,12},{6,14},{8,0},{10,2},{12,4},{14,6},{1,9},{3,11}... | collective-permute-start | bytes 405512 | tf_op jit(solution)/shard_map/ppermute | solution.py:164
  29.9 0.8 shard_map.98
  30.7 0.4 collective-permute-start.7
  31.1 1.5 %shard_map.95 = (bf16[128,2560]{1,0:T(8,128)(2,1)S(1)}, f32[160,128]{1,0:T(8,128)S(1)}) custom-call(f32[16,64]{1,0:T(8,128)S(1)} %bitcast.20, f32[16,64]{1,0:T(8,128)S(1)} %multiply_bitcast_fusion.refs_1_, f32[3,3,64]{2,1,0:T(4,128)S(1)} %bitcast.22, f32[8,128]{1,0:T(8,128)S(1)} %bitcast.23, bf16[528,128]{1,0:T(8,128)(2,1)S(1)} %get-tuple-element.35.refs_4_.refs_0_), custom_call_target="tpu_custom_call" | custom-call | tf_op jit(solution)/shard_map/pallas_call | solution.py:529
  32.7 3.2 %collective-permute-done.5.refs_1_ = bf16[528,128]{1,0:T(8,128)(2,1)S(1)} collective-permute-done((bf16[528,128]{1,0:T(8,128)(2,1)S(1)}, bf16[528,128]{1,0:T(8,128)(2,1)S(1)}, u32[]{:S(2)}, u32[]{:S(2)}) %collective-permute-start.5) | collective-permute-done | bytes 135200 | tf_op jit(solution)/shard_map/ppermute | solution.py:164
  35.9 1.6 %collective-permute-start.6 = (bf16[2,256,128]{2,1,0:T(8,128)(2,1)S(1)}, bf16[2,256,128]{2,1,0:T(8,128)(2,1)S(1)}, u32[]{:S(2)}, u32[]{:S(2)}) collective-permute-start(bf16[2,256,128]{2,1,0:T(8,128)(2,1)S(1)} %shard_map.96.refs_2_.refs_1_), channel_id=1, source_target_pairs={{0,16},{16,0},{1,17},{17,1},{2,18},{18,2},{3,19},{19,3},{4,20},{20... | collective-permute-start | bytes 393224 | tf_op jit(solution)/shard_map/ppermute | solution.py:164
  37.5 5.7 %collective-permute-start.16 = (bf16[256,512]{1,0:T(8,128)(2,1)S(1)}, bf16[256,512]{1,0:T(8,128)(2,1)S(1)}, u32[]{:S(2)}, u32[]{:S(2)}) collective-permute-start(bf16[256,512]{1,0:T(8,128)(2,1)S(1)} %shard_map.100), channel_id=1, source_target_pairs={{0,12},{2,14},{12,0},{14,2},{1,13},{3,15},{13,1},{15,3},{16,28},{1... | collective-permute-start | bytes 786440 | tf_op jit(solution)/shard_map/ppermute | solution.py:713
  43.2 1.9 %collective-permute-start.17 = (bf16[256,512]{1,0:T(8,128)(2,1)S(1)}, bf16[256,512]{1,0:T(8,128)(2,1)S(1)}, u32[]{:S(2)}, u32[]{:S(2)}) collective-permute-start(bf16[256,512]{1,0:T(8,128)(2,1)S(1)} %shard_map.101), channel_id=1, source_target_pairs={{0,12},{2,14},{12,0},{14,2},{1,13},{3,15},{13,1},{15,3},{16,28},{1... | collective-permute-start | bytes 786440 | tf_op jit(solution)/shard_map/ppermute | solution.py:713
  45.2 0.6 collective-permute-start.8
  45.8 2.7 %shard_map.97 = (f32[1024,128]{1,0:T(8,128)S(1)}, bf16[1024,512]{1,0:T(8,128)(2,1)S(1)}) custom-call(bf16[528,128]{1,0:T(8,128)(2,1)S(1)} %get-tuple-element.35.refs_4_.refs_0_, bf16[528,128]{1,0:T(8,128)(2,1)S(1)} %collective-permute-done.5.refs_1_, bf16[2,256,128]{2,1,0:T(8,128)(2,1)S(1)} %shard_map.96.refs_2_.refs_1_, ...), custom_call_target="tpu_custom_call" | custom-call | tf_op jit(solution)/shard_map/pallas_call | solution.py:529
  48.5 1.0 %collective-permute-done.8.refs_2_ = bf16[1,256,128]{2,1,0:T(8,128)(2,1)S(1)} collective-permute-done((bf16[1,256,128]{2,1,0:T(8,128)(2,1)S(1)}, bf16[1,256,128]{2,1,0:T(8,128)(2,1)S(1)}, u32[]{:S(2)}, u32[]{:S(2)}) %collective-permute-start.8) | collective-permute-done | bytes 65568 | tf_op jit(solution)/shard_map/ppermute | solution.py:164
  49.5 0.5 shard_map.99
  50.2 2.7 %collective-permute-start.11 = (bf16[256,128]{1,0:T(8,128)(2,1)S(1)}, bf16[256,128]{1,0:T(8,128)(2,1)S(1)}, u32[]{:S(2)}, u32[]{:S(2)}) collective-permute-start(bf16[256,128]{1,0:T(8,128)(2,1)S(1)} %get-tuple-element.47), channel_id=1, source_target_pairs={{0,9},{1,8},{2,11},{3,10},{4,13},{5,12},{6,15},{7,14},{8,1},{9,0},... | collective-permute-start | bytes 196616 | tf_op jit(solution)/shard_map/ppermute | solution.py:172
  52.9 4.5 %collective-permute-done.10 = bf16[256,128]{1,0:T(8,128)(2,1)S(1)} collective-permute-done((bf16[256,128]{1,0:T(8,128)(2,1)S(1)}, bf16[256,128]{1,0:T(8,128)(2,1)S(1)}, u32[]{:S(2)}, u32[]{:S(2)}) %collective-permute-start.10) | collective-permute-done | bytes 65568 | tf_op jit(solution)/shard_map/ppermute | solution.py:164
  57.4 0.5 collective-permute-done.11
  58.1 0.6 collective-permute-start.19
  58.7 1.4 %collective-permute-start.15 = (bf16[1024,512]{1,0:T(8,128)(2,1)S(1)}, bf16[1024,512]{1,0:T(8,128)(2,1)S(1)}, u32[]{:S(2)}, u32[]{:S(2)}) collective-permute-start(bf16[1024,512]{1,0:T(8,128)(2,1)S(1)} %copy-done.2), channel_id=1, source_target_pairs={{0,1},{1,0},{2,3},{3,2},{4,5},{5,4},{6,7},{7,6},{8,9},{9,8},{10,11... | collective-permute-start | bytes 3145736 | tf_op jit(solution)/shard_map/ppermute | solution.py:164
  60.1 0.5 collective-permute-start.12
  61.0 2.7 %collective-permute-start.14 = (bf16[4,256,128]{2,1,0:T(8,128)(2,1)S(1)}, bf16[4,256,128]{2,1,0:T(8,128)(2,1)S(1)}, u32[]{:S(2)}, u32[]{:S(2)}) collective-permute-start(bf16[4,256,128]{2,1,0:T(8,128)(2,1)S(1)} %pad_maximum_fusion.refs_1_.refs_2_), channel_id=1, source_target_pairs={{0,6},{2,4},{4,2},{6,0},{8,14},{10,12},{12,10},{14,8},{1,7},{3,5},... | collective-permute-start | bytes 786440 | tf_op jit(solution)/shard_map/ppermute | solution.py:164
  63.6 4.8 %collective-permute-done.12.refs_3_.refs_1_ = bf16[4,256,128]{2,1,0:T(8,128)(2,1)S(1)} collective-permute-done((bf16[4,256,128]{2,1,0:T(8,128)(2,1)S(1)}, bf16[4,256,128]{2,1,0:T(8,128)(2,1)S(1)}, u32[]{:S(2)}, u32[]{:S(2)}) %collective-permute-start.12) | collective-permute-done | bytes 262176 | tf_op jit(solution)/shard_map/ppermute | solution.py:164
  68.4 3.9 %collective-permute-done.19.refs_0_ = bf16[512,512]{1,0:T(8,128)(2,1)S(1)} collective-permute-done((bf16[512,512]{1,0:T(8,128)(2,1)S(1)}, bf16[512,512]{1,0:T(8,128)(2,1)S(1)}, u32[]{:S(2)}, u32[]{:S(2)}) %collective-permute-start.19) | collective-permute-done | bytes 524320 | tf_op jit(solution)/shard_map/ppermute | solution.py:164
  72.3 2.8 %collective-permute-done.14.refs_5_.refs_1_ = bf16[4,256,128]{2,1,0:T(8,128)(2,1)S(1)} collective-permute-done((bf16[4,256,128]{2,1,0:T(8,128)(2,1)S(1)}, bf16[4,256,128]{2,1,0:T(8,128)(2,1)S(1)}, u32[]{:S(2)}, u32[]{:S(2)}) %collective-permute-start.14) | collective-permute-done | bytes 262176 | tf_op jit(solution)/shard_map/ppermute | solution.py:164
  75.2 1.7 %shard_map.103 = (bf16[256,512]{1,0:T(8,128)(2,1)S(1)}, f32[256,512]{1,0:T(8,128)S(1)}, bf16[8,256,256]{2,1,0:T(8,128)(2,1)S(1)}) custom-call(bf16[256,512]{1,0:T(8,128)(2,1)S(1)} %get-tuple-element.43.refs_0_, bf16[512,4096]{1,0:T(8,128)(2,1)S(1)} %copy-done.1, bf16[4,256,128]{2,1,0:T(8,128)(2,1)S(1)} %pad_maximum_fusion.refs_1_.refs_2_, ...), custom_call_target="tpu_custom_call" | custom-call | tf_op jit(solution)/shard_map/pallas_call | solution.py:529
  77.1 0.4 shard_map.107
  77.5 0.4 collective-permute-start.24
  77.9 0.8 collective-permute-start.23
  78.8 1.2 %collective-permute-start.22 = (bf16[64,512]{1,0:T(8,128)(2,1)S(1)}, bf16[64,512]{1,0:T(8,128)(2,1)S(1)}, u32[]{:S(2)}, u32[]{:S(2)}) collective-permute-start(bf16[64,512]{1,0:T(8,128)(2,1)S(1)} %get-tuple-element.58), channel_id=1, source_target_pairs={{0,4},{2,6},{4,0},{6,2},{8,12},{10,14},{12,8},{14,10},{1,5},{3,7},... | collective-permute-start | bytes 196616 | tf_op jit(solution)/shard_map/ppermute | solution.py:164
  80.0 1.5 %collective-permute-start.21 = (bf16[64,512]{1,0:T(8,128)(2,1)S(1)}, bf16[64,512]{1,0:T(8,128)(2,1)S(1)}, u32[]{:S(2)}, u32[]{:S(2)}) collective-permute-start(bf16[64,512]{1,0:T(8,128)(2,1)S(1)} %get-tuple-element.59), channel_id=1, source_target_pairs={{0,2},{2,0},{4,6},{6,4},{8,10},{10,8},{12,14},{14,12},{1,3},{3,1},... | collective-permute-start | bytes 196616 | tf_op jit(solution)/shard_map/ppermute | solution.py:164
  81.5 0.8 collective-permute-start.27
  82.3 1.2 %collective-permute-start.26 = (bf16[64,512]{1,0:T(8,128)(2,1)S(1)}, bf16[64,512]{1,0:T(8,128)(2,1)S(1)}, u32[]{:S(2)}, u32[]{:S(2)}) collective-permute-start(bf16[64,512]{1,0:T(8,128)(2,1)S(1)} %get-tuple-element.54), channel_id=1, source_target_pairs={{0,4},{2,6},{4,0},{6,2},{8,12},{10,14},{12,8},{14,10},{1,5},{3,7},... | collective-permute-start | bytes 196616 | tf_op jit(solution)/shard_map/ppermute | solution.py:164
  83.8 1.3 %collective-permute-start.25 = (bf16[64,512]{1,0:T(8,128)(2,1)S(1)}, bf16[64,512]{1,0:T(8,128)(2,1)S(1)}, u32[]{:S(2)}, u32[]{:S(2)}) collective-permute-start(bf16[64,512]{1,0:T(8,128)(2,1)S(1)} %get-tuple-element.55), channel_id=1, source_target_pairs={{0,2},{2,0},{4,6},{6,4},{8,10},{10,8},{12,14},{14,12},{1,3},{3,1},... | collective-permute-start | bytes 196616 | tf_op jit(solution)/shard_map/ppermute | solution.py:164
  85.1 1.7 %collective-permute-done.27.refs_7_ = bf16[64,512]{1,0:T(8,128)(2,1)S(1)} collective-permute-done((bf16[64,512]{1,0:T(8,128)(2,1)S(1)}, bf16[64,512]{1,0:T(8,128)(2,1)S(1)}, u32[]{:S(2)}, u32[]{:S(2)}) %collective-permute-start.27) | collective-permute-done | bytes 65568 | tf_op jit(solution)/shard_map/ppermute | solution.py:164
  86.7 1.3 %collective-permute-done.25.refs_5_ = bf16[64,512]{1,0:T(8,128)(2,1)S(1)} collective-permute-done((bf16[64,512]{1,0:T(8,128)(2,1)S(1)}, bf16[64,512]{1,0:T(8,128)(2,1)S(1)}, u32[]{:S(2)}, u32[]{:S(2)}) %collective-permute-start.25) | collective-permute-done | bytes 65568 | tf_op jit(solution)/shard_map/ppermute | solution.py:164
  88.0 0.8 shard_map.108
  (56 shorter events, 1.5 us)
Async XLA Ops:
  0.0 7.4 %copy-start.2 = (bf16[1024,512]{1,0:T(8,128)(2,1)S(1)}, bf16[1024,512]{1,0:T(8,128)(2,1)}, u32[]{:S(2)}) copy-start(bf16[1024,512]{1,0:T(8,128)(2,1)} %refs_6_.1) | copy-start | bytes 3145732
  0.0 16.0 %copy-start.7 = (f32[4096]{0:T(1024)S(1)}, f32[4096]{0:T(1024)}, u32[]{:S(2)}) copy-start(f32[4096]{0:T(1024)} %param.11) | copy-start | bytes 49156
  2.7 13.3 %collective-permute-start = (bf16[1552,128]{1,0:T(8,128)(2,1)}, bf16[1552,128]{1,0:T(8,128)(2,1)S(1)}, u32[]{:S(2)}, u32[]{:S(2)}) collective-permute-start(bf16[1552,128]{1,0:T(8,128)(2,1)} %get-tuple-element.29), channel_id=1, source_target_pairs={{0,4},{2,6},{4,0},{6,2},{8,12},{10,14},{12,8},{14,10},{1,5},{3,7},... | collective-permute-start | bytes 1191944 | tf_op jit(solution)/shard_map/ppermute | solution.py:164
  5.8 19.2 %collective-permute-start.2 = (bf16[1552,128]{1,0:T(8,128)(2,1)}, bf16[1552,128]{1,0:T(8,128)(2,1)S(1)}, u32[]{:S(2)}, u32[]{:S(2)}) collective-permute-start(bf16[1552,128]{1,0:T(8,128)(2,1)} %get-tuple-element.32), channel_id=1, source_target_pairs={{0,6},{2,4},{4,2},{6,0},{8,14},{10,12},{12,10},{14,8},{1,7},{3,5},... | collective-permute-start | bytes 1191944 | tf_op jit(solution)/shard_map/ppermute | solution.py:164
  7.2 19.1 %collective-permute-start.1 = (bf16[1552,128]{1,0:T(8,128)(2,1)}, bf16[1552,128]{1,0:T(8,128)(2,1)S(1)}, u32[]{:S(2)}, u32[]{:S(2)}) collective-permute-start(bf16[1552,128]{1,0:T(8,128)(2,1)} %get-tuple-element.30.query_ref.packed_ref), channel_id=1, source_target_pairs={{0,2},{2,0},{4,6},{6,4},{8,10},{10,8},{12,14},{14,12},{1,3},{3,1},... | collective-permute-start | bytes 1191944 | tf_op jit(solution)/shard_map/ppermute | solution.py:164
  7.4 1.0 %copy-start.4 = (bf16[1552,128]{1,0:T(8,128)(2,1)S(1)}, bf16[1552,128]{1,0:T(8,128)(2,1)}, u32[]{:S(2)}) copy-start(bf16[1552,128]{1,0:T(8,128)(2,1)} %get-tuple-element.30.query_ref.packed_ref) | copy-start | bytes 1191940
  9.0 12.8 %collective-permute-start.3 = (bf16[256,512]{1,0:T(8,128)(2,1)S(1)}, bf16[256,512]{1,0:T(8,128)(2,1)S(1)}, u32[]{:S(2)}, u32[]{:S(2)}) collective-permute-start(bf16[256,512]{1,0:T(8,128)(2,1)S(1)} %get-tuple-element.33.refs_0_), channel_id=1, source_target_pairs={{4,8},{6,10},{8,4},{10,6},{5,9},{7,11},{9,5},{11,7},{20,24},{22,26... | collective-permute-start | bytes 786440 | tf_op jit(solution)/shard_map/ppermute | solution.py:638
  9.6 12.1 %collective-permute-start.4 = (bf16[256,512]{1,0:T(8,128)(2,1)S(1)}, bf16[256,512]{1,0:T(8,128)(2,1)S(1)}, u32[]{:S(2)}, u32[]{:S(2)}) collective-permute-start(bf16[256,512]{1,0:T(8,128)(2,1)S(1)} %get-tuple-element.34.refs_0_), channel_id=1, source_target_pairs={{4,8},{6,10},{8,4},{10,6},{5,9},{7,11},{9,5},{11,7},{20,24},{22,26... | collective-permute-start | bytes 786440 | tf_op jit(solution)/shard_map/ppermute | solution.py:638
  16.0 2.2 %copy-start = (bf16[512,4096]{1,0:T(8,128)(2,1)S(1)}, bf16[512,4096]{1,0:T(8,128)(2,1)}, u32[]{:S(2)}) copy-start(bf16[512,4096]{1,0:T(8,128)(2,1)} %refs_1_.1) | copy-start | bytes 12582916
  18.2 1.0 %copy-start.5 = (bf16[1552,128]{1,0:T(8,128)(2,1)S(1)}, bf16[1552,128]{1,0:T(8,128)(2,1)}, u32[]{:S(2)}) copy-start(bf16[1552,128]{1,0:T(8,128)(2,1)} %get-tuple-element.30.query_ref.packed_ref) | copy-start | bytes 1191940
  19.2 7.1 %copy-start.3 = (bf16[1552,128]{1,0:T(8,128)(2,1)S(1)}, bf16[1552,128]{1,0:T(8,128)(2,1)}, u32[]{:S(2)}) copy-start(bf16[1552,128]{1,0:T(8,128)(2,1)} %get-tuple-element.31.refs_1_) | copy-start | bytes 1191940
  21.7 8.1 %copy-start.6 = (f32[64,16]{0,1:T(8,128)S(1)}, f32[64,16]{0,1:T(8,128)}, u32[]{:S(2)}) copy-start(f32[64,16]{0,1:T(8,128)} %param.14) | copy-start | bytes 12292
  21.8 8.1 %copy-start.10 = (f32[64,16]{0,1:T(8,128)S(1)}, f32[64,16]{0,1:T(8,128)}, u32[]{:S(2)}) copy-start(f32[64,16]{0,1:T(8,128)} %param.15) | copy-start | bytes 12292
  26.3 4.8 %copy-start.8 = (f32[3,64,3]{1,2,0:T(4,128)S(1)}, f32[3,64,3]{1,2,0:T(4,128)}, u32[]{:S(2)}) copy-start(f32[3,64,3]{1,2,0:T(4,128)} %param.13) | copy-start | bytes 6916
  26.3 4.8 %copy-start.9 = (f32[1024]{0:T(1024)S(1)}, f32[1024]{0:T(1024)}, u32[]{:S(2)}) copy-start(f32[1024]{0:T(1024)} %param.16) | copy-start | bytes 12292
  27.2 8.7 %collective-permute-start.5 = (bf16[528,128]{1,0:T(8,128)(2,1)S(1)}, bf16[528,128]{1,0:T(8,128)(2,1)S(1)}, u32[]{:S(2)}, u32[]{:S(2)}) collective-permute-start(bf16[528,128]{1,0:T(8,128)(2,1)S(1)} %get-tuple-element.35.refs_4_.refs_0_), channel_id=1, source_target_pairs={{0,8},{2,10},{4,12},{6,14},{8,0},{10,2},{12,4},{14,6},{1,9},{3,11}... | collective-permute-start | bytes 405512 | tf_op jit(solution)/shard_map/ppermute | solution.py:164
  30.7 14.4 %collective-permute-start.7 = (bf16[256,128]{1,0:T(8,128)(2,1)S(1)}, bf16[256,128]{1,0:T(8,128)(2,1)S(1)}, u32[]{:S(2)}, u32[]{:S(2)}) collective-permute-start(bf16[256,128]{1,0:T(8,128)(2,1)S(1)} %get-tuple-element.41), channel_id=1, source_target_pairs={{0,8},{2,10},{4,12},{6,14},{8,0},{10,2},{12,4},{14,6},{1,9},{3,11}... | collective-permute-start | bytes 196616 | tf_op jit(solution)/shard_map/ppermute | solution.py:164
  35.9 9.9 %collective-permute-start.6 = (bf16[2,256,128]{2,1,0:T(8,128)(2,1)S(1)}, bf16[2,256,128]{2,1,0:T(8,128)(2,1)S(1)}, u32[]{:S(2)}, u32[]{:S(2)}) collective-permute-start(bf16[2,256,128]{2,1,0:T(8,128)(2,1)S(1)} %shard_map.96.refs_2_.refs_1_), channel_id=1, source_target_pairs={{0,16},{16,0},{1,17},{17,1},{2,18},{18,2},{3,19},{19,3},{4,20},{20... | collective-permute-start | bytes 393224 | tf_op jit(solution)/shard_map/ppermute | solution.py:164
  37.5 20.5 %collective-permute-start.16 = (bf16[256,512]{1,0:T(8,128)(2,1)S(1)}, bf16[256,512]{1,0:T(8,128)(2,1)S(1)}, u32[]{:S(2)}, u32[]{:S(2)}) collective-permute-start(bf16[256,512]{1,0:T(8,128)(2,1)S(1)} %shard_map.100), channel_id=1, source_target_pairs={{0,12},{2,14},{12,0},{14,2},{1,13},{3,15},{13,1},{15,3},{16,28},{1... | collective-permute-start | bytes 786440 | tf_op jit(solution)/shard_map/ppermute | solution.py:713
  43.2 14.8 %collective-permute-start.17 = (bf16[256,512]{1,0:T(8,128)(2,1)S(1)}, bf16[256,512]{1,0:T(8,128)(2,1)S(1)}, u32[]{:S(2)}, u32[]{:S(2)}) collective-permute-start(bf16[256,512]{1,0:T(8,128)(2,1)S(1)} %shard_map.101), channel_id=1, source_target_pairs={{0,12},{2,14},{12,0},{14,2},{1,13},{3,15},{13,1},{15,3},{16,28},{1... | collective-permute-start | bytes 786440 | tf_op jit(solution)/shard_map/ppermute | solution.py:713
  45.2 4.3 %collective-permute-start.8 = (bf16[1,256,128]{2,1,0:T(8,128)(2,1)S(1)}, bf16[1,256,128]{2,1,0:T(8,128)(2,1)S(1)}, u32[]{:S(2)}, u32[]{:S(2)}) collective-permute-start(bf16[1,256,128]{2,1,0:T(8,128)(2,1)S(1)} %fusion.refs_1_), channel_id=1, source_target_pairs={{0,16},{16,0},{1,17},{17,1},{2,18},{18,2},{3,19},{19,3},{4,20},{20... | collective-permute-start | bytes 196616 | tf_op jit(solution)/shard_map/ppermute | solution.py:164
  50.1 2.8 %collective-permute-start.9 = (bf16[256,128]{1,0:T(8,128)(2,1)S(1)}, bf16[256,128]{1,0:T(8,128)(2,1)S(1)}, u32[]{:S(2)}, u32[]{:S(2)}) collective-permute-start(bf16[256,128]{1,0:T(8,128)(2,1)S(1)} %get-tuple-element.45), channel_id=1, source_target_pairs={{0,1},{1,0},{2,3},{3,2},{4,5},{5,4},{6,7},{7,6},{8,9},{9,8},{10,11... | collective-permute-start | bytes 196616 | tf_op jit(solution)/shard_map/ppermute | solution.py:164
  50.1 7.3 %collective-permute-start.10 = (bf16[256,128]{1,0:T(8,128)(2,1)S(1)}, bf16[256,128]{1,0:T(8,128)(2,1)S(1)}, u32[]{:S(2)}, u32[]{:S(2)}) collective-permute-start(bf16[256,128]{1,0:T(8,128)(2,1)S(1)} %get-tuple-element.46), channel_id=1, source_target_pairs={{0,8},{2,10},{4,12},{6,14},{8,0},{10,2},{12,4},{14,6},{1,9},{3,11}... | collective-permute-start | bytes 196616 | tf_op jit(solution)/shard_map/ppermute | solution.py:164
  50.2 7.7 %collective-permute-start.11 = (bf16[256,128]{1,0:T(8,128)(2,1)S(1)}, bf16[256,128]{1,0:T(8,128)(2,1)S(1)}, u32[]{:S(2)}, u32[]{:S(2)}) collective-permute-start(bf16[256,128]{1,0:T(8,128)(2,1)S(1)} %get-tuple-element.47), channel_id=1, source_target_pairs={{0,9},{1,8},{2,11},{3,10},{4,13},{5,12},{6,15},{7,14},{8,1},{9,0},... | collective-permute-start | bytes 196616 | tf_op jit(solution)/shard_map/ppermute | solution.py:172
  57.9 17.2 %copy-start.1 = (bf16[512,4096]{1,0:T(8,128)(2,1)S(1)}, bf16[512,4096]{1,0:T(8,128)(2,1)}, u32[]{:S(2)}) copy-start(bf16[512,4096]{1,0:T(8,128)(2,1)} %refs_1_.1) | copy-start | bytes 12582916
  58.1 14.2 %collective-permute-start.19 = (bf16[512,512]{1,0:T(8,128)(2,1)S(1)}, bf16[512,512]{1,0:T(8,128)(2,1)S(1)}, u32[]{:S(2)}, u32[]{:S(2)}) collective-permute-start(bf16[512,512]{1,0:T(8,128)(2,1)S(1)} %shard_map.102.refs_8_), channel_id=1, source_target_pairs={{0,16},{16,0},{1,17},{17,1},{2,18},{18,2},{3,19},{19,3},{4,20},{20... | collective-permute-start | bytes 1572872 | tf_op jit(solution)/shard_map/ppermute | solution.py:164
  58.7 16.4 %collective-permute-start.15 = (bf16[1024,512]{1,0:T(8,128)(2,1)S(1)}, bf16[1024,512]{1,0:T(8,128)(2,1)S(1)}, u32[]{:S(2)}, u32[]{:S(2)}) collective-permute-start(bf16[1024,512]{1,0:T(8,128)(2,1)S(1)} %copy-done.2), channel_id=1, source_target_pairs={{0,1},{1,0},{2,3},{3,2},{4,5},{5,4},{6,7},{7,6},{8,9},{9,8},{10,11... | collective-permute-start | bytes 3145736 | tf_op jit(solution)/shard_map/ppermute | solution.py:164
  60.1 8.3 %collective-permute-start.12 = (bf16[4,256,128]{2,1,0:T(8,128)(2,1)S(1)}, bf16[4,256,128]{2,1,0:T(8,128)(2,1)S(1)}, u32[]{:S(2)}, u32[]{:S(2)}) collective-permute-start(bf16[4,256,128]{2,1,0:T(8,128)(2,1)S(1)} %pad_maximum_fusion.refs_1_.refs_2_), channel_id=1, source_target_pairs={{0,2},{2,0},{4,6},{6,4},{8,10},{10,8},{12,14},{14,12},{1,3},{3,1},... | collective-permute-start | bytes 786440 | tf_op jit(solution)/shard_map/ppermute | solution.py:164
  60.6 11.7 %collective-permute-start.13 = (bf16[4,256,128]{2,1,0:T(8,128)(2,1)S(1)}, bf16[4,256,128]{2,1,0:T(8,128)(2,1)S(1)}, u32[]{:S(2)}, u32[]{:S(2)}) collective-permute-start(bf16[4,256,128]{2,1,0:T(8,128)(2,1)S(1)} %pad_maximum_fusion.refs_1_.refs_2_), channel_id=1, source_target_pairs={{0,4},{2,6},{4,0},{6,2},{8,12},{10,14},{12,8},{14,10},{1,5},{3,7},... | collective-permute-start | bytes 786440 | tf_op jit(solution)/shard_map/ppermute | solution.py:164
  61.0 14.2 %collective-permute-start.14 = (bf16[4,256,128]{2,1,0:T(8,128)(2,1)S(1)}, bf16[4,256,128]{2,1,0:T(8,128)(2,1)S(1)}, u32[]{:S(2)}, u32[]{:S(2)}) collective-permute-start(bf16[4,256,128]{2,1,0:T(8,128)(2,1)S(1)} %pad_maximum_fusion.refs_1_.refs_2_), channel_id=1, source_target_pairs={{0,6},{2,4},{4,2},{6,0},{8,14},{10,12},{12,10},{14,8},{1,7},{3,5},... | collective-permute-start | bytes 786440 | tf_op jit(solution)/shard_map/ppermute | solution.py:164
  68.4 6.7 %collective-permute-start.18 = (bf16[512,512]{1,0:T(8,128)(2,1)S(1)}, bf16[512,512]{1,0:T(8,128)(2,1)S(1)}, u32[]{:S(2)}, u32[]{:S(2)}) collective-permute-start(bf16[512,512]{1,0:T(8,128)(2,1)S(1)} %shard_map.102.refs_8_), channel_id=1, source_target_pairs={{0,1},{1,0},{2,3},{3,2},{4,5},{5,4},{6,7},{7,6},{8,9},{9,8},{10,11... | collective-permute-start | bytes 1572872 | tf_op jit(solution)/shard_map/ppermute | solution.py:164
  75.1 1.9 %collective-permute-start.20 = (bf16[512,512]{1,0:T(8,128)(2,1)S(1)}, bf16[512,512]{1,0:T(8,128)(2,1)S(1)}, u32[]{:S(2)}, u32[]{:S(2)}) collective-permute-start(bf16[512,512]{1,0:T(8,128)(2,1)S(1)} %shard_map.106.refs_3_), channel_id=1, source_target_pairs={{0,1},{1,0},{2,3},{3,2},{4,5},{5,4},{6,7},{7,6},{8,9},{9,8},{10,11... | collective-permute-start | bytes 1572872 | tf_op jit(solution)/shard_map/ppermute | solution.py:164
  77.5 4.0 %collective-permute-start.24 = (bf16[256,512]{1,0:T(8,128)(2,1)S(1)}, bf16[256,512]{1,0:T(8,128)(2,1)S(1)}, u32[]{:S(2)}, u32[]{:S(2)}) collective-permute-start(bf16[256,512]{1,0:T(8,128)(2,1)S(1)} %get-tuple-element.52), channel_id=1, source_target_pairs={{0,1},{1,0},{2,3},{3,2},{4,5},{5,4},{6,7},{7,6},{8,9},{9,8},{10,11... | collective-permute-start | bytes 786440 | tf_op jit(solution)/shard_map/ppermute | solution.py:164
  77.9 5.8 %collective-permute-start.23 = (bf16[64,512]{1,0:T(8,128)(2,1)S(1)}, bf16[64,512]{1,0:T(8,128)(2,1)S(1)}, u32[]{:S(2)}, u32[]{:S(2)}) collective-permute-start(bf16[64,512]{1,0:T(8,128)(2,1)S(1)} %get-tuple-element.57), channel_id=1, source_target_pairs={{0,6},{2,4},{4,2},{6,0},{8,14},{10,12},{12,10},{14,8},{1,7},{3,5},... | collective-permute-start | bytes 196616 | tf_op jit(solution)/shard_map/ppermute | solution.py:164
  78.8 6.3 %collective-permute-start.22 = (bf16[64,512]{1,0:T(8,128)(2,1)S(1)}, bf16[64,512]{1,0:T(8,128)(2,1)S(1)}, u32[]{:S(2)}, u32[]{:S(2)}) collective-permute-start(bf16[64,512]{1,0:T(8,128)(2,1)S(1)} %get-tuple-element.58), channel_id=1, source_target_pairs={{0,4},{2,6},{4,0},{6,2},{8,12},{10,14},{12,8},{14,10},{1,5},{3,7},... | collective-permute-start | bytes 196616 | tf_op jit(solution)/shard_map/ppermute | solution.py:164
  80.0 5.1 %collective-permute-start.21 = (bf16[64,512]{1,0:T(8,128)(2,1)S(1)}, bf16[64,512]{1,0:T(8,128)(2,1)S(1)}, u32[]{:S(2)}, u32[]{:S(2)}) collective-permute-start(bf16[64,512]{1,0:T(8,128)(2,1)S(1)} %get-tuple-element.59), channel_id=1, source_target_pairs={{0,2},{2,0},{4,6},{6,4},{8,10},{10,8},{12,14},{14,12},{1,3},{3,1},... | collective-permute-start | bytes 196616 | tf_op jit(solution)/shard_map/ppermute | solution.py:164
  81.5 5.2 %collective-permute-start.27 = (bf16[64,512]{1,0:T(8,128)(2,1)S(1)}, bf16[64,512]{1,0:T(8,128)(2,1)S(1)}, u32[]{:S(2)}, u32[]{:S(2)}) collective-permute-start(bf16[64,512]{1,0:T(8,128)(2,1)S(1)} %get-tuple-element.53), channel_id=1, source_target_pairs={{0,6},{2,4},{4,2},{6,0},{8,14},{10,12},{12,10},{14,8},{1,7},{3,5},... | collective-permute-start | bytes 196616 | tf_op jit(solution)/shard_map/ppermute | solution.py:164
  82.3 4.4 %collective-permute-start.26 = (bf16[64,512]{1,0:T(8,128)(2,1)S(1)}, bf16[64,512]{1,0:T(8,128)(2,1)S(1)}, u32[]{:S(2)}, u32[]{:S(2)}) collective-permute-start(bf16[64,512]{1,0:T(8,128)(2,1)S(1)} %get-tuple-element.54), channel_id=1, source_target_pairs={{0,4},{2,6},{4,0},{6,2},{8,12},{10,14},{12,8},{14,10},{1,5},{3,7},... | collective-permute-start | bytes 196616 | tf_op jit(solution)/shard_map/ppermute | solution.py:164
  83.8 4.3 %collective-permute-start.25 = (bf16[64,512]{1,0:T(8,128)(2,1)S(1)}, bf16[64,512]{1,0:T(8,128)(2,1)S(1)}, u32[]{:S(2)}, u32[]{:S(2)}) collective-permute-start(bf16[64,512]{1,0:T(8,128)(2,1)S(1)} %get-tuple-element.55), channel_id=1, source_target_pairs={{0,2},{2,0},{4,6},{6,4},{8,10},{10,8},{12,14},{14,12},{1,3},{3,1},... | collective-permute-start | bytes 196616 | tf_op jit(solution)/shard_map/ppermute | solution.py:164

commit v8 on v7

--- a/solution.py
+++ b/solution.py
@@ -616,7 +616,7 @@
     ]
 
     part = features // 2
-    step = 128
+    step = 256
     normed = pl.pallas_call(
         norm_kernel,
         out_shape=shaped(vocab, part, dtype=bf16),
@@ -651,7 +651,7 @@
         own = (keep + arrived[: keep.shape[0]].astype(f32)).astype(bf16)
         return own.reshape(-1, vocab // 2, LANES)
 
-    pair_keep, pair_send = partials(0, 2, SPARE, tuple(inner_fetched))
+    pair_keep, pair_send = partials(0, 2, SPARE)
     query_keep, query_send = partials(2, 1, 0)
     pair_arrived = swapped(pair_send, "ctx", members)
     query_arrived = swapped(query_send, "ctx", members)
@@ -668,7 +668,7 @@
         amp.T,
         short_filter.transpose(0, 2, 1),
         skip_gain.reshape(-1, LANES),
-        earlier=(pair_send,),
+        earlier=(pair_send, *inner_fetched),
     )
 
     pair_own = after(finished(pair_keep, pair_arrived), matrices)

time: 89.2 us -> 89.2 us (level)
  transfers between devices with their start and end apart: 28 -> 28, of which waited for: 14 -> 14; matrix products, arithmetic and copies ran while one was open for 0% -> 0% of each run, Pallas kernels for 12% -> 13%
where the time goes in v8:
time: 89.2 us; the launch traced here: 88.9 us
  starting transfers between devices  34.5 us (39%)
  waiting for transfers between devices  34.2 us (38%)
  Pallas kernels  15.3 us (17%)
  local copies, waits for them, and re-layouts  4.26 us (5%)
    ppermute x23, waiting for transfers between devices, swapped(): return lax.ppermute(value, axis, [(i, i ^ mask) for i in range(count)])  33.7 us
    ppermute x23, starting transfers between devices, swapped(): return lax.ppermute(value, axis, [(i, i ^ mask) for i in range(count)])  22.8 us
    pallas_call x8, Pallas kernels, called(): pl.pallas_call(body, out_shape=out_shape, in_specs=[smem] * len(scalars)...  9.53 us
    ppermute x2, starting transfers between devices, quad_body(): lax.ppermute(after(rows_part, pair_own), 'ctx', outer)  7.65 us
    unnamed x22, local copies, waits for them, and re-layouts  4.22 us
    ppermute x1, starting transfers between devices, swapped_both(): return lax.ppermute(value, ('ctx', 'chan'), pairs)  2.68 us
    pallas_call x1, Pallas kernels, quad_body(): pl.pallas_call(pack_kernel, out_shape=[shaped(branches * depth + SPARE, L...  2.64 us
    pallas_call x1, Pallas kernels, quad_body(): pl.pallas_call(norm_kernel, out_shape=shaped(vocab, part, dtype=bf16), gr...  2.59 us
  transfers between devices with their start and end apart: 28, of which 14 were waited for; matrix products, arithmetic and copies ran while one was open for 0% of the time, Pallas kernels for 13%

profile of v8, /device:TPU:0, one launch (start us, length us, event | category | flops | bytes accessed | tf_op | source)
XLA Modules:
  0.0 88.9 jit_solution(12859719473153768886)
XLA Ops:
  0.0 2.6 %shard_map.91 = (bf16[1552,128]{1,0:T(8,128)(2,1)}, bf16[1552,128]{1,0:T(8,128)(2,1)}, bf16[1552,128]{1,0:T(8,128)(2,1)}, bf16[1552,128]{1,0:T(8,128)(2,1)}) custom-call(s32[2,64]{1,0:T(2,128)} %tokens_ref.1, bf16[3,512,1024]{2,1,0:T(8,128)(2,1)} %bitcast.24), custom_call_target="tpu_custom_call" | custom-call | tf_op jit(solution)/shard_map/pallas_call | solution.py:580
  2.7 3.1 %collective-permute-start = (bf16[1552,128]{1,0:T(8,128)(2,1)}, bf16[1552,128]{1,0:T(8,128)(2,1)S(1)}, u32[]{:S(2)}, u32[]{:S(2)}) collective-permute-start(bf16[1552,128]{1,0:T(8,128)(2,1)} %get-tuple-element.29), channel_id=1, source_target_pairs={{0,4},{2,6},{4,0},{6,2},{8,12},{10,14},{12,8},{14,10},{1,5},{3,7},... | collective-permute-start | bytes 1191944 | tf_op jit(solution)/shard_map/ppermute | solution.py:164
  5.8 1.4 %collective-permute-start.2 = (bf16[1552,128]{1,0:T(8,128)(2,1)}, bf16[1552,128]{1,0:T(8,128)(2,1)S(1)}, u32[]{:S(2)}, u32[]{:S(2)}) collective-permute-start(bf16[1552,128]{1,0:T(8,128)(2,1)} %get-tuple-element.32), channel_id=1, source_target_pairs={{0,6},{2,4},{4,2},{6,0},{8,14},{10,12},{12,10},{14,8},{1,7},{3,5},... | collective-permute-start | bytes 1191944 | tf_op jit(solution)/shard_map/ppermute | solution.py:164
  7.4 1.0 %copy-done.4 = bf16[1552,128]{1,0:T(8,128)(2,1)S(1)} copy-done((bf16[1552,128]{1,0:T(8,128)(2,1)S(1)}, bf16[1552,128]{1,0:T(8,128)(2,1)}, u32[]{:S(2)}) %copy-start.4) | copy-done | bytes 397336
  8.4 0.6 shard_map.94
  9.0 0.7 collective-permute-start.4
  9.6 0.7 collective-permute-start.5
  10.3 5.7 %collective-permute-done.pair_ref.refs_3_ = bf16[1552,128]{1,0:T(8,128)(2,1)S(1)} collective-permute-done((bf16[1552,128]{1,0:T(8,128)(2,1)}, bf16[1552,128]{1,0:T(8,128)(2,1)S(1)}, u32[]{:S(2)}, u32[]{:S(2)}) %collective-permute-start) | collective-permute-done | bytes 397344 | tf_op jit(solution)/shard_map/ppermute | solution.py:164
  16.0 2.2 %copy-done = bf16[512,4096]{1,0:T(8,128)(2,1)S(1)} copy-done((bf16[512,4096]{1,0:T(8,128)(2,1)S(1)}, bf16[512,4096]{1,0:T(8,128)(2,1)}, u32[]{:S(2)}) %copy-start) | copy-done | bytes 4194328
  18.2 1.0 %copy-done.5 = bf16[1552,128]{1,0:T(8,128)(2,1)S(1)} copy-done((bf16[1552,128]{1,0:T(8,128)(2,1)S(1)}, bf16[1552,128]{1,0:T(8,128)(2,1)}, u32[]{:S(2)}) %copy-start.5) | copy-done | bytes 397336
  19.2 2.6 %shard_map.92.refs_0_ = bf16[512,2048]{1,0:T(8,128)(2,1)S(1)} custom-call(s32[4]{0:T(128)S(1)} %pad_add_fusion.place_ref, bf16[512,4096]{1,0:T(8,128)(2,1)S(1)} %copy-done, f32[1,4096]{1,0:T(1,128)S(1)} %bitcast.21, bf16[512,4096]{1,0:T(8,128)(2,1)S(1)} %copy-done, bf16[1552,128]{1,0:T(8,128)(2,1)S(1)} %collective-permute-done.pair_ref.refs_3_, ...), custom_call_target="tpu_custom_call" | custom-call | tf_op jit(solution)/shard_map/pallas_call | solution.py:620
  21.8 3.1 %collective-permute-done.2.refs_4_ = bf16[1552,128]{1,0:T(8,128)(2,1)S(1)} collective-permute-done((bf16[1552,128]{1,0:T(8,128)(2,1)}, bf16[1552,128]{1,0:T(8,128)(2,1)S(1)}, u32[]{:S(2)}, u32[]{:S(2)}) %collective-permute-start.2) | collective-permute-done | bytes 397344 | tf_op jit(solution)/shard_map/ppermute | solution.py:164
  24.9 1.4 %collective-permute-done.1.refs_2_ = bf16[1552,128]{1,0:T(8,128)(2,1)S(1)} collective-permute-done((bf16[1552,128]{1,0:T(8,128)(2,1)}, bf16[1552,128]{1,0:T(8,128)(2,1)S(1)}, u32[]{:S(2)}, u32[]{:S(2)}) %collective-permute-start.1) | collective-permute-done | bytes 397344 | tf_op jit(solution)/shard_map/ppermute | solution.py:164
  26.3 0.9 %shard_map.93 = (f32[512,128]{1,0:T(8,128)S(1)}, bf16[528,128]{1,0:T(8,128)(2,1)S(1)}) custom-call(bf16[512,2048]{1,0:T(8,128)(2,1)S(1)} %shard_map.92.refs_0_, bf16[1552,128]{1,0:T(8,128)(2,1)S(1)} %copy-done.3, bf16[1552,128]{1,0:T(8,128)(2,1)S(1)} %collective-permute-done.1.refs_2_, bf16[1552,128]{1,0:T(8,128)(2,1)S(1)} %collective-permute-done.pair_ref.refs_3_, ...), custom_call_target="tpu_custom_call" | custom-call | tf_op jit(solution)/shard_map/pallas_call | solution.py:529
  27.2 2.7 %collective-permute-start.3 = (bf16[528,128]{1,0:T(8,128)(2,1)S(1)}, bf16[528,128]{1,0:T(8,128)(2,1)S(1)}, u32[]{:S(2)}, u32[]{:S(2)}) collective-permute-start(bf16[528,128]{1,0:T(8,128)(2,1)S(1)} %get-tuple-element.33.refs_4_.refs_0_), channel_id=1, source_target_pairs={{0,8},{2,10},{4,12},{6,14},{8,0},{10,2},{12,4},{14,6},{1,9},{3,11}... | collective-permute-start | bytes 405512 | tf_op jit(solution)/shard_map/ppermute | solution.py:164
  29.9 0.8 shard_map.98
  30.7 0.4 collective-permute-start.7
  31.1 1.5 %shard_map.95 = (bf16[128,2560]{1,0:T(8,128)(2,1)S(1)}, f32[160,128]{1,0:T(8,128)S(1)}) custom-call(f32[16,64]{1,0:T(8,128)S(1)} %bitcast.20, f32[16,64]{1,0:T(8,128)S(1)} %multiply_bitcast_fusion.refs_1_, f32[3,3,64]{2,1,0:T(4,128)S(1)} %bitcast.22, f32[8,128]{1,0:T(8,128)S(1)} %bitcast.23, bf16[528,128]{1,0:T(8,128)(2,1)S(1)} %get-tuple-element.33.refs_4_.refs_0_, ...), custom_call_target="tpu_custom_call" | custom-call | tf_op jit(solution)/shard_map/pallas_call | solution.py:529
  32.7 3.2 %collective-permute-done.3.refs_1_ = bf16[528,128]{1,0:T(8,128)(2,1)S(1)} collective-permute-done((bf16[528,128]{1,0:T(8,128)(2,1)S(1)}, bf16[528,128]{1,0:T(8,128)(2,1)S(1)}, u32[]{:S(2)}, u32[]{:S(2)}) %collective-permute-start.3) | collective-permute-done | bytes 135200 | tf_op jit(solution)/shard_map/ppermute | solution.py:164
  35.9 1.6 %collective-permute-start.6 = (bf16[2,256,128]{2,1,0:T(8,128)(2,1)S(1)}, bf16[2,256,128]{2,1,0:T(8,128)(2,1)S(1)}, u32[]{:S(2)}, u32[]{:S(2)}) collective-permute-start(bf16[2,256,128]{2,1,0:T(8,128)(2,1)S(1)} %shard_map.96.refs_2_.refs_1_), channel_id=1, source_target_pairs={{0,16},{16,0},{1,17},{17,1},{2,18},{18,2},{3,19},{19,3},{4,20},{20... | collective-permute-start | bytes 393224 | tf_op jit(solution)/shard_map/ppermute | solution.py:164
  37.5 5.7 %collective-permute-start.16 = (bf16[256,512]{1,0:T(8,128)(2,1)S(1)}, bf16[256,512]{1,0:T(8,128)(2,1)S(1)}, u32[]{:S(2)}, u32[]{:S(2)}) collective-permute-start(bf16[256,512]{1,0:T(8,128)(2,1)S(1)} %shard_map.100), channel_id=1, source_target_pairs={{0,12},{2,14},{12,0},{14,2},{1,13},{3,15},{13,1},{15,3},{16,28},{1... | collective-permute-start | bytes 786440 | tf_op jit(solution)/shard_map/ppermute | solution.py:713
  43.2 1.9 %collective-permute-start.17 = (bf16[256,512]{1,0:T(8,128)(2,1)S(1)}, bf16[256,512]{1,0:T(8,128)(2,1)S(1)}, u32[]{:S(2)}, u32[]{:S(2)}) collective-permute-start(bf16[256,512]{1,0:T(8,128)(2,1)S(1)} %shard_map.101), channel_id=1, source_target_pairs={{0,12},{2,14},{12,0},{14,2},{1,13},{3,15},{13,1},{15,3},{16,28},{1... | collective-permute-start | bytes 786440 | tf_op jit(solution)/shard_map/ppermute | solution.py:713
  45.2 0.6 collective-permute-start.8
  45.8 2.7 %shard_map.97 = (f32[1024,128]{1,0:T(8,128)S(1)}, bf16[1024,512]{1,0:T(8,128)(2,1)S(1)}) custom-call(bf16[528,128]{1,0:T(8,128)(2,1)S(1)} %get-tuple-element.33.refs_4_.refs_0_, bf16[528,128]{1,0:T(8,128)(2,1)S(1)} %collective-permute-done.3.refs_1_, bf16[2,256,128]{2,1,0:T(8,128)(2,1)S(1)} %shard_map.96.refs_2_.refs_1_, ...), custom_call_target="tpu_custom_call" | custom-call | tf_op jit(solution)/shard_map/pallas_call | solution.py:529
  48.5 1.0 %collective-permute-done.8.refs_2_ = bf16[1,256,128]{2,1,0:T(8,128)(2,1)S(1)} collective-permute-done((bf16[1,256,128]{2,1,0:T(8,128)(2,1)S(1)}, bf16[1,256,128]{2,1,0:T(8,128)(2,1)S(1)}, u32[]{:S(2)}, u32[]{:S(2)}) %collective-permute-start.8) | collective-permute-done | bytes 65568 | tf_op jit(solution)/shard_map/ppermute | solution.py:164
  49.5 0.5 shard_map.99
  50.2 2.7 %collective-permute-start.11 = (bf16[256,128]{1,0:T(8,128)(2,1)S(1)}, bf16[256,128]{1,0:T(8,128)(2,1)S(1)}, u32[]{:S(2)}, u32[]{:S(2)}) collective-permute-start(bf16[256,128]{1,0:T(8,128)(2,1)S(1)} %get-tuple-element.47), channel_id=1, source_target_pairs={{0,9},{1,8},{2,11},{3,10},{4,13},{5,12},{6,15},{7,14},{8,1},{9,0},... | collective-permute-start | bytes 196616 | tf_op jit(solution)/shard_map/ppermute | solution.py:172
  52.9 4.5 %collective-permute-done.10 = bf16[256,128]{1,0:T(8,128)(2,1)S(1)} collective-permute-done((bf16[256,128]{1,0:T(8,128)(2,1)S(1)}, bf16[256,128]{1,0:T(8,128)(2,1)S(1)}, u32[]{:S(2)}, u32[]{:S(2)}) %collective-permute-start.10) | collective-permute-done | bytes 65568 | tf_op jit(solution)/shard_map/ppermute | solution.py:164
  57.4 0.5 collective-permute-done.11
  58.1 0.6 collective-permute-start.19
  58.7 1.4 %collective-permute-start.15 = (bf16[1024,512]{1,0:T(8,128)(2,1)S(1)}, bf16[1024,512]{1,0:T(8,128)(2,1)S(1)}, u32[]{:S(2)}, u32[]{:S(2)}) collective-permute-start(bf16[1024,512]{1,0:T(8,128)(2,1)S(1)} %copy-done.2), channel_id=1, source_target_pairs={{0,1},{1,0},{2,3},{3,2},{4,5},{5,4},{6,7},{7,6},{8,9},{9,8},{10,11... | collective-permute-start | bytes 3145736 | tf_op jit(solution)/shard_map/ppermute | solution.py:164
  60.1 0.5 collective-permute-start.12
  61.0 2.7 %collective-permute-start.14 = (bf16[4,256,128]{2,1,0:T(8,128)(2,1)S(1)}, bf16[4,256,128]{2,1,0:T(8,128)(2,1)S(1)}, u32[]{:S(2)}, u32[]{:S(2)}) collective-permute-start(bf16[4,256,128]{2,1,0:T(8,128)(2,1)S(1)} %pad_maximum_fusion.refs_1_.refs_2_), channel_id=1, source_target_pairs={{0,6},{2,4},{4,2},{6,0},{8,14},{10,12},{12,10},{14,8},{1,7},{3,5},... | collective-permute-start | bytes 786440 | tf_op jit(solution)/shard_map/ppermute | solution.py:164
  63.6 4.8 %collective-permute-done.12.refs_3_.refs_1_ = bf16[4,256,128]{2,1,0:T(8,128)(2,1)S(1)} collective-permute-done((bf16[4,256,128]{2,1,0:T(8,128)(2,1)S(1)}, bf16[4,256,128]{2,1,0:T(8,128)(2,1)S(1)}, u32[]{:S(2)}, u32[]{:S(2)}) %collective-permute-start.12) | collective-permute-done | bytes 262176 | tf_op jit(solution)/shard_map/ppermute | solution.py:164
  68.4 3.9 %collective-permute-done.19.refs_0_ = bf16[512,512]{1,0:T(8,128)(2,1)S(1)} collective-permute-done((bf16[512,512]{1,0:T(8,128)(2,1)S(1)}, bf16[512,512]{1,0:T(8,128)(2,1)S(1)}, u32[]{:S(2)}, u32[]{:S(2)}) %collective-permute-start.19) | collective-permute-done | bytes 524320 | tf_op jit(solution)/shard_map/ppermute | solution.py:164
  72.3 2.8 %collective-permute-done.14.refs_5_.refs_1_ = bf16[4,256,128]{2,1,0:T(8,128)(2,1)S(1)} collective-permute-done((bf16[4,256,128]{2,1,0:T(8,128)(2,1)S(1)}, bf16[4,256,128]{2,1,0:T(8,128)(2,1)S(1)}, u32[]{:S(2)}, u32[]{:S(2)}) %collective-permute-start.14) | collective-permute-done | bytes 262176 | tf_op jit(solution)/shard_map/ppermute | solution.py:164
  75.2 1.7 %shard_map.103 = (bf16[256,512]{1,0:T(8,128)(2,1)S(1)}, f32[256,512]{1,0:T(8,128)S(1)}, bf16[8,256,256]{2,1,0:T(8,128)(2,1)S(1)}) custom-call(bf16[256,512]{1,0:T(8,128)(2,1)S(1)} %get-tuple-element.43.refs_0_, bf16[512,4096]{1,0:T(8,128)(2,1)S(1)} %copy-done.1, bf16[4,256,128]{2,1,0:T(8,128)(2,1)S(1)} %pad_maximum_fusion.refs_1_.refs_2_, ...), custom_call_target="tpu_custom_call" | custom-call | tf_op jit(solution)/shard_map/pallas_call | solution.py:529
  77.1 0.4 shard_map.107
  77.5 0.4 collective-permute-start.24
  77.9 0.8 collective-permute-start.23
  78.8 1.2 %collective-permute-start.22 = (bf16[64,512]{1,0:T(8,128)(2,1)S(1)}, bf16[64,512]{1,0:T(8,128)(2,1)S(1)}, u32[]{:S(2)}, u32[]{:S(2)}) collective-permute-start(bf16[64,512]{1,0:T(8,128)(2,1)S(1)} %get-tuple-element.58), channel_id=1, source_target_pairs={{0,4},{2,6},{4,0},{6,2},{8,12},{10,14},{12,8},{14,10},{1,5},{3,7},... | collective-permute-start | bytes 196616 | tf_op jit(solution)/shard_map/ppermute | solution.py:164
  80.0 1.5 %collective-permute-start.21 = (bf16[64,512]{1,0:T(8,128)(2,1)S(1)}, bf16[64,512]{1,0:T(8,128)(2,1)S(1)}, u32[]{:S(2)}, u32[]{:S(2)}) collective-permute-start(bf16[64,512]{1,0:T(8,128)(2,1)S(1)} %get-tuple-element.59), channel_id=1, source_target_pairs={{0,2},{2,0},{4,6},{6,4},{8,10},{10,8},{12,14},{14,12},{1,3},{3,1},... | collective-permute-start | bytes 196616 | tf_op jit(solution)/shard_map/ppermute | solution.py:164
  81.5 0.8 collective-permute-start.27
  82.3 1.2 %collective-permute-start.26 = (bf16[64,512]{1,0:T(8,128)(2,1)S(1)}, bf16[64,512]{1,0:T(8,128)(2,1)S(1)}, u32[]{:S(2)}, u32[]{:S(2)}) collective-permute-start(bf16[64,512]{1,0:T(8,128)(2,1)S(1)} %get-tuple-element.54), channel_id=1, source_target_pairs={{0,4},{2,6},{4,0},{6,2},{8,12},{10,14},{12,8},{14,10},{1,5},{3,7},... | collective-permute-start | bytes 196616 | tf_op jit(solution)/shard_map/ppermute | solution.py:164
  83.8 1.3 %collective-permute-start.25 = (bf16[64,512]{1,0:T(8,128)(2,1)S(1)}, bf16[64,512]{1,0:T(8,128)(2,1)S(1)}, u32[]{:S(2)}, u32[]{:S(2)}) collective-permute-start(bf16[64,512]{1,0:T(8,128)(2,1)S(1)} %get-tuple-element.55), channel_id=1, source_target_pairs={{0,2},{2,0},{4,6},{6,4},{8,10},{10,8},{12,14},{14,12},{1,3},{3,1},... | collective-permute-start | bytes 196616 | tf_op jit(solution)/shard_map/ppermute | solution.py:164
  85.1 1.7 %collective-permute-done.27.refs_7_ = bf16[64,512]{1,0:T(8,128)(2,1)S(1)} collective-permute-done((bf16[64,512]{1,0:T(8,128)(2,1)S(1)}, bf16[64,512]{1,0:T(8,128)(2,1)S(1)}, u32[]{:S(2)}, u32[]{:S(2)}) %collective-permute-start.27) | collective-permute-done | bytes 65568 | tf_op jit(solution)/shard_map/ppermute | solution.py:164
  86.7 1.3 %collective-permute-done.25.refs_5_ = bf16[64,512]{1,0:T(8,128)(2,1)S(1)} collective-permute-done((bf16[64,512]{1,0:T(8,128)(2,1)S(1)}, bf16[64,512]{1,0:T(8,128)(2,1)S(1)}, u32[]{:S(2)}, u32[]{:S(2)}) %collective-permute-start.25) | collective-permute-done | bytes 65568 | tf_op jit(solution)/shard_map/ppermute | solution.py:164
  88.0 0.8 shard_map.108
  (56 shorter events, 1.5 us)
Async XLA Ops:
  0.0 7.4 %copy-start.2 = (bf16[1024,512]{1,0:T(8,128)(2,1)S(1)}, bf16[1024,512]{1,0:T(8,128)(2,1)}, u32[]{:S(2)}) copy-start(bf16[1024,512]{1,0:T(8,128)(2,1)} %refs_6_.1) | copy-start | bytes 3145732
  0.0 16.0 %copy-start.7 = (f32[4096]{0:T(1024)S(1)}, f32[4096]{0:T(1024)}, u32[]{:S(2)}) copy-start(f32[4096]{0:T(1024)} %param.11) | copy-start | bytes 49156
  2.7 13.3 %collective-permute-start = (bf16[1552,128]{1,0:T(8,128)(2,1)}, bf16[1552,128]{1,0:T(8,128)(2,1)S(1)}, u32[]{:S(2)}, u32[]{:S(2)}) collective-permute-start(bf16[1552,128]{1,0:T(8,128)(2,1)} %get-tuple-element.29), channel_id=1, source_target_pairs={{0,4},{2,6},{4,0},{6,2},{8,12},{10,14},{12,8},{14,10},{1,5},{3,7},... | collective-permute-start | bytes 1191944 | tf_op jit(solution)/shard_map/ppermute | solution.py:164
  5.8 19.2 %collective-permute-start.2 = (bf16[1552,128]{1,0:T(8,128)(2,1)}, bf16[1552,128]{1,0:T(8,128)(2,1)S(1)}, u32[]{:S(2)}, u32[]{:S(2)}) collective-permute-start(bf16[1552,128]{1,0:T(8,128)(2,1)} %get-tuple-element.32), channel_id=1, source_target_pairs={{0,6},{2,4},{4,2},{6,0},{8,14},{10,12},{12,10},{14,8},{1,7},{3,5},... | collective-permute-start | bytes 1191944 | tf_op jit(solution)/shard_map/ppermute | solution.py:164
  7.2 19.1 %collective-permute-start.1 = (bf16[1552,128]{1,0:T(8,128)(2,1)}, bf16[1552,128]{1,0:T(8,128)(2,1)S(1)}, u32[]{:S(2)}, u32[]{:S(2)}) collective-permute-start(bf16[1552,128]{1,0:T(8,128)(2,1)} %get-tuple-element.30.query_ref.packed_ref), channel_id=1, source_target_pairs={{0,2},{2,0},{4,6},{6,4},{8,10},{10,8},{12,14},{14,12},{1,3},{3,1},... | collective-permute-start | bytes 1191944 | tf_op jit(solution)/shard_map/ppermute | solution.py:164
  7.4 1.0 %copy-start.4 = (bf16[1552,128]{1,0:T(8,128)(2,1)S(1)}, bf16[1552,128]{1,0:T(8,128)(2,1)}, u32[]{:S(2)}) copy-start(bf16[1552,128]{1,0:T(8,128)(2,1)} %get-tuple-element.30.query_ref.packed_ref) | copy-start | bytes 1191940
  9.0 22.2 %collective-permute-start.4 = (bf16[256,512]{1,0:T(8,128)(2,1)S(1)}, bf16[256,512]{1,0:T(8,128)(2,1)S(1)}, u32[]{:S(2)}, u32[]{:S(2)}) collective-permute-start(bf16[256,512]{1,0:T(8,128)(2,1)S(1)} %get-tuple-element.35.refs_0_), channel_id=1, source_target_pairs={{4,8},{6,10},{8,4},{10,6},{5,9},{7,11},{9,5},{11,7},{20,24},{22,26... | collective-permute-start | bytes 786440 | tf_op jit(solution)/shard_map/ppermute | solution.py:638
  9.6 21.5 %collective-permute-start.5 = (bf16[256,512]{1,0:T(8,128)(2,1)S(1)}, bf16[256,512]{1,0:T(8,128)(2,1)S(1)}, u32[]{:S(2)}, u32[]{:S(2)}) collective-permute-start(bf16[256,512]{1,0:T(8,128)(2,1)S(1)} %get-tuple-element.36.refs_0_), channel_id=1, source_target_pairs={{4,8},{6,10},{8,4},{10,6},{5,9},{7,11},{9,5},{11,7},{20,24},{22,26... | collective-permute-start | bytes 786440 | tf_op jit(solution)/shard_map/ppermute | solution.py:638
  16.0 2.2 %copy-start = (bf16[512,4096]{1,0:T(8,128)(2,1)S(1)}, bf16[512,4096]{1,0:T(8,128)(2,1)}, u32[]{:S(2)}) copy-start(bf16[512,4096]{1,0:T(8,128)(2,1)} %refs_1_.1) | copy-start | bytes 12582916
  18.2 1.0 %copy-start.5 = (bf16[1552,128]{1,0:T(8,128)(2,1)S(1)}, bf16[1552,128]{1,0:T(8,128)(2,1)}, u32[]{:S(2)}) copy-start(bf16[1552,128]{1,0:T(8,128)(2,1)} %get-tuple-element.30.query_ref.packed_ref) | copy-start | bytes 1191940
  19.2 7.1 %copy-start.3 = (bf16[1552,128]{1,0:T(8,128)(2,1)S(1)}, bf16[1552,128]{1,0:T(8,128)(2,1)}, u32[]{:S(2)}) copy-start(bf16[1552,128]{1,0:T(8,128)(2,1)} %get-tuple-element.31.refs_1_) | copy-start | bytes 1191940
  21.8 8.1 %copy-start.6 = (f32[64,16]{0,1:T(8,128)S(1)}, f32[64,16]{0,1:T(8,128)}, u32[]{:S(2)}) copy-start(f32[64,16]{0,1:T(8,128)} %param.14) | copy-start | bytes 12292
  21.8 8.0 %copy-start.10 = (f32[64,16]{0,1:T(8,128)S(1)}, f32[64,16]{0,1:T(8,128)}, u32[]{:S(2)}) copy-start(f32[64,16]{0,1:T(8,128)} %param.15) | copy-start | bytes 12292
  26.3 4.9 %copy-start.8 = (f32[3,64,3]{1,2,0:T(4,128)S(1)}, f32[3,64,3]{1,2,0:T(4,128)}, u32[]{:S(2)}) copy-start(f32[3,64,3]{1,2,0:T(4,128)} %param.13) | copy-start | bytes 6916
  26.3 4.9 %copy-start.9 = (f32[1024]{0:T(1024)S(1)}, f32[1024]{0:T(1024)}, u32[]{:S(2)}) copy-start(f32[1024]{0:T(1024)} %param.16) | copy-start | bytes 12292
  27.2 8.7 %collective-permute-start.3 = (bf16[528,128]{1,0:T(8,128)(2,1)S(1)}, bf16[528,128]{1,0:T(8,128)(2,1)S(1)}, u32[]{:S(2)}, u32[]{:S(2)}) collective-permute-start(bf16[528,128]{1,0:T(8,128)(2,1)S(1)} %get-tuple-element.33.refs_4_.refs_0_), channel_id=1, source_target_pairs={{0,8},{2,10},{4,12},{6,14},{8,0},{10,2},{12,4},{14,6},{1,9},{3,11}... | collective-permute-start | bytes 405512 | tf_op jit(solution)/shard_map/ppermute | solution.py:164
  30.7 14.4 %collective-permute-start.7 = (bf16[256,128]{1,0:T(8,128)(2,1)S(1)}, bf16[256,128]{1,0:T(8,128)(2,1)S(1)}, u32[]{:S(2)}, u32[]{:S(2)}) collective-permute-start(bf16[256,128]{1,0:T(8,128)(2,1)S(1)} %get-tuple-element.41), channel_id=1, source_target_pairs={{0,8},{2,10},{4,12},{6,14},{8,0},{10,2},{12,4},{14,6},{1,9},{3,11}... | collective-permute-start | bytes 196616 | tf_op jit(solution)/shard_map/ppermute | solution.py:164
  35.9 9.9 %collective-permute-start.6 = (bf16[2,256,128]{2,1,0:T(8,128)(2,1)S(1)}, bf16[2,256,128]{2,1,0:T(8,128)(2,1)S(1)}, u32[]{:S(2)}, u32[]{:S(2)}) collective-permute-start(bf16[2,256,128]{2,1,0:T(8,128)(2,1)S(1)} %shard_map.96.refs_2_.refs_1_), channel_id=1, source_target_pairs={{0,16},{16,0},{1,17},{17,1},{2,18},{18,2},{3,19},{19,3},{4,20},{20... | collective-permute-start | bytes 393224 | tf_op jit(solution)/shard_map/ppermute | solution.py:164
  37.5 20.5 %collective-permute-start.16 = (bf16[256,512]{1,0:T(8,128)(2,1)S(1)}, bf16[256,512]{1,0:T(8,128)(2,1)S(1)}, u32[]{:S(2)}, u32[]{:S(2)}) collective-permute-start(bf16[256,512]{1,0:T(8,128)(2,1)S(1)} %shard_map.100), channel_id=1, source_target_pairs={{0,12},{2,14},{12,0},{14,2},{1,13},{3,15},{13,1},{15,3},{16,28},{1... | collective-permute-start | bytes 786440 | tf_op jit(solution)/shard_map/ppermute | solution.py:713
  43.2 14.8 %collective-permute-start.17 = (bf16[256,512]{1,0:T(8,128)(2,1)S(1)}, bf16[256,512]{1,0:T(8,128)(2,1)S(1)}, u32[]{:S(2)}, u32[]{:S(2)}) collective-permute-start(bf16[256,512]{1,0:T(8,128)(2,1)S(1)} %shard_map.101), channel_id=1, source_target_pairs={{0,12},{2,14},{12,0},{14,2},{1,13},{3,15},{13,1},{15,3},{16,28},{1... | collective-permute-start | bytes 786440 | tf_op jit(solution)/shard_map/ppermute | solution.py:713
  45.2 4.3 %collective-permute-start.8 = (bf16[1,256,128]{2,1,0:T(8,128)(2,1)S(1)}, bf16[1,256,128]{2,1,0:T(8,128)(2,1)S(1)}, u32[]{:S(2)}, u32[]{:S(2)}) collective-permute-start(bf16[1,256,128]{2,1,0:T(8,128)(2,1)S(1)} %fusion.refs_1_), channel_id=1, source_target_pairs={{0,16},{16,0},{1,17},{17,1},{2,18},{18,2},{3,19},{19,3},{4,20},{20... | collective-permute-start | bytes 196616 | tf_op jit(solution)/shard_map/ppermute | solution.py:164
  50.1 2.8 %collective-permute-start.9 = (bf16[256,128]{1,0:T(8,128)(2,1)S(1)}, bf16[256,128]{1,0:T(8,128)(2,1)S(1)}, u32[]{:S(2)}, u32[]{:S(2)}) collective-permute-start(bf16[256,128]{1,0:T(8,128)(2,1)S(1)} %get-tuple-element.45), channel_id=1, source_target_pairs={{0,1},{1,0},{2,3},{3,2},{4,5},{5,4},{6,7},{7,6},{8,9},{9,8},{10,11... | collective-permute-start | bytes 196616 | tf_op jit(solution)/shard_map/ppermute | solution.py:164
  50.1 7.3 %collective-permute-start.10 = (bf16[256,128]{1,0:T(8,128)(2,1)S(1)}, bf16[256,128]{1,0:T(8,128)(2,1)S(1)}, u32[]{:S(2)}, u32[]{:S(2)}) collective-permute-start(bf16[256,128]{1,0:T(8,128)(2,1)S(1)} %get-tuple-element.46), channel_id=1, source_target_pairs={{0,8},{2,10},{4,12},{6,14},{8,0},{10,2},{12,4},{14,6},{1,9},{3,11}... | collective-permute-start | bytes 196616 | tf_op jit(solution)/shard_map/ppermute | solution.py:164
  50.2 7.7 %collective-permute-start.11 = (bf16[256,128]{1,0:T(8,128)(2,1)S(1)}, bf16[256,128]{1,0:T(8,128)(2,1)S(1)}, u32[]{:S(2)}, u32[]{:S(2)}) collective-permute-start(bf16[256,128]{1,0:T(8,128)(2,1)S(1)} %get-tuple-element.47), channel_id=1, source_target_pairs={{0,9},{1,8},{2,11},{3,10},{4,13},{5,12},{6,15},{7,14},{8,1},{9,0},... | collective-permute-start | bytes 196616 | tf_op jit(solution)/shard_map/ppermute | solution.py:172
  57.9 17.2 %copy-start.1 = (bf16[512,4096]{1,0:T(8,128)(2,1)S(1)}, bf16[512,4096]{1,0:T(8,128)(2,1)}, u32[]{:S(2)}) copy-start(bf16[512,4096]{1,0:T(8,128)(2,1)} %refs_1_.1) | copy-start | bytes 12582916
  58.1 14.2 %collective-permute-start.19 = (bf16[512,512]{1,0:T(8,128)(2,1)S(1)}, bf16[512,512]{1,0:T(8,128)(2,1)S(1)}, u32[]{:S(2)}, u32[]{:S(2)}) collective-permute-start(bf16[512,512]{1,0:T(8,128)(2,1)S(1)} %shard_map.102.refs_8_), channel_id=1, source_target_pairs={{0,16},{16,0},{1,17},{17,1},{2,18},{18,2},{3,19},{19,3},{4,20},{20... | collective-permute-start | bytes 1572872 | tf_op jit(solution)/shard_map/ppermute | solution.py:164
  58.7 16.4 %collective-permute-start.15 = (bf16[1024,512]{1,0:T(8,128)(2,1)S(1)}, bf16[1024,512]{1,0:T(8,128)(2,1)S(1)}, u32[]{:S(2)}, u32[]{:S(2)}) collective-permute-start(bf16[1024,512]{1,0:T(8,128)(2,1)S(1)} %copy-done.2), channel_id=1, source_target_pairs={{0,1},{1,0},{2,3},{3,2},{4,5},{5,4},{6,7},{7,6},{8,9},{9,8},{10,11... | collective-permute-start | bytes 3145736 | tf_op jit(solution)/shard_map/ppermute | solution.py:164
  60.1 8.3 %collective-permute-start.12 = (bf16[4,256,128]{2,1,0:T(8,128)(2,1)S(1)}, bf16[4,256,128]{2,1,0:T(8,128)(2,1)S(1)}, u32[]{:S(2)}, u32[]{:S(2)}) collective-permute-start(bf16[4,256,128]{2,1,0:T(8,128)(2,1)S(1)} %pad_maximum_fusion.refs_1_.refs_2_), channel_id=1, source_target_pairs={{0,2},{2,0},{4,6},{6,4},{8,10},{10,8},{12,14},{14,12},{1,3},{3,1},... | collective-permute-start | bytes 786440 | tf_op jit(solution)/shard_map/ppermute | solution.py:164
  60.6 11.7 %collective-permute-start.13 = (bf16[4,256,128]{2,1,0:T(8,128)(2,1)S(1)}, bf16[4,256,128]{2,1,0:T(8,128)(2,1)S(1)}, u32[]{:S(2)}, u32[]{:S(2)}) collective-permute-start(bf16[4,256,128]{2,1,0:T(8,128)(2,1)S(1)} %pad_maximum_fusion.refs_1_.refs_2_), channel_id=1, source_target_pairs={{0,4},{2,6},{4,0},{6,2},{8,12},{10,14},{12,8},{14,10},{1,5},{3,7},... | collective-permute-start | bytes 786440 | tf_op jit(solution)/shard_map/ppermute | solution.py:164
  61.0 14.2 %collective-permute-start.14 = (bf16[4,256,128]{2,1,0:T(8,128)(2,1)S(1)}, bf16[4,256,128]{2,1,0:T(8,128)(2,1)S(1)}, u32[]{:S(2)}, u32[]{:S(2)}) collective-permute-start(bf16[4,256,128]{2,1,0:T(8,128)(2,1)S(1)} %pad_maximum_fusion.refs_1_.refs_2_), channel_id=1, source_target_pairs={{0,6},{2,4},{4,2},{6,0},{8,14},{10,12},{12,10},{14,8},{1,7},{3,5},... | collective-permute-start | bytes 786440 | tf_op jit(solution)/shard_map/ppermute | solution.py:164
  68.4 6.7 %collective-permute-start.18 = (bf16[512,512]{1,0:T(8,128)(2,1)S(1)}, bf16[512,512]{1,0:T(8,128)(2,1)S(1)}, u32[]{:S(2)}, u32[]{:S(2)}) collective-permute-start(bf16[512,512]{1,0:T(8,128)(2,1)S(1)} %shard_map.102.refs_8_), channel_id=1, source_target_pairs={{0,1},{1,0},{2,3},{3,2},{4,5},{5,4},{6,7},{7,6},{8,9},{9,8},{10,11... | collective-permute-start | bytes 1572872 | tf_op jit(solution)/shard_map/ppermute | solution.py:164
  75.1 1.9 %collective-permute-start.20 = (bf16[512,512]{1,0:T(8,128)(2,1)S(1)}, bf16[512,512]{1,0:T(8,128)(2,1)S(1)}, u32[]{:S(2)}, u32[]{:S(2)}) collective-permute-start(bf16[512,512]{1,0:T(8,128)(2,1)S(1)} %shard_map.106.refs_3_), channel_id=1, source_target_pairs={{0,1},{1,0},{2,3},{3,2},{4,5},{5,4},{6,7},{7,6},{8,9},{9,8},{10,11... | collective-permute-start | bytes 1572872 | tf_op jit(solution)/shard_map/ppermute | solution.py:164
  77.5 4.0 %collective-permute-start.24 = (bf16[256,512]{1,0:T(8,128)(2,1)S(1)}, bf16[256,512]{1,0:T(8,128)(2,1)S(1)}, u32[]{:S(2)}, u32[]{:S(2)}) collective-permute-start(bf16[256,512]{1,0:T(8,128)(2,1)S(1)} %get-tuple-element.52), channel_id=1, source_target_pairs={{0,1},{1,0},{2,3},{3,2},{4,5},{5,4},{6,7},{7,6},{8,9},{9,8},{10,11... | collective-permute-start | bytes 786440 | tf_op jit(solution)/shard_map/ppermute | solution.py:164
  77.9 5.8 %collective-permute-start.23 = (bf16[64,512]{1,0:T(8,128)(2,1)S(1)}, bf16[64,512]{1,0:T(8,128)(2,1)S(1)}, u32[]{:S(2)}, u32[]{:S(2)}) collective-permute-start(bf16[64,512]{1,0:T(8,128)(2,1)S(1)} %get-tuple-element.57), channel_id=1, source_target_pairs={{0,6},{2,4},{4,2},{6,0},{8,14},{10,12},{12,10},{14,8},{1,7},{3,5},... | collective-permute-start | bytes 196616 | tf_op jit(solution)/shard_map/ppermute | solution.py:164
  78.8 6.3 %collective-permute-start.22 = (bf16[64,512]{1,0:T(8,128)(2,1)S(1)}, bf16[64,512]{1,0:T(8,128)(2,1)S(1)}, u32[]{:S(2)}, u32[]{:S(2)}) collective-permute-start(bf16[64,512]{1,0:T(8,128)(2,1)S(1)} %get-tuple-element.58), channel_id=1, source_target_pairs={{0,4},{2,6},{4,0},{6,2},{8,12},{10,14},{12,8},{14,10},{1,5},{3,7},... | collective-permute-start | bytes 196616 | tf_op jit(solution)/shard_map/ppermute | solution.py:164
  80.0 5.1 %collective-permute-start.21 = (bf16[64,512]{1,0:T(8,128)(2,1)S(1)}, bf16[64,512]{1,0:T(8,128)(2,1)S(1)}, u32[]{:S(2)}, u32[]{:S(2)}) collective-permute-start(bf16[64,512]{1,0:T(8,128)(2,1)S(1)} %get-tuple-element.59), channel_id=1, source_target_pairs={{0,2},{2,0},{4,6},{6,4},{8,10},{10,8},{12,14},{14,12},{1,3},{3,1},... | collective-permute-start | bytes 196616 | tf_op jit(solution)/shard_map/ppermute | solution.py:164
  81.5 5.2 %collective-permute-start.27 = (bf16[64,512]{1,0:T(8,128)(2,1)S(1)}, bf16[64,512]{1,0:T(8,128)(2,1)S(1)}, u32[]{:S(2)}, u32[]{:S(2)}) collective-permute-start(bf16[64,512]{1,0:T(8,128)(2,1)S(1)} %get-tuple-element.53), channel_id=1, source_target_pairs={{0,6},{2,4},{4,2},{6,0},{8,14},{10,12},{12,10},{14,8},{1,7},{3,5},... | collective-permute-start | bytes 196616 | tf_op jit(solution)/shard_map/ppermute | solution.py:164
  82.3 4.4 %collective-permute-start.26 = (bf16[64,512]{1,0:T(8,128)(2,1)S(1)}, bf16[64,512]{1,0:T(8,128)(2,1)S(1)}, u32[]{:S(2)}, u32[]{:S(2)}) collective-permute-start(bf16[64,512]{1,0:T(8,128)(2,1)S(1)} %get-tuple-element.54), channel_id=1, source_target_pairs={{0,4},{2,6},{4,0},{6,2},{8,12},{10,14},{12,8},{14,10},{1,5},{3,7},... | collective-permute-start | bytes 196616 | tf_op jit(solution)/shard_map/ppermute | solution.py:164
  83.8 4.3 %collective-permute-start.25 = (bf16[64,512]{1,0:T(8,128)(2,1)S(1)}, bf16[64,512]{1,0:T(8,128)(2,1)S(1)}, u32[]{:S(2)}, u32[]{:S(2)}) collective-permute-start(bf16[64,512]{1,0:T(8,128)(2,1)S(1)} %get-tuple-element.55), channel_id=1, source_target_pairs={{0,2},{2,0},{4,6},{6,4},{8,10},{10,8},{12,14},{14,12},{1,3},{3,1},... | collective-permute-start | bytes 196616 | tf_op jit(solution)/shard_map/ppermute | solution.py:164
